TPU v7x, 512 devices: a whole 4x8x8 slice. The times are simulated.
512 devices in a mesh: seq: 64 (over x, y, core), head: 8 (over z).
Axes of the slice: x: 4, y: 8, z: 8, core: 2. Of those that a mesh axis runs over, the one named last changes fastest.
Arguments:
- queries: bfloat16 [8192, 8, 1024], P(('seq', 'head')), may hold values from -256 to 256
- branch_key_value: bfloat16 [8192, 8, 256], P(('seq', 'head')), may hold values from -4 to 4
- branch_ids: int32 [8192], replicated, may hold values from 0 to 3, never falling along the last dimension, each value on 1 to 4096 neighbouring positions
- pool: bfloat16 [64, 16, 8, 256], P('seq', None, 'head'), may hold values from -4 to 4
- page_table: int32 [8, 32], P('head'), may hold values from 0 to 63, as said below
Outputs:
- attended: bfloat16 [8192, 8, 1024], P(('seq', 'head'))
Inputs may be any that keep to these rules, and one draw needn't show every extreme that they name: `branch_ids`: never falls along the rows; each branch covers 1 to 4096 rows and one covers exactly 4096. `page_table`: row h holds 32 distinct page numbers.
All inputs are finite; a program needn't handle non-finite values.
Results may differ from a plain program's by a relative error of at most 0.0085.
Values may be sent and summed in bfloat16 or wider, within the bound.
No kernel may reach another device: no remote copies, remote signals or barrier semaphores. Data moves between devices by JAX's collectives and lax.ppermute only.
A program may use at most 64 MiB of HBM per device.

v0:
```python
import jax
import jax.numpy as jnp
from jax import lax
from jax.sharding import PartitionSpec as P

HEAD_DIM = 128


def passed_along(value, axis, by):
    count = lax.axis_size(axis)
    pairs = [(i, i + by) for i in range(count) if 0 <= i + by < count]
    return lax.ppermute(value, axis, pairs)


def blend_keys(state, query, pairs, allowed, scale):
    top, total, summed = state
    width = query.shape[-1]
    keys = pairs[..., :width]
    value_rows = pairs[..., width:]
    scores = jnp.einsum("rhgd,khd->rhgk", query, keys, preferred_element_type=jnp.float32) * scale
    scores = jnp.where(allowed, scores, -jnp.inf)
    new_top = jnp.maximum(top, jnp.max(scores, axis=-1))
    factor = jnp.exp(top - new_top)
    weights = jnp.exp(scores - new_top[..., None])
    total = total * factor + jnp.sum(weights, axis=-1)
    rounded = weights.astype(jnp.bfloat16)
    summed = summed * factor[..., None] + jnp.einsum(
        "rhgk,khd->rhgd", rounded, value_rows, preferred_element_type=jnp.float32
    )
    return (new_top, total, summed)


def per_device(queries, branch_key_value, branch_ids, pool, page_table):
    reach_count = min(32, lax.axis_size("seq") // 2)
    query, pairs = (
        lax.all_to_all(queries, "head", split_axis=1, concat_axis=0, tiled=True),
        lax.all_to_all(branch_key_value, "head", split_axis=1, concat_axis=0, tiled=True),
    )
    rows = query.shape[0]
    local_heads = query.shape[1]
    group = query.shape[2] // HEAD_DIM
    query = query.reshape(rows, local_heads, group, HEAD_DIM)
    scale = HEAD_DIM ** (-0.5)
    row_start = lax.axis_index("seq") * rows
    row_ids = jnp.arange(rows, dtype=jnp.int32)
    own_ids = lax.dynamic_slice_in_dim(branch_ids, row_start, rows, 0)
    own_rows = row_start + row_ids
    state = (
        jnp.full((rows, local_heads, group), -1e30, jnp.float32),
        jnp.zeros((rows, local_heads, group), jnp.float32),
        jnp.zeros((rows, local_heads, group, HEAD_DIM), jnp.float32),
    )
    page_rows = pool.shape[1]
    pair_width = pool.shape[3]
    piece = lax.all_gather(pool, "seq", axis=0, tiled=True)
    count = piece.shape[0]
    page_ids = jnp.arange(count, dtype=jnp.int32)
    chosen = jnp.any(page_table[:, :, None] == page_ids[None, None, :], axis=1)
    allowed = jnp.broadcast_to(chosen[:, :, None], (local_heads, count, page_rows))
    allowed = allowed.reshape(local_heads, count * page_rows)
    flat = piece.reshape(count * page_rows, local_heads, pair_width)

    def fold_in_piece(inner):
        return blend_keys(inner, query, flat, allowed[None, :, None, :], scale)

    def keep_state(inner):
        return inner

    state = lax.cond(jnp.any(chosen), fold_in_piece, keep_state, state)

    def causal_step(carry, block, back):
        key_start = row_start - back * rows
        key_ids = lax.dynamic_slice_in_dim(branch_ids, jnp.maximum(key_start, 0), rows, 0)
        key_rows = key_start + row_ids
        allowed = (
            (key_ids[None, :] == own_ids[:, None])
            & (key_rows[None, :] <= own_rows[:, None])
            & (key_start >= 0)
        )
        return blend_keys(carry, query, block, allowed[:, None, None, :], scale)

    state = causal_step(state, pairs, 0)
    for back in range(1, reach_count + 1):
        earlier = passed_along(pairs, "seq", back)
        state = causal_step(state, earlier, back)
    top, total, summed = state
    mixed = (
        (summed / total[..., None])
        .astype(jnp.bfloat16)
        .reshape(rows, local_heads, group * HEAD_DIM)
    )
    return lax.all_to_all(mixed, "head", split_axis=0, concat_axis=1, tiled=True)


def solution(mesh):
    return jax.shard_map(
        per_device,
        mesh=mesh,
        in_specs=(
            P(("seq", "head"), None, None),
            P(("seq", "head"), None, None),
            P(),
            P("seq", None, "head", None),
            P("head", None),
        ),
        out_specs=P(("seq", "head"), None, None),
        check_vma=False,
    )
```

profile of v0, /device:TPU:4, one launch (start us, length us, event | category | flops | bytes accessed | tf_op | source)
XLA Modules:
  0.0 262.9 jit_solution(5094621474257380723)
XLA Ops:
  1.5 10.3 %all-to-all-start.1 = ((bf16[16,8,256]{2,0,1:T(8,128)(2,1)}), bf16[16,8,256]{2,0,1:T(8,128)(2,1)S(1)}, u32[]{:S(2)}, u32[]{:S(2)}) async-start(bf16[16,8,256]{2,0,1:T(8,128)(2,1)} %copy.192), calls=%async_computation.1 | async-start | bytes 131072 | tf_op jit(solution)/shard_map/all_to_all | solution.py:37
  12.2 2.0 iota_compare_fusion
  14.2 54.3 %all_gather.3 = bf16[64,16,1,256]{3,1,2,0:T(8,128)(2,1)} all-gather(bf16[1,16,1,256]{3,1,2,0:T(8,128)(2,1)} %param.10), channel_id=1, replica_groups=mesh['seq'=64,'head'=8] {'seq'}, dimensions={0}, use_global_device_ids=true | all-gather | bytes 532480 | tf_op jit(solution)/shard_map/all_gather | solution.py:55
  77.1 7.2 %all-to-all-start = ((bf16[16,8,1024]{2,0,1:T(8,128)(2,1)}), bf16[16,8,1024]{2,0,1:T(8,128)(2,1)S(1)}, u32[]{:S(2)}, u32[]{:S(2)}) async-start(bf16[16,8,1024]{2,0,1:T(8,128)(2,1)} %copy.188), calls=%async_computation | async-start | bytes 524288 | tf_op jit(solution)/shard_map/all_to_all | solution.py:36
  86.7 2.9 %collective-permute-start.1 = (bf16[128,1,256]{2,0,1:T(8,128)(2,1)S(1)}, bf16[128,1,256]{2,0,1:T(8,128)(2,1)S(1)}, u32[]{:S(2)}, u32[]{:S(2)}) collective-permute-start(bf16[128,1,256]{2,0,1:T(8,128)(2,1)S(1)} %bitcast.1712), channel_id=1, source_target_pairs={{0,16},{8,24},{16,32},{24,40},{32,48},{40,56},{48,64},{56,72},{64,... | collective-permute-start | bytes 196616 | tf_op jit(solution)/shard_map/ppermute | solution.py:12
  89.7 1.9 collective-permute-start
  91.6 5.0 %collective-permute-start.2 = (bf16[128,1,256]{2,0,1:T(8,128)(2,1)S(1)}, bf16[128,1,256]{2,0,1:T(8,128)(2,1)S(1)}, u32[]{:S(2)}, u32[]{:S(2)}) collective-permute-start(bf16[128,1,256]{2,0,1:T(8,128)(2,1)S(1)} %bitcast.1714), channel_id=1, source_target_pairs={{0,24},{8,32},{16,40},{24,48},{32,56},{40,64},{48,72},{56,80},{64,... | collective-permute-start | bytes 196616 | tf_op jit(solution)/shard_map/ppermute | solution.py:12
  96.6 3.2 %collective-permute-start.3 = (bf16[128,1,256]{2,0,1:T(8,128)(2,1)S(1)}, bf16[128,1,256]{2,0,1:T(8,128)(2,1)S(1)}, u32[]{:S(2)}, u32[]{:S(2)}) collective-permute-start(bf16[128,1,256]{2,0,1:T(8,128)(2,1)S(1)} %bitcast.1715), channel_id=1, source_target_pairs={{0,32},{8,40},{16,48},{24,56},{32,64},{40,72},{48,80},{56,88},{64,... | collective-permute-start | bytes 196616 | tf_op jit(solution)/shard_map/ppermute | solution.py:12
  99.8 1.9 collective-permute-start.4
  104.7 5.7 %collective-permute-start.5 = (bf16[128,1,256]{2,0,1:T(8,128)(2,1)S(1)}, bf16[128,1,256]{2,0,1:T(8,128)(2,1)S(1)}, u32[]{:S(2)}, u32[]{:S(2)}) collective-permute-start(bf16[128,1,256]{2,0,1:T(8,128)(2,1)S(1)} %bitcast.1718), channel_id=1, source_target_pairs={{0,48},{8,56},{16,64},{24,72},{32,80},{40,88},{48,96},{56,104},{64... | collective-permute-start | bytes 196616 | tf_op jit(solution)/shard_map/ppermute | solution.py:12
  111.2 4.5 %collective-permute-start.6 = (bf16[128,1,256]{2,0,1:T(8,128)(2,1)S(1)}, bf16[128,1,256]{2,0,1:T(8,128)(2,1)S(1)}, u32[]{:S(2)}, u32[]{:S(2)}) collective-permute-start(bf16[128,1,256]{2,0,1:T(8,128)(2,1)S(1)} %bitcast.1719), channel_id=1, source_target_pairs={{0,56},{8,64},{16,72},{24,80},{32,88},{40,96},{48,104},{56,112},{6... | collective-permute-start | bytes 196616 | tf_op jit(solution)/shard_map/ppermute | solution.py:12
  116.1 3.0 %collective-permute-start.7 = (bf16[128,1,256]{2,0,1:T(8,128)(2,1)S(1)}, bf16[128,1,256]{2,0,1:T(8,128)(2,1)S(1)}, u32[]{:S(2)}, u32[]{:S(2)}) collective-permute-start(bf16[128,1,256]{2,0,1:T(8,128)(2,1)S(1)} %bitcast.1720), channel_id=1, source_target_pairs={{0,64},{8,72},{16,80},{24,88},{32,96},{40,104},{48,112},{56,120},{... | collective-permute-start | bytes 196616 | tf_op jit(solution)/shard_map/ppermute | solution.py:12
  119.3 1.9 collective-permute-start.8
  125.1 1.9 collective-permute-start.10
  130.6 2.4 fusion.447
  134.9 2.4 fusion.448
  162.4 15.7 %conditional.1 = (f32[128,1,8]{0,2,1:T(8,128)S(1)}, f32[128,1,8]{0,2,1:T(8,128)S(1)}, f32[128,1,8,128]{0,3,2,1:T(8,128)}) conditional(s32[]{:T(128)} %convert_element_type.108, () %tuple.13, (pred[1,32,64]{2,1,0:T(8,128)(4,1)}, bf16[64,16,1,256]{3,1,2,0:T(8,128)(2,1)}, bf16[8,16,1,1024]{3,0,1,2:T(8,128)(2,1)}) %tuple.14), branch_computations={%region_1.0_spmd, %region_2.6_spmd} | conditional | flops 548543424 | bytes 34959652 | solution.py:69
  170.2 2.1 fusion.13
  172.3 2.1 copy.397
  174.3 3.1 %fusion.2 = f32[128,8]{0,1:T(8,128)S(1)} fusion(f32[1024,128,8]{1,0,2:T(8,128)} %copy-done, f32[128,8]{0,1:T(8,128)} %copy-done.71, pred[1024]{0:T(1024)(128)(4,1)} %broadcast_in_dim.202), kind=kLoop, calls=%fused_computation.5 | loop fusion | flops 4193280 | bytes 4203520 | tf_op jit(solution)/shard_map/cond/branch_1_fun/reduce_sum | solution.py:25
  178.3 1.9 collective-permute-start.20
  181.9 1.9 collective-permute-start.21
  184.9 1.9 collective-permute-start.22
  188.5 1.9 collective-permute-start.23
  192.2 1.9 collective-permute-start.24
  195.2 1.9 collective-permute-start.25
  197.4 1.9 collective-permute-start.26
  205.1 1.9 collective-permute-start.29
  207.3 2.9 %collective-permute-done.25 = bf16[128,1,256]{2,0,1:T(8,128)(2,1)S(1)} collective-permute-done((bf16[128,1,256]{2,0,1:T(8,128)(2,1)S(1)}, bf16[128,1,256]{2,0,1:T(8,128)(2,1)S(1)}, u32[]{:S(2)}, u32[]{:S(2)}) %collective-permute-start.25) | collective-permute-done | bytes 65568 | tf_op jit(solution)/shard_map/ppermute | solution.py:12
  214.1 2.2 collective-permute-done.27
  217.3 2.0 collective-permute-done.29
  242.6 19.1 %all_to_all.51 = bf16[8,2,8192]{2,1,0:T(2,128)(2,1)S(1)} all-to-all(bf16[8,2,8192]{2,1,0:T(2,128)(2,1)S(1)} %reshape.2783), channel_id=1, replica_groups=mesh['seq'=64,'head'=8] {'head'}, dimensions={0} | all-to-all | bytes 524288 | tf_op jit(solution)/shard_map/all_to_all | solution.py:92
  (358 shorter events, 100.2 us)
Async XLA Ops:
  1.5 75.6 %all-to-all-start.1 = ((bf16[16,8,256]{2,0,1:T(8,128)(2,1)}), bf16[16,8,256]{2,0,1:T(8,128)(2,1)S(1)}, u32[]{:S(2)}, u32[]{:S(2)}) async-start(bf16[16,8,256]{2,0,1:T(8,128)(2,1)} %copy.192), calls=%async_computation.1 | async-start | bytes 131072 | tf_op jit(solution)/shard_map/all_to_all | solution.py:37
  77.1 24.7 %all-to-all-start = ((bf16[16,8,1024]{2,0,1:T(8,128)(2,1)}), bf16[16,8,1024]{2,0,1:T(8,128)(2,1)S(1)}, u32[]{:S(2)}, u32[]{:S(2)}) async-start(bf16[16,8,1024]{2,0,1:T(8,128)(2,1)} %copy.188), calls=%async_computation | async-start | bytes 524288 | tf_op jit(solution)/shard_map/all_to_all | solution.py:36
  86.7 18.0 %collective-permute-start.1 = (bf16[128,1,256]{2,0,1:T(8,128)(2,1)S(1)}, bf16[128,1,256]{2,0,1:T(8,128)(2,1)S(1)}, u32[]{:S(2)}, u32[]{:S(2)}) collective-permute-start(bf16[128,1,256]{2,0,1:T(8,128)(2,1)S(1)} %bitcast.1712), channel_id=1, source_target_pairs={{0,16},{8,24},{16,32},{24,40},{32,48},{40,56},{48,64},{56,72},{64,... | collective-permute-start | bytes 196616 | tf_op jit(solution)/shard_map/ppermute | solution.py:12
  89.7 21.6 %collective-permute-start = (bf16[128,1,256]{2,0,1:T(8,128)(2,1)S(1)}, bf16[128,1,256]{2,0,1:T(8,128)(2,1)S(1)}, u32[]{:S(2)}, u32[]{:S(2)}) collective-permute-start(bf16[128,1,256]{2,0,1:T(8,128)(2,1)S(1)} %bitcast.1713), channel_id=1, source_target_pairs={{0,8},{8,16},{16,24},{24,32},{32,40},{40,48},{48,56},{56,64},{64,7... | collective-permute-start | bytes 196616 | tf_op jit(solution)/shard_map/ppermute | solution.py:12
  91.6 24.4 %collective-permute-start.2 = (bf16[128,1,256]{2,0,1:T(8,128)(2,1)S(1)}, bf16[128,1,256]{2,0,1:T(8,128)(2,1)S(1)}, u32[]{:S(2)}, u32[]{:S(2)}) collective-permute-start(bf16[128,1,256]{2,0,1:T(8,128)(2,1)S(1)} %bitcast.1714), channel_id=1, source_target_pairs={{0,24},{8,32},{16,40},{24,48},{32,56},{40,64},{48,72},{56,80},{64,... | collective-permute-start | bytes 196616 | tf_op jit(solution)/shard_map/ppermute | solution.py:12
  96.6 22.6 %collective-permute-start.3 = (bf16[128,1,256]{2,0,1:T(8,128)(2,1)S(1)}, bf16[128,1,256]{2,0,1:T(8,128)(2,1)S(1)}, u32[]{:S(2)}, u32[]{:S(2)}) collective-permute-start(bf16[128,1,256]{2,0,1:T(8,128)(2,1)S(1)} %bitcast.1715), channel_id=1, source_target_pairs={{0,32},{8,40},{16,48},{24,56},{32,64},{40,72},{48,80},{56,88},{64,... | collective-permute-start | bytes 196616 | tf_op jit(solution)/shard_map/ppermute | solution.py:12
  99.8 22.2 %collective-permute-start.4 = (bf16[128,1,256]{2,0,1:T(8,128)(2,1)S(1)}, bf16[128,1,256]{2,0,1:T(8,128)(2,1)S(1)}, u32[]{:S(2)}, u32[]{:S(2)}) collective-permute-start(bf16[128,1,256]{2,0,1:T(8,128)(2,1)S(1)} %bitcast.1716), channel_id=1, source_target_pairs={{0,40},{8,48},{16,56},{24,64},{32,72},{40,80},{48,88},{56,96},{64,... | collective-permute-start | bytes 196616 | tf_op jit(solution)/shard_map/ppermute | solution.py:12
  104.7 20.4 %collective-permute-start.5 = (bf16[128,1,256]{2,0,1:T(8,128)(2,1)S(1)}, bf16[128,1,256]{2,0,1:T(8,128)(2,1)S(1)}, u32[]{:S(2)}, u32[]{:S(2)}) collective-permute-start(bf16[128,1,256]{2,0,1:T(8,128)(2,1)S(1)} %bitcast.1718), channel_id=1, source_target_pairs={{0,48},{8,56},{16,64},{24,72},{32,80},{40,88},{48,96},{56,104},{64... | collective-permute-start | bytes 196616 | tf_op jit(solution)/shard_map/ppermute | solution.py:12
  111.2 17.4 %collective-permute-start.6 = (bf16[128,1,256]{2,0,1:T(8,128)(2,1)S(1)}, bf16[128,1,256]{2,0,1:T(8,128)(2,1)S(1)}, u32[]{:S(2)}, u32[]{:S(2)}) collective-permute-start(bf16[128,1,256]{2,0,1:T(8,128)(2,1)S(1)} %bitcast.1719), channel_id=1, source_target_pairs={{0,56},{8,64},{16,72},{24,80},{32,88},{40,96},{48,104},{56,112},{6... | collective-permute-start | bytes 196616 | tf_op jit(solution)/shard_map/ppermute | solution.py:12
  116.1 16.9 %collective-permute-start.7 = (bf16[128,1,256]{2,0,1:T(8,128)(2,1)S(1)}, bf16[128,1,256]{2,0,1:T(8,128)(2,1)S(1)}, u32[]{:S(2)}, u32[]{:S(2)}) collective-permute-start(bf16[128,1,256]{2,0,1:T(8,128)(2,1)S(1)} %bitcast.1720), channel_id=1, source_target_pairs={{0,64},{8,72},{16,80},{24,88},{32,96},{40,104},{48,112},{56,120},{... | collective-permute-start | bytes 196616 | tf_op jit(solution)/shard_map/ppermute | solution.py:12
  119.3 17.9 %collective-permute-start.8 = (bf16[128,1,256]{2,0,1:T(8,128)(2,1)S(1)}, bf16[128,1,256]{2,0,1:T(8,128)(2,1)S(1)}, u32[]{:S(2)}, u32[]{:S(2)}) collective-permute-start(bf16[128,1,256]{2,0,1:T(8,128)(2,1)S(1)} %bitcast.1721), channel_id=1, source_target_pairs={{0,72},{8,80},{16,88},{24,96},{32,104},{40,112},{48,120},{56,128},... | collective-permute-start | bytes 196616 | tf_op jit(solution)/shard_map/ppermute | solution.py:12
  122.1 18.7 %collective-permute-start.9 = (bf16[128,1,256]{2,0,1:T(8,128)(2,1)S(1)}, bf16[128,1,256]{2,0,1:T(8,128)(2,1)S(1)}, u32[]{:S(2)}, u32[]{:S(2)}) collective-permute-start(bf16[128,1,256]{2,0,1:T(8,128)(2,1)S(1)} %bitcast.1722), channel_id=1, source_target_pairs={{0,80},{8,88},{16,96},{24,104},{32,112},{40,120},{48,128},{56,136}... | collective-permute-start | bytes 196616 | tf_op jit(solution)/shard_map/ppermute | solution.py:12
  125.1 19.3 %collective-permute-start.10 = (bf16[128,1,256]{2,0,1:T(8,128)(2,1)S(1)}, bf16[128,1,256]{2,0,1:T(8,128)(2,1)S(1)}, u32[]{:S(2)}, u32[]{:S(2)}) collective-permute-start(bf16[128,1,256]{2,0,1:T(8,128)(2,1)S(1)} %bitcast.1723), channel_id=1, source_target_pairs={{0,88},{8,96},{16,104},{24,112},{32,120},{40,128},{48,136},{56,144... | collective-permute-start | bytes 196616 | tf_op jit(solution)/shard_map/ppermute | solution.py:12
  128.7 19.3 %collective-permute-start.11 = (bf16[128,1,256]{2,0,1:T(8,128)(2,1)S(1)}, bf16[128,1,256]{2,0,1:T(8,128)(2,1)S(1)}, u32[]{:S(2)}, u32[]{:S(2)}) collective-permute-start(bf16[128,1,256]{2,0,1:T(8,128)(2,1)S(1)} %bitcast.1724), channel_id=1, source_target_pairs={{0,96},{8,104},{16,112},{24,120},{32,128},{40,136},{48,144},{56,15... | collective-permute-start | bytes 196616 | tf_op jit(solution)/shard_map/ppermute | solution.py:12
  132.9 18.6 %collective-permute-start.12 = (bf16[128,1,256]{2,0,1:T(8,128)(2,1)S(1)}, bf16[128,1,256]{2,0,1:T(8,128)(2,1)S(1)}, u32[]{:S(2)}, u32[]{:S(2)}) collective-permute-start(bf16[128,1,256]{2,0,1:T(8,128)(2,1)S(1)} %bitcast.1725), channel_id=1, source_target_pairs={{0,104},{8,112},{16,120},{24,128},{32,136},{40,144},{48,152},{56,1... | collective-permute-start | bytes 196616 | tf_op jit(solution)/shard_map/ppermute | solution.py:12
  137.2 17.9 %collective-permute-start.13 = (bf16[128,1,256]{2,0,1:T(8,128)(2,1)S(1)}, bf16[128,1,256]{2,0,1:T(8,128)(2,1)S(1)}, u32[]{:S(2)}, u32[]{:S(2)}) collective-permute-start(bf16[128,1,256]{2,0,1:T(8,128)(2,1)S(1)} %bitcast.1726), channel_id=1, source_target_pairs={{0,112},{8,120},{16,128},{24,136},{32,144},{40,152},{48,160},{56,1... | collective-permute-start | bytes 196616 | tf_op jit(solution)/shard_map/ppermute | solution.py:12
  140.8 18.0 %collective-permute-start.14 = (bf16[128,1,256]{2,0,1:T(8,128)(2,1)S(1)}, bf16[128,1,256]{2,0,1:T(8,128)(2,1)S(1)}, u32[]{:S(2)}, u32[]{:S(2)}) collective-permute-start(bf16[128,1,256]{2,0,1:T(8,128)(2,1)S(1)} %bitcast.1727), channel_id=1, source_target_pairs={{0,120},{8,128},{16,136},{24,144},{32,152},{40,160},{48,168},{56,1... | collective-permute-start | bytes 196616 | tf_op jit(solution)/shard_map/ppermute | solution.py:12
  144.4 33.9 %collective-permute-start.15 = (bf16[128,1,256]{2,0,1:T(8,128)(2,1)S(1)}, bf16[128,1,256]{2,0,1:T(8,128)(2,1)}, u32[]{:S(2)}, u32[]{:S(2)}) collective-permute-start(bf16[128,1,256]{2,0,1:T(8,128)(2,1)S(1)} %bitcast.1728), channel_id=1, source_target_pairs={{0,128},{8,136},{16,144},{24,152},{32,160},{40,168},{48,176},{56,1... | collective-permute-start | bytes 196616 | tf_op jit(solution)/shard_map/ppermute | solution.py:12
  147.9 34.0 %collective-permute-start.16 = (bf16[128,1,256]{2,0,1:T(8,128)(2,1)S(1)}, bf16[128,1,256]{2,0,1:T(8,128)(2,1)}, u32[]{:S(2)}, u32[]{:S(2)}) collective-permute-start(bf16[128,1,256]{2,0,1:T(8,128)(2,1)S(1)} %bitcast.1729), channel_id=1, source_target_pairs={{0,136},{8,144},{16,152},{24,160},{32,168},{40,176},{48,184},{56,1... | collective-permute-start | bytes 196616 | tf_op jit(solution)/shard_map/ppermute | solution.py:12
  151.5 33.4 %collective-permute-start.17 = (bf16[128,1,256]{2,0,1:T(8,128)(2,1)S(1)}, bf16[128,1,256]{2,0,1:T(8,128)(2,1)}, u32[]{:S(2)}, u32[]{:S(2)}) collective-permute-start(bf16[128,1,256]{2,0,1:T(8,128)(2,1)S(1)} %bitcast.1730), channel_id=1, source_target_pairs={{0,144},{8,152},{16,160},{24,168},{32,176},{40,184},{48,192},{56,2... | collective-permute-start | bytes 196616 | tf_op jit(solution)/shard_map/ppermute | solution.py:12
  155.1 33.4 %collective-permute-start.18 = (bf16[128,1,256]{2,0,1:T(8,128)(2,1)S(1)}, bf16[128,1,256]{2,0,1:T(8,128)(2,1)}, u32[]{:S(2)}, u32[]{:S(2)}) collective-permute-start(bf16[128,1,256]{2,0,1:T(8,128)(2,1)S(1)} %bitcast.1731), channel_id=1, source_target_pairs={{0,152},{8,160},{16,168},{24,176},{32,184},{40,192},{48,200},{56,2... | collective-permute-start | bytes 196616 | tf_op jit(solution)/shard_map/ppermute | solution.py:12
  158.7 33.4 %collective-permute-start.19 = (bf16[128,1,256]{2,0,1:T(8,128)(2,1)S(1)}, bf16[128,1,256]{2,0,1:T(8,128)(2,1)}, u32[]{:S(2)}, u32[]{:S(2)}) collective-permute-start(bf16[128,1,256]{2,0,1:T(8,128)(2,1)S(1)} %bitcast.1732), channel_id=1, source_target_pairs={{0,160},{8,168},{16,176},{24,184},{32,192},{40,200},{48,208},{56,2... | collective-permute-start | bytes 196616 | tf_op jit(solution)/shard_map/ppermute | solution.py:12
  178.3 16.9 %collective-permute-start.20 = (bf16[128,1,256]{2,0,1:T(8,128)(2,1)S(1)}, bf16[128,1,256]{2,0,1:T(8,128)(2,1)S(1)}, u32[]{:S(2)}, u32[]{:S(2)}) collective-permute-start(bf16[128,1,256]{2,0,1:T(8,128)(2,1)S(1)} %bitcast.1733), channel_id=1, source_target_pairs={{0,168},{8,176},{16,184},{24,192},{32,200},{40,208},{48,216},{56,2... | collective-permute-start | bytes 196616 | tf_op jit(solution)/shard_map/ppermute | solution.py:12
  181.9 15.5 %collective-permute-start.21 = (bf16[128,1,256]{2,0,1:T(8,128)(2,1)S(1)}, bf16[128,1,256]{2,0,1:T(8,128)(2,1)S(1)}, u32[]{:S(2)}, u32[]{:S(2)}) collective-permute-start(bf16[128,1,256]{2,0,1:T(8,128)(2,1)S(1)} %bitcast.1734), channel_id=1, source_target_pairs={{0,176},{8,184},{16,192},{24,200},{32,208},{40,216},{48,224},{56,2... | collective-permute-start | bytes 196616 | tf_op jit(solution)/shard_map/ppermute | solution.py:12
  184.9 15.7 %collective-permute-start.22 = (bf16[128,1,256]{2,0,1:T(8,128)(2,1)S(1)}, bf16[128,1,256]{2,0,1:T(8,128)(2,1)S(1)}, u32[]{:S(2)}, u32[]{:S(2)}) collective-permute-start(bf16[128,1,256]{2,0,1:T(8,128)(2,1)S(1)} %bitcast.1735), channel_id=1, source_target_pairs={{0,184},{8,192},{16,200},{24,208},{32,216},{40,224},{48,232},{56,2... | collective-permute-start | bytes 196616 | tf_op jit(solution)/shard_map/ppermute | solution.py:12
  188.5 14.3 %collective-permute-start.23 = (bf16[128,1,256]{2,0,1:T(8,128)(2,1)S(1)}, bf16[128,1,256]{2,0,1:T(8,128)(2,1)S(1)}, u32[]{:S(2)}, u32[]{:S(2)}) collective-permute-start(bf16[128,1,256]{2,0,1:T(8,128)(2,1)S(1)} %bitcast.1736), channel_id=1, source_target_pairs={{0,192},{8,200},{16,208},{24,216},{32,224},{40,232},{48,240},{56,2... | collective-permute-start | bytes 196616 | tf_op jit(solution)/shard_map/ppermute | solution.py:12
  192.2 12.9 %collective-permute-start.24 = (bf16[128,1,256]{2,0,1:T(8,128)(2,1)S(1)}, bf16[128,1,256]{2,0,1:T(8,128)(2,1)S(1)}, u32[]{:S(2)}, u32[]{:S(2)}) collective-permute-start(bf16[128,1,256]{2,0,1:T(8,128)(2,1)S(1)} %bitcast.1737), channel_id=1, source_target_pairs={{0,200},{8,208},{16,216},{24,224},{32,232},{40,240},{48,248},{56,2... | collective-permute-start | bytes 196616 | tf_op jit(solution)/shard_map/ppermute | solution.py:12
  195.2 14.9 %collective-permute-start.25 = (bf16[128,1,256]{2,0,1:T(8,128)(2,1)S(1)}, bf16[128,1,256]{2,0,1:T(8,128)(2,1)S(1)}, u32[]{:S(2)}, u32[]{:S(2)}) collective-permute-start(bf16[128,1,256]{2,0,1:T(8,128)(2,1)S(1)} %bitcast.1738), channel_id=1, source_target_pairs={{0,208},{8,216},{16,224},{24,232},{32,240},{40,248},{48,256},{56,2... | collective-permute-start | bytes 196616 | tf_op jit(solution)/shard_map/ppermute | solution.py:12
  197.4 14.9 %collective-permute-start.26 = (bf16[128,1,256]{2,0,1:T(8,128)(2,1)S(1)}, bf16[128,1,256]{2,0,1:T(8,128)(2,1)S(1)}, u32[]{:S(2)}, u32[]{:S(2)}) collective-permute-start(bf16[128,1,256]{2,0,1:T(8,128)(2,1)S(1)} %bitcast.1739), channel_id=1, source_target_pairs={{0,216},{8,224},{16,232},{24,240},{32,248},{40,256},{48,264},{56,2... | collective-permute-start | bytes 196616 | tf_op jit(solution)/shard_map/ppermute | solution.py:12
  200.6 15.7 %collective-permute-start.27 = (bf16[128,1,256]{2,0,1:T(8,128)(2,1)S(1)}, bf16[128,1,256]{2,0,1:T(8,128)(2,1)S(1)}, u32[]{:S(2)}, u32[]{:S(2)}) collective-permute-start(bf16[128,1,256]{2,0,1:T(8,128)(2,1)S(1)} %bitcast.1740), channel_id=1, source_target_pairs={{0,224},{8,232},{16,240},{24,248},{32,256},{40,264},{48,272},{56,2... | collective-permute-start | bytes 196616 | tf_op jit(solution)/shard_map/ppermute | solution.py:12
  202.8 14.2 %collective-permute-start.28 = (bf16[128,1,256]{2,0,1:T(8,128)(2,1)S(1)}, bf16[128,1,256]{2,0,1:T(8,128)(2,1)S(1)}, u32[]{:S(2)}, u32[]{:S(2)}) collective-permute-start(bf16[128,1,256]{2,0,1:T(8,128)(2,1)S(1)} %bitcast.1741), channel_id=1, source_target_pairs={{0,232},{8,240},{16,248},{24,256},{32,264},{40,272},{48,280},{56,2... | collective-permute-start | bytes 196616 | tf_op jit(solution)/shard_map/ppermute | solution.py:12
  205.1 14.3 %collective-permute-start.29 = (bf16[128,1,256]{2,0,1:T(8,128)(2,1)S(1)}, bf16[128,1,256]{2,0,1:T(8,128)(2,1)S(1)}, u32[]{:S(2)}, u32[]{:S(2)}) collective-permute-start(bf16[128,1,256]{2,0,1:T(8,128)(2,1)S(1)} %bitcast.1742), channel_id=1, source_target_pairs={{0,240},{8,248},{16,256},{24,264},{32,272},{40,280},{48,288},{56,2... | collective-permute-start | bytes 196616 | tf_op jit(solution)/shard_map/ppermute | solution.py:12
  (77 other events, 1155.7 us)
where the time goes:
time: 266 us; the launch traced here: 263 us
  starting transfers between devices  91.3 us (34%)
  blocking collectives  73.4 us (28%)
  matrix products  48.8 us (18%)
  other arithmetic  19.8 us (7%)
  local copies, waits for them, and re-layouts  16.2 us (6%)
  waiting for transfers between devices  10.2 us (4%)
  between operations  3.12 us (1%)
    ppermute x32, starting transfers between devices, passed_along(): return lax.ppermute(value, axis, pairs)  73.8 us
    all_gather x1, blocking collectives, per_device(): piece = lax.all_gather(pool, 'seq', axis=0, tiled=True)  54.3 us
    dot_general x34, matrix products, blend_keys(): jnp.einsum('rhgd,khd->rhgk', query, keys, preferred_element_type=jnp.floa...  31.5 us
    all_to_all x1, blocking collectives, per_device(): lax.all_to_all(mixed, 'head', split_axis=0, concat_axis=1, tiled=True)  19.1 us
    dot_general x34, matrix products, blend_keys(): jnp.einsum('rhgk,khd->rhgd', rounded, value_rows, preferred_element_type=...  17.3 us
    all_to_all x1, starting transfers between devices, per_device(): lax.all_to_all(branch_key_value, 'head', split_axis=1, concat_axis=0, til...  10.3 us
    ppermute x32, waiting for transfers between devices, passed_along(): return lax.ppermute(value, axis, pairs)  10.2 us
    all_to_all x1, starting transfers between devices, per_device(): lax.all_to_all(queries, 'head', split_axis=1, concat_axis=0, tiled=True)  7.19 us
  transfers between devices with their start and end apart: 34, of which 7 were waited for; matrix products, arithmetic and copies ran while one was open for 23% of the time, Pallas kernels for 0%

commit v1 on v0

v1 whole, which is shorter than its diff:
```python
import functools

import jax
import jax.numpy as jnp
from jax import lax
from jax.experimental import pallas as pl
from jax.experimental.pallas import tpu as pltpu
from jax.sharding import PartitionSpec as P

D = 128
PAIR = 2 * D
ROWS = 128
GROUP = 8
QR = ROWS * GROUP
NX, NY = 4, 8
PAGES = 32
PAGE = 16
SCALE = D ** (-0.5)
LOG2E = 1.4426950408889634
LOW = -1e30


def x_shift(by):
    return [
        ((x * NY + y) * 2 + c, ((x + by) * NY + y) * 2 + c)
        for x in range(NX) for y in range(NY) for c in range(2) if 0 <= x + by < NX
    ]


def x_ring(by):
    return [
        ((x * NY + y) * 2 + c, (((x + by) % NX) * NY + y) * 2 + c)
        for x in range(NX) for y in range(NY) for c in range(2)
    ]


def y_ring(by):
    return [
        ((x * NY + y) * 2 + c, (x * NY + (y + by) % NY) * 2 + c)
        for x in range(NX) for y in range(NY) for c in range(2)
    ]


SWAP = [(i, i ^ 1) for i in range(2 * NX * NY)]
PLANES = [
    [((x * NY + y) * 2 + c) * 8 + z for y in range(NY) for z in range(8)]
    for x in range(NX) for c in range(2)
]


def fold(keys, values, mask, qt_ref, m_ref, l_ref, acc_ref):
    scores = jnp.dot(keys, qt_ref[...], preferred_element_type=jnp.float32)
    if mask is not None:
        scores = jnp.where(jnp.concatenate([mask] * GROUP, axis=1), scores, LOW)
    old = m_ref[...]
    top = jnp.maximum(old, jnp.max(scores, axis=0, keepdims=True))
    weights = jnp.exp2((scores - top) * (SCALE * LOG2E))
    factor = jnp.exp2((old - top) * (SCALE * LOG2E))
    m_ref[...] = top
    l_ref[...] = l_ref[...] * factor + jnp.sum(weights, axis=0, keepdims=True)
    mixed = lax.dot_general(
        values, weights.astype(jnp.bfloat16), (((0,), (0,)), ((), ())),
        preferred_element_type=jnp.float32,
    )
    acc_ref[...] = acc_ref[...] * factor + mixed


def starts_of(ids_ref, own):
    ids = ids_ref[...]
    starts = [jnp.sum((ids < b).astype(jnp.int32)) for b in range(1, 4)]
    own_ids = ids_ref[pl.ds(own, 1), :]
    row_start = jnp.zeros_like(own_ids)
    for b in range(1, 4):
        row_start = jnp.where(own_ids == b, starts[b - 1], row_start)
    return row_start, jnp.min(row_start), jnp.max(row_start)


def fold_block(block, load, own, limits, qt_ref, m_ref, l_ref, acc_ref):
    row_start, first, last = limits
    valid = (block >= 0) & (block <= own) & (block * ROWS + ROWS > first)
    whole = (block < own) & (block * ROWS >= last)

    @pl.when(valid & whole)
    def _():
        keys, values = load()
        fold(keys, values, None, qt_ref, m_ref, l_ref, acc_ref)

    @pl.when(valid & jnp.logical_not(whole))
    def _():
        keys, values = load()
        key_rows = lax.broadcasted_iota(jnp.int32, (ROWS, ROWS), 0) + block * ROWS
        query_rows = lax.broadcasted_iota(jnp.int32, (ROWS, ROWS), 1) + own * ROWS
        mask = (key_rows >= row_start) & (key_rows <= query_rows)
        fold(keys, values, mask, qt_ref, m_ref, l_ref, acc_ref)


def window(kv_ref, own_load, core, x, y, own, limits, qt_ref, m_ref, l_ref, acc_ref):
    state = (own, limits, qt_ref, m_ref, l_ref, acc_ref)
    fold_block((x * NY + y) * 2 + core, own_load, *state)

    def step(i, carry):
        yy = i % NY
        before = i < NY
        plane = jnp.where(before, x - 1, jnp.where(yy < y, x, x - 2))
        block = jnp.where(plane >= 0, (plane * NY + yy) * 2 + core, -1)

        def load():
            rows = pl.ds(pl.multiple_of(yy * ROWS, ROWS), ROWS)
            cols = pl.multiple_of(jnp.where(before, 0, PAIR), PAIR)
            return kv_ref[rows, pl.ds(cols, D)], kv_ref[rows, pl.ds(cols + D, D)]

        fold_block(block, load, *state)
        return carry

    lax.fori_loop(0, 2 * NY, step, 0)


def place(meta_ref):
    own = meta_ref[0]
    return own, own // (2 * NY), (own // 2) % NY, own % 2


def first_kernel(meta_ref, q_ref, kv_ref, ids_ref, m_ref, l_ref, acc_ref, qt_ref):
    own, x, y, core = place(meta_ref)
    limits = starts_of(ids_ref, own)
    for g in range(GROUP):
        qt_ref[:, g * ROWS:(g + 1) * ROWS] = q_ref[:, g * D:(g + 1) * D].T
    m_ref[...] = jnp.full_like(m_ref, LOW)
    l_ref[...] = jnp.zeros_like(l_ref)
    acc_ref[...] = jnp.zeros_like(acc_ref)

    def own_load():
        base = GROUP * D
        return q_ref[:, base:base + D], q_ref[:, base + D:base + PAIR]

    window(kv_ref, own_load, core, x, y, own, limits, qt_ref, m_ref, l_ref, acc_ref)


def last_kernel(meta_ref, table_ref, qt_ref, kv_ref, side_ref, mine_ref, ids_ref, m_in, l_in, acc_in,
                out_ref, m_ref, l_ref, acc_ref, prefix_ref):
    m_ref[...] = m_in[...]
    l_ref[...] = l_in[...]
    acc_ref[...] = acc_in[...]
    own, x, y, core = place(meta_ref)
    limits = starts_of(ids_ref, own)
    for i in range(PAGES):
        page = table_ref[i]
        off = (y + NY - (page // 2) % NY) % NY
        unit = (x + NX - page // (2 * NY)) % NX + 4 * (off // 4) + 8 * ((off // 2) % 2) + 16 * (off % 2)
        rows = pl.ds(pl.multiple_of(ROWS + unit * PAGE, PAGE), PAGE)

        @pl.when(page % 2 == core)
        def _():
            prefix_ref[i * PAGE:(i + 1) * PAGE, :] = mine_ref[rows, :]

        @pl.when(page % 2 != core)
        def _():
            prefix_ref[i * PAGE:(i + 1) * PAGE, :] = side_ref[rows, :]

    fold(prefix_ref[:, :D], prefix_ref[:, D:], None, qt_ref, m_ref, l_ref, acc_ref)

    def own_load():
        return side_ref[:ROWS, :D], side_ref[:ROWS, D:]

    window(kv_ref, own_load, 1 - core, x, y, own, limits, qt_ref, m_ref, l_ref, acc_ref)
    result = (acc_ref[...] * (1.0 / l_ref[...])).astype(jnp.bfloat16)
    for g in range(GROUP):
        out_ref[:, g * D:(g + 1) * D] = result[:, g * ROWS:(g + 1) * ROWS].T


VM = pl.BlockSpec(memory_space=pltpu.VMEM)
SM = pl.BlockSpec(memory_space=pltpu.SMEM)


def per_device(queries, branch_key_value, branch_ids, pool, page_table):
    me = lax.axis_index("seq")
    y = (me // 2) % NY
    raw = jnp.transpose(branch_key_value, (1, 0, 2))
    two_back = lax.ppermute(raw, "seq", x_shift(2))
    one_back = lax.ppermute(raw, "seq", x_shift(1))
    page = pool.reshape(1, PAGE, PAIR)
    pages = jnp.concatenate([page] + [lax.ppermute(page, "seq", x_ring(k)) for k in (1, 2, 3)], axis=0)
    for by in (4, 2, 1):
        pages = jnp.concatenate([pages, lax.ppermute(pages, "seq", y_ring(by))], axis=0)
    wide = jnp.concatenate([queries, branch_key_value], axis=2)
    wide = lax.all_to_all(wide, "head", split_axis=1, concat_axis=0, tiled=True).reshape(ROWS, GROUP * D + PAIR)
    target = jnp.arange(NY, dtype=jnp.int32)[:, None, None, None]
    mixed = jnp.where(target > y, raw[None], two_back[None])
    send = jnp.concatenate([jnp.broadcast_to(one_back[None], mixed.shape), mixed], axis=3)
    kv = lax.all_to_all(
        send.reshape(NY * 8, 16, 2 * PAIR), ("seq", "head"), split_axis=0, concat_axis=0, tiled=True,
        axis_index_groups=PLANES,
    ).reshape(NY * ROWS, 2 * PAIR)
    mine = jnp.concatenate([wide[:, GROUP * D:], pages.reshape(PAGES * PAGE, PAIR)], axis=0)
    side = lax.ppermute(mine, "seq", SWAP)
    kv_side = lax.ppermute(kv, "seq", SWAP)

    ids = branch_ids.reshape(64, ROWS)
    meta = me.astype(jnp.int32).reshape(1)
    state = [
        jax.ShapeDtypeStruct((1, QR), jnp.float32),
        jax.ShapeDtypeStruct((1, QR), jnp.float32),
        jax.ShapeDtypeStruct((D, QR), jnp.float32),
    ]
    params = pltpu.CompilerParams(vmem_limit_bytes=40 * 1024 * 1024)
    m, l, acc, qt = pl.pallas_call(
        first_kernel,
        out_shape=state + [jax.ShapeDtypeStruct((D, QR), jnp.bfloat16)],
        in_specs=[SM, VM, VM, VM],
        out_specs=[VM] * 4,
        compiler_params=params,
        name="own_parity",
    )(meta, wide, kv, ids)
    out = pl.pallas_call(
        last_kernel,
        out_shape=jax.ShapeDtypeStruct((ROWS, GROUP * D), jnp.bfloat16),
        in_specs=[SM, SM] + [VM] * 8,
        out_specs=VM,
        scratch_shapes=[
            pltpu.VMEM((1, QR), jnp.float32),
            pltpu.VMEM((1, QR), jnp.float32),
            pltpu.VMEM((D, QR), jnp.float32),
            pltpu.VMEM((PAGES * PAGE, PAIR), jnp.bfloat16),
        ],
        compiler_params=params,
        name="other_parity",
    )(meta, page_table.reshape(PAGES), qt, kv_side, side, mine, ids, m, l, acc)
    return lax.all_to_all(out.reshape(ROWS, 1, GROUP * D), "head", split_axis=0, concat_axis=1, tiled=True)


def solution(mesh):
    return jax.shard_map(
        per_device,
        mesh=mesh,
        in_specs=(
            P(("seq", "head"), None, None),
            P(("seq", "head"), None, None),
            P(),
            P("seq", None, "head", None),
            P("head", None),
        ),
        out_specs=P(("seq", "head"), None, None),
        check_vma=False,
    )
```

time: 266 us -> 121 us (0.45)
  the two profiles are of different devices: /device:TPU:4 before, /device:TPU:63 now
where the time goes in v1:
time: 121 us; the launch traced here: 120 us
  starting transfers between devices  57.4 us (47%)
  Pallas kernels  20 us (17%)
  blocking collectives  19.1 us (16%)
  waiting for transfers between devices  17 us (14%)
  local copies, waits for them, and re-layouts  3.23 us (3%)
  other arithmetic  2.85 us (2%)
    all_to_all x1, blocking collectives, per_device(): lax.all_to_all(out.reshape(ROWS, 1, GROUP * D), 'head', split_axis=0, con...  19.1 us
    ppermute x3, starting transfers between devices, per_device(): lax.ppermute(pages, 'seq', y_ring(by))  16 us
    all_to_all x1, starting transfers between devices, per_device(): lax.all_to_all(send.reshape(NY * 8, 16, 2 * PAIR), ('seq', 'head'), split...  15.7 us
    pallas_call x1, Pallas kernels, per_device(): pl.pallas_call(last_kernel, out_shape=jax.ShapeDtypeStruct((ROWS, GROUP *...  11.5 us
    ppermute x3, starting transfers between devices, per_device(): lax.ppermute(page, 'seq', x_ring(k))  10.2 us
    pallas_call x1, Pallas kernels, per_device(): pl.pallas_call(first_kernel, out_shape=state + [jax.ShapeDtypeStruct((D,...  8.51 us
    all_to_all x1, waiting for transfers between devices, per_device(): lax.all_to_all(send.reshape(NY * 8, 16, 2 * PAIR), ('seq', 'head'), split...  7.46 us
    ppermute x1, starting transfers between devices, per_device(): kv_side = lax.ppermute(kv, 'seq', SWAP)  5.8 us
  transfers between devices with their start and end apart: 12, of which 5 were waited for; matrix products, arithmetic and copies ran while one was open for 2% of the time, Pallas kernels for 7%

profile of v1, /device:TPU:63, one launch (start us, length us, event | category | flops | bytes accessed | tf_op | source)
XLA Modules:
  0.0 120.0 jit_solution(15195015529907153832)
XLA Ops:
  0.0 1.3 %collective-permute-start.1 = (bf16[8,16,256]{2,0,1:T(8,128)(2,1)}, bf16[8,16,256]{2,0,1:T(8,128)(2,1)S(1)}, u32[]{:S(2)}, u32[]{:S(2)}) collective-permute-start(bf16[8,16,256]{2,0,1:T(8,128)(2,1)} %bitcast.37), channel_id=1, source_target_pairs={{0,256},{8,264},{16,272},{24,280},{32,288},{40,296},{48,304},{56,3... | collective-permute-start | bytes 196616 | tf_op jit(solution)/shard_map/ppermute | solution.py:179
  1.3 1.3 %collective-permute-start = (bf16[8,16,256]{2,0,1:T(8,128)(2,1)}, bf16[8,16,256]{2,0,1:T(8,128)(2,1)S(1)}, u32[]{:S(2)}, u32[]{:S(2)}) collective-permute-start(bf16[8,16,256]{2,0,1:T(8,128)(2,1)} %bitcast.38), channel_id=1, source_target_pairs={{0,128},{8,136},{16,144},{24,152},{32,160},{40,168},{48,176},{56,1... | collective-permute-start | bytes 196616 | tf_op jit(solution)/shard_map/ppermute | solution.py:180
  2.6 0.9 copy.21
  3.6 0.1 broadcast_in_dim.43
  3.7 3.1 %collective-permute-done.1 = bf16[8,16,256]{2,0,1:T(8,128)(2,1)S(1)} collective-permute-done((bf16[8,16,256]{2,0,1:T(8,128)(2,1)}, bf16[8,16,256]{2,0,1:T(8,128)(2,1)S(1)}, u32[]{:S(2)}, u32[]{:S(2)}) %collective-permute-start.1) | collective-permute-done | bytes 65568 | tf_op jit(solution)/shard_map/ppermute | solution.py:179
  6.7 0.1 bitcast_select_fusion
  7.0 1.1 pad_maximum_fusion
  8.1 15.7 %all-to-all-start.1 = ((bf16[64,16,512]{2,1,0:T(8,128)(2,1)}), bf16[64,16,512]{2,1,0:T(8,128)(2,1)S(1)}, u32[]{:S(2)}, u32[]{:S(2)}) async-start(bf16[64,16,512]{2,1,0:T(8,128)(2,1)} %pad_maximum_fusion), calls=%async_computation.1 | async-start | bytes 2097152 | tf_op jit(solution)/shard_map/all_to_all | solution.py:190
  23.9 3.7 %collective-permute-start.3 = (bf16[1,16,256]{2,1,0:T(8,128)(2,1)S(1)}, bf16[1,16,256]{2,1,0:T(8,128)(2,1)S(1)}, u32[]{:S(2)}, u32[]{:S(2)}) collective-permute-start(bf16[1,16,256]{2,1,0:T(8,128)(2,1)S(1)} %bitcast.40), channel_id=1, source_target_pairs={{0,128},{8,136},{16,144},{24,152},{32,160},{40,168},{48,176},{56,1... | collective-permute-start | bytes 24584 | tf_op jit(solution)/shard_map/ppermute | solution.py:182
  27.6 4.6 %collective-permute-start.4 = (bf16[1,16,256]{2,1,0:T(8,128)(2,1)S(1)}, bf16[1,16,256]{2,1,0:T(8,128)(2,1)S(1)}, u32[]{:S(2)}, u32[]{:S(2)}) collective-permute-start(bf16[1,16,256]{2,1,0:T(8,128)(2,1)S(1)} %bitcast.41), channel_id=1, source_target_pairs={{0,256},{8,264},{16,272},{24,280},{32,288},{40,296},{48,304},{56,3... | collective-permute-start | bytes 24584 | tf_op jit(solution)/shard_map/ppermute | solution.py:182
  32.2 1.9 %collective-permute-start.5 = (bf16[1,16,256]{2,1,0:T(8,128)(2,1)S(1)}, bf16[1,16,256]{2,1,0:T(8,128)(2,1)S(1)}, u32[]{:S(2)}, u32[]{:S(2)}) collective-permute-start(bf16[1,16,256]{2,1,0:T(8,128)(2,1)S(1)} %bitcast.42), channel_id=1, source_target_pairs={{0,384},{8,392},{16,400},{24,408},{32,416},{40,424},{48,432},{56,4... | collective-permute-start | bytes 24584 | tf_op jit(solution)/shard_map/ppermute | solution.py:182
  34.1 0.2 copy.18
  34.3 0.8 pad_maximum_fusion.1
  35.0 3.0 %collective-permute-done.5 = bf16[1,16,256]{2,1,0:T(8,128)(2,1)S(1)} collective-permute-done((bf16[1,16,256]{2,1,0:T(8,128)(2,1)S(1)}, bf16[1,16,256]{2,1,0:T(8,128)(2,1)S(1)}, u32[]{:S(2)}, u32[]{:S(2)}) %collective-permute-start.5) | collective-permute-done | bytes 8224 | tf_op jit(solution)/shard_map/ppermute | solution.py:182
  38.1 4.7 %collective-permute-start.6 = (bf16[4,16,256]{2,1,0:T(8,128)(2,1)S(1)}, bf16[4,16,256]{2,1,0:T(8,128)(2,1)S(1)}, u32[]{:S(2)}, u32[]{:S(2)}) collective-permute-start(bf16[4,16,256]{2,1,0:T(8,128)(2,1)S(1)} %pad_maximum_fusion.3), channel_id=1, source_target_pairs={{0,64},{8,72},{16,80},{24,88},{32,96},{40,104},{48,112},{56,120},{... | collective-permute-start | bytes 98312 | tf_op jit(solution)/shard_map/ppermute | solution.py:184
  42.8 7.5 %all-to-all-done.1 = bf16[64,16,512]{2,1,0:T(8,128)(2,1)S(1)} async-done(((bf16[64,16,512]{2,1,0:T(8,128)(2,1)}), bf16[64,16,512]{2,1,0:T(8,128)(2,1)S(1)}, u32[]{:S(2)}, u32[]{:S(2)}) %all-to-all-start.1) | async-done | bytes 1048608 | tf_op jit(solution)/shard_map/all_to_all | solution.py:190
  50.2 3.4 %all-to-all-start = ((bf16[16,8,1280]{2,0,1:T(8,128)(2,1)}), bf16[16,8,1280]{2,0,1:T(8,128)(2,1)S(1)}, u32[]{:S(2)}, u32[]{:S(2)}) async-start(bf16[16,8,1280]{2,0,1:T(8,128)(2,1)} %pad_maximum_fusion.1), calls=%async_computation | async-start | bytes 655360 | tf_op jit(solution)/shard_map/all_to_all | solution.py:186
  53.7 5.8 %collective-permute-start.2 = (bf16[1024,512]{1,0:T(8,128)(2,1)S(1)}, bf16[1024,512]{1,0:T(8,128)(2,1)S(1)}, u32[]{:S(2)}, u32[]{:S(2)}) collective-permute-start(bf16[1024,512]{1,0:T(8,128)(2,1)S(1)} %bitcast.26), channel_id=1, source_target_pairs={{0,8},{8,0},{16,24},{24,16},{32,40},{40,32},{48,56},{56,48},{64,72... | collective-permute-start | bytes 3145736 | tf_op jit(solution)/shard_map/ppermute | solution.py:196
  59.5 5.1 %collective-permute-start.7 = (bf16[8,16,256]{2,1,0:T(8,128)(2,1)S(1)}, bf16[8,16,256]{2,1,0:T(8,128)(2,1)S(1)}, u32[]{:S(2)}, u32[]{:S(2)}) collective-permute-start(bf16[8,16,256]{2,1,0:T(8,128)(2,1)S(1)} %get-tuple-element.17), channel_id=1, source_target_pairs={{0,32},{8,40},{16,48},{24,56},{32,64},{40,72},{48,80},{56,88},{64,... | collective-permute-start | bytes 196616 | tf_op jit(solution)/shard_map/ppermute | solution.py:184
  64.7 1.5 %collective-permute-done.7 = bf16[8,16,256]{2,1,0:T(8,128)(2,1)S(1)} collective-permute-done((bf16[8,16,256]{2,1,0:T(8,128)(2,1)S(1)}, bf16[8,16,256]{2,1,0:T(8,128)(2,1)S(1)}, u32[]{:S(2)}, u32[]{:S(2)}) %collective-permute-start.7) | collective-permute-done | bytes 65568 | tf_op jit(solution)/shard_map/ppermute | solution.py:184
  66.2 6.2 %collective-permute-start.8 = (bf16[16,16,256]{2,1,0:T(8,128)(2,1)S(1)}, bf16[16,16,256]{2,1,0:T(8,128)(2,1)S(1)}, u32[]{:S(2)}, u32[]{:S(2)}) collective-permute-start(bf16[16,16,256]{2,1,0:T(8,128)(2,1)S(1)} %get-tuple-element.13), channel_id=1, source_target_pairs={{0,16},{8,24},{16,32},{24,40},{32,48},{40,56},{48,64},{56,72},{64,... | collective-permute-start | bytes 393224 | tf_op jit(solution)/shard_map/ppermute | solution.py:184
  72.4 1.9 %collective-permute-done.8 = bf16[16,16,256]{2,1,0:T(8,128)(2,1)S(1)} collective-permute-done((bf16[16,16,256]{2,1,0:T(8,128)(2,1)S(1)}, bf16[16,16,256]{2,1,0:T(8,128)(2,1)S(1)}, u32[]{:S(2)}, u32[]{:S(2)}) %collective-permute-start.8) | collective-permute-done | bytes 131104 | tf_op jit(solution)/shard_map/ppermute | solution.py:184
  74.4 3.7 %collective-permute-start.9 = (bf16[640,256]{1,0:T(8,128)(2,1)S(1)}, bf16[640,256]{1,0:T(8,128)(2,1)S(1)}, u32[]{:S(2)}, u32[]{:S(2)}) collective-permute-start(bf16[640,256]{1,0:T(8,128)(2,1)S(1)} %pad_maximum_fusion.2.mine_ref), channel_id=1, source_target_pairs={{0,8},{8,0},{16,24},{24,16},{32,40},{40,32},{48,56},{56,48},{64,72... | collective-permute-start | bytes 983048 | tf_op jit(solution)/shard_map/ppermute | solution.py:195
  78.1 8.5 %own_parity.1 = (f32[1,1024]{1,0:T(1,128)S(1)}, f32[1,1024]{1,0:T(1,128)S(1)}, f32[128,1024]{1,0:T(8,128)S(1)}, bf16[128,1024]{1,0:T(8,128)(2,1)S(1)}) custom-call(s32[1]{0:T(128)} %bitcast.meta_ref, bf16[128,1280]{1,0:T(8,128)(2,1)S(1)} %bitcast.29, bf16[1024,512]{1,0:T(8,128)(2,1)S(1)} %bitcast.27, s32[64,128]{1,0:T(8,128)S(1)} %bitcast.31), custom_call_target="tpu_custom_call" | custom-call | tf_op jit(solution)/shard_map/own_parity/pallas_call | solution.py:206
  86.6 11.5 %other_parity.1 = bf16[128,1024]{1,0:T(8,128)(2,1)S(1)} custom-call(s32[1]{0:T(128)} %bitcast.meta_ref, s32[32]{0:T(128)S(1)} %bitcast.33, bf16[128,1024]{1,0:T(8,128)(2,1)S(1)} %get-tuple-element.9.qt_ref, bf16[1024,512]{1,0:T(8,128)(2,1)S(1)} %collective-permute-done.2.kv_ref, bf16[640,256]{1,0:T(8,128)(2,1)S(1)} %collective-permute-done.9.side_ref, ...), custom_call_target="tpu_custom_call" | custom-call | tf_op jit(solution)/shard_map/other_parity/pallas_call | solution.py:214
  98.1 0.5 broadcast.14
  98.6 0.8 reduce
  99.4 0.2 reshape.47
  99.6 19.1 %all_to_all.38 = bf16[8,2,8192]{2,1,0:T(2,128)(2,1)S(1)} all-to-all(bf16[8,2,8192]{2,1,0:T(2,128)(2,1)S(1)} %reshape.47), channel_id=1, replica_groups=mesh['seq'=64,'head'=8] {'head'}, dimensions={0} | all-to-all | bytes 524288 | tf_op jit(solution)/shard_map/all_to_all | solution.py:228
  118.8 0.3 reshape.48
  119.0 0.1 copy.25
  119.1 0.9 copy.24
  (33 shorter events, 0.3 us)
Async XLA Ops:
  0.0 6.7 %collective-permute-start.1 = (bf16[8,16,256]{2,0,1:T(8,128)(2,1)}, bf16[8,16,256]{2,0,1:T(8,128)(2,1)S(1)}, u32[]{:S(2)}, u32[]{:S(2)}) collective-permute-start(bf16[8,16,256]{2,0,1:T(8,128)(2,1)} %bitcast.37), channel_id=1, source_target_pairs={{0,256},{8,264},{16,272},{24,280},{32,288},{40,296},{48,304},{56,3... | collective-permute-start | bytes 196616 | tf_op jit(solution)/shard_map/ppermute | solution.py:179
  1.3 5.6 %collective-permute-start = (bf16[8,16,256]{2,0,1:T(8,128)(2,1)}, bf16[8,16,256]{2,0,1:T(8,128)(2,1)S(1)}, u32[]{:S(2)}, u32[]{:S(2)}) collective-permute-start(bf16[8,16,256]{2,0,1:T(8,128)(2,1)} %bitcast.38), channel_id=1, source_target_pairs={{0,128},{8,136},{16,144},{24,152},{32,160},{40,168},{48,176},{56,1... | collective-permute-start | bytes 196616 | tf_op jit(solution)/shard_map/ppermute | solution.py:180
  8.1 15.8 %copy-start.4 = (bf16[1,16,1,256]{3,1,2,0:T(8,128)(2,1)S(1)}, bf16[1,16,1,256]{3,1,2,0:T(8,128)(2,1)}, u32[]{:S(2)}) copy-start(bf16[1,16,1,256]{3,1,2,0:T(8,128)(2,1)} %param.8) | copy-start | bytes 24580
  8.1 26.0 %copy-start.3 = (bf16[16,8,256]{2,1,0:T(8,128)(2,1)S(1)}, bf16[16,8,256]{2,1,0:T(8,128)(2,1)}, u32[]{:S(2)}) copy-start(bf16[16,8,256]{2,1,0:T(8,128)(2,1)} %param.6) | copy-start | bytes 196612
  8.1 26.0 %copy-start.2 = (bf16[16,8,1024]{2,1,0:T(8,128)(2,1)S(1)}, bf16[16,8,1024]{2,1,0:T(8,128)(2,1)}, u32[]{:S(2)}) copy-start(bf16[16,8,1024]{2,1,0:T(8,128)(2,1)} %param.5) | copy-start | bytes 786436
  8.1 42.1 %all-to-all-start.1 = ((bf16[64,16,512]{2,1,0:T(8,128)(2,1)}), bf16[64,16,512]{2,1,0:T(8,128)(2,1)S(1)}, u32[]{:S(2)}, u32[]{:S(2)}) async-start(bf16[64,16,512]{2,1,0:T(8,128)(2,1)} %pad_maximum_fusion), calls=%async_computation.1 | async-start | bytes 2097152 | tf_op jit(solution)/shard_map/all_to_all | solution.py:190
  23.9 11.2 %collective-permute-start.3 = (bf16[1,16,256]{2,1,0:T(8,128)(2,1)S(1)}, bf16[1,16,256]{2,1,0:T(8,128)(2,1)S(1)}, u32[]{:S(2)}, u32[]{:S(2)}) collective-permute-start(bf16[1,16,256]{2,1,0:T(8,128)(2,1)S(1)} %bitcast.40), channel_id=1, source_target_pairs={{0,128},{8,136},{16,144},{24,152},{32,160},{40,168},{48,176},{56,1... | collective-permute-start | bytes 24584 | tf_op jit(solution)/shard_map/ppermute | solution.py:182
  27.6 7.5 %collective-permute-start.4 = (bf16[1,16,256]{2,1,0:T(8,128)(2,1)S(1)}, bf16[1,16,256]{2,1,0:T(8,128)(2,1)S(1)}, u32[]{:S(2)}, u32[]{:S(2)}) collective-permute-start(bf16[1,16,256]{2,1,0:T(8,128)(2,1)S(1)} %bitcast.41), channel_id=1, source_target_pairs={{0,256},{8,264},{16,272},{24,280},{32,288},{40,296},{48,304},{56,3... | collective-permute-start | bytes 24584 | tf_op jit(solution)/shard_map/ppermute | solution.py:182
  32.2 5.9 %collective-permute-start.5 = (bf16[1,16,256]{2,1,0:T(8,128)(2,1)S(1)}, bf16[1,16,256]{2,1,0:T(8,128)(2,1)S(1)}, u32[]{:S(2)}, u32[]{:S(2)}) collective-permute-start(bf16[1,16,256]{2,1,0:T(8,128)(2,1)S(1)} %bitcast.42), channel_id=1, source_target_pairs={{0,384},{8,392},{16,400},{24,408},{32,416},{40,424},{48,432},{56,4... | collective-permute-start | bytes 24584 | tf_op jit(solution)/shard_map/ppermute | solution.py:182
  38.1 21.4 %collective-permute-start.6 = (bf16[4,16,256]{2,1,0:T(8,128)(2,1)S(1)}, bf16[4,16,256]{2,1,0:T(8,128)(2,1)S(1)}, u32[]{:S(2)}, u32[]{:S(2)}) collective-permute-start(bf16[4,16,256]{2,1,0:T(8,128)(2,1)S(1)} %pad_maximum_fusion.3), channel_id=1, source_target_pairs={{0,64},{8,72},{16,80},{24,88},{32,96},{40,104},{48,112},{56,120},{... | collective-permute-start | bytes 98312 | tf_op jit(solution)/shard_map/ppermute | solution.py:184
  42.8 35.3 %copy-start = (s32[8192]{0:T(1024)S(1)}, s32[8192]{0:T(1024)}, u32[]{:S(2)}) copy-start(s32[8192]{0:T(1024)} %param.7) | copy-start | bytes 98308
  50.2 24.1 %all-to-all-start = ((bf16[16,8,1280]{2,0,1:T(8,128)(2,1)}), bf16[16,8,1280]{2,0,1:T(8,128)(2,1)S(1)}, u32[]{:S(2)}, u32[]{:S(2)}) async-start(bf16[16,8,1280]{2,0,1:T(8,128)(2,1)} %pad_maximum_fusion.1), calls=%async_computation | async-start | bytes 655360 | tf_op jit(solution)/shard_map/all_to_all | solution.py:186
  53.7 32.9 %collective-permute-start.2 = (bf16[1024,512]{1,0:T(8,128)(2,1)S(1)}, bf16[1024,512]{1,0:T(8,128)(2,1)S(1)}, u32[]{:S(2)}, u32[]{:S(2)}) collective-permute-start(bf16[1024,512]{1,0:T(8,128)(2,1)S(1)} %bitcast.26), channel_id=1, source_target_pairs={{0,8},{8,0},{16,24},{24,16},{32,40},{40,32},{48,56},{56,48},{64,72... | collective-permute-start | bytes 3145736 | tf_op jit(solution)/shard_map/ppermute | solution.py:196
  59.5 6.6 %collective-permute-start.7 = (bf16[8,16,256]{2,1,0:T(8,128)(2,1)S(1)}, bf16[8,16,256]{2,1,0:T(8,128)(2,1)S(1)}, u32[]{:S(2)}, u32[]{:S(2)}) collective-permute-start(bf16[8,16,256]{2,1,0:T(8,128)(2,1)S(1)} %get-tuple-element.17), channel_id=1, source_target_pairs={{0,32},{8,40},{16,48},{24,56},{32,64},{40,72},{48,80},{56,88},{64,... | collective-permute-start | bytes 196616 | tf_op jit(solution)/shard_map/ppermute | solution.py:184
  66.2 8.1 %collective-permute-start.8 = (bf16[16,16,256]{2,1,0:T(8,128)(2,1)S(1)}, bf16[16,16,256]{2,1,0:T(8,128)(2,1)S(1)}, u32[]{:S(2)}, u32[]{:S(2)}) collective-permute-start(bf16[16,16,256]{2,1,0:T(8,128)(2,1)S(1)} %get-tuple-element.13), channel_id=1, source_target_pairs={{0,16},{8,24},{16,32},{24,40},{32,48},{40,56},{48,64},{56,72},{64,... | collective-permute-start | bytes 393224 | tf_op jit(solution)/shard_map/ppermute | solution.py:184
  74.3 12.3 %copy-start.1 = (s32[1,32]{1,0:T(1,128)S(1)}, s32[1,32]{1,0:T(1,128)}, u32[]{:S(2)}) copy-start(s32[1,32]{1,0:T(1,128)} %param.9) | copy-start | bytes 388
  74.4 12.2 %collective-permute-start.9 = (bf16[640,256]{1,0:T(8,128)(2,1)S(1)}, bf16[640,256]{1,0:T(8,128)(2,1)S(1)}, u32[]{:S(2)}, u32[]{:S(2)}) collective-permute-start(bf16[640,256]{1,0:T(8,128)(2,1)S(1)} %pad_maximum_fusion.2.mine_ref), channel_id=1, source_target_pairs={{0,8},{8,0},{16,24},{24,16},{32,40},{40,32},{48,56},{56,48},{64,72... | collective-permute-start | bytes 983048 | tf_op jit(solution)/shard_map/ppermute | solution.py:195

commit v2 on v1

v2 whole, which is shorter than its diff:
```python
import jax
import jax.numpy as jnp
from jax import lax
from jax.experimental import pallas as pl
from jax.experimental.pallas import tpu as pltpu
from jax.sharding import PartitionSpec as P

D = 128
PAIR = 2 * D
ROWS = 128
GROUP = 8
QR = ROWS * GROUP
NX, NY = 4, 8
PAGES = 32
PAGE = 16
BLOCKS = 4
TILE = 512
SCALE2 = D ** (-0.5) * 1.4426950408889634
LOW = -1e30


def x_shift(by):
    return [
        ((x * NY + y) * 2 + c, ((x + by) * NY + y) * 2 + c)
        for x in range(NX) for y in range(NY) for c in range(2) if 0 <= x + by < NX
    ]


def x_ring(by):
    return [
        ((x * NY + y) * 2 + c, (((x + by) % NX) * NY + y) * 2 + c)
        for x in range(NX) for y in range(NY) for c in range(2)
    ]


def y_ring(by):
    return [
        ((x * NY + y) * 2 + c, (x * NY + (y + by) % NY) * 2 + c)
        for x in range(NX) for y in range(NY) for c in range(2)
    ]


SWAP = [(i, i ^ 1) for i in range(2 * NX * NY)]
Y_GROUPS = [[(x * NY + y) * 2 + c for y in range(NY)] for x in range(NX) for c in range(2)]


def fold(keys, values, mask, qt_ref, m_ref, l_ref, acc_ref):
    twice = jnp.concatenate([keys, keys], axis=1)
    lifted = jnp.concatenate([values.T, jnp.ones((16, keys.shape[0]), jnp.bfloat16)], axis=0)

    def scores_of(at):
        scores = jnp.dot(twice, qt_ref[:, at:at + TILE], preferred_element_type=jnp.float32)
        if mask is not None:
            scores = jnp.where(jnp.concatenate([mask] * (TILE // ROWS), axis=1), scores, LOW)
        return scores

    coming = scores_of(0)
    for at in range(0, QR, TILE):
        cols = slice(at, at + TILE)
        scores = coming
        if at + TILE < QR:
            coming = scores_of(at + TILE)
        old = m_ref[:, cols]
        top = jnp.maximum(old, jnp.max(scores, axis=0, keepdims=True))
        weights = jnp.exp2(scores - top).astype(jnp.bfloat16)
        factor = jnp.exp2(old - top)
        m_ref[:, cols] = top
        mixed = jnp.dot(lifted, weights, preferred_element_type=jnp.float32)
        l_ref[:, cols] = l_ref[:, cols] * factor + mixed[D:D + 1]
        acc_ref[:, cols] = acc_ref[:, cols] * factor + mixed[:D]


def starts_of(ids_ref, own):
    ids = ids_ref[...]
    starts = [jnp.sum((ids < b).astype(jnp.int32)) for b in range(1, 4)]
    own_ids = ids_ref[pl.ds(own, 1), :]
    row_start = jnp.zeros_like(own_ids)
    for b in range(1, 4):
        row_start = jnp.where(own_ids == b, starts[b - 1], row_start)
    return row_start, jnp.min(row_start), jnp.max(row_start)


def mask_of(block, own, row_start):
    key_rows = lax.broadcasted_iota(jnp.int32, (ROWS, ROWS), 0) + block * ROWS
    query_rows = lax.broadcasted_iota(jnp.int32, (ROWS, ROWS), 1) + own * ROWS
    return (key_rows >= row_start) & (key_rows <= query_rows)


def near_kernel(meta_ref, table_ref, q_ref, mine_ref, side_ref, ids_ref, qt_ref, m_ref, l_ref, acc_ref, prefix_ref):
    own = meta_ref[0]
    core, y, x = own % 2, (own // 2) % NY, own // (2 * NY)
    row_start, first, last = starts_of(ids_ref, own)
    for g in range(GROUP):
        scaled = q_ref[:, g * D:(g + 1) * D].astype(jnp.float32) * SCALE2
        high = scaled.astype(jnp.bfloat16)
        low = (scaled - high.astype(jnp.float32)).astype(jnp.bfloat16)
        qt_ref[:D, g * ROWS:(g + 1) * ROWS] = high.T
        qt_ref[D:, g * ROWS:(g + 1) * ROWS] = low.T
    m_ref[...] = jnp.full_like(m_ref, LOW)
    l_ref[...] = jnp.zeros_like(l_ref)
    acc_ref[...] = jnp.zeros_like(acc_ref)
    state = (qt_ref, m_ref, l_ref, acc_ref)
    fold(mine_ref[:ROWS, :D], mine_ref[:ROWS, D:], mask_of(own, own, row_start), *state)

    @pl.when((core == 1) & (own * ROWS > first))
    def _():
        fold(side_ref[:ROWS, :D], side_ref[:ROWS, D:], mask_of(own - 1, own, row_start), *state)

    for i in range(PAGES):
        page = table_ref[i]
        off = (y + NY - (page // 2) % NY) % NY
        unit = (x + NX - page // (2 * NY)) % NX + 4 * (off // 4) + 8 * ((off // 2) % 2) + 16 * (off % 2)
        rows = pl.ds(pl.multiple_of(ROWS + unit * PAGE, PAGE), PAGE)

        @pl.when(page % 2 == core)
        def _():
            prefix_ref[i * PAGE:(i + 1) * PAGE, :] = mine_ref[rows, :]

        @pl.when(page % 2 != core)
        def _():
            prefix_ref[i * PAGE:(i + 1) * PAGE, :] = side_ref[rows, :]

    fold(prefix_ref[:, :D], prefix_ref[:, D:], None, *state)


def window(kv_ref, core, own, ids_ref, qt_ref, m_ref, l_ref, acc_ref):
    row_start, first, last = starts_of(ids_ref, own)
    chip = own // 2
    x = chip // NY
    lowest = (jnp.maximum(first // ROWS - core, -1) + 1) // 2
    steps = jnp.maximum(chip - lowest + BLOCKS - 1, 0) // BLOCKS

    def step(i, carry):
        base = chip - BLOCKS * (i + 1)
        pairs = []
        for b in range(BLOCKS):
            at = jnp.maximum(base + b, 0)
            slot = (at % NY) * 2 + jnp.where(at // NY == x - 1, 0, 1)
            pairs.append(kv_ref[pl.ds(pl.multiple_of(slot * ROWS, ROWS), ROWS), :])
        keys = jnp.concatenate([pair[:, :D] for pair in pairs], axis=0)
        values = jnp.concatenate([pair[:, D:] for pair in pairs], axis=0)
        whole = (2 * base + core) * ROWS >= last

        @pl.when(whole)
        def _():
            fold(keys, values, None, qt_ref, m_ref, l_ref, acc_ref)

        @pl.when(jnp.logical_not(whole))
        def _():
            mask = jnp.concatenate(
                [mask_of(2 * (base + b) + core, own, row_start) for b in range(BLOCKS)], axis=0
            )
            fold(keys, values, mask, qt_ref, m_ref, l_ref, acc_ref)

        return carry

    lax.fori_loop(0, steps, step, 0)


def own_kernel(meta_ref, kv_ref, ids_ref, qt_ref, m_in, l_in, acc_in, m_ref, l_ref, acc_ref):
    m_ref[...] = m_in[...]
    l_ref[...] = l_in[...]
    acc_ref[...] = acc_in[...]
    own = meta_ref[0]
    window(kv_ref, own % 2, own, ids_ref, qt_ref, m_ref, l_ref, acc_ref)


def last_kernel(meta_ref, kv_ref, ids_ref, qt_ref, m_in, l_in, acc_in, out_ref, m_ref, l_ref, acc_ref):
    m_ref[...] = m_in[...]
    l_ref[...] = l_in[...]
    acc_ref[...] = acc_in[...]
    own = meta_ref[0]
    window(kv_ref, 1 - own % 2, own, ids_ref, qt_ref, m_ref, l_ref, acc_ref)
    result = (acc_ref[...] * (1.0 / l_ref[...])).astype(jnp.bfloat16)
    for g in range(GROUP):
        out_ref[:, g * D:(g + 1) * D] = result[:, g * ROWS:(g + 1) * ROWS].T


VM = pl.BlockSpec(memory_space=pltpu.VMEM)
SM = pl.BlockSpec(memory_space=pltpu.SMEM)


def cost(keys):
    return pl.CostEstimate(flops=4 * D * QR * keys, bytes_accessed=1 << 20, transcendentals=QR * keys)


def per_device(queries, branch_key_value, branch_ids, pool, page_table):
    me = lax.axis_index("seq")
    y = (me // 2) % NY
    page = pool.reshape(1, PAGE, PAIR)
    pages = jnp.concatenate([page] + [lax.ppermute(page, "seq", x_ring(k)) for k in (1, 2, 3)], axis=0)
    for by in (4, 2, 1):
        pages = jnp.concatenate([pages, lax.ppermute(pages, "seq", y_ring(by))], axis=0)
    wide = jnp.concatenate([queries, branch_key_value], axis=2)
    wide = lax.all_to_all(wide, "head", split_axis=1, concat_axis=0, tiled=True).reshape(ROWS, GROUP * D + PAIR)
    own = wide[:, GROUP * D:]
    two_back = lax.ppermute(own, "seq", x_shift(2))
    one_back = lax.ppermute(own, "seq", x_shift(1))
    target = jnp.arange(NY, dtype=jnp.int32)[:, None, None]
    mixed = jnp.where(target > y, own[None], two_back[None])
    send = jnp.stack([jnp.broadcast_to(one_back[None], mixed.shape), mixed], axis=1)
    kv = lax.all_to_all(send, "seq", split_axis=0, concat_axis=0, tiled=True, axis_index_groups=Y_GROUPS)
    kv = kv.reshape(2 * NY * ROWS, PAIR)
    mine = jnp.concatenate([own, pages.reshape(PAGES * PAGE, PAIR)], axis=0)
    side = lax.ppermute(mine, "seq", SWAP)
    kv_side = lax.ppermute(kv, "seq", SWAP)

    ids = branch_ids.reshape(2 * NX * NY, ROWS)
    meta = me.astype(jnp.int32).reshape(1)
    state = [
        jax.ShapeDtypeStruct((1, QR), jnp.float32),
        jax.ShapeDtypeStruct((1, QR), jnp.float32),
        jax.ShapeDtypeStruct((D, QR), jnp.float32),
    ]
    params = pltpu.CompilerParams(vmem_limit_bytes=40 * 1024 * 1024)
    qt, m, l, acc = pl.pallas_call(
        near_kernel,
        out_shape=[jax.ShapeDtypeStruct((PAIR, QR), jnp.bfloat16)] + state,
        in_specs=[SM, SM, VM, VM, VM, VM],
        out_specs=[VM] * 4,
        scratch_shapes=[pltpu.VMEM((PAGES * PAGE, PAIR), jnp.bfloat16)],
        compiler_params=params,
        cost_estimate=cost(768),
        name="near_keys",
    )(meta, page_table.reshape(PAGES), wide, mine, side, ids)
    m, l, acc = pl.pallas_call(
        own_kernel,
        out_shape=state,
        in_specs=[SM] + [VM] * 6,
        out_specs=[VM] * 3,
        compiler_params=params,
        cost_estimate=cost(2048),
        name="own_parity",
    )(meta, kv, ids, qt, m, l, acc)
    out = pl.pallas_call(
        last_kernel,
        out_shape=jax.ShapeDtypeStruct((ROWS, GROUP * D), jnp.bfloat16),
        in_specs=[SM] + [VM] * 6,
        out_specs=VM,
        scratch_shapes=[
            pltpu.VMEM((1, QR), jnp.float32),
            pltpu.VMEM((1, QR), jnp.float32),
            pltpu.VMEM((D, QR), jnp.float32),
        ],
        compiler_params=params,
        cost_estimate=cost(2048),
        name="other_parity",
    )(meta, kv_side, ids, qt, m, l, acc)
    out = lax.all_to_all(out.reshape(8, ROWS // 8, GROUP * D), "head", split_axis=0, concat_axis=0, tiled=True)
    return jnp.transpose(out, (1, 0, 2))


def solution(mesh):
    return jax.shard_map(
        per_device,
        mesh=mesh,
        in_specs=(
            P(("seq", "head"), None, None),
            P(("seq", "head"), None, None),
            P(),
            P("seq", None, "head", None),
            P("head", None),
        ),
        out_specs=P(("seq", "head"), None, None),
        check_vma=False,
    )
```

time: 121 us -> 120 us (level)
  the two profiles are of different devices: /device:TPU:63 before, /device:TPU:5 now
where the time goes in v2:
time: 120 us; the launch traced here: 119 us
  starting transfers between devices  51.9 us (43%)
  waiting for transfers between devices  36.9 us (31%)
  blocking collectives  14.8 us (12%)
  Pallas kernels  9.42 us (8%)
  local copies, waits for them, and re-layouts  3.56 us (3%)
  other arithmetic  1.98 us (2%)
    all_to_all x1, blocking collectives, per_device(): lax.all_to_all(out.reshape(8, ROWS // 8, GROUP * D), 'head', split_axis=0...  14.8 us
    all_to_all x1, waiting for transfers between devices, per_device(): lax.all_to_all(wide, 'head', split_axis=1, concat_axis=0, tiled=True)  11.9 us
    ppermute x3, starting transfers between devices, per_device(): lax.ppermute(pages, 'seq', y_ring(by))  11.3 us
    ppermute x3, waiting for transfers between devices, per_device(): lax.ppermute(pages, 'seq', y_ring(by))  11 us
    all_to_all x1, starting transfers between devices, per_device(): lax.all_to_all(wide, 'head', split_axis=1, concat_axis=0, tiled=True)  10 us
    ppermute x3, starting transfers between devices, per_device(): lax.ppermute(page, 'seq', x_ring(k))  9.2 us
    all_to_all x1, waiting for transfers between devices, per_device(): lax.all_to_all(send, 'seq', split_axis=0, concat_axis=0, tiled=True, axis...  8.47 us
    all_to_all x1, starting transfers between devices, per_device(): lax.all_to_all(send, 'seq', split_axis=0, concat_axis=0, tiled=True, axis...  6.95 us
  transfers between devices with their start and end apart: 12, of which 9 were waited for; matrix products, arithmetic and copies ran while one was open for 0% of the time, Pallas kernels for 6%

profile of v2, /device:TPU:5, one launch (start us, length us, event | category | flops | bytes accessed | tf_op | source)
XLA Modules:
  0.0 118.8 jit_solution(18175007652441267332)
XLA Ops:
  0.0 0.9 copy.9
  0.9 1.1 copy.8
  2.0 0.8 pad_maximum_fusion.1
  2.7 10.0 %all-to-all-start = ((bf16[16,8,1280]{2,0,1:T(8,128)(2,1)}), bf16[16,8,1280]{2,0,1:T(8,128)(2,1)S(1)}, u32[]{:S(2)}, u32[]{:S(2)}) async-start(bf16[16,8,1280]{2,0,1:T(8,128)(2,1)} %pad_maximum_fusion.1), calls=%async_computation | async-start | bytes 655360 | tf_op jit(solution)/shard_map/all_to_all | solution.py:195
  12.8 11.9 %all-to-all-done = bf16[16,8,1280]{2,0,1:T(8,128)(2,1)S(1)} async-done(((bf16[16,8,1280]{2,0,1:T(8,128)(2,1)}), bf16[16,8,1280]{2,0,1:T(8,128)(2,1)S(1)}, u32[]{:S(2)}, u32[]{:S(2)}) %all-to-all-start) | async-done | bytes 327712 | tf_op jit(solution)/shard_map/all_to_all | solution.py:195
  24.7 1.3 %collective-permute-start.1 = (bf16[128,256]{1,0:T(8,128)(2,1)S(1)}, bf16[128,256]{1,0:T(8,128)(2,1)S(1)}, u32[]{:S(2)}, u32[]{:S(2)}) collective-permute-start(bf16[128,256]{1,0:T(8,128)(2,1)S(1)} %slice.4), channel_id=1, source_target_pairs={{0,256},{8,264},{16,272},{24,280},{32,288},{40,296},{48,304},{56,3... | collective-permute-start | bytes 196616 | tf_op jit(solution)/shard_map/ppermute | solution.py:197
  26.0 2.8 %collective-permute-start = (bf16[128,256]{1,0:T(8,128)(2,1)S(1)}, bf16[128,256]{1,0:T(8,128)(2,1)S(1)}, u32[]{:S(2)}, u32[]{:S(2)}) collective-permute-start(bf16[128,256]{1,0:T(8,128)(2,1)S(1)} %slice.4), channel_id=1, source_target_pairs={{0,128},{8,136},{16,144},{24,152},{32,160},{40,168},{48,176},{56,1... | collective-permute-start | bytes 196616 | tf_op jit(solution)/shard_map/ppermute | solution.py:198
  28.8 2.4 %collective-permute-done.1 = bf16[128,256]{1,0:T(8,128)(2,1)S(1)} collective-permute-done((bf16[128,256]{1,0:T(8,128)(2,1)S(1)}, bf16[128,256]{1,0:T(8,128)(2,1)S(1)}, u32[]{:S(2)}, u32[]{:S(2)}) %collective-permute-start.1) | collective-permute-done | bytes 65568 | tf_op jit(solution)/shard_map/ppermute | solution.py:197
  31.2 0.1 broadcast_select_fusion
  31.3 1.0 collective-permute-done
  32.3 1.1 pad_maximum_fusion
  33.4 7.0 %all-to-all-start.1 = ((bf16[8,2,128,256]{3,2,1,0:T(8,128)(2,1)}), bf16[8,2,128,256]{3,2,1,0:T(8,128)(2,1)S(1)}, u32[]{:S(2)}, u32[]{:S(2)}) async-start(bf16[8,2,128,256]{3,2,1,0:T(8,128)(2,1)} %pad_maximum_fusion), calls=%async_computation.1 | async-start | bytes 2097152 | tf_op jit(solution)/shard_map/all_to_all | solution.py:202
  40.3 3.6 %collective-permute-start.5 = (bf16[1,16,256]{2,1,0:T(8,128)(2,1)S(1)}, bf16[1,16,256]{2,1,0:T(8,128)(2,1)S(1)}, u32[]{:S(2)}, u32[]{:S(2)}) collective-permute-start(bf16[1,16,256]{2,1,0:T(8,128)(2,1)S(1)} %bitcast.27), channel_id=1, source_target_pairs={{0,384},{8,392},{16,400},{24,408},{32,416},{40,424},{48,432},{56,4... | collective-permute-start | bytes 24584 | tf_op jit(solution)/shard_map/ppermute | solution.py:191
  43.9 2.0 %collective-permute-start.4 = (bf16[1,16,256]{2,1,0:T(8,128)(2,1)S(1)}, bf16[1,16,256]{2,1,0:T(8,128)(2,1)S(1)}, u32[]{:S(2)}, u32[]{:S(2)}) collective-permute-start(bf16[1,16,256]{2,1,0:T(8,128)(2,1)S(1)} %bitcast.28), channel_id=1, source_target_pairs={{0,256},{8,264},{16,272},{24,280},{32,288},{40,296},{48,304},{56,3... | collective-permute-start | bytes 24584 | tf_op jit(solution)/shard_map/ppermute | solution.py:191
  45.9 3.6 %collective-permute-start.3 = (bf16[1,16,256]{2,1,0:T(8,128)(2,1)S(1)}, bf16[1,16,256]{2,1,0:T(8,128)(2,1)S(1)}, u32[]{:S(2)}, u32[]{:S(2)}) collective-permute-start(bf16[1,16,256]{2,1,0:T(8,128)(2,1)S(1)} %bitcast.29), channel_id=1, source_target_pairs={{0,128},{8,136},{16,144},{24,152},{32,160},{40,168},{48,176},{56,1... | collective-permute-start | bytes 24584 | tf_op jit(solution)/shard_map/ppermute | solution.py:191
  49.6 0.2 collective-permute-done.4
  49.8 0.8 collective-permute-done.3
  50.6 7.3 %collective-permute-start.6 = (bf16[4,16,256]{2,1,0:T(8,128)(2,1)S(1)}, bf16[4,16,256]{2,1,0:T(8,128)(2,1)S(1)}, u32[]{:S(2)}, u32[]{:S(2)}) collective-permute-start(bf16[4,16,256]{2,1,0:T(8,128)(2,1)S(1)} %pad_maximum_fusion.3), channel_id=1, source_target_pairs={{0,64},{8,72},{16,80},{24,88},{32,96},{40,104},{48,112},{56,120},{... | collective-permute-start | bytes 98312 | tf_op jit(solution)/shard_map/ppermute | solution.py:193
  57.9 8.5 %all-to-all-done.1 = bf16[8,2,128,256]{3,2,1,0:T(8,128)(2,1)S(1)} async-done(((bf16[8,2,128,256]{3,2,1,0:T(8,128)(2,1)}), bf16[8,2,128,256]{3,2,1,0:T(8,128)(2,1)S(1)}, u32[]{:S(2)}, u32[]{:S(2)}) %all-to-all-start.1) | async-done | bytes 1048608 | tf_op jit(solution)/shard_map/all_to_all | solution.py:202
  66.4 6.6 %collective-permute-start.2 = (bf16[2048,256]{1,0:T(8,128)(2,1)S(1)}, bf16[2048,256]{1,0:T(8,128)(2,1)S(1)}, u32[]{:S(2)}, u32[]{:S(2)}) collective-permute-start(bf16[2048,256]{1,0:T(8,128)(2,1)S(1)} %bitcast.16), channel_id=1, source_target_pairs={{0,8},{8,0},{16,24},{24,16},{32,40},{40,32},{48,56},{56,48},{64,72... | collective-permute-start | bytes 3145736 | tf_op jit(solution)/shard_map/ppermute | solution.py:206
  73.0 1.9 %collective-permute-start.7 = (bf16[8,16,256]{2,1,0:T(8,128)(2,1)S(1)}, bf16[8,16,256]{2,1,0:T(8,128)(2,1)S(1)}, u32[]{:S(2)}, u32[]{:S(2)}) collective-permute-start(bf16[8,16,256]{2,1,0:T(8,128)(2,1)S(1)} %get-tuple-element.23), channel_id=1, source_target_pairs={{0,32},{8,40},{16,48},{24,56},{32,64},{40,72},{48,80},{56,88},{64,... | collective-permute-start | bytes 196616 | tf_op jit(solution)/shard_map/ppermute | solution.py:193
  75.0 5.8 %collective-permute-done.7 = bf16[8,16,256]{2,1,0:T(8,128)(2,1)S(1)} collective-permute-done((bf16[8,16,256]{2,1,0:T(8,128)(2,1)S(1)}, bf16[8,16,256]{2,1,0:T(8,128)(2,1)S(1)}, u32[]{:S(2)}, u32[]{:S(2)}) %collective-permute-start.7) | collective-permute-done | bytes 65568 | tf_op jit(solution)/shard_map/ppermute | solution.py:193
  80.8 2.1 %collective-permute-start.8 = (bf16[16,16,256]{2,1,0:T(8,128)(2,1)S(1)}, bf16[16,16,256]{2,1,0:T(8,128)(2,1)S(1)}, u32[]{:S(2)}, u32[]{:S(2)}) collective-permute-start(bf16[16,16,256]{2,1,0:T(8,128)(2,1)S(1)} %get-tuple-element.19), channel_id=1, source_target_pairs={{0,16},{8,24},{16,32},{24,40},{32,48},{40,56},{48,64},{56,72},{64,... | collective-permute-start | bytes 393224 | tf_op jit(solution)/shard_map/ppermute | solution.py:193
  83.0 5.1 %collective-permute-done.8 = bf16[16,16,256]{2,1,0:T(8,128)(2,1)S(1)} collective-permute-done((bf16[16,16,256]{2,1,0:T(8,128)(2,1)S(1)}, bf16[16,16,256]{2,1,0:T(8,128)(2,1)S(1)}, u32[]{:S(2)}, u32[]{:S(2)}) %collective-permute-start.8) | collective-permute-done | bytes 131104 | tf_op jit(solution)/shard_map/ppermute | solution.py:193
  88.1 3.7 %collective-permute-start.9 = (bf16[640,256]{1,0:T(8,128)(2,1)S(1)}, bf16[640,256]{1,0:T(8,128)(2,1)S(1)}, u32[]{:S(2)}, u32[]{:S(2)}) collective-permute-start(bf16[640,256]{1,0:T(8,128)(2,1)S(1)} %pad_maximum_fusion.2.mine_ref), channel_id=1, source_target_pairs={{0,8},{8,0},{16,24},{24,16},{32,40},{40,32},{48,56},{56,48},{64,72... | collective-permute-start | bytes 983048 | tf_op jit(solution)/shard_map/ppermute | solution.py:205
  91.8 1.2 %collective-permute-done.9.side_ref = bf16[640,256]{1,0:T(8,128)(2,1)S(1)} collective-permute-done((bf16[640,256]{1,0:T(8,128)(2,1)S(1)}, bf16[640,256]{1,0:T(8,128)(2,1)S(1)}, u32[]{:S(2)}, u32[]{:S(2)}) %collective-permute-start.9) | collective-permute-done | bytes 327712 | tf_op jit(solution)/shard_map/ppermute | solution.py:205
  93.1 0.7 copy-done.1
  93.7 3.8 %near_keys.1 = (bf16[256,1024]{1,0:T(8,128)(2,1)S(1)}, f32[1,1024]{1,0:T(1,128)S(1)}, f32[1,1024]{1,0:T(1,128)S(1)}, f32[128,1024]{1,0:T(8,128)S(1)}) custom-call(s32[1]{0:T(128)} %bitcast.meta_ref, s32[32]{0:T(128)S(1)} %bitcast.24, bf16[128,1280]{1,0:T(8,128)(2,1)S(1)} %bitcast.19, bf16[640,256]{1,0:T(8,128)(2,1)S(1)} %pad_maximum_fusion.2.mine_ref, ...), custom_call_target="tpu_custom_call" | custom-call | flops 402653184 | bytes 1048576 | tf_op jit(solution)/shard_map/near_keys/pallas_call | solution.py:216
  97.5 3.2 %own_parity.1 = (f32[1,1024]{1,0:T(1,128)S(1)}, f32[1,1024]{1,0:T(1,128)S(1)}, f32[128,1024]{1,0:T(8,128)S(1)}) custom-call(s32[1]{0:T(128)} %bitcast.meta_ref, bf16[2048,256]{1,0:T(8,128)(2,1)S(1)} %bitcast.17, s32[64,128]{1,0:T(8,128)S(1)} %bitcast.22, bf16[256,1024]{1,0:T(8,128)(2,1)S(1)} %get-tuple-element.12.qt_ref, ...), custom_call_target="tpu_custom_call" | custom-call | flops 1073741824 | bytes 1048576 | tf_op jit(solution)/shard_map/own_parity/pallas_call | solution.py:226
  100.8 2.4 %other_parity.1 = bf16[128,1024]{1,0:T(8,128)(2,1)S(1)} custom-call(s32[1]{0:T(128)} %bitcast.meta_ref, bf16[2048,256]{1,0:T(8,128)(2,1)S(1)} %collective-permute-done.2.kv_ref, s32[64,128]{1,0:T(8,128)S(1)} %bitcast.23, bf16[256,1024]{1,0:T(8,128)(2,1)S(1)} %get-tuple-element.12.qt_ref, f32[1,1024]{1,0:T(1,128)S(1)} %get-tuple-element.16.m_in, ...), custom_call_target="tpu_custom_call" | custom-call | flops 1073741824 | bytes 1048576 | tf_op jit(solution)/shard_map/other_parity/pallas_call | solution.py:235
  103.2 14.8 %all_to_all.25 = bf16[8,16,1024]{2,1,0:T(8,128)(2,1)S(1)} all-to-all(bf16[8,16,1024]{2,1,0:T(8,128)(2,1)S(1)} %bitcast.20), channel_id=1, replica_groups=mesh['seq'=64,'head'=8] {'head'}, dimensions={0} | all-to-all | bytes 524288 | tf_op jit(solution)/shard_map/all_to_all | solution.py:249
  118.0 0.9 copy.10
  (20 shorter events, 0.1 us)
Async XLA Ops:
  2.7 22.0 %all-to-all-start = ((bf16[16,8,1280]{2,0,1:T(8,128)(2,1)}), bf16[16,8,1280]{2,0,1:T(8,128)(2,1)S(1)}, u32[]{:S(2)}, u32[]{:S(2)}) async-start(bf16[16,8,1280]{2,0,1:T(8,128)(2,1)} %pad_maximum_fusion.1), calls=%async_computation | async-start | bytes 655360 | tf_op jit(solution)/shard_map/all_to_all | solution.py:195
  24.7 6.5 %collective-permute-start.1 = (bf16[128,256]{1,0:T(8,128)(2,1)S(1)}, bf16[128,256]{1,0:T(8,128)(2,1)S(1)}, u32[]{:S(2)}, u32[]{:S(2)}) collective-permute-start(bf16[128,256]{1,0:T(8,128)(2,1)S(1)} %slice.4), channel_id=1, source_target_pairs={{0,256},{8,264},{16,272},{24,280},{32,288},{40,296},{48,304},{56,3... | collective-permute-start | bytes 196616 | tf_op jit(solution)/shard_map/ppermute | solution.py:197
  26.0 6.3 %collective-permute-start = (bf16[128,256]{1,0:T(8,128)(2,1)S(1)}, bf16[128,256]{1,0:T(8,128)(2,1)S(1)}, u32[]{:S(2)}, u32[]{:S(2)}) collective-permute-start(bf16[128,256]{1,0:T(8,128)(2,1)S(1)} %slice.4), channel_id=1, source_target_pairs={{0,128},{8,136},{16,144},{24,152},{32,160},{40,168},{48,176},{56,1... | collective-permute-start | bytes 196616 | tf_op jit(solution)/shard_map/ppermute | solution.py:198
  33.4 7.0 %copy-start.2 = (bf16[1,16,1,256]{3,1,2,0:T(8,128)(2,1)S(1)}, bf16[1,16,1,256]{3,1,2,0:T(8,128)(2,1)}, u32[]{:S(2)}) copy-start(bf16[1,16,1,256]{3,1,2,0:T(8,128)(2,1)} %param.8) | copy-start | bytes 24580
  33.4 33.0 %all-to-all-start.1 = ((bf16[8,2,128,256]{3,2,1,0:T(8,128)(2,1)}), bf16[8,2,128,256]{3,2,1,0:T(8,128)(2,1)S(1)}, u32[]{:S(2)}, u32[]{:S(2)}) async-start(bf16[8,2,128,256]{3,2,1,0:T(8,128)(2,1)} %pad_maximum_fusion), calls=%async_computation.1 | async-start | bytes 2097152 | tf_op jit(solution)/shard_map/all_to_all | solution.py:202
  40.3 9.2 %collective-permute-start.5 = (bf16[1,16,256]{2,1,0:T(8,128)(2,1)S(1)}, bf16[1,16,256]{2,1,0:T(8,128)(2,1)S(1)}, u32[]{:S(2)}, u32[]{:S(2)}) collective-permute-start(bf16[1,16,256]{2,1,0:T(8,128)(2,1)S(1)} %bitcast.27), channel_id=1, source_target_pairs={{0,384},{8,392},{16,400},{24,408},{32,416},{40,424},{48,432},{56,4... | collective-permute-start | bytes 24584 | tf_op jit(solution)/shard_map/ppermute | solution.py:191
  43.9 5.9 %collective-permute-start.4 = (bf16[1,16,256]{2,1,0:T(8,128)(2,1)S(1)}, bf16[1,16,256]{2,1,0:T(8,128)(2,1)S(1)}, u32[]{:S(2)}, u32[]{:S(2)}) collective-permute-start(bf16[1,16,256]{2,1,0:T(8,128)(2,1)S(1)} %bitcast.28), channel_id=1, source_target_pairs={{0,256},{8,264},{16,272},{24,280},{32,288},{40,296},{48,304},{56,3... | collective-permute-start | bytes 24584 | tf_op jit(solution)/shard_map/ppermute | solution.py:191
  45.9 4.7 %collective-permute-start.3 = (bf16[1,16,256]{2,1,0:T(8,128)(2,1)S(1)}, bf16[1,16,256]{2,1,0:T(8,128)(2,1)S(1)}, u32[]{:S(2)}, u32[]{:S(2)}) collective-permute-start(bf16[1,16,256]{2,1,0:T(8,128)(2,1)S(1)} %bitcast.29), channel_id=1, source_target_pairs={{0,128},{8,136},{16,144},{24,152},{32,160},{40,168},{48,176},{56,1... | collective-permute-start | bytes 24584 | tf_op jit(solution)/shard_map/ppermute | solution.py:191
  50.6 22.4 %collective-permute-start.6 = (bf16[4,16,256]{2,1,0:T(8,128)(2,1)S(1)}, bf16[4,16,256]{2,1,0:T(8,128)(2,1)S(1)}, u32[]{:S(2)}, u32[]{:S(2)}) collective-permute-start(bf16[4,16,256]{2,1,0:T(8,128)(2,1)S(1)} %pad_maximum_fusion.3), channel_id=1, source_target_pairs={{0,64},{8,72},{16,80},{24,88},{32,96},{40,104},{48,112},{56,120},{... | collective-permute-start | bytes 98312 | tf_op jit(solution)/shard_map/ppermute | solution.py:193
  66.4 34.4 %collective-permute-start.2 = (bf16[2048,256]{1,0:T(8,128)(2,1)S(1)}, bf16[2048,256]{1,0:T(8,128)(2,1)S(1)}, u32[]{:S(2)}, u32[]{:S(2)}) collective-permute-start(bf16[2048,256]{1,0:T(8,128)(2,1)S(1)} %bitcast.16), channel_id=1, source_target_pairs={{0,8},{8,0},{16,24},{24,16},{32,40},{40,32},{48,56},{56,48},{64,72... | collective-permute-start | bytes 3145736 | tf_op jit(solution)/shard_map/ppermute | solution.py:206
  73.0 7.8 %collective-permute-start.7 = (bf16[8,16,256]{2,1,0:T(8,128)(2,1)S(1)}, bf16[8,16,256]{2,1,0:T(8,128)(2,1)S(1)}, u32[]{:S(2)}, u32[]{:S(2)}) collective-permute-start(bf16[8,16,256]{2,1,0:T(8,128)(2,1)S(1)} %get-tuple-element.23), channel_id=1, source_target_pairs={{0,32},{8,40},{16,48},{24,56},{32,64},{40,72},{48,80},{56,88},{64,... | collective-permute-start | bytes 196616 | tf_op jit(solution)/shard_map/ppermute | solution.py:193
  80.8 7.3 %collective-permute-start.8 = (bf16[16,16,256]{2,1,0:T(8,128)(2,1)S(1)}, bf16[16,16,256]{2,1,0:T(8,128)(2,1)S(1)}, u32[]{:S(2)}, u32[]{:S(2)}) collective-permute-start(bf16[16,16,256]{2,1,0:T(8,128)(2,1)S(1)} %get-tuple-element.19), channel_id=1, source_target_pairs={{0,16},{8,24},{16,32},{24,40},{32,48},{40,56},{48,64},{56,72},{64,... | collective-permute-start | bytes 393224 | tf_op jit(solution)/shard_map/ppermute | solution.py:193
  88.1 4.9 %copy-start = (s32[8192]{0:T(1024)S(1)}, s32[8192]{0:T(1024)}, u32[]{:S(2)}) copy-start(s32[8192]{0:T(1024)} %param.7) | copy-start | bytes 98308
  88.1 4.9 %collective-permute-start.9 = (bf16[640,256]{1,0:T(8,128)(2,1)S(1)}, bf16[640,256]{1,0:T(8,128)(2,1)S(1)}, u32[]{:S(2)}, u32[]{:S(2)}) collective-permute-start(bf16[640,256]{1,0:T(8,128)(2,1)S(1)} %pad_maximum_fusion.2.mine_ref), channel_id=1, source_target_pairs={{0,8},{8,0},{16,24},{24,16},{32,40},{40,32},{48,56},{56,48},{64,72... | collective-permute-start | bytes 983048 | tf_op jit(solution)/shard_map/ppermute | solution.py:205
  93.0 0.7 copy-start.1

commit v3 on v2

--- a/solution.py
+++ b/solution.py
@@ -109,7 +109,7 @@
     for i in range(PAGES):
         page = table_ref[i]
         off = (y + NY - (page // 2) % NY) % NY
-        unit = (x + NX - page // (2 * NY)) % NX + 4 * (off // 4) + 8 * ((off // 2) % 2) + 16 * (off % 2)
+        unit = NY * ((x + NX - page // (2 * NY)) % NX) + off // 4 + 2 * (off % 4)
         rows = pl.ds(pl.multiple_of(ROWS + unit * PAGE, PAGE), PAGE)
 
         @pl.when(page % 2 == core)
@@ -187,24 +187,25 @@
 def per_device(queries, branch_key_value, branch_ids, pool, page_table):
     me = lax.axis_index("seq")
     y = (me // 2) % NY
-    page = pool.reshape(1, PAGE, PAIR)
-    pages = jnp.concatenate([page] + [lax.ppermute(page, "seq", x_ring(k)) for k in (1, 2, 3)], axis=0)
-    for by in (4, 2, 1):
-        pages = jnp.concatenate([pages, lax.ppermute(pages, "seq", y_ring(by))], axis=0)
+    pages = pool.reshape(1, PAGE, PAIR)
+    pages = jnp.concatenate([pages, lax.ppermute(pages, "seq", y_ring(4))], axis=0)
+    pages = jnp.concatenate([pages] + [lax.ppermute(pages, "seq", y_ring(k)) for k in (1, 2, 3)], axis=0)
+    pages = pages.reshape(NY * PAGE, PAIR)
     wide = jnp.concatenate([queries, branch_key_value], axis=2)
     wide = lax.all_to_all(wide, "head", split_axis=1, concat_axis=0, tiled=True).reshape(ROWS, GROUP * D + PAIR)
     own = wide[:, GROUP * D:]
-    two_back = lax.ppermute(own, "seq", x_shift(2))
-    one_back = lax.ppermute(own, "seq", x_shift(1))
+    near = jnp.concatenate([own, pages], axis=0)
+    two_back = lax.ppermute(near, "seq", x_ring(2))
+    one_back = lax.ppermute(near, "seq", x_ring(1))
     target = jnp.arange(NY, dtype=jnp.int32)[:, None, None]
-    mixed = jnp.where(target > y, own[None], two_back[None])
-    send = jnp.stack([jnp.broadcast_to(one_back[None], mixed.shape), mixed], axis=1)
+    mixed = jnp.where(target > y, own[None], two_back[None, :ROWS])
+    send = jnp.stack([jnp.broadcast_to(one_back[None, :ROWS], mixed.shape), mixed], axis=1)
     kv = lax.all_to_all(send, "seq", split_axis=0, concat_axis=0, tiled=True, axis_index_groups=Y_GROUPS)
     kv = kv.reshape(2 * NY * ROWS, PAIR)
-    mine = jnp.concatenate([own, pages.reshape(PAGES * PAGE, PAIR)], axis=0)
+    far, _ = lax.optimization_barrier((two_back[ROWS:], send))
+    three_back = lax.ppermute(far, "seq", x_ring(1))
+    mine = jnp.concatenate([near, one_back[ROWS:], two_back[ROWS:], three_back], axis=0)
     side = lax.ppermute(mine, "seq", SWAP)
-    kv_side = lax.ppermute(kv, "seq", SWAP)
-
     ids = branch_ids.reshape(2 * NX * NY, ROWS)
     meta = me.astype(jnp.int32).reshape(1)
     state = [
@@ -223,6 +224,8 @@
         cost_estimate=cost(768),
         name="near_keys",
     )(meta, page_table.reshape(PAGES), wide, mine, side, ids)
+    kv, m = lax.optimization_barrier((kv, m))
+    kv_side = lax.ppermute(kv, "seq", SWAP)
     m, l, acc = pl.pallas_call(
         own_kernel,
         out_shape=state,

time: 120 us -> 105 us (0.88)
  the two profiles are of different devices: /device:TPU:5 before, /device:TPU:6 now
where the time goes in v3:
time: 105 us; the launch traced here: 103 us
  starting transfers between devices  46.8 us (45%)
  waiting for transfers between devices  24.2 us (23%)
  blocking collectives  19 us (18%)
  Pallas kernels  7.75 us (7%)
  local copies, waits for them, and re-layouts  3.56 us (3%)
  other arithmetic  1.97 us (2%)
    all_to_all x1, blocking collectives, per_device(): lax.all_to_all(out.reshape(8, ROWS // 8, GROUP * D), 'head', split_axis=0...  19 us
    all_to_all x1, waiting for transfers between devices, per_device(): lax.all_to_all(send, 'seq', split_axis=0, concat_axis=0, tiled=True, axis...  11.6 us
    all_to_all x1, starting transfers between devices, per_device(): lax.all_to_all(wide, 'head', split_axis=1, concat_axis=0, tiled=True)  10.4 us
    ppermute x3, starting transfers between devices, per_device(): lax.ppermute(pages, 'seq', y_ring(k))  8.99 us
    ppermute x1, starting transfers between devices, per_device(): lax.ppermute(pages, 'seq', y_ring(4))  7.72 us
    all_to_all x1, starting transfers between devices, per_device(): lax.all_to_all(send, 'seq', split_axis=0, concat_axis=0, tiled=True, axis...  5.68 us
    ppermute x1, starting transfers between devices, per_device(): two_back = lax.ppermute(near, 'seq', x_ring(2))  4.33 us
    ppermute x1, starting transfers between devices, per_device(): three_back = lax.ppermute(far, 'seq', x_ring(1))  3.39 us
  transfers between devices with their start and end apart: 11, of which 8 were waited for; matrix products, arithmetic and copies ran while one was open for 3% of the time, Pallas kernels for 5%

profile of v3, /device:TPU:6, one launch (start us, length us, event | category | flops | bytes accessed | tf_op | source)
XLA Modules:
  0.0 103.5 jit_solution(11166657760201183172)
XLA Ops:
  0.0 7.7 %collective-permute-start = (bf16[1,16,256]{2,1,0:T(8,128)(2,1)}, bf16[1,16,256]{2,1,0:T(8,128)(2,1)S(1)}, u32[]{:S(2)}, u32[]{:S(2)}) collective-permute-start(bf16[1,16,256]{2,1,0:T(8,128)(2,1)} %bitcast.26), channel_id=1, source_target_pairs={{0,64},{8,72},{16,80},{24,88},{32,96},{40,104},{48,112},{56,120},{... | collective-permute-start | bytes 24584 | tf_op jit(solution)/shard_map/ppermute | solution.py:191
  7.7 0.9 copy.9
  8.6 1.1 %copy.8 = bf16[16,8,1024]{2,0,1:T(8,128)(2,1)S(1)} copy(bf16[16,8,1024]{2,1,0:T(8,128)(2,1)} %param.5) | data formatting | bytes 524288 | tf_op args[0]
  9.7 0.8 pad_maximum_fusion.1
  10.5 10.4 %all-to-all-start = ((bf16[16,8,1280]{2,0,1:T(8,128)(2,1)}), bf16[16,8,1280]{2,0,1:T(8,128)(2,1)S(1)}, u32[]{:S(2)}, u32[]{:S(2)}) async-start(bf16[16,8,1280]{2,0,1:T(8,128)(2,1)} %pad_maximum_fusion.1), calls=%async_computation | async-start | bytes 655360 | tf_op jit(solution)/shard_map/all_to_all | solution.py:195
  20.9 0.0 collective-permute-done
  21.0 2.8 %collective-permute-start.3 = (bf16[2,16,256]{2,1,0:T(8,128)(2,1)S(1)}, bf16[2,16,256]{2,1,0:T(8,128)(2,1)S(1)}, u32[]{:S(2)}, u32[]{:S(2)}) collective-permute-start(bf16[2,16,256]{2,1,0:T(8,128)(2,1)S(1)} %pad_maximum_fusion.3), channel_id=1, source_target_pairs={{0,48},{8,56},{16,64},{24,72},{32,80},{40,88},{48,96},{56,104},{64... | collective-permute-start | bytes 49160 | tf_op jit(solution)/shard_map/ppermute | solution.py:192
  23.8 2.7 %collective-permute-start.2 = (bf16[2,16,256]{2,1,0:T(8,128)(2,1)S(1)}, bf16[2,16,256]{2,1,0:T(8,128)(2,1)S(1)}, u32[]{:S(2)}, u32[]{:S(2)}) collective-permute-start(bf16[2,16,256]{2,1,0:T(8,128)(2,1)S(1)} %pad_maximum_fusion.3), channel_id=1, source_target_pairs={{0,32},{8,40},{16,48},{24,56},{32,64},{40,72},{48,80},{56,88},{64,... | collective-permute-start | bytes 49160 | tf_op jit(solution)/shard_map/ppermute | solution.py:192
  26.5 3.5 %collective-permute-start.1 = (bf16[2,16,256]{2,1,0:T(8,128)(2,1)S(1)}, bf16[2,16,256]{2,1,0:T(8,128)(2,1)S(1)}, u32[]{:S(2)}, u32[]{:S(2)}) collective-permute-start(bf16[2,16,256]{2,1,0:T(8,128)(2,1)S(1)} %pad_maximum_fusion.3), channel_id=1, source_target_pairs={{0,16},{8,24},{16,32},{24,40},{32,48},{40,56},{48,64},{56,72},{64,... | collective-permute-start | bytes 49160 | tf_op jit(solution)/shard_map/ppermute | solution.py:192
  30.0 3.3 %collective-permute-done.1 = bf16[2,16,256]{2,1,0:T(8,128)(2,1)S(1)} collective-permute-done((bf16[2,16,256]{2,1,0:T(8,128)(2,1)S(1)}, bf16[2,16,256]{2,1,0:T(8,128)(2,1)S(1)}, u32[]{:S(2)}, u32[]{:S(2)}) %collective-permute-start.1) | collective-permute-done | bytes 16416 | tf_op jit(solution)/shard_map/ppermute | solution.py:192
  33.3 0.0 collective-permute-done.2
  33.4 0.5 all-to-all-done
  33.9 2.4 %collective-permute-start.4 = (bf16[256,256]{1,0:T(8,128)(2,1)S(1)}, bf16[256,256]{1,0:T(8,128)(2,1)S(1)}, u32[]{:S(2)}, u32[]{:S(2)}) collective-permute-start(bf16[256,256]{1,0:T(8,128)(2,1)S(1)} %pad_maximum_fusion.2), channel_id=1, source_target_pairs={{0,128},{8,136},{16,144},{24,152},{32,160},{40,168},{48,176},{56,1... | collective-permute-start | bytes 393224 | tf_op jit(solution)/shard_map/ppermute | solution.py:199
  36.3 4.3 %collective-permute-start.5 = (bf16[256,256]{1,0:T(8,128)(2,1)S(1)}, bf16[256,256]{1,0:T(8,128)(2,1)S(1)}, u32[]{:S(2)}, u32[]{:S(2)}) collective-permute-start(bf16[256,256]{1,0:T(8,128)(2,1)S(1)} %pad_maximum_fusion.2), channel_id=1, source_target_pairs={{0,256},{8,264},{16,272},{24,280},{32,288},{40,296},{48,304},{56,3... | collective-permute-start | bytes 393224 | tf_op jit(solution)/shard_map/ppermute | solution.py:198
  40.7 0.7 collective-permute-done.4
  41.4 3.3 %collective-permute-done.5 = bf16[256,256]{1,0:T(8,128)(2,1)S(1)} collective-permute-done((bf16[256,256]{1,0:T(8,128)(2,1)S(1)}, bf16[256,256]{1,0:T(8,128)(2,1)S(1)}, u32[]{:S(2)}, u32[]{:S(2)}) %collective-permute-start.5) | collective-permute-done | bytes 131104 | tf_op jit(solution)/shard_map/ppermute | solution.py:198
  44.7 0.1 broadcast_select_fusion
  44.9 1.1 %pad_maximum_fusion = bf16[8,2,128,256]{3,2,1,0:T(8,128)(2,1)} fusion(bf16[8,1,128,256]{3,2,1,0:T(8,128)(2,1)S(1)} %broadcast_select_fusion, bf16[8,1,128,256]{3,2,1,0:T(8,128)(2,1)S(1)} %stack_broadcast_in_dim.2), kind=kLoop, calls=%fused_computation | loop fusion | flops 524288 | bytes 2097152 | tf_op jit(solution)/shard_map/stack | solution.py:202
  46.0 5.7 %all-to-all-start.1 = ((bf16[8,2,128,256]{3,2,1,0:T(8,128)(2,1)}), bf16[8,2,128,256]{3,2,1,0:T(8,128)(2,1)S(1)}, u32[]{:S(2)}, u32[]{:S(2)}) async-start(bf16[8,2,128,256]{3,2,1,0:T(8,128)(2,1)} %pad_maximum_fusion), calls=%async_computation.1 | async-start | bytes 2097152 | tf_op jit(solution)/shard_map/all_to_all | solution.py:203
  51.6 3.4 %collective-permute-start.6 = (bf16[128,256]{1,0:T(8,128)(2,1)S(1)}, bf16[128,256]{1,0:T(8,128)(2,1)S(1)}, u32[]{:S(2)}, u32[]{:S(2)}) collective-permute-start(bf16[128,256]{1,0:T(8,128)(2,1)S(1)} %get-tuple-element.15), channel_id=1, source_target_pairs={{0,128},{8,136},{16,144},{24,152},{32,160},{40,168},{48,176},{56,1... | collective-permute-start | bytes 196616 | tf_op jit(solution)/shard_map/ppermute | solution.py:206
  55.0 2.8 %collective-permute-done.6 = bf16[128,256]{1,0:T(8,128)(2,1)S(1)} collective-permute-done((bf16[128,256]{1,0:T(8,128)(2,1)S(1)}, bf16[128,256]{1,0:T(8,128)(2,1)S(1)}, u32[]{:S(2)}, u32[]{:S(2)}) %collective-permute-start.6) | collective-permute-done | bytes 65568 | tf_op jit(solution)/shard_map/ppermute | solution.py:206
  57.8 1.9 %collective-permute-start.7 = (bf16[640,256]{1,0:T(8,128)(2,1)S(1)}, bf16[640,256]{1,0:T(8,128)(2,1)S(1)}, u32[]{:S(2)}, u32[]{:S(2)}) collective-permute-start(bf16[640,256]{1,0:T(8,128)(2,1)S(1)} %constant_dynamic-update-slice_fusion.5.mine_ref), channel_id=1, source_target_pairs={{0,8},{8,0},{16,24},{24,16},{32,40},{40,32},{48,56},{56,48},{64,72... | collective-permute-start | bytes 983048 | tf_op jit(solution)/shard_map/ppermute | solution.py:208
  59.7 1.6 %collective-permute-done.7.side_ref = bf16[640,256]{1,0:T(8,128)(2,1)S(1)} collective-permute-done((bf16[640,256]{1,0:T(8,128)(2,1)S(1)}, bf16[640,256]{1,0:T(8,128)(2,1)S(1)}, u32[]{:S(2)}, u32[]{:S(2)}) %collective-permute-start.7) | collective-permute-done | bytes 327712 | tf_op jit(solution)/shard_map/ppermute | solution.py:208
  61.3 0.7 copy-done.1
  62.0 3.2 %near_keys.1 = (bf16[256,1024]{1,0:T(8,128)(2,1)S(1)}, f32[1,1024]{1,0:T(1,128)S(1)}, f32[1,1024]{1,0:T(1,128)S(1)}, f32[128,1024]{1,0:T(8,128)S(1)}) custom-call(s32[1]{0:T(128)} %bitcast.meta_ref, s32[32]{0:T(128)S(1)} %bitcast.22, bf16[128,1280]{1,0:T(8,128)(2,1)S(1)} %bitcast.17, bf16[640,256]{1,0:T(8,128)(2,1)S(1)} %constant_dynamic-update-slice_fusion.5.mine_ref, ...), custom_call_target="tpu_custom_call" | custom-call | flops 402653184 | bytes 1048576 | tf_op jit(solution)/shard_map/near_keys/pallas_call | solution.py:217
  65.1 11.6 %all-to-all-done.1 = bf16[8,2,128,256]{3,2,1,0:T(8,128)(2,1)S(1)} async-done(((bf16[8,2,128,256]{3,2,1,0:T(8,128)(2,1)}), bf16[8,2,128,256]{3,2,1,0:T(8,128)(2,1)S(1)}, u32[]{:S(2)}, u32[]{:S(2)}) %all-to-all-start.1) | async-done | bytes 1048608 | tf_op jit(solution)/shard_map/all_to_all | solution.py:203
  76.7 1.9 %collective-permute-start.8 = (bf16[2048,256]{1,0:T(8,128)(2,1)S(1)}, bf16[2048,256]{1,0:T(8,128)(2,1)S(1)}, u32[]{:S(2)}, u32[]{:S(2)}) collective-permute-start(bf16[2048,256]{1,0:T(8,128)(2,1)S(1)} %bitcast.14), channel_id=1, source_target_pairs={{0,8},{8,0},{16,24},{24,16},{32,40},{40,32},{48,56},{56,48},{64,72... | collective-permute-start | bytes 3145736 | tf_op jit(solution)/shard_map/ppermute | solution.py:228
  78.6 2.2 %own_parity.1 = (f32[1,1024]{1,0:T(1,128)S(1)}, f32[1,1024]{1,0:T(1,128)S(1)}, f32[128,1024]{1,0:T(8,128)S(1)}) custom-call(s32[1]{0:T(128)} %bitcast.meta_ref, bf16[2048,256]{1,0:T(8,128)(2,1)S(1)} %bitcast.15, s32[64,128]{1,0:T(8,128)S(1)} %bitcast.20, bf16[256,1024]{1,0:T(8,128)(2,1)S(1)} %get-tuple-element.18.qt_ref, ...), custom_call_target="tpu_custom_call" | custom-call | flops 1073741824 | bytes 1048576 | tf_op jit(solution)/shard_map/own_parity/pallas_call | solution.py:229
  80.9 0.4 collective-permute-done.8.kv_ref
  81.3 2.4 %other_parity.1 = bf16[128,1024]{1,0:T(8,128)(2,1)S(1)} custom-call(s32[1]{0:T(128)} %bitcast.meta_ref, bf16[2048,256]{1,0:T(8,128)(2,1)S(1)} %collective-permute-done.8.kv_ref, s32[64,128]{1,0:T(8,128)S(1)} %bitcast.21, bf16[256,1024]{1,0:T(8,128)(2,1)S(1)} %get-tuple-element.18.qt_ref, f32[1,1024]{1,0:T(1,128)S(1)} %get-tuple-element.22.m_in, ...), custom_call_target="tpu_custom_call" | custom-call | flops 1073741824 | bytes 1048576 | tf_op jit(solution)/shard_map/other_parity/pallas_call | solution.py:238
  83.6 19.0 %all_to_all.25 = bf16[8,16,1024]{2,1,0:T(8,128)(2,1)S(1)} all-to-all(bf16[8,16,1024]{2,1,0:T(8,128)(2,1)S(1)} %bitcast.18), channel_id=1, replica_groups=mesh['seq'=64,'head'=8] {'head'}, dimensions={0} | all-to-all | bytes 524288 | tf_op jit(solution)/shard_map/all_to_all | solution.py:252
  102.6 0.9 copy.10
  (20 shorter events, 0.1 us)
Async XLA Ops:
  0.0 20.9 %collective-permute-start = (bf16[1,16,256]{2,1,0:T(8,128)(2,1)}, bf16[1,16,256]{2,1,0:T(8,128)(2,1)S(1)}, u32[]{:S(2)}, u32[]{:S(2)}) collective-permute-start(bf16[1,16,256]{2,1,0:T(8,128)(2,1)} %bitcast.26), channel_id=1, source_target_pairs={{0,64},{8,72},{16,80},{24,88},{32,96},{40,104},{48,112},{56,120},{... | collective-permute-start | bytes 24584 | tf_op jit(solution)/shard_map/ppermute | solution.py:191
  10.5 10.5 %copy-start.2 = (bf16[1,16,1,256]{3,1,2,0:T(8,128)(2,1)S(1)}, bf16[1,16,1,256]{3,1,2,0:T(8,128)(2,1)}, u32[]{:S(2)}) copy-start(bf16[1,16,1,256]{3,1,2,0:T(8,128)(2,1)} %param.8) | copy-start | bytes 24580
  10.5 23.4 %all-to-all-start = ((bf16[16,8,1280]{2,0,1:T(8,128)(2,1)}), bf16[16,8,1280]{2,0,1:T(8,128)(2,1)S(1)}, u32[]{:S(2)}, u32[]{:S(2)}) async-start(bf16[16,8,1280]{2,0,1:T(8,128)(2,1)} %pad_maximum_fusion.1), calls=%async_computation | async-start | bytes 655360 | tf_op jit(solution)/shard_map/all_to_all | solution.py:195
  21.0 12.4 %collective-permute-start.3 = (bf16[2,16,256]{2,1,0:T(8,128)(2,1)S(1)}, bf16[2,16,256]{2,1,0:T(8,128)(2,1)S(1)}, u32[]{:S(2)}, u32[]{:S(2)}) collective-permute-start(bf16[2,16,256]{2,1,0:T(8,128)(2,1)S(1)} %pad_maximum_fusion.3), channel_id=1, source_target_pairs={{0,48},{8,56},{16,64},{24,72},{32,80},{40,88},{48,96},{56,104},{64... | collective-permute-start | bytes 49160 | tf_op jit(solution)/shard_map/ppermute | solution.py:192
  23.8 9.5 %collective-permute-start.2 = (bf16[2,16,256]{2,1,0:T(8,128)(2,1)S(1)}, bf16[2,16,256]{2,1,0:T(8,128)(2,1)S(1)}, u32[]{:S(2)}, u32[]{:S(2)}) collective-permute-start(bf16[2,16,256]{2,1,0:T(8,128)(2,1)S(1)} %pad_maximum_fusion.3), channel_id=1, source_target_pairs={{0,32},{8,40},{16,48},{24,56},{32,64},{40,72},{48,80},{56,88},{64,... | collective-permute-start | bytes 49160 | tf_op jit(solution)/shard_map/ppermute | solution.py:192
  26.5 6.8 %collective-permute-start.1 = (bf16[2,16,256]{2,1,0:T(8,128)(2,1)S(1)}, bf16[2,16,256]{2,1,0:T(8,128)(2,1)S(1)}, u32[]{:S(2)}, u32[]{:S(2)}) collective-permute-start(bf16[2,16,256]{2,1,0:T(8,128)(2,1)S(1)} %pad_maximum_fusion.3), channel_id=1, source_target_pairs={{0,16},{8,24},{16,32},{24,40},{32,48},{40,56},{48,64},{56,72},{64,... | collective-permute-start | bytes 49160 | tf_op jit(solution)/shard_map/ppermute | solution.py:192
  33.9 7.5 %collective-permute-start.4 = (bf16[256,256]{1,0:T(8,128)(2,1)S(1)}, bf16[256,256]{1,0:T(8,128)(2,1)S(1)}, u32[]{:S(2)}, u32[]{:S(2)}) collective-permute-start(bf16[256,256]{1,0:T(8,128)(2,1)S(1)} %pad_maximum_fusion.2), channel_id=1, source_target_pairs={{0,128},{8,136},{16,144},{24,152},{32,160},{40,168},{48,176},{56,1... | collective-permute-start | bytes 393224 | tf_op jit(solution)/shard_map/ppermute | solution.py:199
  36.3 8.4 %collective-permute-start.5 = (bf16[256,256]{1,0:T(8,128)(2,1)S(1)}, bf16[256,256]{1,0:T(8,128)(2,1)S(1)}, u32[]{:S(2)}, u32[]{:S(2)}) collective-permute-start(bf16[256,256]{1,0:T(8,128)(2,1)S(1)} %pad_maximum_fusion.2), channel_id=1, source_target_pairs={{0,256},{8,264},{16,272},{24,280},{32,288},{40,296},{48,304},{56,3... | collective-permute-start | bytes 393224 | tf_op jit(solution)/shard_map/ppermute | solution.py:198
  46.0 30.8 %all-to-all-start.1 = ((bf16[8,2,128,256]{3,2,1,0:T(8,128)(2,1)}), bf16[8,2,128,256]{3,2,1,0:T(8,128)(2,1)S(1)}, u32[]{:S(2)}, u32[]{:S(2)}) async-start(bf16[8,2,128,256]{3,2,1,0:T(8,128)(2,1)} %pad_maximum_fusion), calls=%async_computation.1 | async-start | bytes 2097152 | tf_op jit(solution)/shard_map/all_to_all | solution.py:203
  51.6 6.1 %collective-permute-start.6 = (bf16[128,256]{1,0:T(8,128)(2,1)S(1)}, bf16[128,256]{1,0:T(8,128)(2,1)S(1)}, u32[]{:S(2)}, u32[]{:S(2)}) collective-permute-start(bf16[128,256]{1,0:T(8,128)(2,1)S(1)} %get-tuple-element.15), channel_id=1, source_target_pairs={{0,128},{8,136},{16,144},{24,152},{32,160},{40,168},{48,176},{56,1... | collective-permute-start | bytes 196616 | tf_op jit(solution)/shard_map/ppermute | solution.py:206
  57.8 3.5 %copy-start = (s32[8192]{0:T(1024)S(1)}, s32[8192]{0:T(1024)}, u32[]{:S(2)}) copy-start(s32[8192]{0:T(1024)} %param.7) | copy-start | bytes 98308
  57.8 3.5 %collective-permute-start.7 = (bf16[640,256]{1,0:T(8,128)(2,1)S(1)}, bf16[640,256]{1,0:T(8,128)(2,1)S(1)}, u32[]{:S(2)}, u32[]{:S(2)}) collective-permute-start(bf16[640,256]{1,0:T(8,128)(2,1)S(1)} %constant_dynamic-update-slice_fusion.5.mine_ref), channel_id=1, source_target_pairs={{0,8},{8,0},{16,24},{24,16},{32,40},{40,32},{48,56},{56,48},{64,72... | collective-permute-start | bytes 983048 | tf_op jit(solution)/shard_map/ppermute | solution.py:208
  61.3 0.7 copy-start.1
  76.7 4.5 %collective-permute-start.8 = (bf16[2048,256]{1,0:T(8,128)(2,1)S(1)}, bf16[2048,256]{1,0:T(8,128)(2,1)S(1)}, u32[]{:S(2)}, u32[]{:S(2)}) collective-permute-start(bf16[2048,256]{1,0:T(8,128)(2,1)S(1)} %bitcast.14), channel_id=1, source_target_pairs={{0,8},{8,0},{16,24},{24,16},{32,40},{40,32},{48,56},{56,48},{64,72... | collective-permute-start | bytes 3145736 | tf_op jit(solution)/shard_map/ppermute | solution.py:228

commit v4 on v2

--- a/solution.py
+++ b/solution.py
@@ -109,7 +109,10 @@
     for i in range(PAGES):
         page = table_ref[i]
         off = (y + NY - (page // 2) % NY) % NY
-        unit = (x + NX - page // (2 * NY)) % NX + 4 * (off // 4) + 8 * ((off // 2) % 2) + 16 * (off % 2)
+        unit = (x + NX - page // (2 * NY)) % NX
+        shift = jnp.where(off % 4 == 3, 2, jnp.where(off % 4 == 2, 3, off % 4))
+        half = jnp.where(off % 4 == 3, 1 - off // 4, off // 4)
+        unit = unit + 4 * half + 8 * shift
         rows = pl.ds(pl.multiple_of(ROWS + unit * PAGE, PAGE), PAGE)
 
         @pl.when(page % 2 == core)
@@ -188,23 +191,25 @@
     me = lax.axis_index("seq")
     y = (me // 2) % NY
     page = pool.reshape(1, PAGE, PAIR)
-    pages = jnp.concatenate([page] + [lax.ppermute(page, "seq", x_ring(k)) for k in (1, 2, 3)], axis=0)
-    for by in (4, 2, 1):
-        pages = jnp.concatenate([pages, lax.ppermute(pages, "seq", y_ring(by))], axis=0)
-    wide = jnp.concatenate([queries, branch_key_value], axis=2)
-    wide = lax.all_to_all(wide, "head", split_axis=1, concat_axis=0, tiled=True).reshape(ROWS, GROUP * D + PAIR)
-    own = wide[:, GROUP * D:]
-    two_back = lax.ppermute(own, "seq", x_shift(2))
-    one_back = lax.ppermute(own, "seq", x_shift(1))
+    raw = jnp.concatenate([jnp.transpose(branch_key_value, (1, 0, 2)), page], axis=0)
+    two_raw = lax.ppermute(raw, "seq", x_ring(2))
+    one_raw = lax.ppermute(raw, "seq", x_ring(1))
+    three_page = lax.ppermute(page, "seq", x_ring(3))
+    wide = jnp.concatenate([jnp.transpose(queries, (1, 0, 2)), raw[:8], one_raw[:8], two_raw[:8]], axis=2)
+    wide = lax.all_to_all(wide, "head", split_axis=0, concat_axis=0, tiled=True).reshape(ROWS, -1)
+    at = GROUP * D
+    own, one_back, two_back = (wide[:, at + i * PAIR:at + (i + 1) * PAIR] for i in range(3))
+    pages = jnp.concatenate([page, one_raw[8:], two_raw[8:], three_page], axis=0)
+    pages = jnp.concatenate([pages, lax.ppermute(pages, "seq", y_ring(4))], axis=0)
     target = jnp.arange(NY, dtype=jnp.int32)[:, None, None]
     mixed = jnp.where(target > y, own[None], two_back[None])
     send = jnp.stack([jnp.broadcast_to(one_back[None], mixed.shape), mixed], axis=1)
     kv = lax.all_to_all(send, "seq", split_axis=0, concat_axis=0, tiled=True, axis_index_groups=Y_GROUPS)
     kv = kv.reshape(2 * NY * ROWS, PAIR)
+    later, _ = lax.optimization_barrier((pages, send))
+    pages = jnp.concatenate([pages] + [lax.ppermute(later, "seq", y_ring(k)) for k in (1, -1, 2)], axis=0)
     mine = jnp.concatenate([own, pages.reshape(PAGES * PAGE, PAIR)], axis=0)
     side = lax.ppermute(mine, "seq", SWAP)
-    kv_side = lax.ppermute(kv, "seq", SWAP)
-
     ids = branch_ids.reshape(2 * NX * NY, ROWS)
     meta = me.astype(jnp.int32).reshape(1)
     state = [
@@ -223,6 +228,8 @@
         cost_estimate=cost(768),
         name="near_keys",
     )(meta, page_table.reshape(PAGES), wide, mine, side, ids)
+    kv, m = lax.optimization_barrier((kv, m))
+    kv_side = lax.ppermute(kv, "seq", SWAP)
     m, l, acc = pl.pallas_call(
         own_kernel,
         out_shape=state,

time: 120 us -> 120 us (level)
  the two profiles are of different devices: /device:TPU:5 before, /device:TPU:58 now
where the time goes in v4:
time: 120 us
  starting transfers between devices  49.6 us (41%)
  waiting for transfers between devices  37 us (31%)
  blocking collectives  15.8 us (13%)
  Pallas kernels  11.7 us (10%)
  other arithmetic  2.74 us (2%)
  local copies, waits for them, and re-layouts  2.66 us (2%)
    ppermute x1, waiting for transfers between devices, per_device(): lax.ppermute(pages, 'seq', y_ring(4))  17.6 us
    all_to_all x1, blocking collectives, per_device(): lax.all_to_all(out.reshape(8, ROWS // 8, GROUP * D), 'head', split_axis=0...  15.8 us
    ppermute x3, starting transfers between devices, per_device(): lax.ppermute(later, 'seq', y_ring(k))  12.1 us
    all_to_all x1, starting transfers between devices, per_device(): lax.all_to_all(wide, 'head', split_axis=0, concat_axis=0, tiled=True)  10.4 us
    all_to_all x1, waiting for transfers between devices, per_device(): lax.all_to_all(wide, 'head', split_axis=0, concat_axis=0, tiled=True)  10.1 us
    all_to_all x1, starting transfers between devices, per_device(): lax.all_to_all(send, 'seq', split_axis=0, concat_axis=0, tiled=True, axis...  6.87 us
    ppermute x1, starting transfers between devices, per_device(): lax.ppermute(pages, 'seq', y_ring(4))  5.17 us
    ppermute x1, starting transfers between devices, per_device(): three_page = lax.ppermute(page, 'seq', x_ring(3))  4.55 us
  transfers between devices with their start and end apart: 11, of which 6 were waited for; matrix products, arithmetic and copies ran while one was open for 1% of the time, Pallas kernels for 6%

profile of v4, /device:TPU:58, one launch (start us, length us, event | category | flops | bytes accessed | tf_op | source)
XLA Modules:
  0.0 119.7 jit_solution(18347957369152754084)
XLA Ops:
  0.0 0.9 copy.18
  0.9 0.7 pad_maximum_fusion.3
  1.6 4.0 %collective-permute-start.1 = (bf16[9,16,256]{2,1,0:T(8,128)(2,1)S(1)}, bf16[9,16,256]{2,1,0:T(8,128)(2,1)S(1)}, u32[]{:S(2)}, u32[]{:S(2)}) collective-permute-start(bf16[9,16,256]{2,1,0:T(8,128)(2,1)S(1)} %pad_maximum_fusion.3), channel_id=1, source_target_pairs={{0,256},{8,264},{16,272},{24,280},{32,288},{40,296},{48,304},{56,3... | collective-permute-start | bytes 221192 | tf_op jit(solution)/shard_map/ppermute | solution.py:195
  5.6 1.9 %collective-permute-start = (bf16[9,16,256]{2,1,0:T(8,128)(2,1)S(1)}, bf16[9,16,256]{2,1,0:T(8,128)(2,1)S(1)}, u32[]{:S(2)}, u32[]{:S(2)}) collective-permute-start(bf16[9,16,256]{2,1,0:T(8,128)(2,1)S(1)} %pad_maximum_fusion.3), channel_id=1, source_target_pairs={{0,128},{8,136},{16,144},{24,152},{32,160},{40,168},{48,176},{56,1... | collective-permute-start | bytes 221192 | tf_op jit(solution)/shard_map/ppermute | solution.py:196
  7.6 0.2 copy.17
  7.7 1.6 %collective-permute-done.1 = bf16[9,16,256]{2,1,0:T(8,128)(2,1)S(1)} collective-permute-done((bf16[9,16,256]{2,1,0:T(8,128)(2,1)S(1)}, bf16[9,16,256]{2,1,0:T(8,128)(2,1)S(1)}, u32[]{:S(2)}, u32[]{:S(2)}) %collective-permute-start.1) | collective-permute-done | bytes 73760 | tf_op jit(solution)/shard_map/ppermute | solution.py:195
  9.4 2.5 %collective-permute-done = bf16[9,16,256]{2,1,0:T(8,128)(2,1)S(1)} collective-permute-done((bf16[9,16,256]{2,1,0:T(8,128)(2,1)S(1)}, bf16[9,16,256]{2,1,0:T(8,128)(2,1)S(1)}, u32[]{:S(2)}, u32[]{:S(2)}) %collective-permute-start) | collective-permute-done | bytes 73760 | tf_op jit(solution)/shard_map/ppermute | solution.py:196
  11.9 0.8 pad_maximum_fusion.1
  12.7 10.4 %all-to-all-start = ((bf16[8,16,1792]{2,1,0:T(8,128)(2,1)}), bf16[8,16,1792]{2,1,0:T(8,128)(2,1)S(1)}, u32[]{:S(2)}, u32[]{:S(2)}) async-start(bf16[8,16,1792]{2,1,0:T(8,128)(2,1)} %pad_maximum_fusion.1), calls=%async_computation | async-start | bytes 917504 | tf_op jit(solution)/shard_map/all_to_all | solution.py:199
  23.2 4.6 %collective-permute-start.2 = (bf16[1,16,256]{2,1,0:T(8,128)(2,1)S(1)}, bf16[1,16,256]{2,1,0:T(8,128)(2,1)S(1)}, u32[]{:S(2)}, u32[]{:S(2)}) collective-permute-start(bf16[1,16,256]{2,1,0:T(8,128)(2,1)S(1)} %bitcast.32), channel_id=1, source_target_pairs={{0,384},{8,392},{16,400},{24,408},{32,416},{40,424},{48,432},{56,4... | collective-permute-start | bytes 24584 | tf_op jit(solution)/shard_map/ppermute | solution.py:197
  27.8 10.1 %all-to-all-done = bf16[8,16,1792]{2,1,0:T(8,128)(2,1)S(1)} async-done(((bf16[8,16,1792]{2,1,0:T(8,128)(2,1)}), bf16[8,16,1792]{2,1,0:T(8,128)(2,1)S(1)}, u32[]{:S(2)}, u32[]{:S(2)}) %all-to-all-start) | async-done | bytes 458784 | tf_op jit(solution)/shard_map/all_to_all | solution.py:199
  37.8 0.1 broadcast_select_fusion
  38.0 1.1 pad_maximum_fusion
  39.1 6.9 %all-to-all-start.1 = ((bf16[8,2,128,256]{3,2,1,0:T(8,128)(2,1)}), bf16[8,2,128,256]{3,2,1,0:T(8,128)(2,1)S(1)}, u32[]{:S(2)}, u32[]{:S(2)}) async-start(bf16[8,2,128,256]{3,2,1,0:T(8,128)(2,1)} %pad_maximum_fusion), calls=%async_computation.1 | async-start | bytes 2097152 | tf_op jit(solution)/shard_map/all_to_all | solution.py:207
  46.0 0.0 collective-permute-done.2
  46.0 5.2 %collective-permute-start.3 = (bf16[4,16,256]{2,1,0:T(8,128)(2,1)S(1)}, bf16[4,16,256]{2,1,0:T(8,128)(2,1)S(1)}, u32[]{:S(2)}, u32[]{:S(2)}) collective-permute-start(bf16[4,16,256]{2,1,0:T(8,128)(2,1)S(1)} %pad_maximum_fusion.4), channel_id=1, source_target_pairs={{0,64},{8,72},{16,80},{24,88},{32,96},{40,104},{48,112},{56,120},{... | collective-permute-start | bytes 98312 | tf_op jit(solution)/shard_map/ppermute | solution.py:203
  51.2 17.6 %collective-permute-done.3 = bf16[4,16,256]{2,1,0:T(8,128)(2,1)S(1)} collective-permute-done((bf16[4,16,256]{2,1,0:T(8,128)(2,1)S(1)}, bf16[4,16,256]{2,1,0:T(8,128)(2,1)S(1)}, u32[]{:S(2)}, u32[]{:S(2)}) %collective-permute-start.3) | collective-permute-done | bytes 32800 | tf_op jit(solution)/shard_map/ppermute | solution.py:203
  68.7 6.5 %collective-permute-start.4 = (bf16[8,16,256]{2,1,0:T(8,128)(2,1)S(1)}, bf16[8,16,256]{2,1,0:T(8,128)(2,1)S(1)}, u32[]{:S(2)}, u32[]{:S(2)}) collective-permute-start(bf16[8,16,256]{2,1,0:T(8,128)(2,1)S(1)} %get-tuple-element.15), channel_id=1, source_target_pairs={{0,16},{8,24},{16,32},{24,40},{32,48},{40,56},{48,64},{56,72},{64,... | collective-permute-start | bytes 196616 | tf_op jit(solution)/shard_map/ppermute | solution.py:210
  75.2 1.9 %collective-permute-start.6 = (bf16[8,16,256]{2,1,0:T(8,128)(2,1)S(1)}, bf16[8,16,256]{2,1,0:T(8,128)(2,1)S(1)}, u32[]{:S(2)}, u32[]{:S(2)}) collective-permute-start(bf16[8,16,256]{2,1,0:T(8,128)(2,1)S(1)} %get-tuple-element.15), channel_id=1, source_target_pairs={{0,32},{8,40},{16,48},{24,56},{32,64},{40,72},{48,80},{56,88},{64,... | collective-permute-start | bytes 196616 | tf_op jit(solution)/shard_map/ppermute | solution.py:210
  77.1 3.7 %collective-permute-start.5 = (bf16[8,16,256]{2,1,0:T(8,128)(2,1)S(1)}, bf16[8,16,256]{2,1,0:T(8,128)(2,1)S(1)}, u32[]{:S(2)}, u32[]{:S(2)}) collective-permute-start(bf16[8,16,256]{2,1,0:T(8,128)(2,1)S(1)} %get-tuple-element.15), channel_id=1, source_target_pairs={{0,112},{8,120},{16,0},{24,8},{32,16},{40,24},{48,32},{56,40},{64,... | collective-permute-start | bytes 196616 | tf_op jit(solution)/shard_map/ppermute | solution.py:210
  80.9 3.6 %collective-permute-done.5 = bf16[8,16,256]{2,1,0:T(8,128)(2,1)S(1)} collective-permute-done((bf16[8,16,256]{2,1,0:T(8,128)(2,1)S(1)}, bf16[8,16,256]{2,1,0:T(8,128)(2,1)S(1)}, u32[]{:S(2)}, u32[]{:S(2)}) %collective-permute-start.5) | collective-permute-done | bytes 65568 | tf_op jit(solution)/shard_map/ppermute | solution.py:210
  84.5 0.0 copy-start
  84.6 1.9 %collective-permute-start.7 = (bf16[640,256]{1,0:T(8,128)(2,1)S(1)}, bf16[640,256]{1,0:T(8,128)(2,1)S(1)}, u32[]{:S(2)}, u32[]{:S(2)}) collective-permute-start(bf16[640,256]{1,0:T(8,128)(2,1)S(1)} %pad_maximum_fusion.2.mine_ref), channel_id=1, source_target_pairs={{0,8},{8,0},{16,24},{24,16},{32,40},{40,32},{48,56},{56,48},{64,72... | collective-permute-start | bytes 983048 | tf_op jit(solution)/shard_map/ppermute | solution.py:212
  86.5 1.6 %collective-permute-done.7.side_ref = bf16[640,256]{1,0:T(8,128)(2,1)S(1)} collective-permute-done((bf16[640,256]{1,0:T(8,128)(2,1)S(1)}, bf16[640,256]{1,0:T(8,128)(2,1)S(1)}, u32[]{:S(2)}, u32[]{:S(2)}) %collective-permute-start.7) | collective-permute-done | bytes 327712 | tf_op jit(solution)/shard_map/ppermute | solution.py:212
  88.1 0.7 copy-done.1
  88.8 3.2 %near_keys.1 = (bf16[256,1024]{1,0:T(8,128)(2,1)S(1)}, f32[1,1024]{1,0:T(1,128)S(1)}, f32[1,1024]{1,0:T(1,128)S(1)}, f32[128,1024]{1,0:T(8,128)S(1)}) custom-call(s32[1]{0:T(128)} %bitcast.meta_ref, s32[32]{0:T(128)S(1)} %bitcast.25, bf16[128,1792]{1,0:T(8,128)(2,1)S(1)} %bitcast.20, bf16[640,256]{1,0:T(8,128)(2,1)S(1)} %pad_maximum_fusion.2.mine_ref, ...), custom_call_target="tpu_custom_call" | custom-call | flops 402653184 | bytes 1048576 | tf_op jit(solution)/shard_map/near_keys/pallas_call | solution.py:221
  92.0 2.6 %collective-permute-start.8 = (bf16[2048,256]{1,0:T(8,128)(2,1)S(1)}, bf16[2048,256]{1,0:T(8,128)(2,1)S(1)}, u32[]{:S(2)}, u32[]{:S(2)}) collective-permute-start(bf16[2048,256]{1,0:T(8,128)(2,1)S(1)} %bitcast.17), channel_id=1, source_target_pairs={{0,8},{8,0},{16,24},{24,16},{32,40},{40,32},{48,56},{56,48},{64,72... | collective-permute-start | bytes 3145736 | tf_op jit(solution)/shard_map/ppermute | solution.py:232
  94.5 4.2 %own_parity.1 = (f32[1,1024]{1,0:T(1,128)S(1)}, f32[1,1024]{1,0:T(1,128)S(1)}, f32[128,1024]{1,0:T(8,128)S(1)}) custom-call(s32[1]{0:T(128)} %bitcast.meta_ref, bf16[2048,256]{1,0:T(8,128)(2,1)S(1)} %bitcast.18, s32[64,128]{1,0:T(8,128)S(1)} %bitcast.23, bf16[256,1024]{1,0:T(8,128)(2,1)S(1)} %get-tuple-element.18.qt_ref, ...), custom_call_target="tpu_custom_call" | custom-call | flops 1073741824 | bytes 1048576 | tf_op jit(solution)/shard_map/own_parity/pallas_call | solution.py:233
  98.7 0.0 collective-permute-done.8.kv_ref
  98.7 4.3 %other_parity.1 = bf16[128,1024]{1,0:T(8,128)(2,1)S(1)} custom-call(s32[1]{0:T(128)} %bitcast.meta_ref, bf16[2048,256]{1,0:T(8,128)(2,1)S(1)} %collective-permute-done.8.kv_ref, s32[64,128]{1,0:T(8,128)S(1)} %bitcast.24, bf16[256,1024]{1,0:T(8,128)(2,1)S(1)} %get-tuple-element.18.qt_ref, f32[1,1024]{1,0:T(1,128)S(1)} %get-tuple-element.22.m_in, ...), custom_call_target="tpu_custom_call" | custom-call | flops 1073741824 | bytes 1048576 | tf_op jit(solution)/shard_map/other_parity/pallas_call | solution.py:242
  103.0 15.8 %all_to_all.15 = bf16[8,16,1024]{2,1,0:T(8,128)(2,1)S(1)} all-to-all(bf16[8,16,1024]{2,1,0:T(8,128)(2,1)S(1)} %bitcast.21), channel_id=1, replica_groups=mesh['seq'=64,'head'=8] {'head'}, dimensions={0} | all-to-all | bytes 524288 | tf_op jit(solution)/shard_map/all_to_all | solution.py:256
  118.8 0.9 copy.14
  (24 shorter events, 0.2 us)
Async XLA Ops:
  0.0 7.6 %copy-start.2 = (bf16[16,8,1024]{2,1,0:T(8,128)(2,1)S(1)}, bf16[16,8,1024]{2,1,0:T(8,128)(2,1)}, u32[]{:S(2)}) copy-start(bf16[16,8,1024]{2,1,0:T(8,128)(2,1)} %param.5) | copy-start | bytes 786436
  1.6 7.7 %collective-permute-start.1 = (bf16[9,16,256]{2,1,0:T(8,128)(2,1)S(1)}, bf16[9,16,256]{2,1,0:T(8,128)(2,1)S(1)}, u32[]{:S(2)}, u32[]{:S(2)}) collective-permute-start(bf16[9,16,256]{2,1,0:T(8,128)(2,1)S(1)} %pad_maximum_fusion.3), channel_id=1, source_target_pairs={{0,256},{8,264},{16,272},{24,280},{32,288},{40,296},{48,304},{56,3... | collective-permute-start | bytes 221192 | tf_op jit(solution)/shard_map/ppermute | solution.py:195
  5.6 6.2 %collective-permute-start = (bf16[9,16,256]{2,1,0:T(8,128)(2,1)S(1)}, bf16[9,16,256]{2,1,0:T(8,128)(2,1)S(1)}, u32[]{:S(2)}, u32[]{:S(2)}) collective-permute-start(bf16[9,16,256]{2,1,0:T(8,128)(2,1)S(1)} %pad_maximum_fusion.3), channel_id=1, source_target_pairs={{0,128},{8,136},{16,144},{24,152},{32,160},{40,168},{48,176},{56,1... | collective-permute-start | bytes 221192 | tf_op jit(solution)/shard_map/ppermute | solution.py:196
  12.7 10.5 %copy-start.3 = (bf16[1,16,1,256]{3,1,2,0:T(8,128)(2,1)S(1)}, bf16[1,16,1,256]{3,1,2,0:T(8,128)(2,1)}, u32[]{:S(2)}) copy-start(bf16[1,16,1,256]{3,1,2,0:T(8,128)(2,1)} %param.8) | copy-start | bytes 24580
  12.7 25.1 %all-to-all-start = ((bf16[8,16,1792]{2,1,0:T(8,128)(2,1)}), bf16[8,16,1792]{2,1,0:T(8,128)(2,1)S(1)}, u32[]{:S(2)}, u32[]{:S(2)}) async-start(bf16[8,16,1792]{2,1,0:T(8,128)(2,1)} %pad_maximum_fusion.1), calls=%async_computation | async-start | bytes 917504 | tf_op jit(solution)/shard_map/all_to_all | solution.py:199
  23.2 22.8 %collective-permute-start.2 = (bf16[1,16,256]{2,1,0:T(8,128)(2,1)S(1)}, bf16[1,16,256]{2,1,0:T(8,128)(2,1)S(1)}, u32[]{:S(2)}, u32[]{:S(2)}) collective-permute-start(bf16[1,16,256]{2,1,0:T(8,128)(2,1)S(1)} %bitcast.32), channel_id=1, source_target_pairs={{0,384},{8,392},{16,400},{24,408},{32,416},{40,424},{48,432},{56,4... | collective-permute-start | bytes 24584 | tf_op jit(solution)/shard_map/ppermute | solution.py:197
  39.1 52.9 %all-to-all-start.1 = ((bf16[8,2,128,256]{3,2,1,0:T(8,128)(2,1)}), bf16[8,2,128,256]{3,2,1,0:T(8,128)(2,1)S(1)}, u32[]{:S(2)}, u32[]{:S(2)}) async-start(bf16[8,2,128,256]{3,2,1,0:T(8,128)(2,1)} %pad_maximum_fusion), calls=%async_computation.1 | async-start | bytes 2097152 | tf_op jit(solution)/shard_map/all_to_all | solution.py:207
  46.0 22.8 %collective-permute-start.3 = (bf16[4,16,256]{2,1,0:T(8,128)(2,1)S(1)}, bf16[4,16,256]{2,1,0:T(8,128)(2,1)S(1)}, u32[]{:S(2)}, u32[]{:S(2)}) collective-permute-start(bf16[4,16,256]{2,1,0:T(8,128)(2,1)S(1)} %pad_maximum_fusion.4), channel_id=1, source_target_pairs={{0,64},{8,72},{16,80},{24,88},{32,96},{40,104},{48,112},{56,120},{... | collective-permute-start | bytes 98312 | tf_op jit(solution)/shard_map/ppermute | solution.py:203
  68.7 12.1 %collective-permute-start.4 = (bf16[8,16,256]{2,1,0:T(8,128)(2,1)S(1)}, bf16[8,16,256]{2,1,0:T(8,128)(2,1)S(1)}, u32[]{:S(2)}, u32[]{:S(2)}) collective-permute-start(bf16[8,16,256]{2,1,0:T(8,128)(2,1)S(1)} %get-tuple-element.15), channel_id=1, source_target_pairs={{0,16},{8,24},{16,32},{24,40},{32,48},{40,56},{48,64},{56,72},{64,... | collective-permute-start | bytes 196616 | tf_op jit(solution)/shard_map/ppermute | solution.py:210
  75.2 9.3 %collective-permute-start.6 = (bf16[8,16,256]{2,1,0:T(8,128)(2,1)S(1)}, bf16[8,16,256]{2,1,0:T(8,128)(2,1)S(1)}, u32[]{:S(2)}, u32[]{:S(2)}) collective-permute-start(bf16[8,16,256]{2,1,0:T(8,128)(2,1)S(1)} %get-tuple-element.15), channel_id=1, source_target_pairs={{0,32},{8,40},{16,48},{24,56},{32,64},{40,72},{48,80},{56,88},{64,... | collective-permute-start | bytes 196616 | tf_op jit(solution)/shard_map/ppermute | solution.py:210
  77.1 7.4 %collective-permute-start.5 = (bf16[8,16,256]{2,1,0:T(8,128)(2,1)S(1)}, bf16[8,16,256]{2,1,0:T(8,128)(2,1)S(1)}, u32[]{:S(2)}, u32[]{:S(2)}) collective-permute-start(bf16[8,16,256]{2,1,0:T(8,128)(2,1)S(1)} %get-tuple-element.15), channel_id=1, source_target_pairs={{0,112},{8,120},{16,0},{24,8},{32,16},{40,24},{48,32},{56,40},{64,... | collective-permute-start | bytes 196616 | tf_op jit(solution)/shard_map/ppermute | solution.py:210
  84.5 3.6 %copy-start = (s32[8192]{0:T(1024)S(1)}, s32[8192]{0:T(1024)}, u32[]{:S(2)}) copy-start(s32[8192]{0:T(1024)} %param.7) | copy-start | bytes 98308
  84.6 3.5 %collective-permute-start.7 = (bf16[640,256]{1,0:T(8,128)(2,1)S(1)}, bf16[640,256]{1,0:T(8,128)(2,1)S(1)}, u32[]{:S(2)}, u32[]{:S(2)}) collective-permute-start(bf16[640,256]{1,0:T(8,128)(2,1)S(1)} %pad_maximum_fusion.2.mine_ref), channel_id=1, source_target_pairs={{0,8},{8,0},{16,24},{24,16},{32,40},{40,32},{48,56},{56,48},{64,72... | collective-permute-start | bytes 983048 | tf_op jit(solution)/shard_map/ppermute | solution.py:212
  88.1 0.7 copy-start.1
  92.0 6.8 %collective-permute-start.8 = (bf16[2048,256]{1,0:T(8,128)(2,1)S(1)}, bf16[2048,256]{1,0:T(8,128)(2,1)S(1)}, u32[]{:S(2)}, u32[]{:S(2)}) collective-permute-start(bf16[2048,256]{1,0:T(8,128)(2,1)S(1)} %bitcast.17), channel_id=1, source_target_pairs={{0,8},{8,0},{16,24},{24,16},{32,40},{40,32},{48,56},{56,48},{64,72... | collective-permute-start | bytes 3145736 | tf_op jit(solution)/shard_map/ppermute | solution.py:232

commit v5 on v4

--- a/solution.py
+++ b/solution.py
@@ -109,10 +109,9 @@
     for i in range(PAGES):
         page = table_ref[i]
         off = (y + NY - (page // 2) % NY) % NY
-        unit = (x + NX - page // (2 * NY)) % NX
         shift = jnp.where(off % 4 == 3, 2, jnp.where(off % 4 == 2, 3, off % 4))
         half = jnp.where(off % 4 == 3, 1 - off // 4, off // 4)
-        unit = unit + 4 * half + 8 * shift
+        unit = NY * ((x + NX - page // (2 * NY)) % NX) + half + 2 * shift
         rows = pl.ds(pl.multiple_of(ROWS + unit * PAGE, PAGE), PAGE)
 
         @pl.when(page % 2 == core)
@@ -191,23 +190,23 @@
     me = lax.axis_index("seq")
     y = (me // 2) % NY
     page = pool.reshape(1, PAGE, PAIR)
-    raw = jnp.concatenate([jnp.transpose(branch_key_value, (1, 0, 2)), page], axis=0)
-    two_raw = lax.ppermute(raw, "seq", x_ring(2))
-    one_raw = lax.ppermute(raw, "seq", x_ring(1))
-    three_page = lax.ppermute(page, "seq", x_ring(3))
-    wide = jnp.concatenate([jnp.transpose(queries, (1, 0, 2)), raw[:8], one_raw[:8], two_raw[:8]], axis=2)
+    pages = jnp.concatenate([page, lax.ppermute(page, "seq", y_ring(4))], axis=0)
+    raw = jnp.transpose(branch_key_value, (1, 0, 2))
+    two_raw = lax.ppermute(raw, "seq", x_shift(2))
+    one_raw = lax.ppermute(raw, "seq", x_shift(1))
+    wide = jnp.concatenate([jnp.transpose(queries, (1, 0, 2)), raw, one_raw, two_raw], axis=2)
     wide = lax.all_to_all(wide, "head", split_axis=0, concat_axis=0, tiled=True).reshape(ROWS, -1)
+    pages = jnp.concatenate([pages] + [lax.ppermute(pages, "seq", y_ring(k)) for k in (1, -1, 2)], axis=0)
+    wide, pages = lax.optimization_barrier((wide, pages))
     at = GROUP * D
     own, one_back, two_back = (wide[:, at + i * PAIR:at + (i + 1) * PAIR] for i in range(3))
-    pages = jnp.concatenate([page, one_raw[8:], two_raw[8:], three_page], axis=0)
-    pages = jnp.concatenate([pages, lax.ppermute(pages, "seq", y_ring(4))], axis=0)
     target = jnp.arange(NY, dtype=jnp.int32)[:, None, None]
     mixed = jnp.where(target > y, own[None], two_back[None])
     send = jnp.stack([jnp.broadcast_to(one_back[None], mixed.shape), mixed], axis=1)
     kv = lax.all_to_all(send, "seq", split_axis=0, concat_axis=0, tiled=True, axis_index_groups=Y_GROUPS)
     kv = kv.reshape(2 * NY * ROWS, PAIR)
     later, _ = lax.optimization_barrier((pages, send))
-    pages = jnp.concatenate([pages] + [lax.ppermute(later, "seq", y_ring(k)) for k in (1, -1, 2)], axis=0)
+    pages = jnp.concatenate([pages] + [lax.ppermute(later, "seq", x_ring(k)) for k in (1, 2, 3)], axis=0)
     mine = jnp.concatenate([own, pages.reshape(PAGES * PAGE, PAIR)], axis=0)
     side = lax.ppermute(mine, "seq", SWAP)
     ids = branch_ids.reshape(2 * NX * NY, ROWS)

time: 120 us -> 101 us (0.84)
  the two profiles are of different devices: /device:TPU:58 before, /device:TPU:11 now
where the time goes in v5:
time: 101 us; the launch traced here: 100 us
  starting transfers between devices  55.7 us (55%)
  blocking collectives  16.6 us (16%)
  waiting for transfers between devices  11.6 us (11%)
  Pallas kernels  10.3 us (10%)
  local copies, waits for them, and re-layouts  3.54 us (4%)
  other arithmetic  2.07 us (2%)
    all_to_all x1, blocking collectives, per_device(): lax.all_to_all(out.reshape(8, ROWS // 8, GROUP * D), 'head', split_axis=0...  16.6 us
    all_to_all x1, starting transfers between devices, per_device(): lax.all_to_all(wide, 'head', split_axis=0, concat_axis=0, tiled=True)  10 us
    ppermute x3, starting transfers between devices, per_device(): lax.ppermute(later, 'seq', x_ring(k))  8.18 us
    ppermute x3, starting transfers between devices, per_device(): lax.ppermute(pages, 'seq', y_ring(k))  7.7 us
    ppermute x1, starting transfers between devices, per_device(): kv_side = lax.ppermute(kv, 'seq', SWAP)  7.29 us
    ppermute x1, starting transfers between devices, per_device(): lax.ppermute(page, 'seq', y_ring(4))  6.55 us
    ppermute x1, starting transfers between devices, per_device(): side = lax.ppermute(mine, 'seq', SWAP)  5.72 us
    all_to_all x1, starting transfers between devices, per_device(): lax.all_to_all(send, 'seq', split_axis=0, concat_axis=0, tiled=True, axis...  4.53 us
  transfers between devices with their start and end apart: 13, of which 6 were waited for; matrix products, arithmetic and copies ran while one was open for 2% of the time, Pallas kernels for 7%

profile of v5, /device:TPU:11, one launch (start us, length us, event | category | flops | bytes accessed | tf_op | source)
XLA Modules:
  0.0 100.0 jit_solution(13850034955001596917)
XLA Ops:
  0.0 0.9 copy.14
  0.9 3.8 %collective-permute-start.1 = (bf16[8,16,256]{2,1,0:T(8,128)(2,1)S(1)}, bf16[8,16,256]{2,1,0:T(8,128)(2,1)S(1)}, u32[]{:S(2)}, u32[]{:S(2)}) collective-permute-start(bf16[8,16,256]{2,1,0:T(8,128)(2,1)S(1)} %bitcast.28), channel_id=1, source_target_pairs={{0,256},{8,264},{16,272},{24,280},{32,288},{40,296},{48,304},{56,3... | collective-permute-start | bytes 196616 | tf_op jit(solution)/shard_map/ppermute | solution.py:195
  4.6 1.9 %collective-permute-start = (bf16[8,16,256]{2,1,0:T(8,128)(2,1)S(1)}, bf16[8,16,256]{2,1,0:T(8,128)(2,1)S(1)}, u32[]{:S(2)}, u32[]{:S(2)}) collective-permute-start(bf16[8,16,256]{2,1,0:T(8,128)(2,1)S(1)} %bitcast.29), channel_id=1, source_target_pairs={{0,128},{8,136},{16,144},{24,152},{32,160},{40,168},{48,176},{56,1... | collective-permute-start | bytes 196616 | tf_op jit(solution)/shard_map/ppermute | solution.py:196
  6.6 6.6 %collective-permute-start.2 = (bf16[1,16,256]{2,1,0:T(8,128)(2,1)S(1)}, bf16[1,16,256]{2,1,0:T(8,128)(2,1)S(1)}, u32[]{:S(2)}, u32[]{:S(2)}) collective-permute-start(bf16[1,16,256]{2,1,0:T(8,128)(2,1)S(1)} %bitcast.31), channel_id=1, source_target_pairs={{0,64},{8,72},{16,80},{24,88},{32,96},{40,104},{48,112},{56,120},{... | collective-permute-start | bytes 24584 | tf_op jit(solution)/shard_map/ppermute | solution.py:193
  13.2 1.1 %copy.13 = bf16[16,8,1024]{2,0,1:T(8,128)(2,1)S(1)} copy(bf16[16,8,1024]{2,1,0:T(8,128)(2,1)} %param.5) | data formatting | bytes 524288 | tf_op args[0]
  14.3 0.0 collective-permute-done
  14.3 0.8 pad_maximum_fusion.1
  15.1 10.0 %all-to-all-start = ((bf16[8,16,1792]{2,1,0:T(8,128)(2,1)}), bf16[8,16,1792]{2,1,0:T(8,128)(2,1)S(1)}, u32[]{:S(2)}, u32[]{:S(2)}) async-start(bf16[8,16,1792]{2,1,0:T(8,128)(2,1)} %pad_maximum_fusion.1), calls=%async_computation | async-start | bytes 917504 | tf_op jit(solution)/shard_map/all_to_all | solution.py:198
  25.2 2.4 %collective-permute-start.5 = (bf16[2,16,256]{2,1,0:T(8,128)(2,1)S(1)}, bf16[2,16,256]{2,1,0:T(8,128)(2,1)S(1)}, u32[]{:S(2)}, u32[]{:S(2)}) collective-permute-start(bf16[2,16,256]{2,1,0:T(8,128)(2,1)S(1)} %pad_maximum_fusion.4), channel_id=1, source_target_pairs={{0,32},{8,40},{16,48},{24,56},{32,64},{40,72},{48,80},{56,88},{64,... | collective-permute-start | bytes 49160 | tf_op jit(solution)/shard_map/ppermute | solution.py:199
  27.6 3.0 %collective-permute-start.4 = (bf16[2,16,256]{2,1,0:T(8,128)(2,1)S(1)}, bf16[2,16,256]{2,1,0:T(8,128)(2,1)S(1)}, u32[]{:S(2)}, u32[]{:S(2)}) collective-permute-start(bf16[2,16,256]{2,1,0:T(8,128)(2,1)S(1)} %pad_maximum_fusion.4), channel_id=1, source_target_pairs={{0,112},{8,120},{16,0},{24,8},{32,16},{40,24},{48,32},{56,40},{64,... | collective-permute-start | bytes 49160 | tf_op jit(solution)/shard_map/ppermute | solution.py:199
  30.6 2.3 %collective-permute-start.3 = (bf16[2,16,256]{2,1,0:T(8,128)(2,1)S(1)}, bf16[2,16,256]{2,1,0:T(8,128)(2,1)S(1)}, u32[]{:S(2)}, u32[]{:S(2)}) collective-permute-start(bf16[2,16,256]{2,1,0:T(8,128)(2,1)S(1)} %pad_maximum_fusion.4), channel_id=1, source_target_pairs={{0,16},{8,24},{16,32},{24,40},{32,48},{40,56},{48,64},{56,72},{64,... | collective-permute-start | bytes 49160 | tf_op jit(solution)/shard_map/ppermute | solution.py:199
  32.9 3.3 %collective-permute-done.3 = bf16[2,16,256]{2,1,0:T(8,128)(2,1)S(1)} collective-permute-done((bf16[2,16,256]{2,1,0:T(8,128)(2,1)S(1)}, bf16[2,16,256]{2,1,0:T(8,128)(2,1)S(1)}, u32[]{:S(2)}, u32[]{:S(2)}) %collective-permute-start.3) | collective-permute-done | bytes 16416 | tf_op jit(solution)/shard_map/ppermute | solution.py:199
  36.2 3.6 %all-to-all-done = bf16[8,16,1792]{2,1,0:T(8,128)(2,1)S(1)} async-done(((bf16[8,16,1792]{2,1,0:T(8,128)(2,1)}), bf16[8,16,1792]{2,1,0:T(8,128)(2,1)S(1)}, u32[]{:S(2)}, u32[]{:S(2)}) %all-to-all-start) | async-done | bytes 458784 | tf_op jit(solution)/shard_map/all_to_all | solution.py:198
  39.8 0.1 broadcast_select_fusion
  40.0 1.1 %pad_maximum_fusion = bf16[8,2,128,256]{3,2,1,0:T(8,128)(2,1)} fusion(bf16[8,1,128,256]{3,2,1,0:T(8,128)(2,1)S(1)} %broadcast_select_fusion, bf16[8,1,128,256]{3,2,1,0:T(8,128)(2,1)S(1)} %stack_broadcast_in_dim.2), kind=kLoop, calls=%fused_computation | loop fusion | flops 524288 | bytes 2097152 | tf_op jit(solution)/shard_map/stack | solution.py:205
  41.0 4.5 %all-to-all-start.1 = ((bf16[8,2,128,256]{3,2,1,0:T(8,128)(2,1)}), bf16[8,2,128,256]{3,2,1,0:T(8,128)(2,1)S(1)}, u32[]{:S(2)}, u32[]{:S(2)}) async-start(bf16[8,2,128,256]{3,2,1,0:T(8,128)(2,1)} %pad_maximum_fusion), calls=%async_computation.1 | async-start | bytes 2097152 | tf_op jit(solution)/shard_map/all_to_all | solution.py:206
  45.6 3.2 %collective-permute-start.8 = (bf16[8,16,256]{2,1,0:T(8,128)(2,1)S(1)}, bf16[8,16,256]{2,1,0:T(8,128)(2,1)S(1)}, u32[]{:S(2)}, u32[]{:S(2)}) collective-permute-start(bf16[8,16,256]{2,1,0:T(8,128)(2,1)S(1)} %constant_dynamic-update-slice_fusion), channel_id=1, source_target_pairs={{0,384},{8,392},{16,400},{24,408},{32,416},{40,424},{48,432},{56,4... | collective-permute-start | bytes 196616 | tf_op jit(solution)/shard_map/ppermute | solution.py:209
  48.7 1.9 %collective-permute-start.7 = (bf16[8,16,256]{2,1,0:T(8,128)(2,1)S(1)}, bf16[8,16,256]{2,1,0:T(8,128)(2,1)S(1)}, u32[]{:S(2)}, u32[]{:S(2)}) collective-permute-start(bf16[8,16,256]{2,1,0:T(8,128)(2,1)S(1)} %constant_dynamic-update-slice_fusion), channel_id=1, source_target_pairs={{0,256},{8,264},{16,272},{24,280},{32,288},{40,296},{48,304},{56,3... | collective-permute-start | bytes 196616 | tf_op jit(solution)/shard_map/ppermute | solution.py:209
  50.7 3.1 %collective-permute-start.6 = (bf16[8,16,256]{2,1,0:T(8,128)(2,1)S(1)}, bf16[8,16,256]{2,1,0:T(8,128)(2,1)S(1)}, u32[]{:S(2)}, u32[]{:S(2)}) collective-permute-start(bf16[8,16,256]{2,1,0:T(8,128)(2,1)S(1)} %constant_dynamic-update-slice_fusion), channel_id=1, source_target_pairs={{0,128},{8,136},{16,144},{24,152},{32,160},{40,168},{48,176},{56,1... | collective-permute-start | bytes 196616 | tf_op jit(solution)/shard_map/ppermute | solution.py:209
  53.8 1.8 %collective-permute-done.7 = bf16[8,16,256]{2,1,0:T(8,128)(2,1)S(1)} collective-permute-done((bf16[8,16,256]{2,1,0:T(8,128)(2,1)S(1)}, bf16[8,16,256]{2,1,0:T(8,128)(2,1)S(1)}, u32[]{:S(2)}, u32[]{:S(2)}) %collective-permute-start.7) | collective-permute-done | bytes 65568 | tf_op jit(solution)/shard_map/ppermute | solution.py:209
  55.6 0.9 collective-permute-done.6
  56.5 0.0 copy-start
  56.6 5.7 %collective-permute-start.9 = (bf16[640,256]{1,0:T(8,128)(2,1)S(1)}, bf16[640,256]{1,0:T(8,128)(2,1)S(1)}, u32[]{:S(2)}, u32[]{:S(2)}) collective-permute-start(bf16[640,256]{1,0:T(8,128)(2,1)S(1)} %pad_maximum_fusion.2.mine_ref), channel_id=1, source_target_pairs={{0,8},{8,0},{16,24},{24,16},{32,40},{40,32},{48,56},{56,48},{64,72... | collective-permute-start | bytes 983048 | tf_op jit(solution)/shard_map/ppermute | solution.py:211
  62.3 1.2 %collective-permute-done.9.side_ref = bf16[640,256]{1,0:T(8,128)(2,1)S(1)} collective-permute-done((bf16[640,256]{1,0:T(8,128)(2,1)S(1)}, bf16[640,256]{1,0:T(8,128)(2,1)S(1)}, u32[]{:S(2)}, u32[]{:S(2)}) %collective-permute-start.9) | collective-permute-done | bytes 327712 | tf_op jit(solution)/shard_map/ppermute | solution.py:211
  63.5 0.7 copy-done.1
  64.2 3.7 %near_keys.1 = (bf16[256,1024]{1,0:T(8,128)(2,1)S(1)}, f32[1,1024]{1,0:T(1,128)S(1)}, f32[1,1024]{1,0:T(1,128)S(1)}, f32[128,1024]{1,0:T(8,128)S(1)}) custom-call(s32[1]{0:T(128)} %bitcast.meta_ref, s32[32]{0:T(128)S(1)} %bitcast.24, bf16[128,1792]{1,0:T(8,128)(2,1)S(1)} %bitcast.19, bf16[640,256]{1,0:T(8,128)(2,1)S(1)} %pad_maximum_fusion.2.mine_ref, ...), custom_call_target="tpu_custom_call" | custom-call | flops 402653184 | bytes 1048576 | tf_op jit(solution)/shard_map/near_keys/pallas_call | solution.py:220
  67.9 0.8 all-to-all-done.1
  68.7 7.3 %collective-permute-start.10 = (bf16[2048,256]{1,0:T(8,128)(2,1)S(1)}, bf16[2048,256]{1,0:T(8,128)(2,1)S(1)}, u32[]{:S(2)}, u32[]{:S(2)}) collective-permute-start(bf16[2048,256]{1,0:T(8,128)(2,1)S(1)} %bitcast.16), channel_id=1, source_target_pairs={{0,8},{8,0},{16,24},{24,16},{32,40},{40,32},{48,56},{56,48},{64,72... | collective-permute-start | bytes 3145736 | tf_op jit(solution)/shard_map/ppermute | solution.py:231
  76.0 3.2 %own_parity.1 = (f32[1,1024]{1,0:T(1,128)S(1)}, f32[1,1024]{1,0:T(1,128)S(1)}, f32[128,1024]{1,0:T(8,128)S(1)}) custom-call(s32[1]{0:T(128)} %bitcast.meta_ref, bf16[2048,256]{1,0:T(8,128)(2,1)S(1)} %bitcast.17, s32[64,128]{1,0:T(8,128)S(1)} %bitcast.22, bf16[256,1024]{1,0:T(8,128)(2,1)S(1)} %get-tuple-element.22.qt_ref, ...), custom_call_target="tpu_custom_call" | custom-call | flops 1073741824 | bytes 1048576 | tf_op jit(solution)/shard_map/own_parity/pallas_call | solution.py:232
  79.3 3.4 %other_parity.1 = bf16[128,1024]{1,0:T(8,128)(2,1)S(1)} custom-call(s32[1]{0:T(128)} %bitcast.meta_ref, bf16[2048,256]{1,0:T(8,128)(2,1)S(1)} %collective-permute-done.10.kv_ref, s32[64,128]{1,0:T(8,128)S(1)} %bitcast.23, bf16[256,1024]{1,0:T(8,128)(2,1)S(1)} %get-tuple-element.22.qt_ref, f32[1,1024]{1,0:T(1,128)S(1)} %get-tuple-element.26.m_in, ...), custom_call_target="tpu_custom_call" | custom-call | flops 1073741824 | bytes 1048576 | tf_op jit(solution)/shard_map/other_parity/pallas_call | solution.py:241
  82.6 16.6 %all_to_all.15 = bf16[8,16,1024]{2,1,0:T(8,128)(2,1)S(1)} all-to-all(bf16[8,16,1024]{2,1,0:T(8,128)(2,1)S(1)} %bitcast.20), channel_id=1, replica_groups=mesh['seq'=64,'head'=8] {'head'}, dimensions={0} | all-to-all | bytes 524288 | tf_op jit(solution)/shard_map/all_to_all | solution.py:255
  99.2 0.9 copy.10
  (21 shorter events, 0.2 us)
Async XLA Ops:
  0.0 6.6 %copy-start.2 = (bf16[1,16,1,256]{3,1,2,0:T(8,128)(2,1)S(1)}, bf16[1,16,1,256]{3,1,2,0:T(8,128)(2,1)}, u32[]{:S(2)}) copy-start(bf16[1,16,1,256]{3,1,2,0:T(8,128)(2,1)} %param.8) | copy-start | bytes 24580
  0.9 13.4 %collective-permute-start.1 = (bf16[8,16,256]{2,1,0:T(8,128)(2,1)S(1)}, bf16[8,16,256]{2,1,0:T(8,128)(2,1)S(1)}, u32[]{:S(2)}, u32[]{:S(2)}) collective-permute-start(bf16[8,16,256]{2,1,0:T(8,128)(2,1)S(1)} %bitcast.28), channel_id=1, source_target_pairs={{0,256},{8,264},{16,272},{24,280},{32,288},{40,296},{48,304},{56,3... | collective-permute-start | bytes 196616 | tf_op jit(solution)/shard_map/ppermute | solution.py:195
  4.6 9.7 %collective-permute-start = (bf16[8,16,256]{2,1,0:T(8,128)(2,1)S(1)}, bf16[8,16,256]{2,1,0:T(8,128)(2,1)S(1)}, u32[]{:S(2)}, u32[]{:S(2)}) collective-permute-start(bf16[8,16,256]{2,1,0:T(8,128)(2,1)S(1)} %bitcast.29), channel_id=1, source_target_pairs={{0,128},{8,136},{16,144},{24,152},{32,160},{40,168},{48,176},{56,1... | collective-permute-start | bytes 196616 | tf_op jit(solution)/shard_map/ppermute | solution.py:196
  6.6 18.6 %collective-permute-start.2 = (bf16[1,16,256]{2,1,0:T(8,128)(2,1)S(1)}, bf16[1,16,256]{2,1,0:T(8,128)(2,1)S(1)}, u32[]{:S(2)}, u32[]{:S(2)}) collective-permute-start(bf16[1,16,256]{2,1,0:T(8,128)(2,1)S(1)} %bitcast.31), channel_id=1, source_target_pairs={{0,64},{8,72},{16,80},{24,88},{32,96},{40,104},{48,112},{56,120},{... | collective-permute-start | bytes 24584 | tf_op jit(solution)/shard_map/ppermute | solution.py:193
  15.1 24.7 %all-to-all-start = ((bf16[8,16,1792]{2,1,0:T(8,128)(2,1)}), bf16[8,16,1792]{2,1,0:T(8,128)(2,1)S(1)}, u32[]{:S(2)}, u32[]{:S(2)}) async-start(bf16[8,16,1792]{2,1,0:T(8,128)(2,1)} %pad_maximum_fusion.1), calls=%async_computation | async-start | bytes 917504 | tf_op jit(solution)/shard_map/all_to_all | solution.py:198
  25.2 11.0 %collective-permute-start.5 = (bf16[2,16,256]{2,1,0:T(8,128)(2,1)S(1)}, bf16[2,16,256]{2,1,0:T(8,128)(2,1)S(1)}, u32[]{:S(2)}, u32[]{:S(2)}) collective-permute-start(bf16[2,16,256]{2,1,0:T(8,128)(2,1)S(1)} %pad_maximum_fusion.4), channel_id=1, source_target_pairs={{0,32},{8,40},{16,48},{24,56},{32,64},{40,72},{48,80},{56,88},{64,... | collective-permute-start | bytes 49160 | tf_op jit(solution)/shard_map/ppermute | solution.py:199
  27.6 8.6 %collective-permute-start.4 = (bf16[2,16,256]{2,1,0:T(8,128)(2,1)S(1)}, bf16[2,16,256]{2,1,0:T(8,128)(2,1)S(1)}, u32[]{:S(2)}, u32[]{:S(2)}) collective-permute-start(bf16[2,16,256]{2,1,0:T(8,128)(2,1)S(1)} %pad_maximum_fusion.4), channel_id=1, source_target_pairs={{0,112},{8,120},{16,0},{24,8},{32,16},{40,24},{48,32},{56,40},{64,... | collective-permute-start | bytes 49160 | tf_op jit(solution)/shard_map/ppermute | solution.py:199
  30.6 5.6 %collective-permute-start.3 = (bf16[2,16,256]{2,1,0:T(8,128)(2,1)S(1)}, bf16[2,16,256]{2,1,0:T(8,128)(2,1)S(1)}, u32[]{:S(2)}, u32[]{:S(2)}) collective-permute-start(bf16[2,16,256]{2,1,0:T(8,128)(2,1)S(1)} %pad_maximum_fusion.4), channel_id=1, source_target_pairs={{0,16},{8,24},{16,32},{24,40},{32,48},{40,56},{48,64},{56,72},{64,... | collective-permute-start | bytes 49160 | tf_op jit(solution)/shard_map/ppermute | solution.py:199
  41.0 27.7 %all-to-all-start.1 = ((bf16[8,2,128,256]{3,2,1,0:T(8,128)(2,1)}), bf16[8,2,128,256]{3,2,1,0:T(8,128)(2,1)S(1)}, u32[]{:S(2)}, u32[]{:S(2)}) async-start(bf16[8,2,128,256]{3,2,1,0:T(8,128)(2,1)} %pad_maximum_fusion), calls=%async_computation.1 | async-start | bytes 2097152 | tf_op jit(solution)/shard_map/all_to_all | solution.py:206
  45.6 8.2 %collective-permute-start.8 = (bf16[8,16,256]{2,1,0:T(8,128)(2,1)S(1)}, bf16[8,16,256]{2,1,0:T(8,128)(2,1)S(1)}, u32[]{:S(2)}, u32[]{:S(2)}) collective-permute-start(bf16[8,16,256]{2,1,0:T(8,128)(2,1)S(1)} %constant_dynamic-update-slice_fusion), channel_id=1, source_target_pairs={{0,384},{8,392},{16,400},{24,408},{32,416},{40,424},{48,432},{56,4... | collective-permute-start | bytes 196616 | tf_op jit(solution)/shard_map/ppermute | solution.py:209
  48.7 6.8 %collective-permute-start.7 = (bf16[8,16,256]{2,1,0:T(8,128)(2,1)S(1)}, bf16[8,16,256]{2,1,0:T(8,128)(2,1)S(1)}, u32[]{:S(2)}, u32[]{:S(2)}) collective-permute-start(bf16[8,16,256]{2,1,0:T(8,128)(2,1)S(1)} %constant_dynamic-update-slice_fusion), channel_id=1, source_target_pairs={{0,256},{8,264},{16,272},{24,280},{32,288},{40,296},{48,304},{56,3... | collective-permute-start | bytes 196616 | tf_op jit(solution)/shard_map/ppermute | solution.py:209
  50.7 5.8 %collective-permute-start.6 = (bf16[8,16,256]{2,1,0:T(8,128)(2,1)S(1)}, bf16[8,16,256]{2,1,0:T(8,128)(2,1)S(1)}, u32[]{:S(2)}, u32[]{:S(2)}) collective-permute-start(bf16[8,16,256]{2,1,0:T(8,128)(2,1)S(1)} %constant_dynamic-update-slice_fusion), channel_id=1, source_target_pairs={{0,128},{8,136},{16,144},{24,152},{32,160},{40,168},{48,176},{56,1... | collective-permute-start | bytes 196616 | tf_op jit(solution)/shard_map/ppermute | solution.py:209
  56.5 7.0 %copy-start = (s32[8192]{0:T(1024)S(1)}, s32[8192]{0:T(1024)}, u32[]{:S(2)}) copy-start(s32[8192]{0:T(1024)} %param.7) | copy-start | bytes 98308
  56.6 7.0 %collective-permute-start.9 = (bf16[640,256]{1,0:T(8,128)(2,1)S(1)}, bf16[640,256]{1,0:T(8,128)(2,1)S(1)}, u32[]{:S(2)}, u32[]{:S(2)}) collective-permute-start(bf16[640,256]{1,0:T(8,128)(2,1)S(1)} %pad_maximum_fusion.2.mine_ref), channel_id=1, source_target_pairs={{0,8},{8,0},{16,24},{24,16},{32,40},{40,32},{48,56},{56,48},{64,72... | collective-permute-start | bytes 983048 | tf_op jit(solution)/shard_map/ppermute | solution.py:211
  63.5 0.7 copy-start.1
  68.7 10.6 %collective-permute-start.10 = (bf16[2048,256]{1,0:T(8,128)(2,1)S(1)}, bf16[2048,256]{1,0:T(8,128)(2,1)S(1)}, u32[]{:S(2)}, u32[]{:S(2)}) collective-permute-start(bf16[2048,256]{1,0:T(8,128)(2,1)S(1)} %bitcast.16), channel_id=1, source_target_pairs={{0,8},{8,0},{16,24},{24,16},{32,40},{40,32},{48,56},{56,48},{64,72... | collective-permute-start | bytes 3145736 | tf_op jit(solution)/shard_map/ppermute | solution.py:231

commit v6 on v3

--- a/solution.py
+++ b/solution.py
@@ -17,25 +17,12 @@
 TILE = 512
 SCALE2 = D ** (-0.5) * 1.4426950408889634
 LOW = -1e30
-
-
-def x_shift(by):
-    return [
-        ((x * NY + y) * 2 + c, ((x + by) * NY + y) * 2 + c)
-        for x in range(NX) for y in range(NY) for c in range(2) if 0 <= x + by < NX
-    ]
+SLOT = 2 * ROWS + NX * PAGE
 
 
 def x_ring(by):
     return [
         ((x * NY + y) * 2 + c, (((x + by) % NX) * NY + y) * 2 + c)
-        for x in range(NX) for y in range(NY) for c in range(2)
-    ]
-
-
-def y_ring(by):
-    return [
-        ((x * NY + y) * 2 + c, (x * NY + (y + by) % NY) * 2 + c)
         for x in range(NX) for y in range(NY) for c in range(2)
     ]
 
@@ -86,10 +73,13 @@
     return (key_rows >= row_start) & (key_rows <= query_rows)
 
 
-def near_kernel(meta_ref, table_ref, q_ref, mine_ref, side_ref, ids_ref, qt_ref, m_ref, l_ref, acc_ref, prefix_ref):
-    own = meta_ref[0]
-    core, y, x = own % 2, (own // 2) % NY, own // (2 * NY)
+def near_kernel(meta_ref, mine_ref, side_ref, ids_ref, *refs):
+    q_refs, (qt_ref, m_ref, l_ref, acc_ref, q_ref) = refs[:8], refs[8:]
+    own, z = meta_ref[0], meta_ref[1]
     row_start, first, last = starts_of(ids_ref, own)
+    for k in range(8):
+        source = (z + 8 - k) % 8
+        q_ref[pl.ds(pl.multiple_of(source * 16, 16), 16), :] = q_refs[k][...]
     for g in range(GROUP):
         scaled = q_ref[:, g * D:(g + 1) * D].astype(jnp.float32) * SCALE2
         high = scaled.astype(jnp.bfloat16)
@@ -100,27 +90,11 @@
     l_ref[...] = jnp.zeros_like(l_ref)
     acc_ref[...] = jnp.zeros_like(acc_ref)
     state = (qt_ref, m_ref, l_ref, acc_ref)
-    fold(mine_ref[:ROWS, :D], mine_ref[:ROWS, D:], mask_of(own, own, row_start), *state)
-
-    @pl.when((core == 1) & (own * ROWS > first))
+    fold(mine_ref[:, :D], mine_ref[:, D:], mask_of(own, own, row_start), *state)
+
+    @pl.when((own % 2 == 1) & (own * ROWS > first))
     def _():
-        fold(side_ref[:ROWS, :D], side_ref[:ROWS, D:], mask_of(own - 1, own, row_start), *state)
-
-    for i in range(PAGES):
-        page = table_ref[i]
-        off = (y + NY - (page // 2) % NY) % NY
-        unit = NY * ((x + NX - page // (2 * NY)) % NX) + off // 4 + 2 * (off % 4)
-        rows = pl.ds(pl.multiple_of(ROWS + unit * PAGE, PAGE), PAGE)
-
-        @pl.when(page % 2 == core)
-        def _():
-            prefix_ref[i * PAGE:(i + 1) * PAGE, :] = mine_ref[rows, :]
-
-        @pl.when(page % 2 != core)
-        def _():
-            prefix_ref[i * PAGE:(i + 1) * PAGE, :] = side_ref[rows, :]
-
-    fold(prefix_ref[:, :D], prefix_ref[:, D:], None, *state)
+        fold(side_ref[:, :D], side_ref[:, D:], mask_of(own - 1, own, row_start), *state)
 
 
 def window(kv_ref, core, own, ids_ref, qt_ref, m_ref, l_ref, acc_ref):
@@ -135,8 +109,8 @@
         pairs = []
         for b in range(BLOCKS):
             at = jnp.maximum(base + b, 0)
-            slot = (at % NY) * 2 + jnp.where(at // NY == x - 1, 0, 1)
-            pairs.append(kv_ref[pl.ds(pl.multiple_of(slot * ROWS, ROWS), ROWS), :])
+            start = (at % NY) * SLOT + jnp.where(at // NY == x - 1, 0, ROWS)
+            pairs.append(kv_ref[pl.ds(pl.multiple_of(start, PAGE), ROWS), :])
         keys = jnp.concatenate([pair[:, :D] for pair in pairs], axis=0)
         values = jnp.concatenate([pair[:, D:] for pair in pairs], axis=0)
         whole = (2 * base + core) * ROWS >= last
@@ -165,12 +139,28 @@
     window(kv_ref, own % 2, own, ids_ref, qt_ref, m_ref, l_ref, acc_ref)
 
 
-def last_kernel(meta_ref, kv_ref, ids_ref, qt_ref, m_in, l_in, acc_in, out_ref, m_ref, l_ref, acc_ref):
+def last_kernel(meta_ref, table_ref, mine_ref, kv_ref, ids_ref, qt_ref, m_in, l_in, acc_in,
+                out_ref, m_ref, l_ref, acc_ref, prefix_ref):
     m_ref[...] = m_in[...]
     l_ref[...] = l_in[...]
     acc_ref[...] = acc_in[...]
     own = meta_ref[0]
-    window(kv_ref, 1 - own % 2, own, ids_ref, qt_ref, m_ref, l_ref, acc_ref)
+    core, x = own % 2, own // (2 * NY)
+    for i in range(PAGES):
+        page = table_ref[i]
+        start = (page // 2) % NY * SLOT + 2 * ROWS + (x + NX - page // (2 * NY)) % NX * PAGE
+        rows = pl.ds(pl.multiple_of(start, PAGE), PAGE)
+
+        @pl.when(page % 2 == core)
+        def _():
+            prefix_ref[i * PAGE:(i + 1) * PAGE, :] = mine_ref[rows, :]
+
+        @pl.when(page % 2 != core)
+        def _():
+            prefix_ref[i * PAGE:(i + 1) * PAGE, :] = kv_ref[rows, :]
+
+    fold(prefix_ref[:, :D], prefix_ref[:, D:], None, qt_ref, m_ref, l_ref, acc_ref)
+    window(kv_ref, 1 - core, own, ids_ref, qt_ref, m_ref, l_ref, acc_ref)
     result = (acc_ref[...] * (1.0 / l_ref[...])).astype(jnp.bfloat16)
     for g in range(GROUP):
         out_ref[:, g * D:(g + 1) * D] = result[:, g * ROWS:(g + 1) * ROWS].T
@@ -187,27 +177,34 @@
 def per_device(queries, branch_key_value, branch_ids, pool, page_table):
     me = lax.axis_index("seq")
     y = (me // 2) % NY
-    pages = pool.reshape(1, PAGE, PAIR)
-    pages = jnp.concatenate([pages, lax.ppermute(pages, "seq", y_ring(4))], axis=0)
-    pages = jnp.concatenate([pages] + [lax.ppermute(pages, "seq", y_ring(k)) for k in (1, 2, 3)], axis=0)
-    pages = pages.reshape(NY * PAGE, PAIR)
-    wide = jnp.concatenate([queries, branch_key_value], axis=2)
-    wide = lax.all_to_all(wide, "head", split_axis=1, concat_axis=0, tiled=True).reshape(ROWS, GROUP * D + PAIR)
-    own = wide[:, GROUP * D:]
-    near = jnp.concatenate([own, pages], axis=0)
+    z = lax.axis_index("head")
+    page = pool.reshape(PAGE, PAIR)
+    own = lax.all_to_all(
+        jnp.transpose(branch_key_value, (1, 0, 2)), "head", split_axis=0, concat_axis=0, tiled=True
+    ).reshape(ROWS, PAIR)
+    three_page = lax.ppermute(page, "seq", x_ring(3))
+    own, three_page = lax.optimization_barrier((own, three_page))
+    near = jnp.concatenate([own, page], axis=0)
     two_back = lax.ppermute(near, "seq", x_ring(2))
     one_back = lax.ppermute(near, "seq", x_ring(1))
     target = jnp.arange(NY, dtype=jnp.int32)[:, None, None]
     mixed = jnp.where(target > y, own[None], two_back[None, :ROWS])
-    send = jnp.stack([jnp.broadcast_to(one_back[None, :ROWS], mixed.shape), mixed], axis=1)
+    pages = jnp.concatenate([page, one_back[ROWS:], two_back[ROWS:], three_page], axis=0)
+    send = jnp.concatenate([
+        jnp.broadcast_to(one_back[None, :ROWS], mixed.shape), mixed,
+        jnp.broadcast_to(pages[None], (NY, NX * PAGE, PAIR)),
+    ], axis=1)
     kv = lax.all_to_all(send, "seq", split_axis=0, concat_axis=0, tiled=True, axis_index_groups=Y_GROUPS)
-    kv = kv.reshape(2 * NY * ROWS, PAIR)
-    far, _ = lax.optimization_barrier((two_back[ROWS:], send))
-    three_back = lax.ppermute(far, "seq", x_ring(1))
-    mine = jnp.concatenate([near, one_back[ROWS:], two_back[ROWS:], three_back], axis=0)
-    side = lax.ppermute(mine, "seq", SWAP)
+    kv = kv.reshape(NY * SLOT, PAIR)
+    by_head, later, _ = lax.optimization_barrier((jnp.transpose(queries, (1, 0, 2)), own, send))
+    side = lax.ppermute(later, "seq", SWAP)
+    parts = [lax.dynamic_index_in_dim(by_head, z, 0, keepdims=False)]
+    for k in range(1, 8):
+        part = lax.dynamic_index_in_dim(by_head, (z + k) % 8, 0, keepdims=False)
+        parts.append(lax.ppermute(part, "head", [(i, (i + k) % 8) for i in range(8)]))
+
     ids = branch_ids.reshape(2 * NX * NY, ROWS)
-    meta = me.astype(jnp.int32).reshape(1)
+    meta = jnp.stack([me, z]).astype(jnp.int32)
     state = [
         jax.ShapeDtypeStruct((1, QR), jnp.float32),
         jax.ShapeDtypeStruct((1, QR), jnp.float32),
@@ -217,13 +214,13 @@
     qt, m, l, acc = pl.pallas_call(
         near_kernel,
         out_shape=[jax.ShapeDtypeStruct((PAIR, QR), jnp.bfloat16)] + state,
-        in_specs=[SM, SM, VM, VM, VM, VM],
+        in_specs=[SM] + [VM] * 11,
         out_specs=[VM] * 4,
-        scratch_shapes=[pltpu.VMEM((PAGES * PAGE, PAIR), jnp.bfloat16)],
+        scratch_shapes=[pltpu.VMEM((ROWS, GROUP * D), jnp.bfloat16)],
         compiler_params=params,
-        cost_estimate=cost(768),
+        cost_estimate=cost(256),
         name="near_keys",
-    )(meta, page_table.reshape(PAGES), wide, mine, side, ids)
+    )(meta, own, side, ids, *parts)
     kv, m = lax.optimization_barrier((kv, m))
     kv_side = lax.ppermute(kv, "seq", SWAP)
     m, l, acc = pl.pallas_call(
@@ -238,17 +235,18 @@
     out = pl.pallas_call(
         last_kernel,
         out_shape=jax.ShapeDtypeStruct((ROWS, GROUP * D), jnp.bfloat16),
-        in_specs=[SM] + [VM] * 6,
+        in_specs=[SM, SM] + [VM] * 7,
         out_specs=VM,
         scratch_shapes=[
             pltpu.VMEM((1, QR), jnp.float32),
             pltpu.VMEM((1, QR), jnp.float32),
             pltpu.VMEM((D, QR), jnp.float32),
+            pltpu.VMEM((PAGES * PAGE, PAIR), jnp.bfloat16),
         ],
         compiler_params=params,
-        cost_estimate=cost(2048),
+        cost_estimate=cost(2560),
         name="other_parity",
-    )(meta, kv_side, ids, qt, m, l, acc)
+    )(meta, page_table.reshape(PAGES), kv, kv_side, ids, qt, m, l, acc)
     out = lax.all_to_all(out.reshape(8, ROWS // 8, GROUP * D), "head", split_axis=0, concat_axis=0, tiled=True)
     return jnp.transpose(out, (1, 0, 2))
 

time: 105 us -> 105 us (level)
  the two profiles are of different devices: /device:TPU:6 before, /device:TPU:15 now
where the time goes in v6:
time: 105 us; the launch traced here: 104 us
  starting transfers between devices  61 us (58%)
  blocking collectives  15.8 us (15%)
  Pallas kernels  12.7 us (12%)
  waiting for transfers between devices  8.97 us (9%)
  other arithmetic  2.77 us (3%)
  local copies, waits for them, and re-layouts  2.6 us (2%)
    ppermute x7, starting transfers between devices, per_device(): lax.ppermute(part, 'head', [(i, (i + k) % 8) for i in range(8)])  24.7 us
    all_to_all x1, blocking collectives, per_device(): lax.all_to_all(out.reshape(8, ROWS // 8, GROUP * D), 'head', split_axis=0...  15.8 us
    all_to_all x1, starting transfers between devices, per_device(): lax.all_to_all(jnp.transpose(branch_key_value, (1, 0, 2)), 'head', split_...  10 us
    all_to_all x1, starting transfers between devices, per_device(): lax.all_to_all(send, 'seq', split_axis=0, concat_axis=0, tiled=True, axis...  7.12 us
    ppermute x1, starting transfers between devices, per_device(): side = lax.ppermute(later, 'seq', SWAP)  6.54 us
    pallas_call x1, Pallas kernels, per_device(): pl.pallas_call(last_kernel, out_shape=jax.ShapeDtypeStruct((ROWS, GROUP *...  6.21 us
    pallas_call x1, Pallas kernels, per_device(): pl.pallas_call(own_kernel, out_shape=state, in_specs=[SM] + [VM] * 6, out...  4.74 us
    ppermute x1, starting transfers between devices, per_device(): one_back = lax.ppermute(near, 'seq', x_ring(1))  3.72 us
  transfers between devices with their start and end apart: 14, of which 4 were waited for; matrix products, arithmetic and copies ran while one was open for 0% of the time, Pallas kernels for 6%

profile of v6, /device:TPU:15, one launch (start us, length us, event | category | flops | bytes accessed | tf_op | source)
XLA Modules:
  0.0 104.2 jit_solution(15490840488774678683)
XLA Ops:
  0.0 1.5 %copy.17 = bf16[16,8,256]{2,0,1:T(8,128)(2,1)} copy(bf16[16,8,256]{2,1,0:T(8,128)(2,1)} %param.6) | data formatting | bytes 131072 | tf_op args[1]
  1.5 10.0 %all-to-all-start = ((bf16[8,16,256]{2,1,0:T(8,128)(2,1)}), bf16[8,16,256]{2,1,0:T(8,128)(2,1)S(1)}, u32[]{:S(2)}, u32[]{:S(2)}) async-start(bf16[8,16,256]{2,1,0:T(8,128)(2,1)} %bitcast.30), calls=%async_computation | async-start | bytes 131072 | tf_op jit(solution)/shard_map/all_to_all | solution.py:182
  11.5 2.4 %collective-permute-start = (bf16[16,256]{1,0:T(8,128)(2,1)}, bf16[16,256]{1,0:T(8,128)(2,1)S(1)}, u32[]{:S(2)}, u32[]{:S(2)}) collective-permute-start(bf16[16,256]{1,0:T(8,128)(2,1)} %bitcast.45), channel_id=1, source_target_pairs={{0,384},{8,392},{16,400},{24,408},{32,416},{40,424},{48,432},{56,4... | collective-permute-start | bytes 24584 | tf_op jit(solution)/shard_map/ppermute | solution.py:185
  14.0 3.6 %collective-permute-done = bf16[16,256]{1,0:T(8,128)(2,1)S(1)} collective-permute-done((bf16[16,256]{1,0:T(8,128)(2,1)}, bf16[16,256]{1,0:T(8,128)(2,1)S(1)}, u32[]{:S(2)}, u32[]{:S(2)}) %collective-permute-start) | collective-permute-done | bytes 8224 | tf_op jit(solution)/shard_map/ppermute | solution.py:185
  17.6 1.1 %all-to-all-done = bf16[8,16,256]{2,1,0:T(8,128)(2,1)S(1)} async-done(((bf16[8,16,256]{2,1,0:T(8,128)(2,1)}), bf16[8,16,256]{2,1,0:T(8,128)(2,1)S(1)}, u32[]{:S(2)}, u32[]{:S(2)}) %all-to-all-start) | async-done | bytes 65568 | tf_op jit(solution)/shard_map/all_to_all | solution.py:182
  18.8 0.7 pad_maximum_fusion.1
  19.5 3.0 %collective-permute-start.2 = (bf16[144,256]{1,0:T(8,128)(2,1)S(1)}, bf16[144,256]{1,0:T(8,128)(2,1)S(1)}, u32[]{:S(2)}, u32[]{:S(2)}) collective-permute-start(bf16[144,256]{1,0:T(8,128)(2,1)S(1)} %pad_maximum_fusion.1), channel_id=1, source_target_pairs={{0,256},{8,264},{16,272},{24,280},{32,288},{40,296},{48,304},{56,3... | collective-permute-start | bytes 221192 | tf_op jit(solution)/shard_map/ppermute | solution.py:188
  22.5 3.7 %collective-permute-start.1 = (bf16[144,256]{1,0:T(8,128)(2,1)S(1)}, bf16[144,256]{1,0:T(8,128)(2,1)S(1)}, u32[]{:S(2)}, u32[]{:S(2)}) collective-permute-start(bf16[144,256]{1,0:T(8,128)(2,1)S(1)} %pad_maximum_fusion.1), channel_id=1, source_target_pairs={{0,128},{8,136},{16,144},{24,152},{32,160},{40,168},{48,176},{56,1... | collective-permute-start | bytes 221192 | tf_op jit(solution)/shard_map/ppermute | solution.py:189
  26.3 0.1 broadcast_select_fusion
  26.4 1.5 %collective-permute-done.1 = bf16[144,256]{1,0:T(8,128)(2,1)S(1)} collective-permute-done((bf16[144,256]{1,0:T(8,128)(2,1)S(1)}, bf16[144,256]{1,0:T(8,128)(2,1)S(1)}, u32[]{:S(2)}, u32[]{:S(2)}) %collective-permute-start.1) | collective-permute-done | bytes 73760 | tf_op jit(solution)/shard_map/ppermute | solution.py:189
  27.9 0.7 pad_maximum_fusion.2
  28.7 1.2 %pad_maximum_fusion = bf16[8,320,256]{2,1,0:T(8,128)(2,1)} fusion(bf16[8,64,256]{2,1,0:T(8,128)(2,1)S(1)} %broadcast_in_dim.43, bf16[8,128,256]{2,1,0:T(8,128)(2,1)S(1)} %broadcast_select_fusion, bf16[8,128,256]{2,1,0:T(8,128)(2,1)S(1)} %broadcast_in_dim.28), kind=kLoop, calls=%fused_computation | loop fusion | flops 3932160 | bytes 2621440 | tf_op jit(solution)/shard_map/concatenate | solution.py:193
  29.8 7.1 %all-to-all-start.1 = ((bf16[8,320,256]{2,1,0:T(8,128)(2,1)}), bf16[8,320,256]{2,1,0:T(8,128)(2,1)S(1)}, u32[]{:S(2)}, u32[]{:S(2)}) async-start(bf16[8,320,256]{2,1,0:T(8,128)(2,1)} %pad_maximum_fusion), calls=%async_computation.1 | async-start | bytes 2621440 | tf_op jit(solution)/shard_map/all_to_all | solution.py:197
  37.0 0.1 copy.16
  37.2 2.0 %collective-permute-start.10 = (bf16[16,1024]{1,0:T(8,128)(2,1)S(1)}, bf16[16,1024]{1,0:T(8,128)(2,1)S(1)}, u32[]{:S(2)}, u32[]{:S(2)}) collective-permute-start(bf16[16,1024]{1,0:T(8,128)(2,1)S(1)} %get-tuple-element.31), channel_id=1, source_target_pairs={{0,7},{1,0},{2,1},{3,2},{4,3},{5,4},{6,5},{7,6},{8,15},{9,8},{10,9... | collective-permute-start | bytes 98312 | tf_op jit(solution)/shard_map/ppermute | solution.py:204
  39.3 4.0 %collective-permute-start.9 = (bf16[16,1024]{1,0:T(8,128)(2,1)S(1)}, bf16[16,1024]{1,0:T(8,128)(2,1)S(1)}, u32[]{:S(2)}, u32[]{:S(2)}) collective-permute-start(bf16[16,1024]{1,0:T(8,128)(2,1)S(1)} %get-tuple-element.32), channel_id=1, source_target_pairs={{0,6},{1,7},{2,0},{3,1},{4,2},{5,3},{6,4},{7,5},{8,14},{9,15},{10,... | collective-permute-start | bytes 98312 | tf_op jit(solution)/shard_map/ppermute | solution.py:204
  43.2 3.5 %collective-permute-start.8 = (bf16[16,1024]{1,0:T(8,128)(2,1)S(1)}, bf16[16,1024]{1,0:T(8,128)(2,1)S(1)}, u32[]{:S(2)}, u32[]{:S(2)}) collective-permute-start(bf16[16,1024]{1,0:T(8,128)(2,1)S(1)} %get-tuple-element.33), channel_id=1, source_target_pairs={{0,5},{1,6},{2,7},{3,0},{4,1},{5,2},{6,3},{7,4},{8,13},{9,14},{10,... | collective-permute-start | bytes 98312 | tf_op jit(solution)/shard_map/ppermute | solution.py:204
  46.7 6.5 %collective-permute-start.3 = (bf16[128,256]{1,0:T(8,128)(2,1)S(1)}, bf16[128,256]{1,0:T(8,128)(2,1)S(1)}, u32[]{:S(2)}, u32[]{:S(2)}) collective-permute-start(bf16[128,256]{1,0:T(8,128)(2,1)S(1)} %bitcast.36), channel_id=1, source_target_pairs={{0,8},{8,0},{16,24},{24,16},{32,40},{40,32},{48,56},{56,48},{64,72... | collective-permute-start | bytes 196616 | tf_op jit(solution)/shard_map/ppermute | solution.py:200
  53.3 5.0 %collective-permute-start.7 = (bf16[16,1024]{1,0:T(8,128)(2,1)S(1)}, bf16[16,1024]{1,0:T(8,128)(2,1)S(1)}, u32[]{:S(2)}, u32[]{:S(2)}) collective-permute-start(bf16[16,1024]{1,0:T(8,128)(2,1)S(1)} %get-tuple-element.34), channel_id=1, source_target_pairs={{0,4},{1,5},{2,6},{3,7},{4,0},{5,1},{6,2},{7,3},{8,12},{9,13},{10,... | collective-permute-start | bytes 98312 | tf_op jit(solution)/shard_map/ppermute | solution.py:204
  58.3 0.0 collective-permute-done.10.refs_7_
  58.3 3.0 %collective-permute-start.6 = (bf16[16,1024]{1,0:T(8,128)(2,1)S(1)}, bf16[16,1024]{1,0:T(8,128)(2,1)S(1)}, u32[]{:S(2)}, u32[]{:S(2)}) collective-permute-start(bf16[16,1024]{1,0:T(8,128)(2,1)S(1)} %get-tuple-element.35), channel_id=1, source_target_pairs={{0,3},{1,4},{2,5},{3,6},{4,7},{5,0},{6,1},{7,2},{8,11},{9,12},{10,... | collective-permute-start | bytes 98312 | tf_op jit(solution)/shard_map/ppermute | solution.py:204
  61.4 4.0 %collective-permute-start.5 = (bf16[16,1024]{1,0:T(8,128)(2,1)S(1)}, bf16[16,1024]{1,0:T(8,128)(2,1)S(1)}, u32[]{:S(2)}, u32[]{:S(2)}) collective-permute-start(bf16[16,1024]{1,0:T(8,128)(2,1)S(1)} %get-tuple-element.36), channel_id=1, source_target_pairs={{0,2},{1,3},{2,4},{3,5},{4,6},{5,7},{6,0},{7,1},{8,10},{9,11},{10,... | collective-permute-start | bytes 98312 | tf_op jit(solution)/shard_map/ppermute | solution.py:204
  65.4 3.1 %collective-permute-start.4 = (bf16[16,1024]{1,0:T(8,128)(2,1)S(1)}, bf16[16,1024]{1,0:T(8,128)(2,1)S(1)}, u32[]{:S(2)}, u32[]{:S(2)}) collective-permute-start(bf16[16,1024]{1,0:T(8,128)(2,1)S(1)} %get-tuple-element.37), channel_id=1, source_target_pairs={{0,1},{1,2},{2,3},{3,4},{4,5},{5,6},{6,7},{7,0},{8,9},{9,10},{10,1... | collective-permute-start | bytes 98312 | tf_op jit(solution)/shard_map/ppermute | solution.py:204
  68.5 0.1 pad_add_fusion.meta_ref
  68.6 2.7 %collective-permute-done.4.refs_1_ = bf16[16,1024]{1,0:T(8,128)(2,1)S(1)} collective-permute-done((bf16[16,1024]{1,0:T(8,128)(2,1)S(1)}, bf16[16,1024]{1,0:T(8,128)(2,1)S(1)}, u32[]{:S(2)}, u32[]{:S(2)}) %collective-permute-start.4) | collective-permute-done | bytes 32800 | tf_op jit(solution)/shard_map/ppermute | solution.py:204
  71.3 1.7 %near_keys.1 = (bf16[256,1024]{1,0:T(8,128)(2,1)S(1)}, f32[1,1024]{1,0:T(1,128)S(1)}, f32[1,1024]{1,0:T(1,128)S(1)}, f32[128,1024]{1,0:T(8,128)S(1)}) custom-call(s32[2]{0:T(128)S(1)} %pad_add_fusion.meta_ref, bf16[128,256]{1,0:T(8,128)(2,1)S(1)} %bitcast.37, bf16[128,256]{1,0:T(8,128)(2,1)S(1)} %collective-permute-done.3.side_ref, s32[64,128]{1,0:T(8,128)S(1)} %bitcast.39, ...), custom_call_target="tpu_custom_call" | custom-call | flops 134217728 | bytes 1048576 | tf_op jit(solution)/shard_map/near_keys/pallas_call | solution.py:214
  73.0 3.4 %collective-permute-start.11 = (bf16[2560,256]{1,0:T(8,128)(2,1)S(1)}, bf16[2560,256]{1,0:T(8,128)(2,1)S(1)}, u32[]{:S(2)}, u32[]{:S(2)}) collective-permute-start(bf16[2560,256]{1,0:T(8,128)(2,1)S(1)} %bitcast.31), channel_id=1, source_target_pairs={{0,8},{8,0},{16,24},{24,16},{32,40},{40,32},{48,56},{56,48},{64,72... | collective-permute-start | bytes 3932168 | tf_op jit(solution)/shard_map/ppermute | solution.py:225
  76.5 0.0 copy-start.1
  76.5 4.7 %own_parity.1 = (f32[1,1024]{1,0:T(1,128)S(1)}, f32[1,1024]{1,0:T(1,128)S(1)}, f32[128,1024]{1,0:T(8,128)S(1)}) custom-call(s32[2]{0:T(128)S(1)} %pad_add_fusion.meta_ref, bf16[2560,256]{1,0:T(8,128)(2,1)S(1)} %bitcast.32, s32[64,128]{1,0:T(8,128)S(1)} %bitcast.40, bf16[256,1024]{1,0:T(8,128)(2,1)S(1)} %get-tuple-element.24.qt_ref, ...), custom_call_target="tpu_custom_call" | custom-call | flops 1073741824 | bytes 1048576 | tf_op jit(solution)/shard_map/own_parity/pallas_call | solution.py:226
  81.3 6.2 %other_parity.1 = bf16[128,1024]{1,0:T(8,128)(2,1)S(1)} custom-call(s32[2]{0:T(128)S(1)} %pad_add_fusion.meta_ref, s32[32]{0:T(128)S(1)} %bitcast.42, bf16[2560,256]{1,0:T(8,128)(2,1)S(1)} %bitcast.33, bf16[2560,256]{1,0:T(8,128)(2,1)S(1)} %collective-permute-done.11.kv_ref, s32[64,128]{1,0:T(8,128)S(1)} %bitcast.41, ...), custom_call_target="tpu_custom_call" | custom-call | flops 1342177280 | bytes 1048576 | tf_op jit(solution)/shard_map/other_parity/pallas_call | solution.py:235
  87.5 15.8 %all_to_all.15 = bf16[8,16,1024]{2,1,0:T(8,128)(2,1)S(1)} all-to-all(bf16[8,16,1024]{2,1,0:T(8,128)(2,1)S(1)} %bitcast.38), channel_id=1, replica_groups=mesh['seq'=64,'head'=8] {'head'}, dimensions={0} | all-to-all | bytes 524288 | tf_op jit(solution)/shard_map/all_to_all | solution.py:250
  103.3 0.9 copy.13
  (22 shorter events, 0.1 us)
Async XLA Ops:
  1.5 17.3 %all-to-all-start = ((bf16[8,16,256]{2,1,0:T(8,128)(2,1)}), bf16[8,16,256]{2,1,0:T(8,128)(2,1)S(1)}, u32[]{:S(2)}, u32[]{:S(2)}) async-start(bf16[8,16,256]{2,1,0:T(8,128)(2,1)} %bitcast.30), calls=%async_computation | async-start | bytes 131072 | tf_op jit(solution)/shard_map/all_to_all | solution.py:182
  11.5 6.1 %collective-permute-start = (bf16[16,256]{1,0:T(8,128)(2,1)}, bf16[16,256]{1,0:T(8,128)(2,1)S(1)}, u32[]{:S(2)}, u32[]{:S(2)}) collective-permute-start(bf16[16,256]{1,0:T(8,128)(2,1)} %bitcast.45), channel_id=1, source_target_pairs={{0,384},{8,392},{16,400},{24,408},{32,416},{40,424},{48,432},{56,4... | collective-permute-start | bytes 24584 | tf_op jit(solution)/shard_map/ppermute | solution.py:185
  19.5 6.8 %collective-permute-start.2 = (bf16[144,256]{1,0:T(8,128)(2,1)S(1)}, bf16[144,256]{1,0:T(8,128)(2,1)S(1)}, u32[]{:S(2)}, u32[]{:S(2)}) collective-permute-start(bf16[144,256]{1,0:T(8,128)(2,1)S(1)} %pad_maximum_fusion.1), channel_id=1, source_target_pairs={{0,256},{8,264},{16,272},{24,280},{32,288},{40,296},{48,304},{56,3... | collective-permute-start | bytes 221192 | tf_op jit(solution)/shard_map/ppermute | solution.py:188
  22.5 5.4 %collective-permute-start.1 = (bf16[144,256]{1,0:T(8,128)(2,1)S(1)}, bf16[144,256]{1,0:T(8,128)(2,1)S(1)}, u32[]{:S(2)}, u32[]{:S(2)}) collective-permute-start(bf16[144,256]{1,0:T(8,128)(2,1)S(1)} %pad_maximum_fusion.1), channel_id=1, source_target_pairs={{0,128},{8,136},{16,144},{24,152},{32,160},{40,168},{48,176},{56,1... | collective-permute-start | bytes 221192 | tf_op jit(solution)/shard_map/ppermute | solution.py:189
  29.8 7.1 %copy-start.2 = (bf16[16,8,1024]{2,1,0:T(8,128)(2,1)S(1)}, bf16[16,8,1024]{2,1,0:T(8,128)(2,1)}, u32[]{:S(2)}) copy-start(bf16[16,8,1024]{2,1,0:T(8,128)(2,1)} %param.5) | copy-start | bytes 786436
  29.8 41.4 %copy-start = (s32[8192]{0:T(1024)S(1)}, s32[8192]{0:T(1024)}, u32[]{:S(2)}) copy-start(s32[8192]{0:T(1024)} %param.7) | copy-start | bytes 98308
  29.8 43.2 %all-to-all-start.1 = ((bf16[8,320,256]{2,1,0:T(8,128)(2,1)}), bf16[8,320,256]{2,1,0:T(8,128)(2,1)S(1)}, u32[]{:S(2)}, u32[]{:S(2)}) async-start(bf16[8,320,256]{2,1,0:T(8,128)(2,1)} %pad_maximum_fusion), calls=%async_computation.1 | async-start | bytes 2621440 | tf_op jit(solution)/shard_map/all_to_all | solution.py:197
  37.2 21.1 %collective-permute-start.10 = (bf16[16,1024]{1,0:T(8,128)(2,1)S(1)}, bf16[16,1024]{1,0:T(8,128)(2,1)S(1)}, u32[]{:S(2)}, u32[]{:S(2)}) collective-permute-start(bf16[16,1024]{1,0:T(8,128)(2,1)S(1)} %get-tuple-element.31), channel_id=1, source_target_pairs={{0,7},{1,0},{2,1},{3,2},{4,3},{5,4},{6,5},{7,6},{8,15},{9,8},{10,9... | collective-permute-start | bytes 98312 | tf_op jit(solution)/shard_map/ppermute | solution.py:204
  39.3 22.1 %collective-permute-start.9 = (bf16[16,1024]{1,0:T(8,128)(2,1)S(1)}, bf16[16,1024]{1,0:T(8,128)(2,1)S(1)}, u32[]{:S(2)}, u32[]{:S(2)}) collective-permute-start(bf16[16,1024]{1,0:T(8,128)(2,1)S(1)} %get-tuple-element.32), channel_id=1, source_target_pairs={{0,6},{1,7},{2,0},{3,1},{4,2},{5,3},{6,4},{7,5},{8,14},{9,15},{10,... | collective-permute-start | bytes 98312 | tf_op jit(solution)/shard_map/ppermute | solution.py:204
  43.2 22.2 %collective-permute-start.8 = (bf16[16,1024]{1,0:T(8,128)(2,1)S(1)}, bf16[16,1024]{1,0:T(8,128)(2,1)S(1)}, u32[]{:S(2)}, u32[]{:S(2)}) collective-permute-start(bf16[16,1024]{1,0:T(8,128)(2,1)S(1)} %get-tuple-element.33), channel_id=1, source_target_pairs={{0,5},{1,6},{2,7},{3,0},{4,1},{5,2},{6,3},{7,4},{8,13},{9,14},{10,... | collective-permute-start | bytes 98312 | tf_op jit(solution)/shard_map/ppermute | solution.py:204
  46.7 24.6 %collective-permute-start.3 = (bf16[128,256]{1,0:T(8,128)(2,1)S(1)}, bf16[128,256]{1,0:T(8,128)(2,1)S(1)}, u32[]{:S(2)}, u32[]{:S(2)}) collective-permute-start(bf16[128,256]{1,0:T(8,128)(2,1)S(1)} %bitcast.36), channel_id=1, source_target_pairs={{0,8},{8,0},{16,24},{24,16},{32,40},{40,32},{48,56},{56,48},{64,72... | collective-permute-start | bytes 196616 | tf_op jit(solution)/shard_map/ppermute | solution.py:200
  53.3 15.3 %collective-permute-start.7 = (bf16[16,1024]{1,0:T(8,128)(2,1)S(1)}, bf16[16,1024]{1,0:T(8,128)(2,1)S(1)}, u32[]{:S(2)}, u32[]{:S(2)}) collective-permute-start(bf16[16,1024]{1,0:T(8,128)(2,1)S(1)} %get-tuple-element.34), channel_id=1, source_target_pairs={{0,4},{1,5},{2,6},{3,7},{4,0},{5,1},{6,2},{7,3},{8,12},{9,13},{10,... | collective-permute-start | bytes 98312 | tf_op jit(solution)/shard_map/ppermute | solution.py:204
  58.3 10.3 %collective-permute-start.6 = (bf16[16,1024]{1,0:T(8,128)(2,1)S(1)}, bf16[16,1024]{1,0:T(8,128)(2,1)S(1)}, u32[]{:S(2)}, u32[]{:S(2)}) collective-permute-start(bf16[16,1024]{1,0:T(8,128)(2,1)S(1)} %get-tuple-element.35), channel_id=1, source_target_pairs={{0,3},{1,4},{2,5},{3,6},{4,7},{5,0},{6,1},{7,2},{8,11},{9,12},{10,... | collective-permute-start | bytes 98312 | tf_op jit(solution)/shard_map/ppermute | solution.py:204
  61.4 7.2 %collective-permute-start.5 = (bf16[16,1024]{1,0:T(8,128)(2,1)S(1)}, bf16[16,1024]{1,0:T(8,128)(2,1)S(1)}, u32[]{:S(2)}, u32[]{:S(2)}) collective-permute-start(bf16[16,1024]{1,0:T(8,128)(2,1)S(1)} %get-tuple-element.36), channel_id=1, source_target_pairs={{0,2},{1,3},{2,4},{3,5},{4,6},{5,7},{6,0},{7,1},{8,10},{9,11},{10,... | collective-permute-start | bytes 98312 | tf_op jit(solution)/shard_map/ppermute | solution.py:204
  65.4 5.9 %collective-permute-start.4 = (bf16[16,1024]{1,0:T(8,128)(2,1)S(1)}, bf16[16,1024]{1,0:T(8,128)(2,1)S(1)}, u32[]{:S(2)}, u32[]{:S(2)}) collective-permute-start(bf16[16,1024]{1,0:T(8,128)(2,1)S(1)} %get-tuple-element.37), channel_id=1, source_target_pairs={{0,1},{1,2},{2,3},{3,4},{4,5},{5,6},{6,7},{7,0},{8,9},{9,10},{10,1... | collective-permute-start | bytes 98312 | tf_op jit(solution)/shard_map/ppermute | solution.py:204
  73.0 8.2 %collective-permute-start.11 = (bf16[2560,256]{1,0:T(8,128)(2,1)S(1)}, bf16[2560,256]{1,0:T(8,128)(2,1)S(1)}, u32[]{:S(2)}, u32[]{:S(2)}) collective-permute-start(bf16[2560,256]{1,0:T(8,128)(2,1)S(1)} %bitcast.31), channel_id=1, source_target_pairs={{0,8},{8,0},{16,24},{24,16},{32,40},{40,32},{48,56},{56,48},{64,72... | collective-permute-start | bytes 3932168 | tf_op jit(solution)/shard_map/ppermute | solution.py:225
  76.5 4.8 %copy-start.1 = (s32[1,32]{1,0:T(1,128)S(1)}, s32[1,32]{1,0:T(1,128)}, u32[]{:S(2)}) copy-start(s32[1,32]{1,0:T(1,128)} %param.9) | copy-start | bytes 388

commit v7 on v6

--- a/solution.py
+++ b/solution.py
@@ -73,13 +73,9 @@
     return (key_rows >= row_start) & (key_rows <= query_rows)
 
 
-def near_kernel(meta_ref, mine_ref, side_ref, ids_ref, *refs):
-    q_refs, (qt_ref, m_ref, l_ref, acc_ref, q_ref) = refs[:8], refs[8:]
-    own, z = meta_ref[0], meta_ref[1]
+def near_kernel(meta_ref, mine_ref, side_ref, ids_ref, q_ref, qt_ref, m_ref, l_ref, acc_ref):
+    own = meta_ref[0]
     row_start, first, last = starts_of(ids_ref, own)
-    for k in range(8):
-        source = (z + 8 - k) % 8
-        q_ref[pl.ds(pl.multiple_of(source * 16, 16), 16), :] = q_refs[k][...]
     for g in range(GROUP):
         scaled = q_ref[:, g * D:(g + 1) * D].astype(jnp.float32) * SCALE2
         high = scaled.astype(jnp.bfloat16)
@@ -178,33 +174,30 @@
     me = lax.axis_index("seq")
     y = (me // 2) % NY
     z = lax.axis_index("head")
-    page = pool.reshape(PAGE, PAIR)
-    own = lax.all_to_all(
-        jnp.transpose(branch_key_value, (1, 0, 2)), "head", split_axis=0, concat_axis=0, tiled=True
-    ).reshape(ROWS, PAIR)
+    gathered = lax.all_gather(jnp.transpose(queries, (1, 0, 2)), "head", axis=0, tiled=False)
+    query = lax.dynamic_index_in_dim(gathered, z, 1, keepdims=False).reshape(ROWS, GROUP * D)
+    page = pool.reshape(1, PAGE, PAIR)
+    raw = jnp.concatenate([jnp.transpose(branch_key_value, (1, 0, 2)), page], axis=0)
+    two_raw = lax.ppermute(raw, "seq", x_ring(2))
+    one_raw = lax.ppermute(raw, "seq", x_ring(1))
     three_page = lax.ppermute(page, "seq", x_ring(3))
-    own, three_page = lax.optimization_barrier((own, three_page))
-    near = jnp.concatenate([own, page], axis=0)
-    two_back = lax.ppermute(near, "seq", x_ring(2))
-    one_back = lax.ppermute(near, "seq", x_ring(1))
+    pages = jnp.concatenate([page, one_raw[8:], two_raw[8:], three_page], axis=0).reshape(NX * PAGE, PAIR)
+    wide = jnp.concatenate([raw[:8], one_raw[:8], two_raw[:8]], axis=2)
+    wide = lax.all_to_all(wide, "head", split_axis=0, concat_axis=0, tiled=True).reshape(ROWS, 3 * PAIR)
+    own, one_back, two_back = (wide[:, i * PAIR:(i + 1) * PAIR] for i in range(3))
     target = jnp.arange(NY, dtype=jnp.int32)[:, None, None]
-    mixed = jnp.where(target > y, own[None], two_back[None, :ROWS])
-    pages = jnp.concatenate([page, one_back[ROWS:], two_back[ROWS:], three_page], axis=0)
+    mixed = jnp.where(target > y, own[None], two_back[None])
     send = jnp.concatenate([
-        jnp.broadcast_to(one_back[None, :ROWS], mixed.shape), mixed,
+        jnp.broadcast_to(one_back[None], mixed.shape), mixed,
         jnp.broadcast_to(pages[None], (NY, NX * PAGE, PAIR)),
     ], axis=1)
     kv = lax.all_to_all(send, "seq", split_axis=0, concat_axis=0, tiled=True, axis_index_groups=Y_GROUPS)
     kv = kv.reshape(NY * SLOT, PAIR)
-    by_head, later, _ = lax.optimization_barrier((jnp.transpose(queries, (1, 0, 2)), own, send))
+    later, _ = lax.optimization_barrier((own, send))
     side = lax.ppermute(later, "seq", SWAP)
-    parts = [lax.dynamic_index_in_dim(by_head, z, 0, keepdims=False)]
-    for k in range(1, 8):
-        part = lax.dynamic_index_in_dim(by_head, (z + k) % 8, 0, keepdims=False)
-        parts.append(lax.ppermute(part, "head", [(i, (i + k) % 8) for i in range(8)]))
 
     ids = branch_ids.reshape(2 * NX * NY, ROWS)
-    meta = jnp.stack([me, z]).astype(jnp.int32)
+    meta = me.astype(jnp.int32).reshape(1)
     state = [
         jax.ShapeDtypeStruct((1, QR), jnp.float32),
         jax.ShapeDtypeStruct((1, QR), jnp.float32),
@@ -214,13 +207,12 @@
     qt, m, l, acc = pl.pallas_call(
         near_kernel,
         out_shape=[jax.ShapeDtypeStruct((PAIR, QR), jnp.bfloat16)] + state,
-        in_specs=[SM] + [VM] * 11,
+        in_specs=[SM] + [VM] * 4,
         out_specs=[VM] * 4,
-        scratch_shapes=[pltpu.VMEM((ROWS, GROUP * D), jnp.bfloat16)],
         compiler_params=params,
         cost_estimate=cost(256),
         name="near_keys",
-    )(meta, own, side, ids, *parts)
+    )(meta, own, side, ids, query)
     kv, m = lax.optimization_barrier((kv, m))
     kv_side = lax.ppermute(kv, "seq", SWAP)
     m, l, acc = pl.pallas_call(

time: 105 us -> 117 us (1.11)
  the two profiles are of different devices: /device:TPU:15 before, /device:TPU:1 now
where the time goes in v7:
time: 117 us; the launch traced here: 116 us
  waiting for transfers between devices  39.7 us (34%)
  starting transfers between devices  36.5 us (31%)
  blocking collectives  14.8 us (13%)
  between operations  13.6 us (12%)
  local copies, waits for them, and re-layouts  4.29 us (4%)
  Pallas kernels  3.92 us (3%)
  other arithmetic  3.37 us (3%)
    all_to_all x1, waiting for transfers between devices, per_device(): lax.all_to_all(send, 'seq', split_axis=0, concat_axis=0, tiled=True, axis...  21.4 us
    all_to_all x1, blocking collectives, per_device(): lax.all_to_all(out.reshape(8, ROWS // 8, GROUP * D), 'head', split_axis=0...  14.8 us
    all_to_all x1, starting transfers between devices, per_device(): lax.all_to_all(wide, 'head', split_axis=0, concat_axis=0, tiled=True)  10 us
    all_to_all x1, starting transfers between devices, per_device(): lax.all_to_all(send, 'seq', split_axis=0, concat_axis=0, tiled=True, axis...  7.03 us
    all_to_all x1, waiting for transfers between devices, per_device(): lax.all_to_all(wide, 'head', split_axis=0, concat_axis=0, tiled=True)  6.02 us
    ppermute x1, starting transfers between devices, per_device(): two_raw = lax.ppermute(raw, 'seq', x_ring(2))  5.48 us
    ppermute x1, starting transfers between devices, per_device(): side = lax.ppermute(later, 'seq', SWAP)  5.24 us
    ppermute x1, starting transfers between devices, per_device(): kv_side = lax.ppermute(kv, 'seq', SWAP)  4.63 us
  transfers between devices with their start and end apart: 8, of which 6 were waited for; matrix products, arithmetic and copies ran while one was open for 6% of the time, Pallas kernels for 1%

profile of v7, /device:TPU:1, one launch (start us, length us, event | category | flops | bytes accessed | tf_op | source)
XLA Modules:
  0.0 116.2 jit_solution(3637205810151797624)
XLA Ops:
  6.5 0.0 all-gather.3.cloned.1.call-start
  6.5 0.7 all-gather.3.cloned.1.call-update
  7.3 0.9 copy.14
  8.1 0.7 pad_maximum_fusion.2
  8.8 5.5 %collective-permute-start.1 = (bf16[9,16,256]{2,1,0:T(8,128)(2,1)S(1)}, bf16[9,16,256]{2,1,0:T(8,128)(2,1)S(1)}, u32[]{:S(2)}, u32[]{:S(2)}) collective-permute-start(bf16[9,16,256]{2,1,0:T(8,128)(2,1)S(1)} %pad_maximum_fusion.2), channel_id=1, source_target_pairs={{0,256},{8,264},{16,272},{24,280},{32,288},{40,296},{48,304},{56,3... | collective-permute-start | bytes 221192 | tf_op jit(solution)/shard_map/ppermute | solution.py:181
  14.3 2.2 %collective-permute-start = (bf16[9,16,256]{2,1,0:T(8,128)(2,1)S(1)}, bf16[9,16,256]{2,1,0:T(8,128)(2,1)S(1)}, u32[]{:S(2)}, u32[]{:S(2)}) collective-permute-start(bf16[9,16,256]{2,1,0:T(8,128)(2,1)S(1)} %pad_maximum_fusion.2), channel_id=1, source_target_pairs={{0,128},{8,136},{16,144},{24,152},{32,160},{40,168},{48,176},{56,1... | collective-permute-start | bytes 221192 | tf_op jit(solution)/shard_map/ppermute | solution.py:182
  16.5 0.0 collective-permute-done.1
  16.6 4.1 %collective-permute-done = bf16[9,16,256]{2,1,0:T(8,128)(2,1)S(1)} collective-permute-done((bf16[9,16,256]{2,1,0:T(8,128)(2,1)S(1)}, bf16[9,16,256]{2,1,0:T(8,128)(2,1)S(1)}, u32[]{:S(2)}, u32[]{:S(2)}) %collective-permute-start) | collective-permute-done | bytes 73760 | tf_op jit(solution)/shard_map/ppermute | solution.py:182
  20.6 0.7 pad_maximum_fusion.1
  21.3 10.0 %all-to-all-start = ((bf16[8,16,768]{2,1,0:T(8,128)(2,1)}), bf16[8,16,768]{2,1,0:T(8,128)(2,1)S(1)}, u32[]{:S(2)}, u32[]{:S(2)}) async-start(bf16[8,16,768]{2,1,0:T(8,128)(2,1)} %pad_maximum_fusion.1), calls=%async_computation | async-start | bytes 393216 | tf_op jit(solution)/shard_map/all_to_all | solution.py:186
  31.3 1.9 %collective-permute-start.2 = (bf16[1,16,256]{2,1,0:T(8,128)(2,1)}, bf16[1,16,256]{2,1,0:T(8,128)(2,1)S(1)}, u32[]{:S(2)}, u32[]{:S(2)}) collective-permute-start(bf16[1,16,256]{2,1,0:T(8,128)(2,1)} %bitcast.32), channel_id=1, source_target_pairs={{0,384},{8,392},{16,400},{24,408},{32,416},{40,424},{48,432},{56,4... | collective-permute-start | bytes 24584 | tf_op jit(solution)/shard_map/ppermute | solution.py:183
  33.3 3.0 %collective-permute-done.2 = bf16[1,16,256]{2,1,0:T(8,128)(2,1)S(1)} collective-permute-done((bf16[1,16,256]{2,1,0:T(8,128)(2,1)}, bf16[1,16,256]{2,1,0:T(8,128)(2,1)S(1)}, u32[]{:S(2)}, u32[]{:S(2)}) %collective-permute-start.2) | collective-permute-done | bytes 8224 | tf_op jit(solution)/shard_map/ppermute | solution.py:183
  36.3 0.7 pad_maximum_fusion.3
  37.0 6.0 %all-to-all-done = bf16[8,16,768]{2,1,0:T(8,128)(2,1)S(1)} async-done(((bf16[8,16,768]{2,1,0:T(8,128)(2,1)}), bf16[8,16,768]{2,1,0:T(8,128)(2,1)S(1)}, u32[]{:S(2)}, u32[]{:S(2)}) %all-to-all-start) | async-done | bytes 196640 | tf_op jit(solution)/shard_map/all_to_all | solution.py:186
  43.1 0.1 broadcast_select_fusion
  43.3 1.2 pad_maximum_fusion
  44.4 7.0 %all-to-all-start.1 = ((bf16[8,320,256]{2,1,0:T(8,128)(2,1)}), bf16[8,320,256]{2,1,0:T(8,128)(2,1)S(1)}, u32[]{:S(2)}, u32[]{:S(2)}) async-start(bf16[8,320,256]{2,1,0:T(8,128)(2,1)} %pad_maximum_fusion), calls=%async_computation.1 | async-start | bytes 2621440 | tf_op jit(solution)/shard_map/all_to_all | solution.py:194
  51.5 5.2 %collective-permute-start.3 = (bf16[128,256]{1,0:T(8,128)(2,1)S(1)}, bf16[128,256]{1,0:T(8,128)(2,1)S(1)}, u32[]{:S(2)}, u32[]{:S(2)}) collective-permute-start(bf16[128,256]{1,0:T(8,128)(2,1)S(1)} %get-tuple-element.15.mine_ref), channel_id=1, source_target_pairs={{0,8},{8,0},{16,24},{24,16},{32,40},{40,32},{48,56},{56,48},{64,72... | collective-permute-start | bytes 196616 | tf_op jit(solution)/shard_map/ppermute | solution.py:197
  56.7 2.2 %all-gather.3.cloned.1.call-done = bf16[64,16,1024]{2,0,1:T(8,128)(2,1)} async-done(((bf16[8,16,1024]{2,0,1:T(8,128)(2,1)}), bf16[64,16,1024]{2,0,1:T(8,128)(2,1)}) %all-gather.3.cloned.1.call-update) | async-done | bytes 2097168 | tf_op jit(solution)/shard_map/all_gather | solution.py:177
  58.9 2.2 %constant_dynamic-slice_fusion = bf16[8,1,16,1024]{3,1,0,2:T(2,128)(2,1)S(1)} fusion(bf16[8,8,16,1024]{3,1,0,2:T(8,128)(2,1)} %bitcast.30, s32[]{:T(128)S(6)} %select_n.22), kind=kLoop, calls=%fused_computation.7 | loop fusion | bytes 524292 | tf_op jit(solution)/shard_map/jit(dynamic_index_in_dim)/dynamic_slice | solution.py:178
  61.1 0.3 copy.12
  61.4 0.0 collective-permute-done.3.side_ref
  61.4 0.0 copy-done
  61.4 1.1 near_keys.1
  62.6 0.0 copy-start.1
  62.6 21.4 %all-to-all-done.1 = bf16[8,320,256]{2,1,0:T(8,128)(2,1)S(1)} async-done(((bf16[8,320,256]{2,1,0:T(8,128)(2,1)}), bf16[8,320,256]{2,1,0:T(8,128)(2,1)S(1)}, u32[]{:S(2)}, u32[]{:S(2)}) %all-to-all-start.1) | async-done | bytes 1310752 | tf_op jit(solution)/shard_map/all_to_all | solution.py:194
  84.0 4.6 %collective-permute-start.4 = (bf16[2560,256]{1,0:T(8,128)(2,1)S(1)}, bf16[2560,256]{1,0:T(8,128)(2,1)S(1)}, u32[]{:S(2)}, u32[]{:S(2)}) collective-permute-start(bf16[2560,256]{1,0:T(8,128)(2,1)S(1)} %bitcast.15), channel_id=1, source_target_pairs={{0,8},{8,0},{16,24},{24,16},{32,40},{40,32},{48,56},{56,48},{64,72... | collective-permute-start | bytes 3932168 | tf_op jit(solution)/shard_map/ppermute | solution.py:217
  88.7 0.4 own_parity.1
  89.0 2.3 %collective-permute-done.4.kv_ref = bf16[2560,256]{1,0:T(8,128)(2,1)S(1)} collective-permute-done((bf16[2560,256]{1,0:T(8,128)(2,1)S(1)}, bf16[2560,256]{1,0:T(8,128)(2,1)S(1)}, u32[]{:S(2)}, u32[]{:S(2)}) %collective-permute-start.4) | collective-permute-done | bytes 1310752 | tf_op jit(solution)/shard_map/ppermute | solution.py:217
  91.3 2.4 %other_parity.1 = bf16[128,1024]{1,0:T(8,128)(2,1)S(1)} custom-call(s32[1]{0:T(128)} %bitcast.meta_ref, s32[32]{0:T(128)S(1)} %bitcast.23, bf16[2560,256]{1,0:T(8,128)(2,1)S(1)} %bitcast.17, bf16[2560,256]{1,0:T(8,128)(2,1)S(1)} %collective-permute-done.4.kv_ref, s32[64,128]{1,0:T(8,128)S(1)} %bitcast.22, bf16[256,1024]{1,0:T(8,128)(2,1)S(1)} %get-tuple-element.18.qt_ref, ...), custom_call_target="tpu_custom_call" | custom-call | flops 1342177280 | bytes 1048576 | tf_op jit(solution)/shard_map/other_parity/pallas_call | solution.py:227
  93.7 14.8 %all_to_all.15 = bf16[8,16,1024]{2,1,0:T(8,128)(2,1)S(1)} all-to-all(bf16[8,16,1024]{2,1,0:T(8,128)(2,1)S(1)} %bitcast.19), channel_id=1, replica_groups=mesh['seq'=64,'head'=8] {'head'}, dimensions={0} | all-to-all | bytes 524288 | tf_op jit(solution)/shard_map/all_to_all | solution.py:242
  108.5 0.9 copy.11
  (10 shorter events, 0.1 us)
Async XLA Ops:
  6.5 52.4 %all-gather.3.cloned.1.call-start = ((), (), s32[]{:S(2)}) async-start(), calls=%async_computation.3 | async-start | bytes 2359296 | tf_op jit(solution)/shard_map/all_gather | solution.py:177
  8.8 7.7 %collective-permute-start.1 = (bf16[9,16,256]{2,1,0:T(8,128)(2,1)S(1)}, bf16[9,16,256]{2,1,0:T(8,128)(2,1)S(1)}, u32[]{:S(2)}, u32[]{:S(2)}) collective-permute-start(bf16[9,16,256]{2,1,0:T(8,128)(2,1)S(1)} %pad_maximum_fusion.2), channel_id=1, source_target_pairs={{0,256},{8,264},{16,272},{24,280},{32,288},{40,296},{48,304},{56,3... | collective-permute-start | bytes 221192 | tf_op jit(solution)/shard_map/ppermute | solution.py:181
  14.3 6.3 %collective-permute-start = (bf16[9,16,256]{2,1,0:T(8,128)(2,1)S(1)}, bf16[9,16,256]{2,1,0:T(8,128)(2,1)S(1)}, u32[]{:S(2)}, u32[]{:S(2)}) collective-permute-start(bf16[9,16,256]{2,1,0:T(8,128)(2,1)S(1)} %pad_maximum_fusion.2), channel_id=1, source_target_pairs={{0,128},{8,136},{16,144},{24,152},{32,160},{40,168},{48,176},{56,1... | collective-permute-start | bytes 221192 | tf_op jit(solution)/shard_map/ppermute | solution.py:182
  21.3 21.7 %all-to-all-start = ((bf16[8,16,768]{2,1,0:T(8,128)(2,1)}), bf16[8,16,768]{2,1,0:T(8,128)(2,1)S(1)}, u32[]{:S(2)}, u32[]{:S(2)}) async-start(bf16[8,16,768]{2,1,0:T(8,128)(2,1)} %pad_maximum_fusion.1), calls=%async_computation | async-start | bytes 393216 | tf_op jit(solution)/shard_map/all_to_all | solution.py:186
  31.3 5.0 %collective-permute-start.2 = (bf16[1,16,256]{2,1,0:T(8,128)(2,1)}, bf16[1,16,256]{2,1,0:T(8,128)(2,1)S(1)}, u32[]{:S(2)}, u32[]{:S(2)}) collective-permute-start(bf16[1,16,256]{2,1,0:T(8,128)(2,1)} %bitcast.32), channel_id=1, source_target_pairs={{0,384},{8,392},{16,400},{24,408},{32,416},{40,424},{48,432},{56,4... | collective-permute-start | bytes 24584 | tf_op jit(solution)/shard_map/ppermute | solution.py:183
  44.4 17.0 %copy-start = (s32[8192]{0:T(1024)S(1)}, s32[8192]{0:T(1024)}, u32[]{:S(2)}) copy-start(s32[8192]{0:T(1024)} %param.7) | copy-start | bytes 98308
  44.4 39.6 %all-to-all-start.1 = ((bf16[8,320,256]{2,1,0:T(8,128)(2,1)}), bf16[8,320,256]{2,1,0:T(8,128)(2,1)S(1)}, u32[]{:S(2)}, u32[]{:S(2)}) async-start(bf16[8,320,256]{2,1,0:T(8,128)(2,1)} %pad_maximum_fusion), calls=%async_computation.1 | async-start | bytes 2621440 | tf_op jit(solution)/shard_map/all_to_all | solution.py:194
  51.5 10.0 %collective-permute-start.3 = (bf16[128,256]{1,0:T(8,128)(2,1)S(1)}, bf16[128,256]{1,0:T(8,128)(2,1)S(1)}, u32[]{:S(2)}, u32[]{:S(2)}) collective-permute-start(bf16[128,256]{1,0:T(8,128)(2,1)S(1)} %get-tuple-element.15.mine_ref), channel_id=1, source_target_pairs={{0,8},{8,0},{16,24},{24,16},{32,40},{40,32},{48,56},{56,48},{64,72... | collective-permute-start | bytes 196616 | tf_op jit(solution)/shard_map/ppermute | solution.py:197
  62.6 28.7 %copy-start.1 = (s32[1,32]{1,0:T(1,128)S(1)}, s32[1,32]{1,0:T(1,128)}, u32[]{:S(2)}) copy-start(s32[1,32]{1,0:T(1,128)} %param.9) | copy-start | bytes 388
  84.0 7.3 %collective-permute-start.4 = (bf16[2560,256]{1,0:T(8,128)(2,1)S(1)}, bf16[2560,256]{1,0:T(8,128)(2,1)S(1)}, u32[]{:S(2)}, u32[]{:S(2)}) collective-permute-start(bf16[2560,256]{1,0:T(8,128)(2,1)S(1)} %bitcast.15), channel_id=1, source_target_pairs={{0,8},{8,0},{16,24},{24,16},{32,40},{40,32},{48,56},{56,48},{64,72... | collective-permute-start | bytes 3932168 | tf_op jit(solution)/shard_map/ppermute | solution.py:217
Sparse Core Ops, SparseCore 0:
  9.4 49.4 all-gather.2

commit v8 on v7

--- a/solution.py
+++ b/solution.py
@@ -17,7 +17,8 @@
 TILE = 512
 SCALE2 = D ** (-0.5) * 1.4426950408889634
 LOW = -1e30
-SLOT = 2 * ROWS + NX * PAGE
+SLOT = ROWS + PAGE
+NEAR = 8
 
 
 def x_ring(by):
@@ -73,7 +74,7 @@
     return (key_rows >= row_start) & (key_rows <= query_rows)
 
 
-def near_kernel(meta_ref, mine_ref, side_ref, ids_ref, q_ref, qt_ref, m_ref, l_ref, acc_ref):
+def own_kernel(meta_ref, mine_ref, side_ref, ids_ref, q_ref, qt_ref, m_ref, l_ref, acc_ref):
     own = meta_ref[0]
     row_start, first, last = starts_of(ids_ref, own)
     for g in range(GROUP):
@@ -93,19 +94,17 @@
         fold(side_ref[:, :D], side_ref[:, D:], mask_of(own - 1, own, row_start), *state)
 
 
-def window(kv_ref, core, own, ids_ref, qt_ref, m_ref, l_ref, acc_ref):
-    row_start, first, last = starts_of(ids_ref, own)
-    chip = own // 2
-    x = chip // NY
-    lowest = (jnp.maximum(first // ROWS - core, -1) + 1) // 2
+def window(kv_ref, skip, core, own, limits, qt_ref, m_ref, l_ref, acc_ref):
+    row_start, first, last = limits
+    chip = own // 2 - skip
+    lowest = jnp.maximum((jnp.maximum(first // ROWS - core, -1) + 1) // 2, chip - NEAR)
     steps = jnp.maximum(chip - lowest + BLOCKS - 1, 0) // BLOCKS
 
     def step(i, carry):
         base = chip - BLOCKS * (i + 1)
         pairs = []
         for b in range(BLOCKS):
-            at = jnp.maximum(base + b, 0)
-            start = (at % NY) * SLOT + jnp.where(at // NY == x - 1, 0, ROWS)
+            start = (base + b + 4 * NY) % NY * SLOT
             pairs.append(kv_ref[pl.ds(pl.multiple_of(start, PAGE), ROWS), :])
         keys = jnp.concatenate([pair[:, :D] for pair in pairs], axis=0)
         values = jnp.concatenate([pair[:, D:] for pair in pairs], axis=0)
@@ -127,36 +126,51 @@
     lax.fori_loop(0, steps, step, 0)
 
 
-def own_kernel(meta_ref, kv_ref, ids_ref, qt_ref, m_in, l_in, acc_in, m_ref, l_ref, acc_ref):
+def near_kernel(meta_ref, kv_ref, side_ref, ids_ref, qt_ref, m_in, l_in, acc_in, m_ref, l_ref, acc_ref):
     m_ref[...] = m_in[...]
     l_ref[...] = l_in[...]
     acc_ref[...] = acc_in[...]
     own = meta_ref[0]
-    window(kv_ref, own % 2, own, ids_ref, qt_ref, m_ref, l_ref, acc_ref)
-
-
-def last_kernel(meta_ref, table_ref, mine_ref, kv_ref, ids_ref, qt_ref, m_in, l_in, acc_in,
-                out_ref, m_ref, l_ref, acc_ref, prefix_ref):
+    limits = starts_of(ids_ref, own)
+    window(kv_ref, 0, own % 2, own, limits, qt_ref, m_ref, l_ref, acc_ref)
+    window(side_ref, 0, 1 - own % 2, own, limits, qt_ref, m_ref, l_ref, acc_ref)
+
+
+def far_kernel(meta_ref, kv_ref, ids_ref, qt_ref, m_in, l_in, acc_in, m_ref, l_ref, acc_ref):
     m_ref[...] = m_in[...]
     l_ref[...] = l_in[...]
     acc_ref[...] = acc_in[...]
     own = meta_ref[0]
+    window(kv_ref, NEAR, own % 2, own, starts_of(ids_ref, own), qt_ref, m_ref, l_ref, acc_ref)
+
+
+def last_kernel(meta_ref, table_ref, near_ref, near_side_ref, far_ref, far_side_ref, two_ref, three_ref, ids_ref,
+                qt_ref, m_in, l_in, acc_in, out_ref, m_ref, l_ref, acc_ref, prefix_ref):
+    m_ref[...] = m_in[...]
+    l_ref[...] = l_in[...]
+    acc_ref[...] = acc_in[...]
+    own = meta_ref[0]
     core, x = own % 2, own // (2 * NY)
     for i in range(PAGES):
         page = table_ref[i]
-        start = (page // 2) % NY * SLOT + 2 * ROWS + (x + NX - page // (2 * NY)) % NX * PAGE
-        rows = pl.ds(pl.multiple_of(start, PAGE), PAGE)
-
-        @pl.when(page % 2 == core)
-        def _():
-            prefix_ref[i * PAGE:(i + 1) * PAGE, :] = mine_ref[rows, :]
-
-        @pl.when(page % 2 != core)
-        def _():
-            prefix_ref[i * PAGE:(i + 1) * PAGE, :] = kv_ref[rows, :]
+        yy = (page // 2) % NY
+        back = (x + NX - page // (2 * NY)) % NX
+        side = jnp.where(page % 2 == core, 0, 1)
+        in_slot = pl.ds(pl.multiple_of(yy * SLOT + ROWS, PAGE), PAGE)
+        in_page = pl.ds(pl.multiple_of((side * NY + yy) * PAGE, PAGE), PAGE)
+        into = slice(i * PAGE, (i + 1) * PAGE)
+        places = [
+            (near_ref, in_slot), (near_side_ref, in_slot), (far_ref, in_slot), (far_side_ref, in_slot),
+            (two_ref, in_page), (three_ref, in_page),
+        ]
+        for n, (ref, rows) in enumerate(places):
+
+            @pl.when(jnp.where(back < 2, 2 * back + side, back + 2) == n)
+            def _():
+                prefix_ref[into, :] = ref[rows, :]
 
     fold(prefix_ref[:, :D], prefix_ref[:, D:], None, qt_ref, m_ref, l_ref, acc_ref)
-    window(kv_ref, 1 - core, own, ids_ref, qt_ref, m_ref, l_ref, acc_ref)
+    window(far_side_ref, NEAR, 1 - core, own, starts_of(ids_ref, own), qt_ref, m_ref, l_ref, acc_ref)
     result = (acc_ref[...] * (1.0 / l_ref[...])).astype(jnp.bfloat16)
     for g in range(GROUP):
         out_ref[:, g * D:(g + 1) * D] = result[:, g * ROWS:(g + 1) * ROWS].T
@@ -173,28 +187,25 @@
 def per_device(queries, branch_key_value, branch_ids, pool, page_table):
     me = lax.axis_index("seq")
     y = (me // 2) % NY
-    z = lax.axis_index("head")
-    gathered = lax.all_gather(jnp.transpose(queries, (1, 0, 2)), "head", axis=0, tiled=False)
-    query = lax.dynamic_index_in_dim(gathered, z, 1, keepdims=False).reshape(ROWS, GROUP * D)
-    page = pool.reshape(1, PAGE, PAIR)
-    raw = jnp.concatenate([jnp.transpose(branch_key_value, (1, 0, 2)), page], axis=0)
-    two_raw = lax.ppermute(raw, "seq", x_ring(2))
+    page = pool.reshape(PAGE, PAIR)
+    raw = jnp.transpose(branch_key_value, (1, 0, 2))
     one_raw = lax.ppermute(raw, "seq", x_ring(1))
-    three_page = lax.ppermute(page, "seq", x_ring(3))
-    pages = jnp.concatenate([page, one_raw[8:], two_raw[8:], three_page], axis=0).reshape(NX * PAGE, PAIR)
-    wide = jnp.concatenate([raw[:8], one_raw[:8], two_raw[:8]], axis=2)
-    wide = lax.all_to_all(wide, "head", split_axis=0, concat_axis=0, tiled=True).reshape(ROWS, 3 * PAIR)
-    own, one_back, two_back = (wide[:, i * PAIR:(i + 1) * PAIR] for i in range(3))
+    wide = jnp.concatenate([jnp.transpose(queries, (1, 0, 2)), raw, one_raw], axis=2)
+    wide = lax.all_to_all(wide, "head", split_axis=0, concat_axis=0, tiled=True).reshape(ROWS, -1)
+    own, before = wide[:, GROUP * D:GROUP * D + PAIR], wide[:, GROUP * D + PAIR:]
     target = jnp.arange(NY, dtype=jnp.int32)[:, None, None]
-    mixed = jnp.where(target > y, own[None], two_back[None])
-    send = jnp.concatenate([
-        jnp.broadcast_to(one_back[None], mixed.shape), mixed,
-        jnp.broadcast_to(pages[None], (NY, NX * PAGE, PAIR)),
-    ], axis=1)
-    kv = lax.all_to_all(send, "seq", split_axis=0, concat_axis=0, tiled=True, axis_index_groups=Y_GROUPS)
-    kv = kv.reshape(NY * SLOT, PAIR)
+    block = jnp.where(target > y, own[None], before[None])
+    send = jnp.concatenate([block, jnp.broadcast_to(page[None], (NY, PAGE, PAIR))], axis=1)
+    near = lax.all_to_all(send, "seq", split_axis=0, concat_axis=0, tiled=True, axis_index_groups=Y_GROUPS)
+    far = lax.ppermute(near, "seq", x_ring(1))
     later, _ = lax.optimization_barrier((own, send))
     side = lax.ppermute(later, "seq", SWAP)
+    near_side = lax.ppermute(near, "seq", SWAP)
+    far_side = lax.ppermute(far, "seq", SWAP)
+    pages = jnp.concatenate([near[:, ROWS:], near_side[:, ROWS:]], axis=0).reshape(2 * NY * PAGE, PAIR)
+    two_pages = lax.ppermute(pages, "seq", x_ring(2))
+    three_pages = lax.ppermute(pages, "seq", x_ring(3))
+    near, near_side, far, far_side = (a.reshape(NY * SLOT, PAIR) for a in (near, near_side, far, far_side))
 
     ids = branch_ids.reshape(2 * NX * NY, ROWS)
     meta = me.astype(jnp.int32).reshape(1)
@@ -204,30 +215,37 @@
         jax.ShapeDtypeStruct((D, QR), jnp.float32),
     ]
     params = pltpu.CompilerParams(vmem_limit_bytes=40 * 1024 * 1024)
-    qt, m, l, acc = pl.pallas_call(
-        near_kernel,
+    qt, *now = pl.pallas_call(
+        own_kernel,
         out_shape=[jax.ShapeDtypeStruct((PAIR, QR), jnp.bfloat16)] + state,
         in_specs=[SM] + [VM] * 4,
         out_specs=[VM] * 4,
         compiler_params=params,
         cost_estimate=cost(256),
-        name="near_keys",
-    )(meta, own, side, ids, query)
-    kv, m = lax.optimization_barrier((kv, m))
-    kv_side = lax.ppermute(kv, "seq", SWAP)
-    m, l, acc = pl.pallas_call(
-        own_kernel,
+        name="own_chip",
+    )(meta, own, side, ids, wide)
+    now = pl.pallas_call(
+        near_kernel,
+        out_shape=state,
+        in_specs=[SM] + [VM] * 7,
+        out_specs=[VM] * 3,
+        compiler_params=params,
+        cost_estimate=cost(2048),
+        name="near_window",
+    )(meta, near, near_side, ids, qt, *now)
+    now = pl.pallas_call(
+        far_kernel,
         out_shape=state,
         in_specs=[SM] + [VM] * 6,
         out_specs=[VM] * 3,
         compiler_params=params,
-        cost_estimate=cost(2048),
-        name="own_parity",
-    )(meta, kv, ids, qt, m, l, acc)
+        cost_estimate=cost(1024),
+        name="far_window",
+    )(meta, far, ids, qt, *now)
     out = pl.pallas_call(
         last_kernel,
         out_shape=jax.ShapeDtypeStruct((ROWS, GROUP * D), jnp.bfloat16),
-        in_specs=[SM, SM] + [VM] * 7,
+        in_specs=[SM, SM] + [VM] * 11,
         out_specs=VM,
         scratch_shapes=[
             pltpu.VMEM((1, QR), jnp.float32),
@@ -236,9 +254,9 @@
             pltpu.VMEM((PAGES * PAGE, PAIR), jnp.bfloat16),
         ],
         compiler_params=params,
-        cost_estimate=cost(2560),
-        name="other_parity",
-    )(meta, page_table.reshape(PAGES), kv, kv_side, ids, qt, m, l, acc)
+        cost_estimate=cost(1536),
+        name="far_other_core_and_prefix",
+    )(meta, page_table.reshape(PAGES), near, near_side, far, far_side, two_pages, three_pages, ids, qt, *now)
     out = lax.all_to_all(out.reshape(8, ROWS // 8, GROUP * D), "head", split_axis=0, concat_axis=0, tiled=True)
     return jnp.transpose(out, (1, 0, 2))
 

time: 117 us -> 110 us (0.940)
  the two profiles are of different devices: /device:TPU:1 before, /device:TPU:6 now
where the time goes in v8:
time: 110 us
  blocking collectives  39.7 us (36%)
  starting transfers between devices  32 us (29%)
  waiting for transfers between devices  21.7 us (20%)
  Pallas kernels  12.2 us (11%)
  local copies, waits for them, and re-layouts  2.85 us (3%)
    all_to_all x1, blocking collectives, per_device(): lax.all_to_all(send, 'seq', split_axis=0, concat_axis=0, tiled=True, axis...  23 us
    all_to_all x1, blocking collectives, per_device(): lax.all_to_all(out.reshape(8, ROWS // 8, GROUP * D), 'head', split_axis=0...  16.7 us
    all_to_all x1, waiting for transfers between devices, per_device(): lax.all_to_all(wide, 'head', split_axis=0, concat_axis=0, tiled=True)  13.5 us
    ppermute x1, starting transfers between devices, per_device(): one_raw = lax.ppermute(raw, 'seq', x_ring(1))  7.76 us
    all_to_all x1, starting transfers between devices, per_device(): lax.all_to_all(wide, 'head', split_axis=0, concat_axis=0, tiled=True)  6.82 us
    ppermute x1, waiting for transfers between devices, per_device(): far = lax.ppermute(near, 'seq', x_ring(1))  6.55 us
    pallas_call x1, Pallas kernels, per_device(): pl.pallas_call(last_kernel, out_shape=jax.ShapeDtypeStruct((ROWS, GROUP *...  5.11 us
    ppermute x1, starting transfers between devices, per_device(): three_pages = lax.ppermute(pages, 'seq', x_ring(3))  4.25 us
  transfers between devices with their start and end apart: 8, of which 4 were waited for; matrix products, arithmetic and copies ran while one was open for 1% of the time, Pallas kernels for 6%

profile of v8, /device:TPU:6, one launch (start us, length us, event | category | flops | bytes accessed | tf_op | source)
XLA Modules:
  0.0 109.7 jit_solution(14620095042350362145)
XLA Ops:
  0.0 0.9 copy.14
  0.9 7.8 %collective-permute-start = (bf16[8,16,256]{2,1,0:T(8,128)(2,1)S(1)}, bf16[8,16,256]{2,1,0:T(8,128)(2,1)S(1)}, u32[]{:S(2)}, u32[]{:S(2)}) collective-permute-start(bf16[8,16,256]{2,1,0:T(8,128)(2,1)S(1)} %bitcast.35), channel_id=1, source_target_pairs={{0,128},{8,136},{16,144},{24,152},{32,160},{40,168},{48,176},{56,1... | collective-permute-start | bytes 196616 | tf_op jit(solution)/shard_map/ppermute | solution.py:192
  8.6 1.1 %copy.13 = bf16[16,8,1024]{2,0,1:T(8,128)(2,1)S(1)} copy(bf16[16,8,1024]{2,1,0:T(8,128)(2,1)} %param.5) | data formatting | bytes 524288 | tf_op args[0]
  9.7 0.8 collective-permute-done
  10.5 0.8 pad_maximum_fusion.1
  11.3 6.8 %all-to-all-start = ((bf16[8,16,1536]{2,1,0:T(8,128)(2,1)}), bf16[8,16,1536]{2,1,0:T(8,128)(2,1)S(1)}, u32[]{:S(2)}, u32[]{:S(2)}) async-start(bf16[8,16,1536]{2,1,0:T(8,128)(2,1)} %pad_maximum_fusion.1), calls=%async_computation | async-start | bytes 786432 | tf_op jit(solution)/shard_map/all_to_all | solution.py:194
  18.2 13.5 %all-to-all-done = bf16[8,16,1536]{2,1,0:T(8,128)(2,1)S(1)} async-done(((bf16[8,16,1536]{2,1,0:T(8,128)(2,1)}), bf16[8,16,1536]{2,1,0:T(8,128)(2,1)S(1)}, u32[]{:S(2)}, u32[]{:S(2)}) %all-to-all-start) | async-done | bytes 393248 | tf_op jit(solution)/shard_map/all_to_all | solution.py:194
  31.7 0.1 broadcast_select_fusion
  31.8 0.0 copy-done.2
  31.8 0.0 copy-start
  31.9 23.0 %all_to_all.15 = bf16[8,144,256]{2,1,0:T(8,128)(2,1)S(1)} all-to-all(bf16[8,144,256]{2,1,0:T(8,128)(2,1)S(1)} %pad_maximum_fusion), channel_id=1, replica_groups={{0,16,32,48,64,80,96,112},{8,24,40,56,72,88,104,120},{128,144,160,176,1..., dimensions={0} | all-to-all | bytes 1179648 | tf_op jit(solution)/shard_map/all_to_all | solution.py:199
  54.9 3.6 %collective-permute-start.2 = (bf16[8,144,256]{2,1,0:T(8,128)(2,1)S(1)}, bf16[8,144,256]{2,1,0:T(8,128)(2,1)S(1)}, u32[]{:S(2)}, u32[]{:S(2)}) collective-permute-start(bf16[8,144,256]{2,1,0:T(8,128)(2,1)S(1)} %all_to_all.15), channel_id=1, source_target_pairs={{0,128},{8,136},{16,144},{24,152},{32,160},{40,168},{48,176},{56,1... | collective-permute-start | bytes 1769480 | tf_op jit(solution)/shard_map/ppermute | solution.py:200
  58.5 1.9 %collective-permute-start.1 = (bf16[8,144,256]{2,1,0:T(8,128)(2,1)S(1)}, bf16[8,144,256]{2,1,0:T(8,128)(2,1)S(1)}, u32[]{:S(2)}, u32[]{:S(2)}) collective-permute-start(bf16[8,144,256]{2,1,0:T(8,128)(2,1)S(1)} %all_to_all.15), channel_id=1, source_target_pairs={{0,8},{8,0},{16,24},{24,16},{32,40},{40,32},{48,56},{56,48},{64,72... | collective-permute-start | bytes 1769480 | tf_op jit(solution)/shard_map/ppermute | solution.py:203
  60.4 6.5 %collective-permute-done.2 = bf16[8,144,256]{2,1,0:T(8,128)(2,1)S(1)} collective-permute-done((bf16[8,144,256]{2,1,0:T(8,128)(2,1)S(1)}, bf16[8,144,256]{2,1,0:T(8,128)(2,1)S(1)}, u32[]{:S(2)}, u32[]{:S(2)}) %collective-permute-start.2) | collective-permute-done | bytes 589856 | tf_op jit(solution)/shard_map/ppermute | solution.py:200
  67.0 1.9 %collective-permute-start.3 = (bf16[8,144,256]{2,1,0:T(8,128)(2,1)S(1)}, bf16[8,144,256]{2,1,0:T(8,128)(2,1)S(1)}, u32[]{:S(2)}, u32[]{:S(2)}) collective-permute-start(bf16[8,144,256]{2,1,0:T(8,128)(2,1)S(1)} %collective-permute-done.2), channel_id=1, source_target_pairs={{0,8},{8,0},{16,24},{24,16},{32,40},{40,32},{48,56},{56,48},{64,72... | collective-permute-start | bytes 1769480 | tf_op jit(solution)/shard_map/ppermute | solution.py:204
  68.9 2.4 %collective-permute-start.6 = (bf16[128,256]{1,0:T(8,128)(2,1)S(1)}, bf16[128,256]{1,0:T(8,128)(2,1)S(1)}, u32[]{:S(2)}, u32[]{:S(2)}) collective-permute-start(bf16[128,256]{1,0:T(8,128)(2,1)S(1)} %get-tuple-element.16.mine_ref), channel_id=1, source_target_pairs={{0,8},{8,0},{16,24},{24,16},{32,40},{40,32},{48,56},{56,48},{64,72... | collective-permute-start | bytes 196616 | tf_op jit(solution)/shard_map/ppermute | solution.py:202
  71.3 0.9 collective-permute-done.6.side_ref
  72.2 0.0 copy-done
  72.2 0.7 own_chip.1
  72.8 0.0 collective-permute-done.1
  72.9 3.3 %collective-permute-start.4 = (bf16[256,256]{1,0:T(8,128)(2,1)S(1)}, bf16[256,256]{1,0:T(8,128)(2,1)S(1)}, u32[]{:S(2)}, u32[]{:S(2)}) collective-permute-start(bf16[256,256]{1,0:T(8,128)(2,1)S(1)} %bitcast.37), channel_id=1, source_target_pairs={{0,256},{8,264},{16,272},{24,280},{32,288},{40,296},{48,304},{56,3... | collective-permute-start | bytes 393224 | tf_op jit(solution)/shard_map/ppermute | solution.py:206
  76.2 4.2 %collective-permute-start.5 = (bf16[256,256]{1,0:T(8,128)(2,1)S(1)}, bf16[256,256]{1,0:T(8,128)(2,1)S(1)}, u32[]{:S(2)}, u32[]{:S(2)}) collective-permute-start(bf16[256,256]{1,0:T(8,128)(2,1)S(1)} %bitcast.38), channel_id=1, source_target_pairs={{0,384},{8,392},{16,400},{24,408},{32,416},{40,424},{48,432},{56,4... | collective-permute-start | bytes 393224 | tf_op jit(solution)/shard_map/ppermute | solution.py:207
  80.5 4.2 %near_window.1 = (f32[1,1024]{1,0:T(1,128)S(1)}, f32[1,1024]{1,0:T(1,128)S(1)}, f32[128,1024]{1,0:T(8,128)S(1)}) custom-call(s32[1]{0:T(128)} %bitcast.meta_ref, bf16[1152,256]{1,0:T(8,128)(2,1)S(1)} %bitcast.18, bf16[1152,256]{1,0:T(8,128)(2,1)S(1)} %bitcast.23, s32[64,128]{1,0:T(8,128)S(1)} %bitcast.29, bf16[256,1024]{1,0:T(8,128)(2,1)S(1)} %get-tuple-element.17.qt_ref, ...), custom_call_target="tpu_custom_call" | custom-call | flops 1073741824 | bytes 1048576 | tf_op jit(solution)/shard_map/near_window/pallas_call | solution.py:227
  84.6 0.0 copy-start.1
  84.7 2.3 %far_window.1 = (f32[1,1024]{1,0:T(1,128)S(1)}, f32[1,1024]{1,0:T(1,128)S(1)}, f32[128,1024]{1,0:T(8,128)S(1)}) custom-call(s32[1]{0:T(128)} %bitcast.meta_ref, bf16[1152,256]{1,0:T(8,128)(2,1)S(1)} %bitcast.25, s32[64,128]{1,0:T(8,128)S(1)} %bitcast.30, bf16[256,1024]{1,0:T(8,128)(2,1)S(1)} %get-tuple-element.17.qt_ref, ...), custom_call_target="tpu_custom_call" | custom-call | flops 536870912 | bytes 1048576 | tf_op jit(solution)/shard_map/far_window/pallas_call | solution.py:236
  87.0 0.0 collective-permute-done.4.two_ref
  87.0 0.0 collective-permute-done.5.three_ref
  87.0 0.0 collective-permute-done.3
  87.0 0.0 copy-done.1
  87.0 5.1 %far_other_core_and_prefix.1 = bf16[128,1024]{1,0:T(8,128)(2,1)S(1)} custom-call(s32[1]{0:T(128)} %bitcast.meta_ref, s32[32]{0:T(128)S(1)} %bitcast.32, bf16[1152,256]{1,0:T(8,128)(2,1)S(1)} %bitcast.19, bf16[1152,256]{1,0:T(8,128)(2,1)S(1)} %bitcast.24, bf16[1152,256]{1,0:T(8,128)(2,1)S(1)} %bitcast.26, bf16[1152,256]{1,0:T(8,128)(2,1)S(1)} %bitcast.27, ...), custom_call_target="tpu_custom_call" | custom-call | flops 805306368 | bytes 1048576 | tf_op jit(solution)/shard_map/far_other_core_and_prefix/pallas_call | solution.py:245
  92.1 16.7 %all_to_all.16 = bf16[8,16,1024]{2,1,0:T(8,128)(2,1)S(1)} all-to-all(bf16[8,16,1024]{2,1,0:T(8,128)(2,1)S(1)} %bitcast.22), channel_id=1, replica_groups=mesh['seq'=64,'head'=8] {'head'}, dimensions={0} | all-to-all | bytes 524288 | tf_op jit(solution)/shard_map/all_to_all | solution.py:260
  108.8 0.9 copy.10
  (8 shorter events, 0.1 us)
Async XLA Ops:
  0.9 9.7 %collective-permute-start = (bf16[8,16,256]{2,1,0:T(8,128)(2,1)S(1)}, bf16[8,16,256]{2,1,0:T(8,128)(2,1)S(1)}, u32[]{:S(2)}, u32[]{:S(2)}) collective-permute-start(bf16[8,16,256]{2,1,0:T(8,128)(2,1)S(1)} %bitcast.35), channel_id=1, source_target_pairs={{0,128},{8,136},{16,144},{24,152},{32,160},{40,168},{48,176},{56,1... | collective-permute-start | bytes 196616 | tf_op jit(solution)/shard_map/ppermute | solution.py:192
  11.3 20.4 %all-to-all-start = ((bf16[8,16,1536]{2,1,0:T(8,128)(2,1)}), bf16[8,16,1536]{2,1,0:T(8,128)(2,1)S(1)}, u32[]{:S(2)}, u32[]{:S(2)}) async-start(bf16[8,16,1536]{2,1,0:T(8,128)(2,1)} %pad_maximum_fusion.1), calls=%async_computation | async-start | bytes 786432 | tf_op jit(solution)/shard_map/all_to_all | solution.py:194
  18.1 13.7 %copy-start.2 = (bf16[1,16,1,256]{3,1,2,0:T(8,128)(2,1)S(1)}, bf16[1,16,1,256]{3,1,2,0:T(8,128)(2,1)}, u32[]{:S(2)}) copy-start(bf16[1,16,1,256]{3,1,2,0:T(8,128)(2,1)} %param.8) | copy-start | bytes 24580
  31.8 40.3 %copy-start = (s32[8192]{0:T(1024)S(1)}, s32[8192]{0:T(1024)}, u32[]{:S(2)}) copy-start(s32[8192]{0:T(1024)} %param.7) | copy-start | bytes 98308
  54.9 12.1 %collective-permute-start.2 = (bf16[8,144,256]{2,1,0:T(8,128)(2,1)S(1)}, bf16[8,144,256]{2,1,0:T(8,128)(2,1)S(1)}, u32[]{:S(2)}, u32[]{:S(2)}) collective-permute-start(bf16[8,144,256]{2,1,0:T(8,128)(2,1)S(1)} %all_to_all.15), channel_id=1, source_target_pairs={{0,128},{8,136},{16,144},{24,152},{32,160},{40,168},{48,176},{56,1... | collective-permute-start | bytes 1769480 | tf_op jit(solution)/shard_map/ppermute | solution.py:200
  58.5 14.4 %collective-permute-start.1 = (bf16[8,144,256]{2,1,0:T(8,128)(2,1)S(1)}, bf16[8,144,256]{2,1,0:T(8,128)(2,1)S(1)}, u32[]{:S(2)}, u32[]{:S(2)}) collective-permute-start(bf16[8,144,256]{2,1,0:T(8,128)(2,1)S(1)} %all_to_all.15), channel_id=1, source_target_pairs={{0,8},{8,0},{16,24},{24,16},{32,40},{40,32},{48,56},{56,48},{64,72... | collective-permute-start | bytes 1769480 | tf_op jit(solution)/shard_map/ppermute | solution.py:203
  67.0 20.0 %collective-permute-start.3 = (bf16[8,144,256]{2,1,0:T(8,128)(2,1)S(1)}, bf16[8,144,256]{2,1,0:T(8,128)(2,1)S(1)}, u32[]{:S(2)}, u32[]{:S(2)}) collective-permute-start(bf16[8,144,256]{2,1,0:T(8,128)(2,1)S(1)} %collective-permute-done.2), channel_id=1, source_target_pairs={{0,8},{8,0},{16,24},{24,16},{32,40},{40,32},{48,56},{56,48},{64,72... | collective-permute-start | bytes 1769480 | tf_op jit(solution)/shard_map/ppermute | solution.py:204
  68.9 3.3 %collective-permute-start.6 = (bf16[128,256]{1,0:T(8,128)(2,1)S(1)}, bf16[128,256]{1,0:T(8,128)(2,1)S(1)}, u32[]{:S(2)}, u32[]{:S(2)}) collective-permute-start(bf16[128,256]{1,0:T(8,128)(2,1)S(1)} %get-tuple-element.16.mine_ref), channel_id=1, source_target_pairs={{0,8},{8,0},{16,24},{24,16},{32,40},{40,32},{48,56},{56,48},{64,72... | collective-permute-start | bytes 196616 | tf_op jit(solution)/shard_map/ppermute | solution.py:202
  72.9 14.1 %collective-permute-start.4 = (bf16[256,256]{1,0:T(8,128)(2,1)S(1)}, bf16[256,256]{1,0:T(8,128)(2,1)S(1)}, u32[]{:S(2)}, u32[]{:S(2)}) collective-permute-start(bf16[256,256]{1,0:T(8,128)(2,1)S(1)} %bitcast.37), channel_id=1, source_target_pairs={{0,256},{8,264},{16,272},{24,280},{32,288},{40,296},{48,304},{56,3... | collective-permute-start | bytes 393224 | tf_op jit(solution)/shard_map/ppermute | solution.py:206
  76.2 10.7 %collective-permute-start.5 = (bf16[256,256]{1,0:T(8,128)(2,1)S(1)}, bf16[256,256]{1,0:T(8,128)(2,1)S(1)}, u32[]{:S(2)}, u32[]{:S(2)}) collective-permute-start(bf16[256,256]{1,0:T(8,128)(2,1)S(1)} %bitcast.38), channel_id=1, source_target_pairs={{0,384},{8,392},{16,400},{24,408},{32,416},{40,424},{48,432},{56,4... | collective-permute-start | bytes 393224 | tf_op jit(solution)/shard_map/ppermute | solution.py:207
  84.6 2.3 %copy-start.1 = (s32[1,32]{1,0:T(1,128)S(1)}, s32[1,32]{1,0:T(1,128)}, u32[]{:S(2)}) copy-start(s32[1,32]{1,0:T(1,128)} %param.9) | copy-start | bytes 388

commit v9 on v8

--- a/solution.py
+++ b/solution.py
@@ -17,7 +17,7 @@
 TILE = 512
 SCALE2 = D ** (-0.5) * 1.4426950408889634
 LOW = -1e30
-SLOT = ROWS + PAGE
+SLOT = ROWS + NX * PAGE
 NEAR = 8
 
 
@@ -94,7 +94,7 @@
         fold(side_ref[:, :D], side_ref[:, D:], mask_of(own - 1, own, row_start), *state)
 
 
-def window(kv_ref, skip, core, own, limits, qt_ref, m_ref, l_ref, acc_ref):
+def window(kv_ref, skip, slot, core, own, limits, qt_ref, m_ref, l_ref, acc_ref):
     row_start, first, last = limits
     chip = own // 2 - skip
     lowest = jnp.maximum((jnp.maximum(first // ROWS - core, -1) + 1) // 2, chip - NEAR)
@@ -104,7 +104,7 @@
         base = chip - BLOCKS * (i + 1)
         pairs = []
         for b in range(BLOCKS):
-            start = (base + b + 4 * NY) % NY * SLOT
+            start = (base + b + 4 * NY) % NY * slot
             pairs.append(kv_ref[pl.ds(pl.multiple_of(start, PAGE), ROWS), :])
         keys = jnp.concatenate([pair[:, :D] for pair in pairs], axis=0)
         values = jnp.concatenate([pair[:, D:] for pair in pairs], axis=0)
@@ -126,14 +126,30 @@
     lax.fori_loop(0, steps, step, 0)
 
 
-def near_kernel(meta_ref, kv_ref, side_ref, ids_ref, qt_ref, m_in, l_in, acc_in, m_ref, l_ref, acc_ref):
+def near_kernel(meta_ref, table_ref, kv_ref, side_ref, ids_ref, qt_ref, m_in, l_in, acc_in,
+                m_ref, l_ref, acc_ref, prefix_ref):
     m_ref[...] = m_in[...]
     l_ref[...] = l_in[...]
     acc_ref[...] = acc_in[...]
     own = meta_ref[0]
+    core, x = own % 2, own // (2 * NY)
+    for i in range(PAGES):
+        page = table_ref[i]
+        start = (page // 2) % NY * SLOT + ROWS + (x + NX - page // (2 * NY)) % NX * PAGE
+        rows = pl.ds(pl.multiple_of(start, PAGE), PAGE)
+
+        @pl.when(page % 2 == core)
+        def _():
+            prefix_ref[i * PAGE:(i + 1) * PAGE, :] = kv_ref[rows, :]
+
+        @pl.when(page % 2 != core)
+        def _():
+            prefix_ref[i * PAGE:(i + 1) * PAGE, :] = side_ref[rows, :]
+
+    fold(prefix_ref[:, :D], prefix_ref[:, D:], None, qt_ref, m_ref, l_ref, acc_ref)
     limits = starts_of(ids_ref, own)
-    window(kv_ref, 0, own % 2, own, limits, qt_ref, m_ref, l_ref, acc_ref)
-    window(side_ref, 0, 1 - own % 2, own, limits, qt_ref, m_ref, l_ref, acc_ref)
+    window(kv_ref, 0, SLOT, core, own, limits, qt_ref, m_ref, l_ref, acc_ref)
+    window(side_ref, 0, SLOT, 1 - core, own, limits, qt_ref, m_ref, l_ref, acc_ref)
 
 
 def far_kernel(meta_ref, kv_ref, ids_ref, qt_ref, m_in, l_in, acc_in, m_ref, l_ref, acc_ref):
@@ -141,36 +157,15 @@
     l_ref[...] = l_in[...]
     acc_ref[...] = acc_in[...]
     own = meta_ref[0]
-    window(kv_ref, NEAR, own % 2, own, starts_of(ids_ref, own), qt_ref, m_ref, l_ref, acc_ref)
-
-
-def last_kernel(meta_ref, table_ref, near_ref, near_side_ref, far_ref, far_side_ref, two_ref, three_ref, ids_ref,
-                qt_ref, m_in, l_in, acc_in, out_ref, m_ref, l_ref, acc_ref, prefix_ref):
+    window(kv_ref, NEAR, ROWS, own % 2, own, starts_of(ids_ref, own), qt_ref, m_ref, l_ref, acc_ref)
+
+
+def last_kernel(meta_ref, kv_ref, ids_ref, qt_ref, m_in, l_in, acc_in, out_ref, m_ref, l_ref, acc_ref):
     m_ref[...] = m_in[...]
     l_ref[...] = l_in[...]
     acc_ref[...] = acc_in[...]
     own = meta_ref[0]
-    core, x = own % 2, own // (2 * NY)
-    for i in range(PAGES):
-        page = table_ref[i]
-        yy = (page // 2) % NY
-        back = (x + NX - page // (2 * NY)) % NX
-        side = jnp.where(page % 2 == core, 0, 1)
-        in_slot = pl.ds(pl.multiple_of(yy * SLOT + ROWS, PAGE), PAGE)
-        in_page = pl.ds(pl.multiple_of((side * NY + yy) * PAGE, PAGE), PAGE)
-        into = slice(i * PAGE, (i + 1) * PAGE)
-        places = [
-            (near_ref, in_slot), (near_side_ref, in_slot), (far_ref, in_slot), (far_side_ref, in_slot),
-            (two_ref, in_page), (three_ref, in_page),
-        ]
-        for n, (ref, rows) in enumerate(places):
-
-            @pl.when(jnp.where(back < 2, 2 * back + side, back + 2) == n)
-            def _():
-                prefix_ref[into, :] = ref[rows, :]
-
-    fold(prefix_ref[:, :D], prefix_ref[:, D:], None, qt_ref, m_ref, l_ref, acc_ref)
-    window(far_side_ref, NEAR, 1 - core, own, starts_of(ids_ref, own), qt_ref, m_ref, l_ref, acc_ref)
+    window(kv_ref, NEAR, ROWS, 1 - own % 2, own, starts_of(ids_ref, own), qt_ref, m_ref, l_ref, acc_ref)
     result = (acc_ref[...] * (1.0 / l_ref[...])).astype(jnp.bfloat16)
     for g in range(GROUP):
         out_ref[:, g * D:(g + 1) * D] = result[:, g * ROWS:(g + 1) * ROWS].T
@@ -187,25 +182,21 @@
 def per_device(queries, branch_key_value, branch_ids, pool, page_table):
     me = lax.axis_index("seq")
     y = (me // 2) % NY
-    page = pool.reshape(PAGE, PAIR)
-    raw = jnp.transpose(branch_key_value, (1, 0, 2))
+    page = pool.reshape(1, PAGE, PAIR)
+    raw = jnp.concatenate([jnp.transpose(branch_key_value, (1, 0, 2)), page], axis=0)
     one_raw = lax.ppermute(raw, "seq", x_ring(1))
-    wide = jnp.concatenate([jnp.transpose(queries, (1, 0, 2)), raw, one_raw], axis=2)
+    wide = jnp.concatenate([jnp.transpose(queries, (1, 0, 2)), raw[:8], one_raw[:8]], axis=2)
     wide = lax.all_to_all(wide, "head", split_axis=0, concat_axis=0, tiled=True).reshape(ROWS, -1)
     own, before = wide[:, GROUP * D:GROUP * D + PAIR], wide[:, GROUP * D + PAIR:]
+    two_page = lax.ppermute(page, "seq", x_ring(2))
+    three_page = lax.ppermute(page, "seq", x_ring(3))
     target = jnp.arange(NY, dtype=jnp.int32)[:, None, None]
     block = jnp.where(target > y, own[None], before[None])
-    send = jnp.concatenate([block, jnp.broadcast_to(page[None], (NY, PAGE, PAIR))], axis=1)
+    pages = jnp.concatenate([page, one_raw[8:], two_page, three_page], axis=0).reshape(1, NX * PAGE, PAIR)
+    send = jnp.concatenate([block, jnp.broadcast_to(pages, (NY, NX * PAGE, PAIR))], axis=1)
     near = lax.all_to_all(send, "seq", split_axis=0, concat_axis=0, tiled=True, axis_index_groups=Y_GROUPS)
-    far = lax.ppermute(near, "seq", x_ring(1))
     later, _ = lax.optimization_barrier((own, send))
     side = lax.ppermute(later, "seq", SWAP)
-    near_side = lax.ppermute(near, "seq", SWAP)
-    far_side = lax.ppermute(far, "seq", SWAP)
-    pages = jnp.concatenate([near[:, ROWS:], near_side[:, ROWS:]], axis=0).reshape(2 * NY * PAGE, PAIR)
-    two_pages = lax.ppermute(pages, "seq", x_ring(2))
-    three_pages = lax.ppermute(pages, "seq", x_ring(3))
-    near, near_side, far, far_side = (a.reshape(NY * SLOT, PAIR) for a in (near, near_side, far, far_side))
 
     ids = branch_ids.reshape(2 * NX * NY, ROWS)
     meta = me.astype(jnp.int32).reshape(1)
@@ -224,15 +215,23 @@
         cost_estimate=cost(256),
         name="own_chip",
     )(meta, own, side, ids, wide)
+    near, now = lax.optimization_barrier((near, now))
+    far = lax.ppermute(near[:, :ROWS], "seq", x_ring(1))
+    near = near.reshape(NY * SLOT, PAIR)
+    near_side = lax.ppermute(near, "seq", SWAP)
     now = pl.pallas_call(
         near_kernel,
         out_shape=state,
-        in_specs=[SM] + [VM] * 7,
+        in_specs=[SM, SM] + [VM] * 7,
         out_specs=[VM] * 3,
-        compiler_params=params,
-        cost_estimate=cost(2048),
-        name="near_window",
-    )(meta, near, near_side, ids, qt, *now)
+        scratch_shapes=[pltpu.VMEM((PAGES * PAGE, PAIR), jnp.bfloat16)],
+        compiler_params=params,
+        cost_estimate=cost(2560),
+        name="near_window_and_prefix",
+    )(meta, page_table.reshape(PAGES), near, near_side, ids, qt, *now)
+    far, now = lax.optimization_barrier((far, now))
+    far = far.reshape(NY * ROWS, PAIR)
+    far_side = lax.ppermute(far, "seq", SWAP)
     now = pl.pallas_call(
         far_kernel,
         out_shape=state,
@@ -245,18 +244,17 @@
     out = pl.pallas_call(
         last_kernel,
         out_shape=jax.ShapeDtypeStruct((ROWS, GROUP * D), jnp.bfloat16),
-        in_specs=[SM, SM] + [VM] * 11,
+        in_specs=[SM] + [VM] * 6,
         out_specs=VM,
         scratch_shapes=[
             pltpu.VMEM((1, QR), jnp.float32),
             pltpu.VMEM((1, QR), jnp.float32),
             pltpu.VMEM((D, QR), jnp.float32),
-            pltpu.VMEM((PAGES * PAGE, PAIR), jnp.bfloat16),
         ],
         compiler_params=params,
-        cost_estimate=cost(1536),
-        name="far_other_core_and_prefix",
-    )(meta, page_table.reshape(PAGES), near, near_side, far, far_side, two_pages, three_pages, ids, qt, *now)
+        cost_estimate=cost(1024),
+        name="far_other_core",
+    )(meta, far_side, ids, qt, *now)
     out = lax.all_to_all(out.reshape(8, ROWS // 8, GROUP * D), "head", split_axis=0, concat_axis=0, tiled=True)
     return jnp.transpose(out, (1, 0, 2))
 

time: 110 us -> 103 us (0.936); the launches traced: 110 us -> 101 us
  blocking collectives: 39.7 us -> 15.7 us
  waiting for transfers between devices: 21.7 us -> 32.8 us
  starting transfers between devices: 32 us -> 37.5 us
  Pallas kernels: 12.2 us -> 9.55 us
  other arithmetic: 0.94 us -> 2.57 us
    all_to_all x1 -> x0, blocking collectives: 23 us -> none  [per_device(): lax.all_to_all(send, 'seq', split_axis=0, concat_axis=0, tiled=True, axis...]
    all_to_all x0 -> x1, waiting for transfers between devices: none -> 16.6 us  [per_device(): lax.all_to_all(send, 'seq', split_axis=0, concat_axis=0, tiled=True, axis...]
    all_to_all x1, waiting for transfers between devices: 13.5 us -> 3.45 us  [per_device(): lax.all_to_all(wide, 'head', split_axis=0, concat_axis=0, tiled=True)]
    all_to_all x0 -> x1, starting transfers between devices: none -> 7.23 us  [per_device(): lax.all_to_all(send, 'seq', split_axis=0, concat_axis=0, tiled=True, axis...]
    pallas_call x1, Pallas kernels: 5.11 us -> 1.47 us  [per_device(): pl.pallas_call(last_kernel, out_shape=jax.ShapeDtypeStruct((ROWS, GROUP *...]
    ppermute x3, waiting for transfers between devices: 6.55 us -> 10.2 us  [the longest x1 6.52 us: per_device(): far = lax.ppermute(near[:, :ROWS], 'seq', x_ring(1))]
    pallas_call x1, Pallas kernels: 4.16 us -> 6.07 us  [per_device(): pl.pallas_call(near_kernel, out_shape=state, in_specs=[SM, SM] + [VM] * 7...]
    concatenate x3 -> x4, other arithmetic: 0.83 us -> 2.45 us  [the longest x1 0.95 us: per_device(): jnp.concatenate([block, jnp.broadcast_to(pages, (NY, NX * PAGE, PAIR))],...]
  transfers between devices with their start and end apart: 8 -> 9, of which waited for: 4 -> 8; matrix products, arithmetic and copies ran while one was open for 1% -> 1% of each run, Pallas kernels for 6% -> 8%
where the time goes in v9:
time: 103 us; the launch traced here: 101 us
  starting transfers between devices  37.5 us (36%)
  waiting for transfers between devices  32.8 us (32%)
  blocking collectives  15.7 us (15%)
  Pallas kernels  9.55 us (9%)
  local copies, waits for them, and re-layouts  2.89 us (3%)
  other arithmetic  2.57 us (2%)
    all_to_all x1, waiting for transfers between devices, per_device(): lax.all_to_all(send, 'seq', split_axis=0, concat_axis=0, tiled=True, axis...  16.6 us
    all_to_all x1, blocking collectives, per_device(): lax.all_to_all(out.reshape(8, ROWS // 8, GROUP * D), 'head', split_axis=0...  15.7 us
    ppermute x1, starting transfers between devices, per_device(): one_raw = lax.ppermute(raw, 'seq', x_ring(1))  7.75 us
    all_to_all x1, starting transfers between devices, per_device(): lax.all_to_all(send, 'seq', split_axis=0, concat_axis=0, tiled=True, axis...  7.23 us
    all_to_all x1, starting transfers between devices, per_device(): lax.all_to_all(wide, 'head', split_axis=0, concat_axis=0, tiled=True)  6.84 us
    ppermute x1, waiting for transfers between devices, per_device(): far = lax.ppermute(near[:, :ROWS], 'seq', x_ring(1))  6.52 us
    pallas_call x1, Pallas kernels, per_device(): pl.pallas_call(near_kernel, out_shape=state, in_specs=[SM, SM] + [VM] * 7...  6.07 us
    ppermute x1, starting transfers between devices, per_device(): far = lax.ppermute(near[:, :ROWS], 'seq', x_ring(1))  3.6 us
  transfers between devices with their start and end apart: 9, of which 8 were waited for; matrix products, arithmetic and copies ran while one was open for 1% of the time, Pallas kernels for 8%

profile of v9, /device:TPU:6, one launch (start us, length us, event | category | flops | bytes accessed | tf_op | source)
XLA Modules:
  0.0 101.1 jit_solution(12714449341059548326)
XLA Ops:
  0.0 0.9 copy.17
  0.9 0.7 pad_maximum_fusion.2
  1.6 7.7 %collective-permute-start = (bf16[9,16,256]{2,1,0:T(8,128)(2,1)S(1)}, bf16[9,16,256]{2,1,0:T(8,128)(2,1)S(1)}, u32[]{:S(2)}, u32[]{:S(2)}) collective-permute-start(bf16[9,16,256]{2,1,0:T(8,128)(2,1)S(1)} %pad_maximum_fusion.2), channel_id=1, source_target_pairs={{0,128},{8,136},{16,144},{24,152},{32,160},{40,168},{48,176},{56,1... | collective-permute-start | bytes 221192 | tf_op jit(solution)/shard_map/ppermute | solution.py:187
  9.3 1.1 %copy.16 = bf16[16,8,1024]{2,0,1:T(8,128)(2,1)S(1)} copy(bf16[16,8,1024]{2,1,0:T(8,128)(2,1)} %param.5) | data formatting | bytes 524288 | tf_op args[0]
  10.4 0.9 collective-permute-done
  11.3 0.8 pad_maximum_fusion.1
  12.1 6.8 %all-to-all-start = ((bf16[8,16,1536]{2,1,0:T(8,128)(2,1)}), bf16[8,16,1536]{2,1,0:T(8,128)(2,1)S(1)}, u32[]{:S(2)}, u32[]{:S(2)}) async-start(bf16[8,16,1536]{2,1,0:T(8,128)(2,1)} %pad_maximum_fusion.1), calls=%async_computation | async-start | bytes 786432 | tf_op jit(solution)/shard_map/all_to_all | solution.py:189
  18.9 0.0 copy-done.2
  18.9 3.3 %collective-permute-start.1 = (bf16[1,16,256]{2,1,0:T(8,128)(2,1)S(1)}, bf16[1,16,256]{2,1,0:T(8,128)(2,1)S(1)}, u32[]{:S(2)}, u32[]{:S(2)}) collective-permute-start(bf16[1,16,256]{2,1,0:T(8,128)(2,1)S(1)} %bitcast.34), channel_id=1, source_target_pairs={{0,256},{8,264},{16,272},{24,280},{32,288},{40,296},{48,304},{56,3... | collective-permute-start | bytes 24584 | tf_op jit(solution)/shard_map/ppermute | solution.py:191
  22.2 3.0 %collective-permute-start.2 = (bf16[1,16,256]{2,1,0:T(8,128)(2,1)S(1)}, bf16[1,16,256]{2,1,0:T(8,128)(2,1)S(1)}, u32[]{:S(2)}, u32[]{:S(2)}) collective-permute-start(bf16[1,16,256]{2,1,0:T(8,128)(2,1)S(1)} %bitcast.35), channel_id=1, source_target_pairs={{0,384},{8,392},{16,400},{24,408},{32,416},{40,424},{48,432},{56,4... | collective-permute-start | bytes 24584 | tf_op jit(solution)/shard_map/ppermute | solution.py:192
  25.3 0.6 collective-permute-done.1
  26.0 3.0 %collective-permute-done.2 = bf16[1,16,256]{2,1,0:T(8,128)(2,1)S(1)} collective-permute-done((bf16[1,16,256]{2,1,0:T(8,128)(2,1)S(1)}, bf16[1,16,256]{2,1,0:T(8,128)(2,1)S(1)}, u32[]{:S(2)}, u32[]{:S(2)}) %collective-permute-start.2) | collective-permute-done | bytes 8224 | tf_op jit(solution)/shard_map/ppermute | solution.py:192
  29.0 3.4 %all-to-all-done = bf16[8,16,1536]{2,1,0:T(8,128)(2,1)S(1)} async-done(((bf16[8,16,1536]{2,1,0:T(8,128)(2,1)}), bf16[8,16,1536]{2,1,0:T(8,128)(2,1)S(1)}, u32[]{:S(2)}, u32[]{:S(2)}) %all-to-all-start) | async-done | bytes 393248 | tf_op jit(solution)/shard_map/all_to_all | solution.py:189
  32.5 0.1 broadcast_select_fusion
  32.6 1.0 pad_maximum_fusion
  33.6 7.2 %all-to-all-start.1 = ((bf16[8,192,256]{2,1,0:T(8,128)(2,1)}), bf16[8,192,256]{2,1,0:T(8,128)(2,1)S(1)}, u32[]{:S(2)}, u32[]{:S(2)}) async-start(bf16[8,192,256]{2,1,0:T(8,128)(2,1)} %pad_maximum_fusion), calls=%async_computation.1 | async-start | bytes 1572864 | tf_op jit(solution)/shard_map/all_to_all | solution.py:197
  40.8 1.9 %collective-permute-start.3 = (bf16[128,256]{1,0:T(8,128)(2,1)S(1)}, bf16[128,256]{1,0:T(8,128)(2,1)S(1)}, u32[]{:S(2)}, u32[]{:S(2)}) collective-permute-start(bf16[128,256]{1,0:T(8,128)(2,1)S(1)} %get-tuple-element.24.mine_ref), channel_id=1, source_target_pairs={{0,8},{8,0},{16,24},{24,16},{32,40},{40,32},{48,56},{56,48},{64,72... | collective-permute-start | bytes 196616 | tf_op jit(solution)/shard_map/ppermute | solution.py:199
  42.7 1.2 %collective-permute-done.3.side_ref = bf16[128,256]{1,0:T(8,128)(2,1)S(1)} collective-permute-done((bf16[128,256]{1,0:T(8,128)(2,1)S(1)}, bf16[128,256]{1,0:T(8,128)(2,1)S(1)}, u32[]{:S(2)}, u32[]{:S(2)}) %collective-permute-start.3) | collective-permute-done | bytes 65568 | tf_op jit(solution)/shard_map/ppermute | solution.py:199
  43.9 0.0 copy-done
  43.9 0.7 own_chip.1
  44.6 16.6 %all-to-all-done.1 = bf16[8,192,256]{2,1,0:T(8,128)(2,1)S(1)} async-done(((bf16[8,192,256]{2,1,0:T(8,128)(2,1)}), bf16[8,192,256]{2,1,0:T(8,128)(2,1)S(1)}, u32[]{:S(2)}, u32[]{:S(2)}) %all-to-all-start.1) | async-done | bytes 786464 | tf_op jit(solution)/shard_map/all_to_all | solution.py:197
  61.2 1.9 %collective-permute-start.5 = (bf16[1536,256]{1,0:T(8,128)(2,1)S(1)}, bf16[1536,256]{1,0:T(8,128)(2,1)S(1)}, u32[]{:S(2)}, u32[]{:S(2)}) collective-permute-start(bf16[1536,256]{1,0:T(8,128)(2,1)S(1)} %bitcast.16), channel_id=1, source_target_pairs={{0,8},{8,0},{16,24},{24,16},{32,40},{40,32},{48,56},{56,48},{64,72... | collective-permute-start | bytes 2359304 | tf_op jit(solution)/shard_map/ppermute | solution.py:221
  63.1 3.6 %collective-permute-start.4 = (bf16[8,128,256]{2,1,0:T(8,128)(2,1)S(1)}, bf16[8,128,256]{2,1,0:T(8,128)(2,1)S(1)}, u32[]{:S(2)}, u32[]{:S(2)}) collective-permute-start(bf16[8,128,256]{2,1,0:T(8,128)(2,1)S(1)} %slice.19), channel_id=1, source_target_pairs={{0,128},{8,136},{16,144},{24,152},{32,160},{40,168},{48,176},{56,1... | collective-permute-start | bytes 1572872 | tf_op jit(solution)/shard_map/ppermute | solution.py:219
  66.7 0.0 collective-permute-done.5.side_ref
  66.8 6.1 %near_window_and_prefix.1 = (f32[1,1024]{1,0:T(1,128)S(1)}, f32[1,1024]{1,0:T(1,128)S(1)}, f32[128,1024]{1,0:T(8,128)S(1)}) custom-call(s32[1]{0:T(128)} %bitcast.meta_ref, s32[32]{0:T(128)S(1)} %bitcast.27, bf16[1536,256]{1,0:T(8,128)(2,1)S(1)} %bitcast.17, bf16[1536,256]{1,0:T(8,128)(2,1)S(1)} %collective-permute-done.5.side_ref, s32[64,128]{1,0:T(8,128)S(1)} %bitcast.22, ...), custom_call_target="tpu_custom_call" | custom-call | flops 1342177280 | bytes 1048576 | tf_op jit(solution)/shard_map/near_window_and_prefix/pallas_call | solution.py:222
  72.8 6.5 %collective-permute-done.4 = bf16[8,128,256]{2,1,0:T(8,128)(2,1)S(1)} collective-permute-done((bf16[8,128,256]{2,1,0:T(8,128)(2,1)S(1)}, bf16[8,128,256]{2,1,0:T(8,128)(2,1)S(1)}, u32[]{:S(2)}, u32[]{:S(2)}) %collective-permute-start.4) | collective-permute-done | bytes 524320 | tf_op jit(solution)/shard_map/ppermute | solution.py:219
  79.4 1.9 %collective-permute-start.6 = (bf16[1024,256]{1,0:T(8,128)(2,1)S(1)}, bf16[1024,256]{1,0:T(8,128)(2,1)S(1)}, u32[]{:S(2)}, u32[]{:S(2)}) collective-permute-start(bf16[1024,256]{1,0:T(8,128)(2,1)S(1)} %bitcast.25), channel_id=1, source_target_pairs={{0,8},{8,0},{16,24},{24,16},{32,40},{40,32},{48,56},{56,48},{64,72... | collective-permute-start | bytes 1572872 | tf_op jit(solution)/shard_map/ppermute | solution.py:234
  81.3 1.3 %far_window.1 = (f32[1,1024]{1,0:T(1,128)S(1)}, f32[1,1024]{1,0:T(1,128)S(1)}, f32[128,1024]{1,0:T(8,128)S(1)}) custom-call(s32[1]{0:T(128)} %bitcast.meta_ref, bf16[1024,256]{1,0:T(8,128)(2,1)S(1)} %bitcast.26, s32[64,128]{1,0:T(8,128)S(1)} %bitcast.23, bf16[256,1024]{1,0:T(8,128)(2,1)S(1)} %get-tuple-element.29.qt_ref, ...), custom_call_target="tpu_custom_call" | custom-call | flops 536870912 | bytes 1048576 | tf_op jit(solution)/shard_map/far_window/pallas_call | solution.py:235
  82.6 0.5 collective-permute-done.6.kv_ref
  83.2 1.5 %far_other_core.1 = bf16[128,1024]{1,0:T(8,128)(2,1)S(1)} custom-call(s32[1]{0:T(128)} %bitcast.meta_ref, bf16[1024,256]{1,0:T(8,128)(2,1)S(1)} %collective-permute-done.6.kv_ref, s32[64,128]{1,0:T(8,128)S(1)} %bitcast.24, bf16[256,1024]{1,0:T(8,128)(2,1)S(1)} %get-tuple-element.29.qt_ref, f32[1,1024]{1,0:T(1,128)S(1)} %get-tuple-element.40.m_in, ...), custom_call_target="tpu_custom_call" | custom-call | flops 536870912 | bytes 1048576 | tf_op jit(solution)/shard_map/far_other_core/pallas_call | solution.py:244
  84.6 15.7 %all_to_all.15 = bf16[8,16,1024]{2,1,0:T(8,128)(2,1)S(1)} all-to-all(bf16[8,16,1024]{2,1,0:T(8,128)(2,1)S(1)} %bitcast.20), channel_id=1, replica_groups=mesh['seq'=64,'head'=8] {'head'}, dimensions={0} | all-to-all | bytes 524288 | tf_op jit(solution)/shard_map/all_to_all | solution.py:258
  100.3 0.9 copy.13
  (11 shorter events, 0.1 us)
Async XLA Ops:
  1.6 9.7 %collective-permute-start = (bf16[9,16,256]{2,1,0:T(8,128)(2,1)S(1)}, bf16[9,16,256]{2,1,0:T(8,128)(2,1)S(1)}, u32[]{:S(2)}, u32[]{:S(2)}) collective-permute-start(bf16[9,16,256]{2,1,0:T(8,128)(2,1)S(1)} %pad_maximum_fusion.2), channel_id=1, source_target_pairs={{0,128},{8,136},{16,144},{24,152},{32,160},{40,168},{48,176},{56,1... | collective-permute-start | bytes 221192 | tf_op jit(solution)/shard_map/ppermute | solution.py:187
  11.3 7.6 %copy-start.2 = (bf16[1,16,1,256]{3,1,2,0:T(8,128)(2,1)S(1)}, bf16[1,16,1,256]{3,1,2,0:T(8,128)(2,1)}, u32[]{:S(2)}) copy-start(bf16[1,16,1,256]{3,1,2,0:T(8,128)(2,1)} %param.8) | copy-start | bytes 24580
  12.1 20.4 %all-to-all-start = ((bf16[8,16,1536]{2,1,0:T(8,128)(2,1)}), bf16[8,16,1536]{2,1,0:T(8,128)(2,1)S(1)}, u32[]{:S(2)}, u32[]{:S(2)}) async-start(bf16[8,16,1536]{2,1,0:T(8,128)(2,1)} %pad_maximum_fusion.1), calls=%async_computation | async-start | bytes 786432 | tf_op jit(solution)/shard_map/all_to_all | solution.py:189
  18.9 7.0 %collective-permute-start.1 = (bf16[1,16,256]{2,1,0:T(8,128)(2,1)S(1)}, bf16[1,16,256]{2,1,0:T(8,128)(2,1)S(1)}, u32[]{:S(2)}, u32[]{:S(2)}) collective-permute-start(bf16[1,16,256]{2,1,0:T(8,128)(2,1)S(1)} %bitcast.34), channel_id=1, source_target_pairs={{0,256},{8,264},{16,272},{24,280},{32,288},{40,296},{48,304},{56,3... | collective-permute-start | bytes 24584 | tf_op jit(solution)/shard_map/ppermute | solution.py:191
  22.2 6.8 %collective-permute-start.2 = (bf16[1,16,256]{2,1,0:T(8,128)(2,1)S(1)}, bf16[1,16,256]{2,1,0:T(8,128)(2,1)S(1)}, u32[]{:S(2)}, u32[]{:S(2)}) collective-permute-start(bf16[1,16,256]{2,1,0:T(8,128)(2,1)S(1)} %bitcast.35), channel_id=1, source_target_pairs={{0,384},{8,392},{16,400},{24,408},{32,416},{40,424},{48,432},{56,4... | collective-permute-start | bytes 24584 | tf_op jit(solution)/shard_map/ppermute | solution.py:192
  33.6 10.4 %copy-start = (s32[8192]{0:T(1024)S(1)}, s32[8192]{0:T(1024)}, u32[]{:S(2)}) copy-start(s32[8192]{0:T(1024)} %param.7) | copy-start | bytes 98308
  33.6 27.6 %all-to-all-start.1 = ((bf16[8,192,256]{2,1,0:T(8,128)(2,1)}), bf16[8,192,256]{2,1,0:T(8,128)(2,1)S(1)}, u32[]{:S(2)}, u32[]{:S(2)}) async-start(bf16[8,192,256]{2,1,0:T(8,128)(2,1)} %pad_maximum_fusion), calls=%async_computation.1 | async-start | bytes 1572864 | tf_op jit(solution)/shard_map/all_to_all | solution.py:197
  40.8 3.1 %collective-permute-start.3 = (bf16[128,256]{1,0:T(8,128)(2,1)S(1)}, bf16[128,256]{1,0:T(8,128)(2,1)S(1)}, u32[]{:S(2)}, u32[]{:S(2)}) collective-permute-start(bf16[128,256]{1,0:T(8,128)(2,1)S(1)} %get-tuple-element.24.mine_ref), channel_id=1, source_target_pairs={{0,8},{8,0},{16,24},{24,16},{32,40},{40,32},{48,56},{56,48},{64,72... | collective-permute-start | bytes 196616 | tf_op jit(solution)/shard_map/ppermute | solution.py:199
  43.9 22.8 %copy-start.1 = (s32[1,32]{1,0:T(1,128)S(1)}, s32[1,32]{1,0:T(1,128)}, u32[]{:S(2)}) copy-start(s32[1,32]{1,0:T(1,128)} %param.9) | copy-start | bytes 388
  61.2 5.6 %collective-permute-start.5 = (bf16[1536,256]{1,0:T(8,128)(2,1)S(1)}, bf16[1536,256]{1,0:T(8,128)(2,1)S(1)}, u32[]{:S(2)}, u32[]{:S(2)}) collective-permute-start(bf16[1536,256]{1,0:T(8,128)(2,1)S(1)} %bitcast.16), channel_id=1, source_target_pairs={{0,8},{8,0},{16,24},{24,16},{32,40},{40,32},{48,56},{56,48},{64,72... | collective-permute-start | bytes 2359304 | tf_op jit(solution)/shard_map/ppermute | solution.py:221
  63.1 16.2 %collective-permute-start.4 = (bf16[8,128,256]{2,1,0:T(8,128)(2,1)S(1)}, bf16[8,128,256]{2,1,0:T(8,128)(2,1)S(1)}, u32[]{:S(2)}, u32[]{:S(2)}) collective-permute-start(bf16[8,128,256]{2,1,0:T(8,128)(2,1)S(1)} %slice.19), channel_id=1, source_target_pairs={{0,128},{8,136},{16,144},{24,152},{32,160},{40,168},{48,176},{56,1... | collective-permute-start | bytes 1572872 | tf_op jit(solution)/shard_map/ppermute | solution.py:219
  79.4 3.8 %collective-permute-start.6 = (bf16[1024,256]{1,0:T(8,128)(2,1)S(1)}, bf16[1024,256]{1,0:T(8,128)(2,1)S(1)}, u32[]{:S(2)}, u32[]{:S(2)}) collective-permute-start(bf16[1024,256]{1,0:T(8,128)(2,1)S(1)} %bitcast.25), channel_id=1, source_target_pairs={{0,8},{8,0},{16,24},{24,16},{32,40},{40,32},{48,56},{56,48},{64,72... | collective-permute-start | bytes 1572872 | tf_op jit(solution)/shard_map/ppermute | solution.py:234

commit v10 on v7

--- a/solution.py
+++ b/solution.py
@@ -173,18 +173,16 @@
 def per_device(queries, branch_key_value, branch_ids, pool, page_table):
     me = lax.axis_index("seq")
     y = (me // 2) % NY
-    z = lax.axis_index("head")
-    gathered = lax.all_gather(jnp.transpose(queries, (1, 0, 2)), "head", axis=0, tiled=False)
-    query = lax.dynamic_index_in_dim(gathered, z, 1, keepdims=False).reshape(ROWS, GROUP * D)
     page = pool.reshape(1, PAGE, PAIR)
     raw = jnp.concatenate([jnp.transpose(branch_key_value, (1, 0, 2)), page], axis=0)
     two_raw = lax.ppermute(raw, "seq", x_ring(2))
     one_raw = lax.ppermute(raw, "seq", x_ring(1))
     three_page = lax.ppermute(page, "seq", x_ring(3))
     pages = jnp.concatenate([page, one_raw[8:], two_raw[8:], three_page], axis=0).reshape(NX * PAGE, PAIR)
-    wide = jnp.concatenate([raw[:8], one_raw[:8], two_raw[:8]], axis=2)
-    wide = lax.all_to_all(wide, "head", split_axis=0, concat_axis=0, tiled=True).reshape(ROWS, 3 * PAIR)
-    own, one_back, two_back = (wide[:, i * PAIR:(i + 1) * PAIR] for i in range(3))
+    wide = jnp.concatenate([jnp.transpose(queries, (1, 0, 2)), raw[:8], one_raw[:8], two_raw[:8]], axis=2)
+    wide = lax.all_to_all(wide, "head", split_axis=0, concat_axis=0, tiled=True).reshape(ROWS, -1)
+    at = GROUP * D
+    own, one_back, two_back = (wide[:, at + i * PAIR:at + (i + 1) * PAIR] for i in range(3))
     target = jnp.arange(NY, dtype=jnp.int32)[:, None, None]
     mixed = jnp.where(target > y, own[None], two_back[None])
     send = jnp.concatenate([
@@ -212,7 +210,7 @@
         compiler_params=params,
         cost_estimate=cost(256),
         name="near_keys",
-    )(meta, own, side, ids, query)
+    )(meta, own, side, ids, wide)
     kv, m = lax.optimization_barrier((kv, m))
     kv_side = lax.ppermute(kv, "seq", SWAP)
     m, l, acc = pl.pallas_call(

time: 117 us -> 105 us (0.90)
  the two profiles are of different devices: /device:TPU:1 before, /device:TPU:11 now
where the time goes in v10:
time: 105 us; the launch traced here: 104 us
  starting transfers between devices  43.8 us (42%)
  waiting for transfers between devices  29.2 us (28%)
  blocking collectives  15.8 us (15%)
  Pallas kernels  9.66 us (9%)
  local copies, waits for them, and re-layouts  2.91 us (3%)
  other arithmetic  2.79 us (3%)
    all_to_all x1, waiting for transfers between devices, per_device(): lax.all_to_all(send, 'seq', split_axis=0, concat_axis=0, tiled=True, axis...  17.2 us
    all_to_all x1, blocking collectives, per_device(): lax.all_to_all(out.reshape(8, ROWS // 8, GROUP * D), 'head', split_axis=0...  15.8 us
    ppermute x1, starting transfers between devices, per_device(): kv_side = lax.ppermute(kv, 'seq', SWAP)  10.6 us
    all_to_all x1, starting transfers between devices, per_device(): lax.all_to_all(wide, 'head', split_axis=0, concat_axis=0, tiled=True)  10 us
    all_to_all x1, waiting for transfers between devices, per_device(): lax.all_to_all(wide, 'head', split_axis=0, concat_axis=0, tiled=True)  8.32 us
    all_to_all x1, starting transfers between devices, per_device(): lax.all_to_all(send, 'seq', split_axis=0, concat_axis=0, tiled=True, axis...  7.12 us
    ppermute x1, starting transfers between devices, per_device(): side = lax.ppermute(later, 'seq', SWAP)  6.12 us
    pallas_call x1, Pallas kernels, per_device(): pl.pallas_call(last_kernel, out_shape=jax.ShapeDtypeStruct((ROWS, GROUP *...  5.26 us
  transfers between devices with their start and end apart: 7, of which 5 were waited for; matrix products, arithmetic and copies ran while one was open for 1% of the time, Pallas kernels for 4%

profile of v10, /device:TPU:11, one launch (start us, length us, event | category | flops | bytes accessed | tf_op | source)
XLA Modules:
  0.0 104.4 jit_solution(847378080837728766)
XLA Ops:
  0.0 0.9 copy.18
  0.9 0.7 pad_maximum_fusion.2
  1.6 0.0 copy-start.2
  1.6 3.8 %collective-permute-start.1 = (bf16[9,16,256]{2,1,0:T(8,128)(2,1)S(1)}, bf16[9,16,256]{2,1,0:T(8,128)(2,1)S(1)}, u32[]{:S(2)}, u32[]{:S(2)}) collective-permute-start(bf16[9,16,256]{2,1,0:T(8,128)(2,1)S(1)} %pad_maximum_fusion.2), channel_id=1, source_target_pairs={{0,256},{8,264},{16,272},{24,280},{32,288},{40,296},{48,304},{56,3... | collective-permute-start | bytes 221192 | tf_op jit(solution)/shard_map/ppermute | solution.py:178
  5.3 1.9 %collective-permute-start = (bf16[9,16,256]{2,1,0:T(8,128)(2,1)S(1)}, bf16[9,16,256]{2,1,0:T(8,128)(2,1)S(1)}, u32[]{:S(2)}, u32[]{:S(2)}) collective-permute-start(bf16[9,16,256]{2,1,0:T(8,128)(2,1)S(1)} %pad_maximum_fusion.2), channel_id=1, source_target_pairs={{0,128},{8,136},{16,144},{24,152},{32,160},{40,168},{48,176},{56,1... | collective-permute-start | bytes 221192 | tf_op jit(solution)/shard_map/ppermute | solution.py:179
  7.3 1.1 %copy.17 = bf16[16,8,1024]{2,0,1:T(8,128)(2,1)S(1)} copy(bf16[16,8,1024]{2,1,0:T(8,128)(2,1)} %param.5) | data formatting | bytes 524288 | tf_op args[0]
  8.4 0.0 collective-permute-done.1
  8.4 2.0 %collective-permute-done = bf16[9,16,256]{2,1,0:T(8,128)(2,1)S(1)} collective-permute-done((bf16[9,16,256]{2,1,0:T(8,128)(2,1)S(1)}, bf16[9,16,256]{2,1,0:T(8,128)(2,1)S(1)}, u32[]{:S(2)}, u32[]{:S(2)}) %collective-permute-start) | collective-permute-done | bytes 73760 | tf_op jit(solution)/shard_map/ppermute | solution.py:179
  10.4 0.8 pad_maximum_fusion.1
  11.2 10.0 %all-to-all-start = ((bf16[8,16,1792]{2,1,0:T(8,128)(2,1)}), bf16[8,16,1792]{2,1,0:T(8,128)(2,1)S(1)}, u32[]{:S(2)}, u32[]{:S(2)}) async-start(bf16[8,16,1792]{2,1,0:T(8,128)(2,1)} %pad_maximum_fusion.1), calls=%async_computation | async-start | bytes 917504 | tf_op jit(solution)/shard_map/all_to_all | solution.py:183
  21.3 0.0 copy-done.2
  21.3 4.3 %collective-permute-start.2 = (bf16[1,16,256]{2,1,0:T(8,128)(2,1)S(1)}, bf16[1,16,256]{2,1,0:T(8,128)(2,1)S(1)}, u32[]{:S(2)}, u32[]{:S(2)}) collective-permute-start(bf16[1,16,256]{2,1,0:T(8,128)(2,1)S(1)} %bitcast.31), channel_id=1, source_target_pairs={{0,384},{8,392},{16,400},{24,408},{32,416},{40,424},{48,432},{56,4... | collective-permute-start | bytes 24584 | tf_op jit(solution)/shard_map/ppermute | solution.py:180
  25.6 0.7 collective-permute-done.2
  26.3 8.3 %all-to-all-done = bf16[8,16,1792]{2,1,0:T(8,128)(2,1)S(1)} async-done(((bf16[8,16,1792]{2,1,0:T(8,128)(2,1)}), bf16[8,16,1792]{2,1,0:T(8,128)(2,1)S(1)}, u32[]{:S(2)}, u32[]{:S(2)}) %all-to-all-start) | async-done | bytes 458784 | tf_op jit(solution)/shard_map/all_to_all | solution.py:183
  34.7 0.1 broadcast_select_fusion
  34.9 1.2 %pad_maximum_fusion = bf16[8,320,256]{2,1,0:T(8,128)(2,1)} fusion(bf16[8,64,256]{2,1,0:T(8,128)(2,1)S(1)} %broadcast_in_dim.45, bf16[8,128,256]{2,1,0:T(8,128)(2,1)S(1)} %broadcast_select_fusion, bf16[8,128,256]{2,1,0:T(8,128)(2,1)S(1)} %broadcast_in_dim.40), kind=kLoop, calls=%fused_computation | loop fusion | flops 3932160 | bytes 2621440 | tf_op jit(solution)/shard_map/concatenate | solution.py:188
  36.0 0.0 copy-start
  36.0 7.1 %all-to-all-start.1 = ((bf16[8,320,256]{2,1,0:T(8,128)(2,1)}), bf16[8,320,256]{2,1,0:T(8,128)(2,1)S(1)}, u32[]{:S(2)}, u32[]{:S(2)}) async-start(bf16[8,320,256]{2,1,0:T(8,128)(2,1)} %pad_maximum_fusion), calls=%async_computation.1 | async-start | bytes 2621440 | tf_op jit(solution)/shard_map/all_to_all | solution.py:192
  43.1 6.1 %collective-permute-start.3 = (bf16[128,256]{1,0:T(8,128)(2,1)S(1)}, bf16[128,256]{1,0:T(8,128)(2,1)S(1)}, u32[]{:S(2)}, u32[]{:S(2)}) collective-permute-start(bf16[128,256]{1,0:T(8,128)(2,1)S(1)} %get-tuple-element.15.mine_ref), channel_id=1, source_target_pairs={{0,8},{8,0},{16,24},{24,16},{32,40},{40,32},{48,56},{56,48},{64,72... | collective-permute-start | bytes 196616 | tf_op jit(solution)/shard_map/ppermute | solution.py:195
  49.3 0.9 collective-permute-done.3.side_ref
  50.2 0.0 copy-done
  50.2 1.1 %near_keys.1 = (bf16[256,1024]{1,0:T(8,128)(2,1)S(1)}, f32[1,1024]{1,0:T(1,128)S(1)}, f32[1,1024]{1,0:T(1,128)S(1)}, f32[128,1024]{1,0:T(8,128)S(1)}) custom-call(s32[1]{0:T(128)} %bitcast.meta_ref, bf16[128,256]{1,0:T(8,128)(2,1)S(1)} %get-tuple-element.15.mine_ref, bf16[128,256]{1,0:T(8,128)(2,1)S(1)} %collective-permute-done.3.side_ref, ...), custom_call_target="tpu_custom_call" | custom-call | flops 134217728 | bytes 1048576 | tf_op jit(solution)/shard_map/near_keys/pallas_call | solution.py:205
  51.3 17.2 %all-to-all-done.1 = bf16[8,320,256]{2,1,0:T(8,128)(2,1)S(1)} async-done(((bf16[8,320,256]{2,1,0:T(8,128)(2,1)}), bf16[8,320,256]{2,1,0:T(8,128)(2,1)S(1)}, u32[]{:S(2)}, u32[]{:S(2)}) %all-to-all-start.1) | async-done | bytes 1310752 | tf_op jit(solution)/shard_map/all_to_all | solution.py:192
  68.5 10.6 %collective-permute-start.4 = (bf16[2560,256]{1,0:T(8,128)(2,1)S(1)}, bf16[2560,256]{1,0:T(8,128)(2,1)S(1)}, u32[]{:S(2)}, u32[]{:S(2)}) collective-permute-start(bf16[2560,256]{1,0:T(8,128)(2,1)S(1)} %bitcast.17), channel_id=1, source_target_pairs={{0,8},{8,0},{16,24},{24,16},{32,40},{40,32},{48,56},{56,48},{64,72... | collective-permute-start | bytes 3932168 | tf_op jit(solution)/shard_map/ppermute | solution.py:215
  79.2 0.0 copy-start.1
  79.2 3.2 %own_parity.1 = (f32[1,1024]{1,0:T(1,128)S(1)}, f32[1,1024]{1,0:T(1,128)S(1)}, f32[128,1024]{1,0:T(8,128)S(1)}) custom-call(s32[1]{0:T(128)} %bitcast.meta_ref, bf16[2560,256]{1,0:T(8,128)(2,1)S(1)} %bitcast.18, s32[64,128]{1,0:T(8,128)S(1)} %bitcast.22, bf16[256,1024]{1,0:T(8,128)(2,1)S(1)} %get-tuple-element.18.qt_ref, ...), custom_call_target="tpu_custom_call" | custom-call | flops 1073741824 | bytes 1048576 | tf_op jit(solution)/shard_map/own_parity/pallas_call | solution.py:216
  82.4 0.0 collective-permute-done.4.kv_ref
  82.5 0.0 copy-done.1
  82.5 5.3 %other_parity.1 = bf16[128,1024]{1,0:T(8,128)(2,1)S(1)} custom-call(s32[1]{0:T(128)} %bitcast.meta_ref, s32[32]{0:T(128)S(1)} %bitcast.24, bf16[2560,256]{1,0:T(8,128)(2,1)S(1)} %bitcast.19, bf16[2560,256]{1,0:T(8,128)(2,1)S(1)} %collective-permute-done.4.kv_ref, s32[64,128]{1,0:T(8,128)S(1)} %bitcast.23, bf16[256,1024]{1,0:T(8,128)(2,1)S(1)} %get-tuple-element.18.qt_ref, ...), custom_call_target="tpu_custom_call" | custom-call | flops 1342177280 | bytes 1048576 | tf_op jit(solution)/shard_map/other_parity/pallas_call | solution.py:225
  87.7 15.8 %all_to_all.15 = bf16[8,16,1024]{2,1,0:T(8,128)(2,1)S(1)} all-to-all(bf16[8,16,1024]{2,1,0:T(8,128)(2,1)S(1)} %bitcast.20), channel_id=1, replica_groups=mesh['seq'=64,'head'=8] {'head'}, dimensions={0} | all-to-all | bytes 524288 | tf_op jit(solution)/shard_map/all_to_all | solution.py:240
  103.5 0.9 copy.14
  (9 shorter events, 0.1 us)
Async XLA Ops:
  1.6 19.7 %copy-start.2 = (bf16[1,16,1,256]{3,1,2,0:T(8,128)(2,1)S(1)}, bf16[1,16,1,256]{3,1,2,0:T(8,128)(2,1)}, u32[]{:S(2)}) copy-start(bf16[1,16,1,256]{3,1,2,0:T(8,128)(2,1)} %param.8) | copy-start | bytes 24580
  1.6 6.8 %collective-permute-start.1 = (bf16[9,16,256]{2,1,0:T(8,128)(2,1)S(1)}, bf16[9,16,256]{2,1,0:T(8,128)(2,1)S(1)}, u32[]{:S(2)}, u32[]{:S(2)}) collective-permute-start(bf16[9,16,256]{2,1,0:T(8,128)(2,1)S(1)} %pad_maximum_fusion.2), channel_id=1, source_target_pairs={{0,256},{8,264},{16,272},{24,280},{32,288},{40,296},{48,304},{56,3... | collective-permute-start | bytes 221192 | tf_op jit(solution)/shard_map/ppermute | solution.py:178
  5.3 5.1 %collective-permute-start = (bf16[9,16,256]{2,1,0:T(8,128)(2,1)S(1)}, bf16[9,16,256]{2,1,0:T(8,128)(2,1)S(1)}, u32[]{:S(2)}, u32[]{:S(2)}) collective-permute-start(bf16[9,16,256]{2,1,0:T(8,128)(2,1)S(1)} %pad_maximum_fusion.2), channel_id=1, source_target_pairs={{0,128},{8,136},{16,144},{24,152},{32,160},{40,168},{48,176},{56,1... | collective-permute-start | bytes 221192 | tf_op jit(solution)/shard_map/ppermute | solution.py:179
  11.2 23.4 %all-to-all-start = ((bf16[8,16,1792]{2,1,0:T(8,128)(2,1)}), bf16[8,16,1792]{2,1,0:T(8,128)(2,1)S(1)}, u32[]{:S(2)}, u32[]{:S(2)}) async-start(bf16[8,16,1792]{2,1,0:T(8,128)(2,1)} %pad_maximum_fusion.1), calls=%async_computation | async-start | bytes 917504 | tf_op jit(solution)/shard_map/all_to_all | solution.py:183
  21.3 5.1 %collective-permute-start.2 = (bf16[1,16,256]{2,1,0:T(8,128)(2,1)S(1)}, bf16[1,16,256]{2,1,0:T(8,128)(2,1)S(1)}, u32[]{:S(2)}, u32[]{:S(2)}) collective-permute-start(bf16[1,16,256]{2,1,0:T(8,128)(2,1)S(1)} %bitcast.31), channel_id=1, source_target_pairs={{0,384},{8,392},{16,400},{24,408},{32,416},{40,424},{48,432},{56,4... | collective-permute-start | bytes 24584 | tf_op jit(solution)/shard_map/ppermute | solution.py:180
  36.0 14.1 %copy-start = (s32[8192]{0:T(1024)S(1)}, s32[8192]{0:T(1024)}, u32[]{:S(2)}) copy-start(s32[8192]{0:T(1024)} %param.7) | copy-start | bytes 98308
  36.0 32.5 %all-to-all-start.1 = ((bf16[8,320,256]{2,1,0:T(8,128)(2,1)}), bf16[8,320,256]{2,1,0:T(8,128)(2,1)S(1)}, u32[]{:S(2)}, u32[]{:S(2)}) async-start(bf16[8,320,256]{2,1,0:T(8,128)(2,1)} %pad_maximum_fusion), calls=%async_computation.1 | async-start | bytes 2621440 | tf_op jit(solution)/shard_map/all_to_all | solution.py:192
  43.1 7.0 %collective-permute-start.3 = (bf16[128,256]{1,0:T(8,128)(2,1)S(1)}, bf16[128,256]{1,0:T(8,128)(2,1)S(1)}, u32[]{:S(2)}, u32[]{:S(2)}) collective-permute-start(bf16[128,256]{1,0:T(8,128)(2,1)S(1)} %get-tuple-element.15.mine_ref), channel_id=1, source_target_pairs={{0,8},{8,0},{16,24},{24,16},{32,40},{40,32},{48,56},{56,48},{64,72... | collective-permute-start | bytes 196616 | tf_op jit(solution)/shard_map/ppermute | solution.py:195
  68.5 13.9 %collective-permute-start.4 = (bf16[2560,256]{1,0:T(8,128)(2,1)S(1)}, bf16[2560,256]{1,0:T(8,128)(2,1)S(1)}, u32[]{:S(2)}, u32[]{:S(2)}) collective-permute-start(bf16[2560,256]{1,0:T(8,128)(2,1)S(1)} %bitcast.17), channel_id=1, source_target_pairs={{0,8},{8,0},{16,24},{24,16},{32,40},{40,32},{48,56},{56,48},{64,72... | collective-permute-start | bytes 3932168 | tf_op jit(solution)/shard_map/ppermute | solution.py:215
  79.2 3.3 %copy-start.1 = (s32[1,32]{1,0:T(1,128)S(1)}, s32[1,32]{1,0:T(1,128)}, u32[]{:S(2)}) copy-start(s32[1,32]{1,0:T(1,128)} %param.9) | copy-start | bytes 388

commit v11 on v9

--- a/solution.py
+++ b/solution.py
@@ -197,6 +197,8 @@
     near = lax.all_to_all(send, "seq", split_axis=0, concat_axis=0, tiled=True, axis_index_groups=Y_GROUPS)
     later, _ = lax.optimization_barrier((own, send))
     side = lax.ppermute(later, "seq", SWAP)
+    far = lax.ppermute(near[:, :ROWS], "seq", x_ring(1))
+    near, own = lax.optimization_barrier((near, own))
 
     ids = branch_ids.reshape(2 * NX * NY, ROWS)
     meta = me.astype(jnp.int32).reshape(1)
@@ -216,7 +218,6 @@
         name="own_chip",
     )(meta, own, side, ids, wide)
     near, now = lax.optimization_barrier((near, now))
-    far = lax.ppermute(near[:, :ROWS], "seq", x_ring(1))
     near = near.reshape(NY * SLOT, PAIR)
     near_side = lax.ppermute(near, "seq", SWAP)
     now = pl.pallas_call(

time: 103 us -> 103 us (level)
  the two profiles are of different devices: /device:TPU:6 before, /device:TPU:1 now
where the time goes in v11:
time: 103 us
  starting transfers between devices  43 us (42%)
  waiting for transfers between devices  35.8 us (35%)
  blocking collectives  13.8 us (13%)
  Pallas kernels  4.28 us (4%)
  local copies, waits for them, and re-layouts  2.89 us (3%)
  other arithmetic  2.57 us (2%)
    all_to_all x1, waiting for transfers between devices, per_device(): lax.all_to_all(send, 'seq', split_axis=0, concat_axis=0, tiled=True, axis...  14.5 us
    all_to_all x1, blocking collectives, per_device(): lax.all_to_all(out.reshape(8, ROWS // 8, GROUP * D), 'head', split_axis=0...  13.8 us
    ppermute x1, waiting for transfers between devices, per_device(): far = lax.ppermute(near[:, :ROWS], 'seq', x_ring(1))  12.4 us
    all_to_all x1, starting transfers between devices, per_device(): lax.all_to_all(wide, 'head', split_axis=0, concat_axis=0, tiled=True)  10.2 us
    all_to_all x1, starting transfers between devices, per_device(): lax.all_to_all(send, 'seq', split_axis=0, concat_axis=0, tiled=True, axis...  6.95 us
    ppermute x1, starting transfers between devices, per_device(): side = lax.ppermute(later, 'seq', SWAP)  5.62 us
    ppermute x1, starting transfers between devices, per_device(): near_side = lax.ppermute(near, 'seq', SWAP)  5.45 us
    all_to_all x1, waiting for transfers between devices, per_device(): lax.all_to_all(wide, 'head', split_axis=0, concat_axis=0, tiled=True)  4.04 us
  transfers between devices with their start and end apart: 9, of which 6 were waited for; matrix products, arithmetic and copies ran while one was open for 1% of the time, Pallas kernels for 3%

profile of v11, /device:TPU:1, one launch (start us, length us, event | category | flops | bytes accessed | tf_op | source)
XLA Modules:
  0.0 102.6 jit_solution(982616451262898050)
XLA Ops:
  0.0 0.9 copy.17
  0.9 0.7 pad_maximum_fusion.2
  1.6 3.9 %collective-permute-start = (bf16[9,16,256]{2,1,0:T(8,128)(2,1)S(1)}, bf16[9,16,256]{2,1,0:T(8,128)(2,1)S(1)}, u32[]{:S(2)}, u32[]{:S(2)}) collective-permute-start(bf16[9,16,256]{2,1,0:T(8,128)(2,1)S(1)} %pad_maximum_fusion.2), channel_id=1, source_target_pairs={{0,128},{8,136},{16,144},{24,152},{32,160},{40,168},{48,176},{56,1... | collective-permute-start | bytes 221192 | tf_op jit(solution)/shard_map/ppermute | solution.py:187
  5.5 1.1 %copy.16 = bf16[16,8,1024]{2,0,1:T(8,128)(2,1)S(1)} copy(bf16[16,8,1024]{2,1,0:T(8,128)(2,1)} %param.5) | data formatting | bytes 524288 | tf_op args[0]
  6.6 1.9 %collective-permute-done = bf16[9,16,256]{2,1,0:T(8,128)(2,1)S(1)} collective-permute-done((bf16[9,16,256]{2,1,0:T(8,128)(2,1)S(1)}, bf16[9,16,256]{2,1,0:T(8,128)(2,1)S(1)}, u32[]{:S(2)}, u32[]{:S(2)}) %collective-permute-start) | collective-permute-done | bytes 73760 | tf_op jit(solution)/shard_map/ppermute | solution.py:187
  8.5 0.8 pad_maximum_fusion.1
  9.3 10.2 %all-to-all-start = ((bf16[8,16,1536]{2,1,0:T(8,128)(2,1)}), bf16[8,16,1536]{2,1,0:T(8,128)(2,1)S(1)}, u32[]{:S(2)}, u32[]{:S(2)}) async-start(bf16[8,16,1536]{2,1,0:T(8,128)(2,1)} %pad_maximum_fusion.1), calls=%async_computation | async-start | bytes 786432 | tf_op jit(solution)/shard_map/all_to_all | solution.py:189
  19.5 0.0 copy-done.2
  19.5 3.4 %collective-permute-start.1 = (bf16[1,16,256]{2,1,0:T(8,128)(2,1)S(1)}, bf16[1,16,256]{2,1,0:T(8,128)(2,1)S(1)}, u32[]{:S(2)}, u32[]{:S(2)}) collective-permute-start(bf16[1,16,256]{2,1,0:T(8,128)(2,1)S(1)} %bitcast.34), channel_id=1, source_target_pairs={{0,256},{8,264},{16,272},{24,280},{32,288},{40,296},{48,304},{56,3... | collective-permute-start | bytes 24584 | tf_op jit(solution)/shard_map/ppermute | solution.py:191
  23.0 2.8 %collective-permute-start.2 = (bf16[1,16,256]{2,1,0:T(8,128)(2,1)S(1)}, bf16[1,16,256]{2,1,0:T(8,128)(2,1)S(1)}, u32[]{:S(2)}, u32[]{:S(2)}) collective-permute-start(bf16[1,16,256]{2,1,0:T(8,128)(2,1)S(1)} %bitcast.35), channel_id=1, source_target_pairs={{0,384},{8,392},{16,400},{24,408},{32,416},{40,424},{48,432},{56,4... | collective-permute-start | bytes 24584 | tf_op jit(solution)/shard_map/ppermute | solution.py:192
  25.8 0.0 collective-permute-done.1
  25.8 1.9 %collective-permute-done.2 = bf16[1,16,256]{2,1,0:T(8,128)(2,1)S(1)} collective-permute-done((bf16[1,16,256]{2,1,0:T(8,128)(2,1)S(1)}, bf16[1,16,256]{2,1,0:T(8,128)(2,1)S(1)}, u32[]{:S(2)}, u32[]{:S(2)}) %collective-permute-start.2) | collective-permute-done | bytes 8224 | tf_op jit(solution)/shard_map/ppermute | solution.py:192
  27.7 4.0 %all-to-all-done = bf16[8,16,1536]{2,1,0:T(8,128)(2,1)S(1)} async-done(((bf16[8,16,1536]{2,1,0:T(8,128)(2,1)}), bf16[8,16,1536]{2,1,0:T(8,128)(2,1)S(1)}, u32[]{:S(2)}, u32[]{:S(2)}) %all-to-all-start) | async-done | bytes 393248 | tf_op jit(solution)/shard_map/all_to_all | solution.py:189
  31.7 0.1 broadcast_select_fusion
  31.9 1.0 pad_maximum_fusion
  32.8 7.0 %all-to-all-start.1 = ((bf16[8,192,256]{2,1,0:T(8,128)(2,1)}), bf16[8,192,256]{2,1,0:T(8,128)(2,1)S(1)}, u32[]{:S(2)}, u32[]{:S(2)}) async-start(bf16[8,192,256]{2,1,0:T(8,128)(2,1)} %pad_maximum_fusion), calls=%async_computation.1 | async-start | bytes 1572864 | tf_op jit(solution)/shard_map/all_to_all | solution.py:197
  39.8 5.6 %collective-permute-start.4 = (bf16[128,256]{1,0:T(8,128)(2,1)S(1)}, bf16[128,256]{1,0:T(8,128)(2,1)S(1)}, u32[]{:S(2)}, u32[]{:S(2)}) collective-permute-start(bf16[128,256]{1,0:T(8,128)(2,1)S(1)} %get-tuple-element.28.mine_ref), channel_id=1, source_target_pairs={{0,8},{8,0},{16,24},{24,16},{32,40},{40,32},{48,56},{56,48},{64,72... | collective-permute-start | bytes 196616 | tf_op jit(solution)/shard_map/ppermute | solution.py:199
  45.4 14.5 %all-to-all-done.1 = bf16[8,192,256]{2,1,0:T(8,128)(2,1)S(1)} async-done(((bf16[8,192,256]{2,1,0:T(8,128)(2,1)}), bf16[8,192,256]{2,1,0:T(8,128)(2,1)S(1)}, u32[]{:S(2)}, u32[]{:S(2)}) %all-to-all-start.1) | async-done | bytes 786464 | tf_op jit(solution)/shard_map/all_to_all | solution.py:197
  59.9 0.0 collective-permute-done.4.side_ref
  59.9 0.0 copy-done
  59.9 1.1 %own_chip.1 = (bf16[256,1024]{1,0:T(8,128)(2,1)S(1)}, f32[1,1024]{1,0:T(1,128)S(1)}, f32[1,1024]{1,0:T(1,128)S(1)}, f32[128,1024]{1,0:T(8,128)S(1)}) custom-call(s32[1]{0:T(128)} %bitcast.meta_ref, bf16[128,256]{1,0:T(8,128)(2,1)S(1)} %get-tuple-element.28.mine_ref, bf16[128,256]{1,0:T(8,128)(2,1)S(1)} %collective-permute-done.4.side_ref, ...), custom_call_target="tpu_custom_call" | custom-call | flops 134217728 | bytes 1048576 | tf_op jit(solution)/shard_map/own_chip/pallas_call | solution.py:211
  61.0 5.5 %collective-permute-start.5 = (bf16[1536,256]{1,0:T(8,128)(2,1)S(1)}, bf16[1536,256]{1,0:T(8,128)(2,1)S(1)}, u32[]{:S(2)}, u32[]{:S(2)}) collective-permute-start(bf16[1536,256]{1,0:T(8,128)(2,1)S(1)} %bitcast.16), channel_id=1, source_target_pairs={{0,8},{8,0},{16,24},{24,16},{32,40},{40,32},{48,56},{56,48},{64,72... | collective-permute-start | bytes 2359304 | tf_op jit(solution)/shard_map/ppermute | solution.py:222
  66.5 1.9 %collective-permute-start.3 = (bf16[8,128,256]{2,1,0:T(8,128)(2,1)S(1)}, bf16[8,128,256]{2,1,0:T(8,128)(2,1)S(1)}, u32[]{:S(2)}, u32[]{:S(2)}) collective-permute-start(bf16[8,128,256]{2,1,0:T(8,128)(2,1)S(1)} %slice.24), channel_id=1, source_target_pairs={{0,128},{8,136},{16,144},{24,152},{32,160},{40,168},{48,176},{56,1... | collective-permute-start | bytes 1572872 | tf_op jit(solution)/shard_map/ppermute | solution.py:200
  68.5 0.0 collective-permute-done.5.side_ref
  68.5 2.3 %near_window_and_prefix.1 = (f32[1,1024]{1,0:T(1,128)S(1)}, f32[1,1024]{1,0:T(1,128)S(1)}, f32[128,1024]{1,0:T(8,128)S(1)}) custom-call(s32[1]{0:T(128)} %bitcast.meta_ref, s32[32]{0:T(128)S(1)} %bitcast.27, bf16[1536,256]{1,0:T(8,128)(2,1)S(1)} %bitcast.17, bf16[1536,256]{1,0:T(8,128)(2,1)S(1)} %collective-permute-done.5.side_ref, s32[64,128]{1,0:T(8,128)S(1)} %bitcast.22, ...), custom_call_target="tpu_custom_call" | custom-call | flops 1342177280 | bytes 1048576 | tf_op jit(solution)/shard_map/near_window_and_prefix/pallas_call | solution.py:223
  70.8 12.4 %collective-permute-done.3 = bf16[8,128,256]{2,1,0:T(8,128)(2,1)S(1)} collective-permute-done((bf16[8,128,256]{2,1,0:T(8,128)(2,1)S(1)}, bf16[8,128,256]{2,1,0:T(8,128)(2,1)S(1)}, u32[]{:S(2)}, u32[]{:S(2)}) %collective-permute-start.3) | collective-permute-done | bytes 524320 | tf_op jit(solution)/shard_map/ppermute | solution.py:200
  83.2 2.7 %collective-permute-start.6 = (bf16[1024,256]{1,0:T(8,128)(2,1)S(1)}, bf16[1024,256]{1,0:T(8,128)(2,1)S(1)}, u32[]{:S(2)}, u32[]{:S(2)}) collective-permute-start(bf16[1024,256]{1,0:T(8,128)(2,1)S(1)} %bitcast.25), channel_id=1, source_target_pairs={{0,8},{8,0},{16,24},{24,16},{32,40},{40,32},{48,56},{56,48},{64,72... | collective-permute-start | bytes 1572872 | tf_op jit(solution)/shard_map/ppermute | solution.py:235
  85.9 0.4 far_window.1
  86.3 1.1 %collective-permute-done.6.kv_ref = bf16[1024,256]{1,0:T(8,128)(2,1)S(1)} collective-permute-done((bf16[1024,256]{1,0:T(8,128)(2,1)S(1)}, bf16[1024,256]{1,0:T(8,128)(2,1)S(1)}, u32[]{:S(2)}, u32[]{:S(2)}) %collective-permute-start.6) | collective-permute-done | bytes 524320 | tf_op jit(solution)/shard_map/ppermute | solution.py:235
  87.4 0.5 far_other_core.1
  87.9 13.8 %all_to_all.15 = bf16[8,16,1024]{2,1,0:T(8,128)(2,1)S(1)} all-to-all(bf16[8,16,1024]{2,1,0:T(8,128)(2,1)S(1)} %bitcast.20), channel_id=1, replica_groups=mesh['seq'=64,'head'=8] {'head'}, dimensions={0} | all-to-all | bytes 524288 | tf_op jit(solution)/shard_map/all_to_all | solution.py:259
  101.7 0.9 copy.13
  (11 shorter events, 0.1 us)
Async XLA Ops:
  1.6 6.9 %collective-permute-start = (bf16[9,16,256]{2,1,0:T(8,128)(2,1)S(1)}, bf16[9,16,256]{2,1,0:T(8,128)(2,1)S(1)}, u32[]{:S(2)}, u32[]{:S(2)}) collective-permute-start(bf16[9,16,256]{2,1,0:T(8,128)(2,1)S(1)} %pad_maximum_fusion.2), channel_id=1, source_target_pairs={{0,128},{8,136},{16,144},{24,152},{32,160},{40,168},{48,176},{56,1... | collective-permute-start | bytes 221192 | tf_op jit(solution)/shard_map/ppermute | solution.py:187
  8.5 11.0 %copy-start.2 = (bf16[1,16,1,256]{3,1,2,0:T(8,128)(2,1)S(1)}, bf16[1,16,1,256]{3,1,2,0:T(8,128)(2,1)}, u32[]{:S(2)}) copy-start(bf16[1,16,1,256]{3,1,2,0:T(8,128)(2,1)} %param.8) | copy-start | bytes 24580
  9.3 22.4 %all-to-all-start = ((bf16[8,16,1536]{2,1,0:T(8,128)(2,1)}), bf16[8,16,1536]{2,1,0:T(8,128)(2,1)S(1)}, u32[]{:S(2)}, u32[]{:S(2)}) async-start(bf16[8,16,1536]{2,1,0:T(8,128)(2,1)} %pad_maximum_fusion.1), calls=%async_computation | async-start | bytes 786432 | tf_op jit(solution)/shard_map/all_to_all | solution.py:189
  19.5 6.3 %collective-permute-start.1 = (bf16[1,16,256]{2,1,0:T(8,128)(2,1)S(1)}, bf16[1,16,256]{2,1,0:T(8,128)(2,1)S(1)}, u32[]{:S(2)}, u32[]{:S(2)}) collective-permute-start(bf16[1,16,256]{2,1,0:T(8,128)(2,1)S(1)} %bitcast.34), channel_id=1, source_target_pairs={{0,256},{8,264},{16,272},{24,280},{32,288},{40,296},{48,304},{56,3... | collective-permute-start | bytes 24584 | tf_op jit(solution)/shard_map/ppermute | solution.py:191
  23.0 4.7 %collective-permute-start.2 = (bf16[1,16,256]{2,1,0:T(8,128)(2,1)S(1)}, bf16[1,16,256]{2,1,0:T(8,128)(2,1)S(1)}, u32[]{:S(2)}, u32[]{:S(2)}) collective-permute-start(bf16[1,16,256]{2,1,0:T(8,128)(2,1)S(1)} %bitcast.35), channel_id=1, source_target_pairs={{0,384},{8,392},{16,400},{24,408},{32,416},{40,424},{48,432},{56,4... | collective-permute-start | bytes 24584 | tf_op jit(solution)/shard_map/ppermute | solution.py:192
  32.8 27.0 %copy-start = (s32[8192]{0:T(1024)S(1)}, s32[8192]{0:T(1024)}, u32[]{:S(2)}) copy-start(s32[8192]{0:T(1024)} %param.7) | copy-start | bytes 98308
  32.8 27.0 %all-to-all-start.1 = ((bf16[8,192,256]{2,1,0:T(8,128)(2,1)}), bf16[8,192,256]{2,1,0:T(8,128)(2,1)S(1)}, u32[]{:S(2)}, u32[]{:S(2)}) async-start(bf16[8,192,256]{2,1,0:T(8,128)(2,1)} %pad_maximum_fusion), calls=%async_computation.1 | async-start | bytes 1572864 | tf_op jit(solution)/shard_map/all_to_all | solution.py:197
  39.8 20.1 %collective-permute-start.4 = (bf16[128,256]{1,0:T(8,128)(2,1)S(1)}, bf16[128,256]{1,0:T(8,128)(2,1)S(1)}, u32[]{:S(2)}, u32[]{:S(2)}) collective-permute-start(bf16[128,256]{1,0:T(8,128)(2,1)S(1)} %get-tuple-element.28.mine_ref), channel_id=1, source_target_pairs={{0,8},{8,0},{16,24},{24,16},{32,40},{40,32},{48,56},{56,48},{64,72... | collective-permute-start | bytes 196616 | tf_op jit(solution)/shard_map/ppermute | solution.py:199
  59.9 8.6 %copy-start.1 = (s32[1,32]{1,0:T(1,128)S(1)}, s32[1,32]{1,0:T(1,128)}, u32[]{:S(2)}) copy-start(s32[1,32]{1,0:T(1,128)} %param.9) | copy-start | bytes 388
  61.0 7.4 %collective-permute-start.5 = (bf16[1536,256]{1,0:T(8,128)(2,1)S(1)}, bf16[1536,256]{1,0:T(8,128)(2,1)S(1)}, u32[]{:S(2)}, u32[]{:S(2)}) collective-permute-start(bf16[1536,256]{1,0:T(8,128)(2,1)S(1)} %bitcast.16), channel_id=1, source_target_pairs={{0,8},{8,0},{16,24},{24,16},{32,40},{40,32},{48,56},{56,48},{64,72... | collective-permute-start | bytes 2359304 | tf_op jit(solution)/shard_map/ppermute | solution.py:222
  66.5 16.6 %collective-permute-start.3 = (bf16[8,128,256]{2,1,0:T(8,128)(2,1)S(1)}, bf16[8,128,256]{2,1,0:T(8,128)(2,1)S(1)}, u32[]{:S(2)}, u32[]{:S(2)}) collective-permute-start(bf16[8,128,256]{2,1,0:T(8,128)(2,1)S(1)} %slice.24), channel_id=1, source_target_pairs={{0,128},{8,136},{16,144},{24,152},{32,160},{40,168},{48,176},{56,1... | collective-permute-start | bytes 1572872 | tf_op jit(solution)/shard_map/ppermute | solution.py:200
  83.2 4.2 %collective-permute-start.6 = (bf16[1024,256]{1,0:T(8,128)(2,1)S(1)}, bf16[1024,256]{1,0:T(8,128)(2,1)S(1)}, u32[]{:S(2)}, u32[]{:S(2)}) collective-permute-start(bf16[1024,256]{1,0:T(8,128)(2,1)S(1)} %bitcast.25), channel_id=1, source_target_pairs={{0,8},{8,0},{16,24},{24,16},{32,40},{40,32},{48,56},{56,48},{64,72... | collective-permute-start | bytes 1572872 | tf_op jit(solution)/shard_map/ppermute | solution.py:235

commit v12 on v11

--- a/solution.py
+++ b/solution.py
@@ -214,7 +214,7 @@
         in_specs=[SM] + [VM] * 4,
         out_specs=[VM] * 4,
         compiler_params=params,
-        cost_estimate=cost(256),
+        cost_estimate=cost(8),
         name="own_chip",
     )(meta, own, side, ids, wide)
     near, now = lax.optimization_barrier((near, now))
@@ -227,7 +227,7 @@
         out_specs=[VM] * 3,
         scratch_shapes=[pltpu.VMEM((PAGES * PAGE, PAIR), jnp.bfloat16)],
         compiler_params=params,
-        cost_estimate=cost(2560),
+        cost_estimate=cost(8),
         name="near_window_and_prefix",
     )(meta, page_table.reshape(PAGES), near, near_side, ids, qt, *now)
     far, now = lax.optimization_barrier((far, now))

time: 103 us -> 103 us (level)
  no operation moved by 1% of the time
where the time goes in v12:
time: 103 us
  starting transfers between devices  43 us (42%)
  waiting for transfers between devices  35.8 us (35%)
  blocking collectives  13.8 us (13%)
  Pallas kernels  4.28 us (4%)
  local copies, waits for them, and re-layouts  2.89 us (3%)
  other arithmetic  2.57 us (2%)
    all_to_all x1, waiting for transfers between devices, per_device(): lax.all_to_all(send, 'seq', split_axis=0, concat_axis=0, tiled=True, axis...  14.5 us
    all_to_all x1, blocking collectives, per_device(): lax.all_to_all(out.reshape(8, ROWS // 8, GROUP * D), 'head', split_axis=0...  13.8 us
    ppermute x1, waiting for transfers between devices, per_device(): far = lax.ppermute(near[:, :ROWS], 'seq', x_ring(1))  12.4 us
    all_to_all x1, starting transfers between devices, per_device(): lax.all_to_all(wide, 'head', split_axis=0, concat_axis=0, tiled=True)  10.2 us
    all_to_all x1, starting transfers between devices, per_device(): lax.all_to_all(send, 'seq', split_axis=0, concat_axis=0, tiled=True, axis...  6.95 us
    ppermute x1, starting transfers between devices, per_device(): side = lax.ppermute(later, 'seq', SWAP)  5.62 us
    ppermute x1, starting transfers between devices, per_device(): near_side = lax.ppermute(near, 'seq', SWAP)  5.45 us
    all_to_all x1, waiting for transfers between devices, per_device(): lax.all_to_all(wide, 'head', split_axis=0, concat_axis=0, tiled=True)  4.04 us
  transfers between devices with their start and end apart: 9, of which 6 were waited for; matrix products, arithmetic and copies ran while one was open for 1% of the time, Pallas kernels for 3%

profile of v12, /device:TPU:1, one launch (start us, length us, event | category | flops | bytes accessed | tf_op | source)
XLA Modules:
  0.0 102.6 jit_solution(5192458050603094366)
XLA Ops:
  0.0 0.9 copy.17
  0.9 0.7 pad_maximum_fusion.2
  1.6 3.9 %collective-permute-start = (bf16[9,16,256]{2,1,0:T(8,128)(2,1)S(1)}, bf16[9,16,256]{2,1,0:T(8,128)(2,1)S(1)}, u32[]{:S(2)}, u32[]{:S(2)}) collective-permute-start(bf16[9,16,256]{2,1,0:T(8,128)(2,1)S(1)} %pad_maximum_fusion.2), channel_id=1, source_target_pairs={{0,128},{8,136},{16,144},{24,152},{32,160},{40,168},{48,176},{56,1... | collective-permute-start | bytes 221192 | tf_op jit(solution)/shard_map/ppermute | solution.py:187
  5.5 1.1 %copy.16 = bf16[16,8,1024]{2,0,1:T(8,128)(2,1)S(1)} copy(bf16[16,8,1024]{2,1,0:T(8,128)(2,1)} %param.5) | data formatting | bytes 524288 | tf_op args[0]
  6.6 1.9 %collective-permute-done = bf16[9,16,256]{2,1,0:T(8,128)(2,1)S(1)} collective-permute-done((bf16[9,16,256]{2,1,0:T(8,128)(2,1)S(1)}, bf16[9,16,256]{2,1,0:T(8,128)(2,1)S(1)}, u32[]{:S(2)}, u32[]{:S(2)}) %collective-permute-start) | collective-permute-done | bytes 73760 | tf_op jit(solution)/shard_map/ppermute | solution.py:187
  8.5 0.8 pad_maximum_fusion.1
  9.3 10.2 %all-to-all-start = ((bf16[8,16,1536]{2,1,0:T(8,128)(2,1)}), bf16[8,16,1536]{2,1,0:T(8,128)(2,1)S(1)}, u32[]{:S(2)}, u32[]{:S(2)}) async-start(bf16[8,16,1536]{2,1,0:T(8,128)(2,1)} %pad_maximum_fusion.1), calls=%async_computation | async-start | bytes 786432 | tf_op jit(solution)/shard_map/all_to_all | solution.py:189
  19.5 0.0 copy-done.2
  19.5 3.4 %collective-permute-start.1 = (bf16[1,16,256]{2,1,0:T(8,128)(2,1)S(1)}, bf16[1,16,256]{2,1,0:T(8,128)(2,1)S(1)}, u32[]{:S(2)}, u32[]{:S(2)}) collective-permute-start(bf16[1,16,256]{2,1,0:T(8,128)(2,1)S(1)} %bitcast.34), channel_id=1, source_target_pairs={{0,256},{8,264},{16,272},{24,280},{32,288},{40,296},{48,304},{56,3... | collective-permute-start | bytes 24584 | tf_op jit(solution)/shard_map/ppermute | solution.py:191
  23.0 2.8 %collective-permute-start.2 = (bf16[1,16,256]{2,1,0:T(8,128)(2,1)S(1)}, bf16[1,16,256]{2,1,0:T(8,128)(2,1)S(1)}, u32[]{:S(2)}, u32[]{:S(2)}) collective-permute-start(bf16[1,16,256]{2,1,0:T(8,128)(2,1)S(1)} %bitcast.35), channel_id=1, source_target_pairs={{0,384},{8,392},{16,400},{24,408},{32,416},{40,424},{48,432},{56,4... | collective-permute-start | bytes 24584 | tf_op jit(solution)/shard_map/ppermute | solution.py:192
  25.8 0.0 collective-permute-done.1
  25.8 1.9 %collective-permute-done.2 = bf16[1,16,256]{2,1,0:T(8,128)(2,1)S(1)} collective-permute-done((bf16[1,16,256]{2,1,0:T(8,128)(2,1)S(1)}, bf16[1,16,256]{2,1,0:T(8,128)(2,1)S(1)}, u32[]{:S(2)}, u32[]{:S(2)}) %collective-permute-start.2) | collective-permute-done | bytes 8224 | tf_op jit(solution)/shard_map/ppermute | solution.py:192
  27.7 4.0 %all-to-all-done = bf16[8,16,1536]{2,1,0:T(8,128)(2,1)S(1)} async-done(((bf16[8,16,1536]{2,1,0:T(8,128)(2,1)}), bf16[8,16,1536]{2,1,0:T(8,128)(2,1)S(1)}, u32[]{:S(2)}, u32[]{:S(2)}) %all-to-all-start) | async-done | bytes 393248 | tf_op jit(solution)/shard_map/all_to_all | solution.py:189
  31.7 0.1 broadcast_select_fusion
  31.9 1.0 pad_maximum_fusion
  32.8 7.0 %all-to-all-start.1 = ((bf16[8,192,256]{2,1,0:T(8,128)(2,1)}), bf16[8,192,256]{2,1,0:T(8,128)(2,1)S(1)}, u32[]{:S(2)}, u32[]{:S(2)}) async-start(bf16[8,192,256]{2,1,0:T(8,128)(2,1)} %pad_maximum_fusion), calls=%async_computation.1 | async-start | bytes 1572864 | tf_op jit(solution)/shard_map/all_to_all | solution.py:197
  39.8 5.6 %collective-permute-start.4 = (bf16[128,256]{1,0:T(8,128)(2,1)S(1)}, bf16[128,256]{1,0:T(8,128)(2,1)S(1)}, u32[]{:S(2)}, u32[]{:S(2)}) collective-permute-start(bf16[128,256]{1,0:T(8,128)(2,1)S(1)} %get-tuple-element.28.mine_ref), channel_id=1, source_target_pairs={{0,8},{8,0},{16,24},{24,16},{32,40},{40,32},{48,56},{56,48},{64,72... | collective-permute-start | bytes 196616 | tf_op jit(solution)/shard_map/ppermute | solution.py:199
  45.4 14.5 %all-to-all-done.1 = bf16[8,192,256]{2,1,0:T(8,128)(2,1)S(1)} async-done(((bf16[8,192,256]{2,1,0:T(8,128)(2,1)}), bf16[8,192,256]{2,1,0:T(8,128)(2,1)S(1)}, u32[]{:S(2)}, u32[]{:S(2)}) %all-to-all-start.1) | async-done | bytes 786464 | tf_op jit(solution)/shard_map/all_to_all | solution.py:197
  59.9 0.0 collective-permute-done.4.side_ref
  59.9 0.0 copy-done
  59.9 1.1 %own_chip.1 = (bf16[256,1024]{1,0:T(8,128)(2,1)S(1)}, f32[1,1024]{1,0:T(1,128)S(1)}, f32[1,1024]{1,0:T(1,128)S(1)}, f32[128,1024]{1,0:T(8,128)S(1)}) custom-call(s32[1]{0:T(128)} %bitcast.meta_ref, bf16[128,256]{1,0:T(8,128)(2,1)S(1)} %get-tuple-element.28.mine_ref, bf16[128,256]{1,0:T(8,128)(2,1)S(1)} %collective-permute-done.4.side_ref, ...), custom_call_target="tpu_custom_call" | custom-call | flops 4194304 | bytes 1048576 | tf_op jit(solution)/shard_map/own_chip/pallas_call | solution.py:211
  61.0 5.5 %collective-permute-start.5 = (bf16[1536,256]{1,0:T(8,128)(2,1)S(1)}, bf16[1536,256]{1,0:T(8,128)(2,1)S(1)}, u32[]{:S(2)}, u32[]{:S(2)}) collective-permute-start(bf16[1536,256]{1,0:T(8,128)(2,1)S(1)} %bitcast.16), channel_id=1, source_target_pairs={{0,8},{8,0},{16,24},{24,16},{32,40},{40,32},{48,56},{56,48},{64,72... | collective-permute-start | bytes 2359304 | tf_op jit(solution)/shard_map/ppermute | solution.py:222
  66.5 1.9 %collective-permute-start.3 = (bf16[8,128,256]{2,1,0:T(8,128)(2,1)S(1)}, bf16[8,128,256]{2,1,0:T(8,128)(2,1)S(1)}, u32[]{:S(2)}, u32[]{:S(2)}) collective-permute-start(bf16[8,128,256]{2,1,0:T(8,128)(2,1)S(1)} %slice.24), channel_id=1, source_target_pairs={{0,128},{8,136},{16,144},{24,152},{32,160},{40,168},{48,176},{56,1... | collective-permute-start | bytes 1572872 | tf_op jit(solution)/shard_map/ppermute | solution.py:200
  68.5 0.0 collective-permute-done.5.side_ref
  68.5 2.3 %near_window_and_prefix.1 = (f32[1,1024]{1,0:T(1,128)S(1)}, f32[1,1024]{1,0:T(1,128)S(1)}, f32[128,1024]{1,0:T(8,128)S(1)}) custom-call(s32[1]{0:T(128)} %bitcast.meta_ref, s32[32]{0:T(128)S(1)} %bitcast.25, bf16[1536,256]{1,0:T(8,128)(2,1)S(1)} %bitcast.17, bf16[1536,256]{1,0:T(8,128)(2,1)S(1)} %collective-permute-done.5.side_ref, s32[64,128]{1,0:T(8,128)S(1)} %bitcast.22, ...), custom_call_target="tpu_custom_call" | custom-call | flops 4194304 | bytes 1048576 | tf_op jit(solution)/shard_map/near_window_and_prefix/pallas_call | solution.py:223
  70.8 12.4 %collective-permute-done.3 = bf16[8,128,256]{2,1,0:T(8,128)(2,1)S(1)} collective-permute-done((bf16[8,128,256]{2,1,0:T(8,128)(2,1)S(1)}, bf16[8,128,256]{2,1,0:T(8,128)(2,1)S(1)}, u32[]{:S(2)}, u32[]{:S(2)}) %collective-permute-start.3) | collective-permute-done | bytes 524320 | tf_op jit(solution)/shard_map/ppermute | solution.py:200
  83.2 2.7 %collective-permute-start.6 = (bf16[1024,256]{1,0:T(8,128)(2,1)S(1)}, bf16[1024,256]{1,0:T(8,128)(2,1)S(1)}, u32[]{:S(2)}, u32[]{:S(2)}) collective-permute-start(bf16[1024,256]{1,0:T(8,128)(2,1)S(1)} %bitcast.26), channel_id=1, source_target_pairs={{0,8},{8,0},{16,24},{24,16},{32,40},{40,32},{48,56},{56,48},{64,72... | collective-permute-start | bytes 1572872 | tf_op jit(solution)/shard_map/ppermute | solution.py:235
  85.9 0.4 far_window.1
  86.3 1.1 %collective-permute-done.6.kv_ref = bf16[1024,256]{1,0:T(8,128)(2,1)S(1)} collective-permute-done((bf16[1024,256]{1,0:T(8,128)(2,1)S(1)}, bf16[1024,256]{1,0:T(8,128)(2,1)S(1)}, u32[]{:S(2)}, u32[]{:S(2)}) %collective-permute-start.6) | collective-permute-done | bytes 524320 | tf_op jit(solution)/shard_map/ppermute | solution.py:235
  87.4 0.5 far_other_core.1
  87.9 13.8 %all_to_all.15 = bf16[8,16,1024]{2,1,0:T(8,128)(2,1)S(1)} all-to-all(bf16[8,16,1024]{2,1,0:T(8,128)(2,1)S(1)} %bitcast.20), channel_id=1, replica_groups=mesh['seq'=64,'head'=8] {'head'}, dimensions={0} | all-to-all | bytes 524288 | tf_op jit(solution)/shard_map/all_to_all | solution.py:259
  101.7 0.9 copy.13
  (11 shorter events, 0.1 us)
Async XLA Ops:
  1.6 6.9 %collective-permute-start = (bf16[9,16,256]{2,1,0:T(8,128)(2,1)S(1)}, bf16[9,16,256]{2,1,0:T(8,128)(2,1)S(1)}, u32[]{:S(2)}, u32[]{:S(2)}) collective-permute-start(bf16[9,16,256]{2,1,0:T(8,128)(2,1)S(1)} %pad_maximum_fusion.2), channel_id=1, source_target_pairs={{0,128},{8,136},{16,144},{24,152},{32,160},{40,168},{48,176},{56,1... | collective-permute-start | bytes 221192 | tf_op jit(solution)/shard_map/ppermute | solution.py:187
  8.5 11.0 %copy-start.2 = (bf16[1,16,1,256]{3,1,2,0:T(8,128)(2,1)S(1)}, bf16[1,16,1,256]{3,1,2,0:T(8,128)(2,1)}, u32[]{:S(2)}) copy-start(bf16[1,16,1,256]{3,1,2,0:T(8,128)(2,1)} %param.8) | copy-start | bytes 24580
  9.3 22.4 %all-to-all-start = ((bf16[8,16,1536]{2,1,0:T(8,128)(2,1)}), bf16[8,16,1536]{2,1,0:T(8,128)(2,1)S(1)}, u32[]{:S(2)}, u32[]{:S(2)}) async-start(bf16[8,16,1536]{2,1,0:T(8,128)(2,1)} %pad_maximum_fusion.1), calls=%async_computation | async-start | bytes 786432 | tf_op jit(solution)/shard_map/all_to_all | solution.py:189
  19.5 6.3 %collective-permute-start.1 = (bf16[1,16,256]{2,1,0:T(8,128)(2,1)S(1)}, bf16[1,16,256]{2,1,0:T(8,128)(2,1)S(1)}, u32[]{:S(2)}, u32[]{:S(2)}) collective-permute-start(bf16[1,16,256]{2,1,0:T(8,128)(2,1)S(1)} %bitcast.34), channel_id=1, source_target_pairs={{0,256},{8,264},{16,272},{24,280},{32,288},{40,296},{48,304},{56,3... | collective-permute-start | bytes 24584 | tf_op jit(solution)/shard_map/ppermute | solution.py:191
  23.0 4.7 %collective-permute-start.2 = (bf16[1,16,256]{2,1,0:T(8,128)(2,1)S(1)}, bf16[1,16,256]{2,1,0:T(8,128)(2,1)S(1)}, u32[]{:S(2)}, u32[]{:S(2)}) collective-permute-start(bf16[1,16,256]{2,1,0:T(8,128)(2,1)S(1)} %bitcast.35), channel_id=1, source_target_pairs={{0,384},{8,392},{16,400},{24,408},{32,416},{40,424},{48,432},{56,4... | collective-permute-start | bytes 24584 | tf_op jit(solution)/shard_map/ppermute | solution.py:192
  32.8 27.0 %copy-start = (s32[8192]{0:T(1024)S(1)}, s32[8192]{0:T(1024)}, u32[]{:S(2)}) copy-start(s32[8192]{0:T(1024)} %param.7) | copy-start | bytes 98308
  32.8 27.0 %all-to-all-start.1 = ((bf16[8,192,256]{2,1,0:T(8,128)(2,1)}), bf16[8,192,256]{2,1,0:T(8,128)(2,1)S(1)}, u32[]{:S(2)}, u32[]{:S(2)}) async-start(bf16[8,192,256]{2,1,0:T(8,128)(2,1)} %pad_maximum_fusion), calls=%async_computation.1 | async-start | bytes 1572864 | tf_op jit(solution)/shard_map/all_to_all | solution.py:197
  39.8 20.1 %collective-permute-start.4 = (bf16[128,256]{1,0:T(8,128)(2,1)S(1)}, bf16[128,256]{1,0:T(8,128)(2,1)S(1)}, u32[]{:S(2)}, u32[]{:S(2)}) collective-permute-start(bf16[128,256]{1,0:T(8,128)(2,1)S(1)} %get-tuple-element.28.mine_ref), channel_id=1, source_target_pairs={{0,8},{8,0},{16,24},{24,16},{32,40},{40,32},{48,56},{56,48},{64,72... | collective-permute-start | bytes 196616 | tf_op jit(solution)/shard_map/ppermute | solution.py:199
  59.9 8.6 %copy-start.1 = (s32[1,32]{1,0:T(1,128)S(1)}, s32[1,32]{1,0:T(1,128)}, u32[]{:S(2)}) copy-start(s32[1,32]{1,0:T(1,128)} %param.9) | copy-start | bytes 388
  61.0 7.4 %collective-permute-start.5 = (bf16[1536,256]{1,0:T(8,128)(2,1)S(1)}, bf16[1536,256]{1,0:T(8,128)(2,1)S(1)}, u32[]{:S(2)}, u32[]{:S(2)}) collective-permute-start(bf16[1536,256]{1,0:T(8,128)(2,1)S(1)} %bitcast.16), channel_id=1, source_target_pairs={{0,8},{8,0},{16,24},{24,16},{32,40},{40,32},{48,56},{56,48},{64,72... | collective-permute-start | bytes 2359304 | tf_op jit(solution)/shard_map/ppermute | solution.py:222
  66.5 16.6 %collective-permute-start.3 = (bf16[8,128,256]{2,1,0:T(8,128)(2,1)S(1)}, bf16[8,128,256]{2,1,0:T(8,128)(2,1)S(1)}, u32[]{:S(2)}, u32[]{:S(2)}) collective-permute-start(bf16[8,128,256]{2,1,0:T(8,128)(2,1)S(1)} %slice.24), channel_id=1, source_target_pairs={{0,128},{8,136},{16,144},{24,152},{32,160},{40,168},{48,176},{56,1... | collective-permute-start | bytes 1572872 | tf_op jit(solution)/shard_map/ppermute | solution.py:200
  83.2 4.2 %collective-permute-start.6 = (bf16[1024,256]{1,0:T(8,128)(2,1)S(1)}, bf16[1024,256]{1,0:T(8,128)(2,1)S(1)}, u32[]{:S(2)}, u32[]{:S(2)}) collective-permute-start(bf16[1024,256]{1,0:T(8,128)(2,1)S(1)} %bitcast.26), channel_id=1, source_target_pairs={{0,8},{8,0},{16,24},{24,16},{32,40},{40,32},{48,56},{56,48},{64,72... | collective-permute-start | bytes 1572872 | tf_op jit(solution)/shard_map/ppermute | solution.py:235

commit v13 on v12

--- a/solution.py
+++ b/solution.py
@@ -208,28 +208,35 @@
         jax.ShapeDtypeStruct((D, QR), jnp.float32),
     ]
     params = pltpu.CompilerParams(vmem_limit_bytes=40 * 1024 * 1024)
-    qt, *now = pl.pallas_call(
-        own_kernel,
-        out_shape=[jax.ShapeDtypeStruct((PAIR, QR), jnp.bfloat16)] + state,
-        in_specs=[SM] + [VM] * 4,
-        out_specs=[VM] * 4,
-        compiler_params=params,
-        cost_estimate=cost(8),
-        name="own_chip",
-    )(meta, own, side, ids, wide)
-    near, now = lax.optimization_barrier((near, now))
-    near = near.reshape(NY * SLOT, PAIR)
-    near_side = lax.ppermute(near, "seq", SWAP)
-    now = pl.pallas_call(
-        near_kernel,
-        out_shape=state,
-        in_specs=[SM, SM] + [VM] * 7,
-        out_specs=[VM] * 3,
-        scratch_shapes=[pltpu.VMEM((PAGES * PAGE, PAIR), jnp.bfloat16)],
-        compiler_params=params,
-        cost_estimate=cost(8),
-        name="near_window_and_prefix",
-    )(meta, page_table.reshape(PAGES), near, near_side, ids, qt, *now)
+    def near_part(operands):
+        near, own, side, wide = operands
+        near = near.reshape(NY * SLOT, PAIR)
+        near_side = lax.ppermute(near, "seq", SWAP)
+        qt, *now = pl.pallas_call(
+            own_kernel,
+            out_shape=[jax.ShapeDtypeStruct((PAIR, QR), jnp.bfloat16)] + state,
+            in_specs=[SM] + [VM] * 4,
+            out_specs=[VM] * 4,
+            compiler_params=params,
+            cost_estimate=cost(256),
+            name="own_chip",
+        )(meta, own, side, ids, wide)
+        now = pl.pallas_call(
+            near_kernel,
+            out_shape=state,
+            in_specs=[SM, SM] + [VM] * 7,
+            out_specs=[VM] * 3,
+            scratch_shapes=[pltpu.VMEM((PAGES * PAGE, PAIR), jnp.bfloat16)],
+            compiler_params=params,
+            cost_estimate=cost(2560),
+            name="near_window_and_prefix",
+        )(meta, page_table.reshape(PAGES), near, near_side, ids, qt, *now)
+        return [qt, *now]
+
+    def nothing(operands):
+        return [jnp.zeros(a.shape, a.dtype) for a in [jax.ShapeDtypeStruct((PAIR, QR), jnp.bfloat16)] + state]
+
+    qt, *now = lax.cond(branch_ids[0] >= 0, near_part, nothing, (near, own, side, wide))
     far, now = lax.optimization_barrier((far, now))
     far = far.reshape(NY * ROWS, PAIR)
     far_side = lax.ppermute(far, "seq", SWAP)

time: 103 us -> 101 us (0.981)
  the two profiles are of different devices: /device:TPU:1 before, /device:TPU:6 now
where the time goes in v13:
time: 101 us; the launch traced here: 99.1 us
  blocking collectives  42.7 us (42%)
  starting transfers between devices  31 us (31%)
  Pallas kernels  11 us (11%)
  waiting for transfers between devices  8.65 us (9%)
  local copies, waits for them, and re-layouts  3.37 us (3%)
  other arithmetic  1.67 us (2%)
    all_to_all x1, blocking collectives, per_device(): lax.all_to_all(send, 'seq', split_axis=0, concat_axis=0, tiled=True, axis...  27.2 us
    all_to_all x1, blocking collectives, per_device(): lax.all_to_all(out.reshape(8, ROWS // 8, GROUP * D), 'head', split_axis=0...  15.4 us
    ppermute x1, starting transfers between devices, per_device(): one_raw = lax.ppermute(raw, 'seq', x_ring(1))  7.75 us
    all_to_all x1, starting transfers between devices, per_device(): lax.all_to_all(wide, 'head', split_axis=0, concat_axis=0, tiled=True)  6.84 us
    pallas_call x1, Pallas kernels, near_part(): pl.pallas_call(near_kernel, out_shape=state, in_specs=[SM, SM] + [VM] * 7...  6.53 us
    ppermute x1, starting transfers between devices, per_device(): far = lax.ppermute(near[:, :ROWS], 'seq', x_ring(1))  3.6 us
    all_to_all x1, waiting for transfers between devices, per_device(): lax.all_to_all(wide, 'head', split_axis=0, concat_axis=0, tiled=True)  3.45 us
    ppermute x1, starting transfers between devices, per_device(): two_page = lax.ppermute(page, 'seq', x_ring(2))  3.31 us
  transfers between devices with their start and end apart: 8, of which 7 were waited for; matrix products, arithmetic and copies ran while one was open for 2% of the time, Pallas kernels for 10%

profile of v13, /device:TPU:6, one launch (start us, length us, event | category | flops | bytes accessed | tf_op | source)
XLA Modules:
  0.0 99.1 jit_solution(8722942428116158660)
XLA Ops:
  0.0 0.9 copy.18
  0.9 0.7 pad_maximum_fusion.2
  1.6 7.7 %collective-permute-start.1 = (bf16[9,16,256]{2,1,0:T(8,128)(2,1)S(1)}, bf16[9,16,256]{2,1,0:T(8,128)(2,1)S(1)}, u32[]{:S(2)}, u32[]{:S(2)}) collective-permute-start(bf16[9,16,256]{2,1,0:T(8,128)(2,1)S(1)} %pad_maximum_fusion.2), channel_id=1, source_target_pairs={{0,128},{8,136},{16,144},{24,152},{32,160},{40,168},{48,176},{56,1... | collective-permute-start | bytes 221192 | tf_op jit(solution)/shard_map/ppermute | solution.py:187
  9.3 1.1 %copy.17 = bf16[16,8,1024]{2,0,1:T(8,128)(2,1)S(1)} copy(bf16[16,8,1024]{2,1,0:T(8,128)(2,1)} %param.7) | data formatting | bytes 524288 | tf_op args[0]
  10.4 0.9 collective-permute-done.1
  11.3 0.8 pad_maximum_fusion.1
  12.1 6.8 %all-to-all-start = ((bf16[8,16,1536]{2,1,0:T(8,128)(2,1)}), bf16[8,16,1536]{2,1,0:T(8,128)(2,1)S(1)}, u32[]{:S(2)}, u32[]{:S(2)}) async-start(bf16[8,16,1536]{2,1,0:T(8,128)(2,1)} %pad_maximum_fusion.1), calls=%async_computation | async-start | bytes 786432 | tf_op jit(solution)/shard_map/all_to_all | solution.py:189
  18.9 0.0 copy-done.1
  18.9 3.3 %collective-permute-start.2 = (bf16[1,16,256]{2,1,0:T(8,128)(2,1)S(1)}, bf16[1,16,256]{2,1,0:T(8,128)(2,1)S(1)}, u32[]{:S(2)}, u32[]{:S(2)}) collective-permute-start(bf16[1,16,256]{2,1,0:T(8,128)(2,1)S(1)} %bitcast.33), channel_id=1, source_target_pairs={{0,256},{8,264},{16,272},{24,280},{32,288},{40,296},{48,304},{56,3... | collective-permute-start | bytes 24584 | tf_op jit(solution)/shard_map/ppermute | solution.py:191
  22.2 3.0 %collective-permute-start.3 = (bf16[1,16,256]{2,1,0:T(8,128)(2,1)S(1)}, bf16[1,16,256]{2,1,0:T(8,128)(2,1)S(1)}, u32[]{:S(2)}, u32[]{:S(2)}) collective-permute-start(bf16[1,16,256]{2,1,0:T(8,128)(2,1)S(1)} %bitcast.34), channel_id=1, source_target_pairs={{0,384},{8,392},{16,400},{24,408},{32,416},{40,424},{48,432},{56,4... | collective-permute-start | bytes 24584 | tf_op jit(solution)/shard_map/ppermute | solution.py:192
  25.3 0.6 collective-permute-done.2
  26.0 3.0 %collective-permute-done.3 = bf16[1,16,256]{2,1,0:T(8,128)(2,1)S(1)} collective-permute-done((bf16[1,16,256]{2,1,0:T(8,128)(2,1)S(1)}, bf16[1,16,256]{2,1,0:T(8,128)(2,1)S(1)}, u32[]{:S(2)}, u32[]{:S(2)}) %collective-permute-start.3) | collective-permute-done | bytes 8224 | tf_op jit(solution)/shard_map/ppermute | solution.py:192
  29.0 3.4 %all-to-all-done = bf16[8,16,1536]{2,1,0:T(8,128)(2,1)S(1)} async-done(((bf16[8,16,1536]{2,1,0:T(8,128)(2,1)}), bf16[8,16,1536]{2,1,0:T(8,128)(2,1)S(1)}, u32[]{:S(2)}, u32[]{:S(2)}) %all-to-all-start) | async-done | bytes 393248 | tf_op jit(solution)/shard_map/all_to_all | solution.py:189
  32.5 0.1 broadcast_select_fusion
  32.6 0.1 pad_maximum_fusion
  32.7 27.2 %all_to_all.15 = bf16[8,192,256]{2,1,0:T(8,128)(2,1)S(1)} all-to-all(bf16[8,192,256]{2,1,0:T(8,128)(2,1)S(1)} %pad_maximum_fusion), channel_id=1, replica_groups={{0,16,32,48,64,80,96,112},{8,24,40,56,72,88,104,120},{128,144,160,176,1..., dimensions={0} | all-to-all | bytes 1572864 | tf_op jit(solution)/shard_map/all_to_all | solution.py:197
  59.9 3.6 %collective-permute-start.4 = (bf16[8,128,256]{2,1,0:T(8,128)(2,1)S(1)}, bf16[8,128,256]{2,1,0:T(8,128)(2,1)S(1)}, u32[]{:S(2)}, u32[]{:S(2)}) collective-permute-start(bf16[8,128,256]{2,1,0:T(8,128)(2,1)S(1)} %slice.28), channel_id=1, source_target_pairs={{0,128},{8,136},{16,144},{24,152},{32,160},{40,168},{48,176},{56,1... | collective-permute-start | bytes 1572872 | tf_op jit(solution)/shard_map/ppermute | solution.py:200
  63.6 1.9 %collective-permute-start.5 = (bf16[128,256]{1,0:T(8,128)(2,1)S(1)}, bf16[128,256]{1,0:T(8,128)(2,1)S(1)}, u32[]{:S(2)}, u32[]{:S(2)}) collective-permute-start(bf16[128,256]{1,0:T(8,128)(2,1)S(1)} %get-tuple-element.48), channel_id=1, source_target_pairs={{0,8},{8,0},{16,24},{24,16},{32,40},{40,32},{48,56},{56,48},{64,72... | collective-permute-start | bytes 196616 | tf_op jit(solution)/shard_map/ppermute | solution.py:199
  65.5 0.5 slice.23
  66.5 0.2 collective-permute-done.5
  66.7 10.7 %conditional.1 = (bf16[256,1024]{1,0:T(8,128)(2,1)}, f32[1,1024]{1,0:T(1,128)S(1)}, f32[1,1024]{1,0:T(1,128)S(1)}, f32[128,1024]{1,0:T(8,128)S(1)}) conditional(s32[]{:T(128)} %bitcast.8, () %tuple.16, (s32[1]{0:T(128)}, bf16[128,256]{1,0:T(8,128)(2,1)S(1)}, bf16[128,256]{1,0:T(8,128)(2,1)S(1)}, s32[64,128]{1,0:T(8,128)S(1)}, ...), branch_computations={%region_0.1_spmd, %region_1.2_spmd} | conditional | flops 1476395008 | bytes 5242952 | solution.py:239
  66.7 2.3 %collective-permute-start = (bf16[1536,256]{1,0:T(8,128)(2,1)S(1)}, bf16[1536,256]{1,0:T(8,128)(2,1)S(1)}, u32[]{:S(2)}, u32[]{:S(2)}) collective-permute-start(bf16[1536,256]{1,0:T(8,128)(2,1)S(1)} %bitcast.20), channel_id=1, source_target_pairs={{0,8},{8,0},{16,24},{24,16},{32,40},{40,32},{48,56},{56,48},{64,72... | collective-permute-start | bytes 2359304 | tf_op jit(solution)/shard_map/cond/branch_1_fun/ppermute | solution.py:214
  69.0 1.5 %own_chip.1 = (bf16[256,1024]{1,0:T(8,128)(2,1)}, f32[1,1024]{1,0:T(1,128)S(1)}, f32[1,1024]{1,0:T(1,128)S(1)}, f32[128,1024]{1,0:T(8,128)S(1)}) custom-call(s32[1]{0:T(128)} %get-tuple-element.19.meta_ref, bf16[128,256]{1,0:T(8,128)(2,1)S(1)} %get-tuple-element.20.mine_ref, bf16[128,256]{1,0:T(8,128)(2,1)S(1)} %get-tuple-element.21.side_ref, ...), custom_call_target="tpu_custom_call" | custom-call | flops 134217728 | bytes 1048576 | tf_op jit(solution)/shard_map/cond/branch_1_fun/own_chip/pallas_call | solution.py:215
  70.4 0.4 collective-permute-done.side_ref
  70.9 6.5 %near_window_and_prefix.1 = (f32[1,1024]{1,0:T(1,128)S(1)}, f32[1,1024]{1,0:T(1,128)S(1)}, f32[128,1024]{1,0:T(8,128)S(1)}) custom-call(s32[1]{0:T(128)} %get-tuple-element.19.meta_ref, s32[32]{0:T(128)S(1)} %bitcast.36, bf16[1536,256]{1,0:T(8,128)(2,1)S(1)} %bitcast.21, bf16[1536,256]{1,0:T(8,128)(2,1)S(1)} %collective-permute-done.side_ref, ...), custom_call_target="tpu_custom_call" | custom-call | flops 1342177280 | bytes 1048576 | tf_op jit(solution)/shard_map/cond/branch_1_fun/near_window_and_prefix/pallas_call | solution.py:224
  77.4 0.0 collective-permute-done.4
  77.4 2.3 %collective-permute-start.6 = (bf16[1024,256]{1,0:T(8,128)(2,1)S(1)}, bf16[1024,256]{1,0:T(8,128)(2,1)S(1)}, u32[]{:S(2)}, u32[]{:S(2)}) collective-permute-start(bf16[1024,256]{1,0:T(8,128)(2,1)S(1)} %bitcast.18), channel_id=1, source_target_pairs={{0,8},{8,0},{16,24},{24,16},{32,40},{40,32},{48,56},{56,48},{64,72... | collective-permute-start | bytes 1572872 | tf_op jit(solution)/shard_map/ppermute | solution.py:242
  79.7 1.4 %far_window.1 = (f32[1,1024]{1,0:T(1,128)S(1)}, f32[1,1024]{1,0:T(1,128)S(1)}, f32[128,1024]{1,0:T(8,128)S(1)}) custom-call(s32[1]{0:T(128)} %bitcast.2.meta_ref, bf16[1024,256]{1,0:T(8,128)(2,1)S(1)} %bitcast.19, s32[64,128]{1,0:T(8,128)S(1)} %bitcast.30, bf16[256,1024]{1,0:T(8,128)(2,1)} %get-tuple-element.54.qt_ref, ...), custom_call_target="tpu_custom_call" | custom-call | flops 536870912 | bytes 1048576 | tf_op jit(solution)/shard_map/far_window/pallas_call | solution.py:243
  81.2 0.1 collective-permute-done.6.kv_ref
  81.2 1.6 %far_other_core.1 = bf16[128,1024]{1,0:T(8,128)(2,1)S(1)} custom-call(s32[1]{0:T(128)} %bitcast.2.meta_ref, bf16[1024,256]{1,0:T(8,128)(2,1)S(1)} %collective-permute-done.6.kv_ref, s32[64,128]{1,0:T(8,128)S(1)} %bitcast.31, bf16[256,1024]{1,0:T(8,128)(2,1)} %get-tuple-element.54.qt_ref, f32[1,1024]{1,0:T(1,128)S(1)} %get-tuple-element.58.m_in, ...), custom_call_target="tpu_custom_call" | custom-call | flops 536870912 | bytes 1048576 | tf_op jit(solution)/shard_map/far_other_core/pallas_call | solution.py:252
  82.8 15.4 %all_to_all.16 = bf16[8,16,1024]{2,1,0:T(8,128)(2,1)S(1)} all-to-all(bf16[8,16,1024]{2,1,0:T(8,128)(2,1)S(1)} %bitcast.17), channel_id=1, replica_groups=mesh['seq'=64,'head'=8] {'head'}, dimensions={0} | all-to-all | bytes 524288 | tf_op jit(solution)/shard_map/all_to_all | solution.py:266
  98.2 0.9 copy.14
  (12 shorter events, 0.1 us)
Async XLA Ops:
  1.6 9.7 %collective-permute-start.1 = (bf16[9,16,256]{2,1,0:T(8,128)(2,1)S(1)}, bf16[9,16,256]{2,1,0:T(8,128)(2,1)S(1)}, u32[]{:S(2)}, u32[]{:S(2)}) collective-permute-start(bf16[9,16,256]{2,1,0:T(8,128)(2,1)S(1)} %pad_maximum_fusion.2), channel_id=1, source_target_pairs={{0,128},{8,136},{16,144},{24,152},{32,160},{40,168},{48,176},{56,1... | collective-permute-start | bytes 221192 | tf_op jit(solution)/shard_map/ppermute | solution.py:187
  11.3 7.6 %copy-start.1 = (bf16[1,16,1,256]{3,1,2,0:T(8,128)(2,1)S(1)}, bf16[1,16,1,256]{3,1,2,0:T(8,128)(2,1)}, u32[]{:S(2)}) copy-start(bf16[1,16,1,256]{3,1,2,0:T(8,128)(2,1)} %param.10) | copy-start | bytes 24580
  12.1 20.4 %all-to-all-start = ((bf16[8,16,1536]{2,1,0:T(8,128)(2,1)}), bf16[8,16,1536]{2,1,0:T(8,128)(2,1)S(1)}, u32[]{:S(2)}, u32[]{:S(2)}) async-start(bf16[8,16,1536]{2,1,0:T(8,128)(2,1)} %pad_maximum_fusion.1), calls=%async_computation | async-start | bytes 786432 | tf_op jit(solution)/shard_map/all_to_all | solution.py:189
  18.9 7.0 %collective-permute-start.2 = (bf16[1,16,256]{2,1,0:T(8,128)(2,1)S(1)}, bf16[1,16,256]{2,1,0:T(8,128)(2,1)S(1)}, u32[]{:S(2)}, u32[]{:S(2)}) collective-permute-start(bf16[1,16,256]{2,1,0:T(8,128)(2,1)S(1)} %bitcast.33), channel_id=1, source_target_pairs={{0,256},{8,264},{16,272},{24,280},{32,288},{40,296},{48,304},{56,3... | collective-permute-start | bytes 24584 | tf_op jit(solution)/shard_map/ppermute | solution.py:191
  22.2 6.8 %collective-permute-start.3 = (bf16[1,16,256]{2,1,0:T(8,128)(2,1)S(1)}, bf16[1,16,256]{2,1,0:T(8,128)(2,1)S(1)}, u32[]{:S(2)}, u32[]{:S(2)}) collective-permute-start(bf16[1,16,256]{2,1,0:T(8,128)(2,1)S(1)} %bitcast.34), channel_id=1, source_target_pairs={{0,384},{8,392},{16,400},{24,408},{32,416},{40,424},{48,432},{56,4... | collective-permute-start | bytes 24584 | tf_op jit(solution)/shard_map/ppermute | solution.py:192
  59.9 5.6 %copy-start = (s32[8192]{0:T(1024)S(1)}, s32[8192]{0:T(1024)}, u32[]{:S(2)}) copy-start(s32[8192]{0:T(1024)} %param.9) | copy-start | bytes 98308
  59.9 6.8 %copy-start.2 = (s32[1,32]{1,0:T(1,128)S(1)}, s32[1,32]{1,0:T(1,128)}, u32[]{:S(2)}) copy-start(s32[1,32]{1,0:T(1,128)} %param.11) | copy-start | bytes 388
  59.9 17.5 %collective-permute-start.4 = (bf16[8,128,256]{2,1,0:T(8,128)(2,1)S(1)}, bf16[8,128,256]{2,1,0:T(8,128)(2,1)S(1)}, u32[]{:S(2)}, u32[]{:S(2)}) collective-permute-start(bf16[8,128,256]{2,1,0:T(8,128)(2,1)S(1)} %slice.28), channel_id=1, source_target_pairs={{0,128},{8,136},{16,144},{24,152},{32,160},{40,168},{48,176},{56,1... | collective-permute-start | bytes 1572872 | tf_op jit(solution)/shard_map/ppermute | solution.py:200
  63.6 3.1 %collective-permute-start.5 = (bf16[128,256]{1,0:T(8,128)(2,1)S(1)}, bf16[128,256]{1,0:T(8,128)(2,1)S(1)}, u32[]{:S(2)}, u32[]{:S(2)}) collective-permute-start(bf16[128,256]{1,0:T(8,128)(2,1)S(1)} %get-tuple-element.48), channel_id=1, source_target_pairs={{0,8},{8,0},{16,24},{24,16},{32,40},{40,32},{48,56},{56,48},{64,72... | collective-permute-start | bytes 196616 | tf_op jit(solution)/shard_map/ppermute | solution.py:199
  66.7 4.2 %collective-permute-start = (bf16[1536,256]{1,0:T(8,128)(2,1)S(1)}, bf16[1536,256]{1,0:T(8,128)(2,1)S(1)}, u32[]{:S(2)}, u32[]{:S(2)}) collective-permute-start(bf16[1536,256]{1,0:T(8,128)(2,1)S(1)} %bitcast.20), channel_id=1, source_target_pairs={{0,8},{8,0},{16,24},{24,16},{32,40},{40,32},{48,56},{56,48},{64,72... | collective-permute-start | bytes 2359304 | tf_op jit(solution)/shard_map/cond/branch_1_fun/ppermute | solution.py:214
  77.4 3.8 %collective-permute-start.6 = (bf16[1024,256]{1,0:T(8,128)(2,1)S(1)}, bf16[1024,256]{1,0:T(8,128)(2,1)S(1)}, u32[]{:S(2)}, u32[]{:S(2)}) collective-permute-start(bf16[1024,256]{1,0:T(8,128)(2,1)S(1)} %bitcast.18), channel_id=1, source_target_pairs={{0,8},{8,0},{16,24},{24,16},{32,40},{40,32},{48,56},{56,48},{64,72... | collective-permute-start | bytes 1572872 | tf_op jit(solution)/shard_map/ppermute | solution.py:242

commit v14 on v9

--- a/solution.py
+++ b/solution.py
@@ -197,7 +197,6 @@
     near = lax.all_to_all(send, "seq", split_axis=0, concat_axis=0, tiled=True, axis_index_groups=Y_GROUPS)
     later, _ = lax.optimization_barrier((own, send))
     side = lax.ppermute(later, "seq", SWAP)
-
     ids = branch_ids.reshape(2 * NX * NY, ROWS)
     meta = me.astype(jnp.int32).reshape(1)
     state = [
@@ -215,20 +214,25 @@
         cost_estimate=cost(256),
         name="own_chip",
     )(meta, own, side, ids, wide)
-    near, now = lax.optimization_barrier((near, now))
+    near, qt, now = lax.optimization_barrier((near, qt, now))
     far = lax.ppermute(near[:, :ROWS], "seq", x_ring(1))
-    near = near.reshape(NY * SLOT, PAIR)
-    near_side = lax.ppermute(near, "seq", SWAP)
-    now = pl.pallas_call(
-        near_kernel,
-        out_shape=state,
-        in_specs=[SM, SM] + [VM] * 7,
-        out_specs=[VM] * 3,
-        scratch_shapes=[pltpu.VMEM((PAGES * PAGE, PAIR), jnp.bfloat16)],
-        compiler_params=params,
-        cost_estimate=cost(2560),
-        name="near_window_and_prefix",
-    )(meta, page_table.reshape(PAGES), near, near_side, ids, qt, *now)
+
+    def near_part(operands):
+        near, qt, now = operands
+        near = near.reshape(NY * SLOT, PAIR)
+        near_side = lax.ppermute(near, "seq", SWAP)
+        return list(pl.pallas_call(
+            near_kernel,
+            out_shape=state,
+            in_specs=[SM, SM] + [VM] * 7,
+            out_specs=[VM] * 3,
+            scratch_shapes=[pltpu.VMEM((PAGES * PAGE, PAIR), jnp.bfloat16)],
+            compiler_params=params,
+            cost_estimate=cost(2560),
+            name="near_window_and_prefix",
+        )(meta, page_table.reshape(PAGES), near, near_side, ids, qt, *now))
+
+    now = lax.cond(branch_ids[0] >= 0, near_part, lambda operands: list(operands[2]), (near, qt, now))
     far, now = lax.optimization_barrier((far, now))
     far = far.reshape(NY * ROWS, PAIR)
     far_side = lax.ppermute(far, "seq", SWAP)

time: 103 us -> 98.9 us (0.960)
  the two profiles are of different devices: /device:TPU:6 before, /device:TPU:13 now
where the time goes in v14:
time: 98.9 us; the launch traced here: 98.2 us
  starting transfers between devices  47.5 us (48%)
  waiting for transfers between devices  16.6 us (17%)
  blocking collectives  15.3 us (15%)
  Pallas kernels  11.9 us (12%)
  local copies, waits for them, and re-layouts  3.52 us (4%)
  other arithmetic  2.55 us (3%)
    all_to_all x1, blocking collectives, per_device(): lax.all_to_all(out.reshape(8, ROWS // 8, GROUP * D), 'head', split_axis=0...  15.3 us
    all_to_all x1, starting transfers between devices, per_device(): lax.all_to_all(wide, 'head', split_axis=0, concat_axis=0, tiled=True)  10 us
    ppermute x1, starting transfers between devices, near_part(): near_side = lax.ppermute(near, 'seq', SWAP)  9.95 us
    all_to_all x1, waiting for transfers between devices, per_device(): lax.all_to_all(send, 'seq', split_axis=0, concat_axis=0, tiled=True, axis...  7.18 us
    all_to_all x1, starting transfers between devices, per_device(): lax.all_to_all(send, 'seq', split_axis=0, concat_axis=0, tiled=True, axis...  7.12 us
    pallas_call x1, Pallas kernels, near_part(): pl.pallas_call(near_kernel, out_shape=state, in_specs=[SM, SM] + [VM] * 7...  6.02 us
    ppermute x1, starting transfers between devices, per_device(): side = lax.ppermute(later, 'seq', SWAP)  5.9 us
    ppermute x1, starting transfers between devices, per_device(): two_page = lax.ppermute(page, 'seq', x_ring(2))  4.36 us
  transfers between devices with their start and end apart: 9, of which 6 were waited for; matrix products, arithmetic and copies ran while one was open for 2% of the time, Pallas kernels for 10%

profile of v14, /device:TPU:13, one launch (start us, length us, event | category | flops | bytes accessed | tf_op | source)
XLA Modules:
  0.0 98.2 jit_solution(2040965330573770120)
XLA Ops:
  0.0 0.9 copy.18
  0.9 0.7 pad_maximum_fusion.2
  1.6 2.8 %collective-permute-start.1 = (bf16[9,16,256]{2,1,0:T(8,128)(2,1)S(1)}, bf16[9,16,256]{2,1,0:T(8,128)(2,1)S(1)}, u32[]{:S(2)}, u32[]{:S(2)}) collective-permute-start(bf16[9,16,256]{2,1,0:T(8,128)(2,1)S(1)} %pad_maximum_fusion.2), channel_id=1, source_target_pairs={{0,128},{8,136},{16,144},{24,152},{32,160},{40,168},{48,176},{56,1... | collective-permute-start | bytes 221192 | tf_op jit(solution)/shard_map/ppermute | solution.py:187
  4.4 1.1 %copy.17 = bf16[16,8,1024]{2,0,1:T(8,128)(2,1)S(1)} copy(bf16[16,8,1024]{2,1,0:T(8,128)(2,1)} %param.7) | data formatting | bytes 524288 | tf_op args[0]
  5.5 1.2 %collective-permute-done.1 = bf16[9,16,256]{2,1,0:T(8,128)(2,1)S(1)} collective-permute-done((bf16[9,16,256]{2,1,0:T(8,128)(2,1)S(1)}, bf16[9,16,256]{2,1,0:T(8,128)(2,1)S(1)}, u32[]{:S(2)}, u32[]{:S(2)}) %collective-permute-start.1) | collective-permute-done | bytes 73760 | tf_op jit(solution)/shard_map/ppermute | solution.py:187
  6.7 0.8 pad_maximum_fusion.1
  7.4 10.0 %all-to-all-start = ((bf16[8,16,1536]{2,1,0:T(8,128)(2,1)}), bf16[8,16,1536]{2,1,0:T(8,128)(2,1)S(1)}, u32[]{:S(2)}, u32[]{:S(2)}) async-start(bf16[8,16,1536]{2,1,0:T(8,128)(2,1)} %pad_maximum_fusion.1), calls=%async_computation | async-start | bytes 786432 | tf_op jit(solution)/shard_map/all_to_all | solution.py:189
  17.5 2.2 %collective-permute-start.3 = (bf16[1,16,256]{2,1,0:T(8,128)(2,1)S(1)}, bf16[1,16,256]{2,1,0:T(8,128)(2,1)S(1)}, u32[]{:S(2)}, u32[]{:S(2)}) collective-permute-start(bf16[1,16,256]{2,1,0:T(8,128)(2,1)S(1)} %bitcast.34), channel_id=1, source_target_pairs={{0,384},{8,392},{16,400},{24,408},{32,416},{40,424},{48,432},{56,4... | collective-permute-start | bytes 24584 | tf_op jit(solution)/shard_map/ppermute | solution.py:192
  19.6 4.4 %collective-permute-start.2 = (bf16[1,16,256]{2,1,0:T(8,128)(2,1)S(1)}, bf16[1,16,256]{2,1,0:T(8,128)(2,1)S(1)}, u32[]{:S(2)}, u32[]{:S(2)}) collective-permute-start(bf16[1,16,256]{2,1,0:T(8,128)(2,1)S(1)} %bitcast.35), channel_id=1, source_target_pairs={{0,256},{8,264},{16,272},{24,280},{32,288},{40,296},{48,304},{56,3... | collective-permute-start | bytes 24584 | tf_op jit(solution)/shard_map/ppermute | solution.py:191
  24.1 0.0 collective-permute-done.3
  24.1 1.5 %collective-permute-done.2 = bf16[1,16,256]{2,1,0:T(8,128)(2,1)S(1)} collective-permute-done((bf16[1,16,256]{2,1,0:T(8,128)(2,1)S(1)}, bf16[1,16,256]{2,1,0:T(8,128)(2,1)S(1)}, u32[]{:S(2)}, u32[]{:S(2)}) %collective-permute-start.2) | collective-permute-done | bytes 8224 | tf_op jit(solution)/shard_map/ppermute | solution.py:191
  25.6 4.1 %all-to-all-done = bf16[8,16,1536]{2,1,0:T(8,128)(2,1)S(1)} async-done(((bf16[8,16,1536]{2,1,0:T(8,128)(2,1)}), bf16[8,16,1536]{2,1,0:T(8,128)(2,1)S(1)}, u32[]{:S(2)}, u32[]{:S(2)}) %all-to-all-start) | async-done | bytes 393248 | tf_op jit(solution)/shard_map/all_to_all | solution.py:189
  29.7 0.1 broadcast_select_fusion
  29.8 0.9 pad_maximum_fusion
  30.8 7.1 %all-to-all-start.1 = ((bf16[8,192,256]{2,1,0:T(8,128)(2,1)}), bf16[8,192,256]{2,1,0:T(8,128)(2,1)S(1)}, u32[]{:S(2)}, u32[]{:S(2)}) async-start(bf16[8,192,256]{2,1,0:T(8,128)(2,1)} %pad_maximum_fusion), calls=%async_computation.1 | async-start | bytes 1572864 | tf_op jit(solution)/shard_map/all_to_all | solution.py:197
  37.9 5.9 %collective-permute-start.4 = (bf16[128,256]{1,0:T(8,128)(2,1)S(1)}, bf16[128,256]{1,0:T(8,128)(2,1)S(1)}, u32[]{:S(2)}, u32[]{:S(2)}) collective-permute-start(bf16[128,256]{1,0:T(8,128)(2,1)S(1)} %get-tuple-element.55.mine_ref), channel_id=1, source_target_pairs={{0,8},{8,0},{16,24},{24,16},{32,40},{40,32},{48,56},{56,48},{64,72... | collective-permute-start | bytes 196616 | tf_op jit(solution)/shard_map/ppermute | solution.py:199
  43.8 0.9 collective-permute-done.4.side_ref
  44.7 1.2 %own_chip.1 = (bf16[256,1024]{1,0:T(8,128)(2,1)S(1)}, f32[1,1024]{1,0:T(1,128)S(1)}, f32[1,1024]{1,0:T(1,128)S(1)}, f32[128,1024]{1,0:T(8,128)S(1)}) custom-call(s32[1]{0:T(128)} %bitcast.2.meta_ref, bf16[128,256]{1,0:T(8,128)(2,1)S(1)} %get-tuple-element.55.mine_ref, bf16[128,256]{1,0:T(8,128)(2,1)S(1)} %collective-permute-done.4.side_ref, ...), custom_call_target="tpu_custom_call" | custom-call | flops 134217728 | bytes 1048576 | tf_op jit(solution)/shard_map/own_chip/pallas_call | solution.py:208
  45.8 7.2 %all-to-all-done.1 = bf16[8,192,256]{2,1,0:T(8,128)(2,1)S(1)} async-done(((bf16[8,192,256]{2,1,0:T(8,128)(2,1)}), bf16[8,192,256]{2,1,0:T(8,128)(2,1)S(1)}, u32[]{:S(2)}, u32[]{:S(2)}) %all-to-all-start.1) | async-done | bytes 786464 | tf_op jit(solution)/shard_map/all_to_all | solution.py:197
  53.1 2.8 %collective-permute-start.5 = (bf16[8,128,256]{2,1,0:T(8,128)(2,1)S(1)}, bf16[8,128,256]{2,1,0:T(8,128)(2,1)S(1)}, u32[]{:S(2)}, u32[]{:S(2)}) collective-permute-start(bf16[8,128,256]{2,1,0:T(8,128)(2,1)S(1)} %slice.22), channel_id=1, source_target_pairs={{0,128},{8,136},{16,144},{24,152},{32,160},{40,168},{48,176},{56,1... | collective-permute-start | bytes 1572872 | tf_op jit(solution)/shard_map/ppermute | solution.py:218
  55.9 0.6 slice.23
  57.2 17.9 %conditional.1 = ((f32[1,1024]{1,0:T(1,128)S(1)}, f32[1,1024]{1,0:T(1,128)S(1)}, f32[128,1024]{1,0:T(8,128)S(1)})) conditional(s32[]{:T(128)} %bitcast.9, (f32[1,1024]{1,0:T(1,128)S(1)}, f32[1,1024]{1,0:T(1,128)S(1)}, f32[128,1024]{1,0:T(8,128)S(1)}) %tuple.16, (s32[1,32]{1,0:T(1,128)S(1)}, bf16[8,192,256]{2,1,0:T(8,128)(2,1)S(1)}, s32[1]{0:T(128)}, ...), branch_computations={%region_0.1_spmd, %region_1.2_spmd} | conditional | flops 1342177280 | bytes 5259312 | solution.py:235
  57.2 9.9 %collective-permute-start = (bf16[1536,256]{1,0:T(8,128)(2,1)S(1)}, bf16[1536,256]{1,0:T(8,128)(2,1)S(1)}, u32[]{:S(2)}, u32[]{:S(2)}) collective-permute-start(bf16[1536,256]{1,0:T(8,128)(2,1)S(1)} %bitcast.22), channel_id=1, source_target_pairs={{0,8},{8,0},{16,24},{24,16},{32,40},{40,32},{48,56},{56,48},{64,72... | collective-permute-start | bytes 2359304 | tf_op jit(solution)/shard_map/cond/branch_1_fun/ppermute | solution.py:223
  67.2 1.8 %collective-permute-done.side_ref = bf16[1536,256]{1,0:T(8,128)(2,1)S(1)} collective-permute-done((bf16[1536,256]{1,0:T(8,128)(2,1)S(1)}, bf16[1536,256]{1,0:T(8,128)(2,1)S(1)}, u32[]{:S(2)}, u32[]{:S(2)}) %collective-permute-start) | collective-permute-done | bytes 786464 | tf_op jit(solution)/shard_map/cond/branch_1_fun/ppermute | solution.py:223
  69.0 6.0 %near_window_and_prefix.1 = (f32[1,1024]{1,0:T(1,128)S(1)}, f32[1,1024]{1,0:T(1,128)S(1)}, f32[128,1024]{1,0:T(8,128)S(1)}) custom-call(s32[1]{0:T(128)} %get-tuple-element.27.meta_ref, s32[32]{0:T(128)S(1)} %bitcast.37, bf16[1536,256]{1,0:T(8,128)(2,1)S(1)} %bitcast.23, bf16[1536,256]{1,0:T(8,128)(2,1)S(1)} %collective-permute-done.side_ref, ...), custom_call_target="tpu_custom_call" | custom-call | flops 1342177280 | bytes 1048576 | tf_op jit(solution)/shard_map/cond/branch_1_fun/near_window_and_prefix/pallas_call | solution.py:224
  75.1 0.0 collective-permute-done.5
  75.1 2.3 %collective-permute-start.6 = (bf16[1024,256]{1,0:T(8,128)(2,1)S(1)}, bf16[1024,256]{1,0:T(8,128)(2,1)S(1)}, u32[]{:S(2)}, u32[]{:S(2)}) collective-permute-start(bf16[1024,256]{1,0:T(8,128)(2,1)S(1)} %bitcast.20), channel_id=1, source_target_pairs={{0,8},{8,0},{16,24},{24,16},{32,40},{40,32},{48,56},{56,48},{64,72... | collective-permute-start | bytes 1572872 | tf_op jit(solution)/shard_map/ppermute | solution.py:238
  77.4 2.3 %far_window.1 = (f32[1,1024]{1,0:T(1,128)S(1)}, f32[1,1024]{1,0:T(1,128)S(1)}, f32[128,1024]{1,0:T(8,128)S(1)}) custom-call(s32[1]{0:T(128)} %bitcast.2.meta_ref, bf16[1024,256]{1,0:T(8,128)(2,1)S(1)} %bitcast.21, s32[64,128]{1,0:T(8,128)S(1)} %bitcast.31, bf16[256,1024]{1,0:T(8,128)(2,1)S(1)} %get-tuple-element.64.qt_ref, ...), custom_call_target="tpu_custom_call" | custom-call | flops 536870912 | bytes 1048576 | tf_op jit(solution)/shard_map/far_window/pallas_call | solution.py:239
  79.7 0.0 collective-permute-done.6.kv_ref
  79.7 2.4 %far_other_core.1 = bf16[128,1024]{1,0:T(8,128)(2,1)S(1)} custom-call(s32[1]{0:T(128)} %bitcast.2.meta_ref, bf16[1024,256]{1,0:T(8,128)(2,1)S(1)} %collective-permute-done.6.kv_ref, s32[64,128]{1,0:T(8,128)S(1)} %bitcast.32, bf16[256,1024]{1,0:T(8,128)(2,1)S(1)} %get-tuple-element.64.qt_ref, f32[1,1024]{1,0:T(1,128)S(1)} %get-tuple-element.72.m_in, ...), custom_call_target="tpu_custom_call" | custom-call | flops 536870912 | bytes 1048576 | tf_op jit(solution)/shard_map/far_other_core/pallas_call | solution.py:248
  82.1 15.3 %all_to_all.15 = bf16[8,16,1024]{2,1,0:T(8,128)(2,1)S(1)} all-to-all(bf16[8,16,1024]{2,1,0:T(8,128)(2,1)S(1)} %bitcast.19), channel_id=1, replica_groups=mesh['seq'=64,'head'=8] {'head'}, dimensions={0} | all-to-all | bytes 524288 | tf_op jit(solution)/shard_map/all_to_all | solution.py:262
  97.4 0.9 copy.14
  (16 shorter events, 0.1 us)
Async XLA Ops:
  1.6 5.1 %collective-permute-start.1 = (bf16[9,16,256]{2,1,0:T(8,128)(2,1)S(1)}, bf16[9,16,256]{2,1,0:T(8,128)(2,1)S(1)}, u32[]{:S(2)}, u32[]{:S(2)}) collective-permute-start(bf16[9,16,256]{2,1,0:T(8,128)(2,1)S(1)} %pad_maximum_fusion.2), channel_id=1, source_target_pairs={{0,128},{8,136},{16,144},{24,152},{32,160},{40,168},{48,176},{56,1... | collective-permute-start | bytes 221192 | tf_op jit(solution)/shard_map/ppermute | solution.py:187
  6.7 10.8 %copy-start.1 = (bf16[1,16,1,256]{3,1,2,0:T(8,128)(2,1)S(1)}, bf16[1,16,1,256]{3,1,2,0:T(8,128)(2,1)}, u32[]{:S(2)}) copy-start(bf16[1,16,1,256]{3,1,2,0:T(8,128)(2,1)} %param.10) | copy-start | bytes 24580
  7.4 22.2 %all-to-all-start = ((bf16[8,16,1536]{2,1,0:T(8,128)(2,1)}), bf16[8,16,1536]{2,1,0:T(8,128)(2,1)S(1)}, u32[]{:S(2)}, u32[]{:S(2)}) async-start(bf16[8,16,1536]{2,1,0:T(8,128)(2,1)} %pad_maximum_fusion.1), calls=%async_computation | async-start | bytes 786432 | tf_op jit(solution)/shard_map/all_to_all | solution.py:189
  17.5 6.6 %collective-permute-start.3 = (bf16[1,16,256]{2,1,0:T(8,128)(2,1)S(1)}, bf16[1,16,256]{2,1,0:T(8,128)(2,1)S(1)}, u32[]{:S(2)}, u32[]{:S(2)}) collective-permute-start(bf16[1,16,256]{2,1,0:T(8,128)(2,1)S(1)} %bitcast.34), channel_id=1, source_target_pairs={{0,384},{8,392},{16,400},{24,408},{32,416},{40,424},{48,432},{56,4... | collective-permute-start | bytes 24584 | tf_op jit(solution)/shard_map/ppermute | solution.py:192
  19.6 5.9 %collective-permute-start.2 = (bf16[1,16,256]{2,1,0:T(8,128)(2,1)S(1)}, bf16[1,16,256]{2,1,0:T(8,128)(2,1)S(1)}, u32[]{:S(2)}, u32[]{:S(2)}) collective-permute-start(bf16[1,16,256]{2,1,0:T(8,128)(2,1)S(1)} %bitcast.35), channel_id=1, source_target_pairs={{0,256},{8,264},{16,272},{24,280},{32,288},{40,296},{48,304},{56,3... | collective-permute-start | bytes 24584 | tf_op jit(solution)/shard_map/ppermute | solution.py:191
  30.8 13.9 %copy-start = (s32[8192]{0:T(1024)S(1)}, s32[8192]{0:T(1024)}, u32[]{:S(2)}) copy-start(s32[8192]{0:T(1024)} %param.9) | copy-start | bytes 98308
  30.8 22.2 %all-to-all-start.1 = ((bf16[8,192,256]{2,1,0:T(8,128)(2,1)}), bf16[8,192,256]{2,1,0:T(8,128)(2,1)S(1)}, u32[]{:S(2)}, u32[]{:S(2)}) async-start(bf16[8,192,256]{2,1,0:T(8,128)(2,1)} %pad_maximum_fusion), calls=%async_computation.1 | async-start | bytes 1572864 | tf_op jit(solution)/shard_map/all_to_all | solution.py:197
  37.9 6.8 %collective-permute-start.4 = (bf16[128,256]{1,0:T(8,128)(2,1)S(1)}, bf16[128,256]{1,0:T(8,128)(2,1)S(1)}, u32[]{:S(2)}, u32[]{:S(2)}) collective-permute-start(bf16[128,256]{1,0:T(8,128)(2,1)S(1)} %get-tuple-element.55.mine_ref), channel_id=1, source_target_pairs={{0,8},{8,0},{16,24},{24,16},{32,40},{40,32},{48,56},{56,48},{64,72... | collective-permute-start | bytes 196616 | tf_op jit(solution)/shard_map/ppermute | solution.py:199
  44.7 12.5 %copy-start.2 = (s32[1,32]{1,0:T(1,128)S(1)}, s32[1,32]{1,0:T(1,128)}, u32[]{:S(2)}) copy-start(s32[1,32]{1,0:T(1,128)} %param.11) | copy-start | bytes 388
  53.1 22.0 %collective-permute-start.5 = (bf16[8,128,256]{2,1,0:T(8,128)(2,1)S(1)}, bf16[8,128,256]{2,1,0:T(8,128)(2,1)S(1)}, u32[]{:S(2)}, u32[]{:S(2)}) collective-permute-start(bf16[8,128,256]{2,1,0:T(8,128)(2,1)S(1)} %slice.22), channel_id=1, source_target_pairs={{0,128},{8,136},{16,144},{24,152},{32,160},{40,168},{48,176},{56,1... | collective-permute-start | bytes 1572872 | tf_op jit(solution)/shard_map/ppermute | solution.py:218
  57.2 11.8 %collective-permute-start = (bf16[1536,256]{1,0:T(8,128)(2,1)S(1)}, bf16[1536,256]{1,0:T(8,128)(2,1)S(1)}, u32[]{:S(2)}, u32[]{:S(2)}) collective-permute-start(bf16[1536,256]{1,0:T(8,128)(2,1)S(1)} %bitcast.22), channel_id=1, source_target_pairs={{0,8},{8,0},{16,24},{24,16},{32,40},{40,32},{48,56},{56,48},{64,72... | collective-permute-start | bytes 2359304 | tf_op jit(solution)/shard_map/cond/branch_1_fun/ppermute | solution.py:223
  75.1 4.6 %collective-permute-start.6 = (bf16[1024,256]{1,0:T(8,128)(2,1)S(1)}, bf16[1024,256]{1,0:T(8,128)(2,1)S(1)}, u32[]{:S(2)}, u32[]{:S(2)}) collective-permute-start(bf16[1024,256]{1,0:T(8,128)(2,1)S(1)} %bitcast.20), channel_id=1, source_target_pairs={{0,8},{8,0},{16,24},{24,16},{32,40},{40,32},{48,56},{56,48},{64,72... | collective-permute-start | bytes 1572872 | tf_op jit(solution)/shard_map/ppermute | solution.py:238

commit v15 on v14

--- a/solution.py
+++ b/solution.py
@@ -126,8 +126,16 @@
     lax.fori_loop(0, steps, step, 0)
 
 
-def near_kernel(meta_ref, table_ref, kv_ref, side_ref, ids_ref, qt_ref, m_in, l_in, acc_in,
-                m_ref, l_ref, acc_ref, prefix_ref):
+def near_kernel(meta_ref, kv_ref, ids_ref, qt_ref, m_in, l_in, acc_in, m_ref, l_ref, acc_ref):
+    m_ref[...] = m_in[...]
+    l_ref[...] = l_in[...]
+    acc_ref[...] = acc_in[...]
+    own = meta_ref[0]
+    window(kv_ref, 0, SLOT, own % 2, own, starts_of(ids_ref, own), qt_ref, m_ref, l_ref, acc_ref)
+
+
+def near_side_kernel(meta_ref, table_ref, kv_ref, side_ref, ids_ref, qt_ref, m_in, l_in, acc_in,
+                     m_ref, l_ref, acc_ref, prefix_ref):
     m_ref[...] = m_in[...]
     l_ref[...] = l_in[...]
     acc_ref[...] = acc_in[...]
@@ -137,19 +145,10 @@
         page = table_ref[i]
         start = (page // 2) % NY * SLOT + ROWS + (x + NX - page // (2 * NY)) % NX * PAGE
         rows = pl.ds(pl.multiple_of(start, PAGE), PAGE)
-
-        @pl.when(page % 2 == core)
-        def _():
-            prefix_ref[i * PAGE:(i + 1) * PAGE, :] = kv_ref[rows, :]
-
-        @pl.when(page % 2 != core)
-        def _():
-            prefix_ref[i * PAGE:(i + 1) * PAGE, :] = side_ref[rows, :]
+        prefix_ref[i * PAGE:(i + 1) * PAGE, :] = jnp.where(page % 2 == core, kv_ref[rows, :], side_ref[rows, :])
 
     fold(prefix_ref[:, :D], prefix_ref[:, D:], None, qt_ref, m_ref, l_ref, acc_ref)
-    limits = starts_of(ids_ref, own)
-    window(kv_ref, 0, SLOT, core, own, limits, qt_ref, m_ref, l_ref, acc_ref)
-    window(side_ref, 0, SLOT, 1 - core, own, limits, qt_ref, m_ref, l_ref, acc_ref)
+    window(side_ref, 0, SLOT, 1 - core, own, starts_of(ids_ref, own), qt_ref, m_ref, l_ref, acc_ref)
 
 
 def far_kernel(meta_ref, kv_ref, ids_ref, qt_ref, m_in, l_in, acc_in, m_ref, l_ref, acc_ref):
@@ -221,18 +220,27 @@
         near, qt, now = operands
         near = near.reshape(NY * SLOT, PAIR)
         near_side = lax.ppermute(near, "seq", SWAP)
+        now = pl.pallas_call(
+            near_kernel,
+            out_shape=state,
+            in_specs=[SM] + [VM] * 6,
+            out_specs=[VM] * 3,
+            compiler_params=params,
+            cost_estimate=cost(1024),
+            name="near_window",
+        )(meta, near, ids, qt, *now)
         return list(pl.pallas_call(
-            near_kernel,
+            near_side_kernel,
             out_shape=state,
             in_specs=[SM, SM] + [VM] * 7,
             out_specs=[VM] * 3,
             scratch_shapes=[pltpu.VMEM((PAGES * PAGE, PAIR), jnp.bfloat16)],
             compiler_params=params,
-            cost_estimate=cost(2560),
-            name="near_window_and_prefix",
+            cost_estimate=cost(1536),
+            name="near_other_core_and_prefix",
         )(meta, page_table.reshape(PAGES), near, near_side, ids, qt, *now))
 
-    now = lax.cond(branch_ids[0] >= 0, near_part, lambda operands: list(operands[2]), (near, qt, now))
+    now = lax.cond(me < 2 * NX * NY, near_part, lambda operands: list(operands[2]), (near, qt, now))
     far, now = lax.optimization_barrier((far, now))
     far = far.reshape(NY * ROWS, PAIR)
     far_side = lax.ppermute(far, "seq", SWAP)

time: 98.9 us -> 97.3 us (0.984)
  the two profiles are of different devices: /device:TPU:13 before, /device:TPU:1 now
where the time goes in v15:
time: 97.3 us; the launch traced here: 96.7 us
  starting transfers between devices  47.3 us (49%)
  waiting for transfers between devices  25 us (26%)
  blocking collectives  14.6 us (15%)
  Pallas kernels  4.16 us (4%)
  local copies, waits for them, and re-layouts  2.89 us (3%)
  other arithmetic  2.55 us (3%)
    all_to_all x1, blocking collectives, per_device(): lax.all_to_all(out.reshape(8, ROWS // 8, GROUP * D), 'head', split_axis=0...  14.6 us
    all_to_all x1, waiting for transfers between devices, per_device(): lax.all_to_all(send, 'seq', split_axis=0, concat_axis=0, tiled=True, axis...  12.4 us
    all_to_all x1, starting transfers between devices, per_device(): lax.all_to_all(wide, 'head', split_axis=0, concat_axis=0, tiled=True)  10.2 us
    all_to_all x1, starting transfers between devices, per_device(): lax.all_to_all(send, 'seq', split_axis=0, concat_axis=0, tiled=True, axis...  6.95 us
    ppermute x1, starting transfers between devices, per_device(): far_side = lax.ppermute(far, 'seq', SWAP)  6.85 us
    ppermute x1, starting transfers between devices, near_part(): near_side = lax.ppermute(near, 'seq', SWAP)  6.2 us
    ppermute x1, starting transfers between devices, per_device(): side = lax.ppermute(later, 'seq', SWAP)  5.62 us
    ppermute x1, starting transfers between devices, per_device(): one_raw = lax.ppermute(raw, 'seq', x_ring(1))  3.94 us
  transfers between devices with their start and end apart: 9, of which 8 were waited for; matrix products, arithmetic and copies ran while one was open for 1% of the time, Pallas kernels for 4%

profile of v15, /device:TPU:1, one launch (start us, length us, event | category | flops | bytes accessed | tf_op | source)
XLA Modules:
  0.0 96.7 jit_solution(6276290406636032347)
XLA Ops:
  0.0 0.9 copy.18
  0.9 0.7 pad_maximum_fusion.2
  1.6 3.9 %collective-permute-start.1 = (bf16[9,16,256]{2,1,0:T(8,128)(2,1)S(1)}, bf16[9,16,256]{2,1,0:T(8,128)(2,1)S(1)}, u32[]{:S(2)}, u32[]{:S(2)}) collective-permute-start(bf16[9,16,256]{2,1,0:T(8,128)(2,1)S(1)} %pad_maximum_fusion.2), channel_id=1, source_target_pairs={{0,128},{8,136},{16,144},{24,152},{32,160},{40,168},{48,176},{56,1... | collective-permute-start | bytes 221192 | tf_op jit(solution)/shard_map/ppermute | solution.py:186
  5.5 1.1 %copy.17 = bf16[16,8,1024]{2,0,1:T(8,128)(2,1)S(1)} copy(bf16[16,8,1024]{2,1,0:T(8,128)(2,1)} %param.7) | data formatting | bytes 524288 | tf_op args[0]
  6.6 1.9 %collective-permute-done.1 = bf16[9,16,256]{2,1,0:T(8,128)(2,1)S(1)} collective-permute-done((bf16[9,16,256]{2,1,0:T(8,128)(2,1)S(1)}, bf16[9,16,256]{2,1,0:T(8,128)(2,1)S(1)}, u32[]{:S(2)}, u32[]{:S(2)}) %collective-permute-start.1) | collective-permute-done | bytes 73760 | tf_op jit(solution)/shard_map/ppermute | solution.py:186
  8.5 0.8 pad_maximum_fusion.1
  9.3 10.2 %all-to-all-start = ((bf16[8,16,1536]{2,1,0:T(8,128)(2,1)}), bf16[8,16,1536]{2,1,0:T(8,128)(2,1)S(1)}, u32[]{:S(2)}, u32[]{:S(2)}) async-start(bf16[8,16,1536]{2,1,0:T(8,128)(2,1)} %pad_maximum_fusion.1), calls=%async_computation | async-start | bytes 786432 | tf_op jit(solution)/shard_map/all_to_all | solution.py:188
  19.5 3.2 %collective-permute-start.3 = (bf16[1,16,256]{2,1,0:T(8,128)(2,1)S(1)}, bf16[1,16,256]{2,1,0:T(8,128)(2,1)S(1)}, u32[]{:S(2)}, u32[]{:S(2)}) collective-permute-start(bf16[1,16,256]{2,1,0:T(8,128)(2,1)S(1)} %bitcast.34), channel_id=1, source_target_pairs={{0,384},{8,392},{16,400},{24,408},{32,416},{40,424},{48,432},{56,4... | collective-permute-start | bytes 24584 | tf_op jit(solution)/shard_map/ppermute | solution.py:191
  22.7 2.4 %collective-permute-start.2 = (bf16[1,16,256]{2,1,0:T(8,128)(2,1)S(1)}, bf16[1,16,256]{2,1,0:T(8,128)(2,1)S(1)}, u32[]{:S(2)}, u32[]{:S(2)}) collective-permute-start(bf16[1,16,256]{2,1,0:T(8,128)(2,1)S(1)} %bitcast.35), channel_id=1, source_target_pairs={{0,256},{8,264},{16,272},{24,280},{32,288},{40,296},{48,304},{56,3... | collective-permute-start | bytes 24584 | tf_op jit(solution)/shard_map/ppermute | solution.py:190
  25.2 0.0 collective-permute-done.3
  25.2 3.7 %collective-permute-done.2 = bf16[1,16,256]{2,1,0:T(8,128)(2,1)S(1)} collective-permute-done((bf16[1,16,256]{2,1,0:T(8,128)(2,1)S(1)}, bf16[1,16,256]{2,1,0:T(8,128)(2,1)S(1)}, u32[]{:S(2)}, u32[]{:S(2)}) %collective-permute-start.2) | collective-permute-done | bytes 8224 | tf_op jit(solution)/shard_map/ppermute | solution.py:190
  28.9 2.8 %all-to-all-done = bf16[8,16,1536]{2,1,0:T(8,128)(2,1)S(1)} async-done(((bf16[8,16,1536]{2,1,0:T(8,128)(2,1)}), bf16[8,16,1536]{2,1,0:T(8,128)(2,1)S(1)}, u32[]{:S(2)}, u32[]{:S(2)}) %all-to-all-start) | async-done | bytes 393248 | tf_op jit(solution)/shard_map/all_to_all | solution.py:188
  31.7 0.1 broadcast_select_fusion
  31.9 0.9 pad_maximum_fusion
  32.8 7.0 %all-to-all-start.1 = ((bf16[8,192,256]{2,1,0:T(8,128)(2,1)}), bf16[8,192,256]{2,1,0:T(8,128)(2,1)S(1)}, u32[]{:S(2)}, u32[]{:S(2)}) async-start(bf16[8,192,256]{2,1,0:T(8,128)(2,1)} %pad_maximum_fusion), calls=%async_computation.1 | async-start | bytes 1572864 | tf_op jit(solution)/shard_map/all_to_all | solution.py:196
  39.8 5.6 %collective-permute-start.4 = (bf16[128,256]{1,0:T(8,128)(2,1)S(1)}, bf16[128,256]{1,0:T(8,128)(2,1)S(1)}, u32[]{:S(2)}, u32[]{:S(2)}) collective-permute-start(bf16[128,256]{1,0:T(8,128)(2,1)S(1)} %get-tuple-element.58.mine_ref), channel_id=1, source_target_pairs={{0,8},{8,0},{16,24},{24,16},{32,40},{40,32},{48,56},{56,48},{64,72... | collective-permute-start | bytes 196616 | tf_op jit(solution)/shard_map/ppermute | solution.py:198
  45.4 0.9 collective-permute-done.4.side_ref
  46.3 1.1 %own_chip.1 = (bf16[256,1024]{1,0:T(8,128)(2,1)S(1)}, f32[1,1024]{1,0:T(1,128)S(1)}, f32[1,1024]{1,0:T(1,128)S(1)}, f32[128,1024]{1,0:T(8,128)S(1)}) custom-call(s32[1]{0:T(128)} %bitcast.2.meta_ref, bf16[128,256]{1,0:T(8,128)(2,1)S(1)} %get-tuple-element.58.mine_ref, bf16[128,256]{1,0:T(8,128)(2,1)S(1)} %collective-permute-done.4.side_ref, ...), custom_call_target="tpu_custom_call" | custom-call | flops 134217728 | bytes 1048576 | tf_op jit(solution)/shard_map/own_chip/pallas_call | solution.py:207
  47.4 12.4 %all-to-all-done.1 = bf16[8,192,256]{2,1,0:T(8,128)(2,1)S(1)} async-done(((bf16[8,192,256]{2,1,0:T(8,128)(2,1)}), bf16[8,192,256]{2,1,0:T(8,128)(2,1)S(1)}, u32[]{:S(2)}, u32[]{:S(2)}) %all-to-all-start.1) | async-done | bytes 786464 | tf_op jit(solution)/shard_map/all_to_all | solution.py:196
  59.9 1.9 %collective-permute-start.5 = (bf16[8,128,256]{2,1,0:T(8,128)(2,1)S(1)}, bf16[8,128,256]{2,1,0:T(8,128)(2,1)S(1)}, u32[]{:S(2)}, u32[]{:S(2)}) collective-permute-start(bf16[8,128,256]{2,1,0:T(8,128)(2,1)S(1)} %slice.19), channel_id=1, source_target_pairs={{0,128},{8,136},{16,144},{24,152},{32,160},{40,168},{48,176},{56,1... | collective-permute-start | bytes 1572872 | tf_op jit(solution)/shard_map/ppermute | solution.py:217
  61.8 9.9 %conditional.1 = ((f32[1,1024]{1,0:T(1,128)S(1)}, f32[1,1024]{1,0:T(1,128)S(1)}, f32[128,1024]{1,0:T(8,128)S(1)})) conditional(s32[]{:T(128)} %convert_element_type.3, (f32[1,1024]{1,0:T(1,128)S(1)}, f32[1,1024]{1,0:T(1,128)S(1)}, f32[128,1024]{1,0:T(8,128)S(1)}) %tuple.16, (s32[1,32]{1,0:T(1,128)S(1)}, bf16[8,192,256]{2,1,0:T(8,128)(2,1)S(1)}, ...), branch_computations={%region_0.1_spmd, %region_1.2_spmd} | conditional | flops 1342177280 | bytes 5242928 | solution.py:243
  61.8 6.2 %collective-permute-start = (bf16[1536,256]{1,0:T(8,128)(2,1)S(1)}, bf16[1536,256]{1,0:T(8,128)(2,1)S(1)}, u32[]{:S(2)}, u32[]{:S(2)}) collective-permute-start(bf16[1536,256]{1,0:T(8,128)(2,1)S(1)} %bitcast.21), channel_id=1, source_target_pairs={{0,8},{8,0},{16,24},{24,16},{32,40},{40,32},{48,56},{56,48},{64,72... | collective-permute-start | bytes 2359304 | tf_op jit(solution)/shard_map/cond/branch_1_fun/ppermute | solution.py:222
  68.0 0.4 near_window.1
  68.4 1.5 %collective-permute-done.side_ref = bf16[1536,256]{1,0:T(8,128)(2,1)S(1)} collective-permute-done((bf16[1536,256]{1,0:T(8,128)(2,1)S(1)}, bf16[1536,256]{1,0:T(8,128)(2,1)S(1)}, u32[]{:S(2)}, u32[]{:S(2)}) %collective-permute-start) | collective-permute-done | bytes 786464 | tf_op jit(solution)/shard_map/cond/branch_1_fun/ppermute | solution.py:222
  69.9 1.8 %near_other_core_and_prefix.1 = (f32[1,1024]{1,0:T(1,128)S(1)}, f32[1,1024]{1,0:T(1,128)S(1)}, f32[128,1024]{1,0:T(8,128)S(1)}) custom-call(s32[1]{0:T(128)} %get-tuple-element.27.meta_ref, s32[32]{0:T(128)S(1)} %bitcast.37, bf16[1536,256]{1,0:T(8,128)(2,1)S(1)} %bitcast.23, bf16[1536,256]{1,0:T(8,128)(2,1)S(1)} %collective-permute-done.side_ref, ...), custom_call_target="tpu_custom_call" | custom-call | flops 805306368 | bytes 1048576 | tf_op jit(solution)/shard_map/cond/branch_1_fun/near_other_core_and_prefix/pallas_call | solution.py:232
  71.8 0.6 collective-permute-done.5
  72.4 6.9 %collective-permute-start.6 = (bf16[1024,256]{1,0:T(8,128)(2,1)S(1)}, bf16[1024,256]{1,0:T(8,128)(2,1)S(1)}, u32[]{:S(2)}, u32[]{:S(2)}) collective-permute-start(bf16[1024,256]{1,0:T(8,128)(2,1)S(1)} %bitcast.19), channel_id=1, source_target_pairs={{0,8},{8,0},{16,24},{24,16},{32,40},{40,32},{48,56},{56,48},{64,72... | collective-permute-start | bytes 1572872 | tf_op jit(solution)/shard_map/ppermute | solution.py:246
  79.2 0.4 far_window.1
  79.6 1.1 %collective-permute-done.6.kv_ref = bf16[1024,256]{1,0:T(8,128)(2,1)S(1)} collective-permute-done((bf16[1024,256]{1,0:T(8,128)(2,1)S(1)}, bf16[1024,256]{1,0:T(8,128)(2,1)S(1)}, u32[]{:S(2)}, u32[]{:S(2)}) %collective-permute-start.6) | collective-permute-done | bytes 524320 | tf_op jit(solution)/shard_map/ppermute | solution.py:246
  80.8 0.5 far_other_core.1
  81.2 14.6 %all_to_all.15 = bf16[8,16,1024]{2,1,0:T(8,128)(2,1)S(1)} all-to-all(bf16[8,16,1024]{2,1,0:T(8,128)(2,1)S(1)} %bitcast.18), channel_id=1, replica_groups=mesh['seq'=64,'head'=8] {'head'}, dimensions={0} | all-to-all | bytes 524288 | tf_op jit(solution)/shard_map/all_to_all | solution.py:270
  95.8 0.9 copy.14
  (13 shorter events, 0.1 us)
Async XLA Ops:
  1.6 6.9 %collective-permute-start.1 = (bf16[9,16,256]{2,1,0:T(8,128)(2,1)S(1)}, bf16[9,16,256]{2,1,0:T(8,128)(2,1)S(1)}, u32[]{:S(2)}, u32[]{:S(2)}) collective-permute-start(bf16[9,16,256]{2,1,0:T(8,128)(2,1)S(1)} %pad_maximum_fusion.2), channel_id=1, source_target_pairs={{0,128},{8,136},{16,144},{24,152},{32,160},{40,168},{48,176},{56,1... | collective-permute-start | bytes 221192 | tf_op jit(solution)/shard_map/ppermute | solution.py:186
  8.5 11.0 %copy-start.1 = (bf16[1,16,1,256]{3,1,2,0:T(8,128)(2,1)S(1)}, bf16[1,16,1,256]{3,1,2,0:T(8,128)(2,1)}, u32[]{:S(2)}) copy-start(bf16[1,16,1,256]{3,1,2,0:T(8,128)(2,1)} %param.10) | copy-start | bytes 24580
  9.3 22.4 %all-to-all-start = ((bf16[8,16,1536]{2,1,0:T(8,128)(2,1)}), bf16[8,16,1536]{2,1,0:T(8,128)(2,1)S(1)}, u32[]{:S(2)}, u32[]{:S(2)}) async-start(bf16[8,16,1536]{2,1,0:T(8,128)(2,1)} %pad_maximum_fusion.1), calls=%async_computation | async-start | bytes 786432 | tf_op jit(solution)/shard_map/all_to_all | solution.py:188
  19.5 5.7 %collective-permute-start.3 = (bf16[1,16,256]{2,1,0:T(8,128)(2,1)S(1)}, bf16[1,16,256]{2,1,0:T(8,128)(2,1)S(1)}, u32[]{:S(2)}, u32[]{:S(2)}) collective-permute-start(bf16[1,16,256]{2,1,0:T(8,128)(2,1)S(1)} %bitcast.34), channel_id=1, source_target_pairs={{0,384},{8,392},{16,400},{24,408},{32,416},{40,424},{48,432},{56,4... | collective-permute-start | bytes 24584 | tf_op jit(solution)/shard_map/ppermute | solution.py:191
  22.7 6.2 %collective-permute-start.2 = (bf16[1,16,256]{2,1,0:T(8,128)(2,1)S(1)}, bf16[1,16,256]{2,1,0:T(8,128)(2,1)S(1)}, u32[]{:S(2)}, u32[]{:S(2)}) collective-permute-start(bf16[1,16,256]{2,1,0:T(8,128)(2,1)S(1)} %bitcast.35), channel_id=1, source_target_pairs={{0,256},{8,264},{16,272},{24,280},{32,288},{40,296},{48,304},{56,3... | collective-permute-start | bytes 24584 | tf_op jit(solution)/shard_map/ppermute | solution.py:190
  32.8 13.5 %copy-start = (s32[8192]{0:T(1024)S(1)}, s32[8192]{0:T(1024)}, u32[]{:S(2)}) copy-start(s32[8192]{0:T(1024)} %param.9) | copy-start | bytes 98308
  32.8 27.0 %all-to-all-start.1 = ((bf16[8,192,256]{2,1,0:T(8,128)(2,1)}), bf16[8,192,256]{2,1,0:T(8,128)(2,1)S(1)}, u32[]{:S(2)}, u32[]{:S(2)}) async-start(bf16[8,192,256]{2,1,0:T(8,128)(2,1)} %pad_maximum_fusion), calls=%async_computation.1 | async-start | bytes 1572864 | tf_op jit(solution)/shard_map/all_to_all | solution.py:196
  39.8 6.5 %collective-permute-start.4 = (bf16[128,256]{1,0:T(8,128)(2,1)S(1)}, bf16[128,256]{1,0:T(8,128)(2,1)S(1)}, u32[]{:S(2)}, u32[]{:S(2)}) collective-permute-start(bf16[128,256]{1,0:T(8,128)(2,1)S(1)} %get-tuple-element.58.mine_ref), channel_id=1, source_target_pairs={{0,8},{8,0},{16,24},{24,16},{32,40},{40,32},{48,56},{56,48},{64,72... | collective-permute-start | bytes 196616 | tf_op jit(solution)/shard_map/ppermute | solution.py:198
  46.3 15.5 %copy-start.2 = (s32[1,32]{1,0:T(1,128)S(1)}, s32[1,32]{1,0:T(1,128)}, u32[]{:S(2)}) copy-start(s32[1,32]{1,0:T(1,128)} %param.11) | copy-start | bytes 388
  59.9 12.5 %collective-permute-start.5 = (bf16[8,128,256]{2,1,0:T(8,128)(2,1)S(1)}, bf16[8,128,256]{2,1,0:T(8,128)(2,1)S(1)}, u32[]{:S(2)}, u32[]{:S(2)}) collective-permute-start(bf16[8,128,256]{2,1,0:T(8,128)(2,1)S(1)} %slice.19), channel_id=1, source_target_pairs={{0,128},{8,136},{16,144},{24,152},{32,160},{40,168},{48,176},{56,1... | collective-permute-start | bytes 1572872 | tf_op jit(solution)/shard_map/ppermute | solution.py:217
  61.8 8.1 %collective-permute-start = (bf16[1536,256]{1,0:T(8,128)(2,1)S(1)}, bf16[1536,256]{1,0:T(8,128)(2,1)S(1)}, u32[]{:S(2)}, u32[]{:S(2)}) collective-permute-start(bf16[1536,256]{1,0:T(8,128)(2,1)S(1)} %bitcast.21), channel_id=1, source_target_pairs={{0,8},{8,0},{16,24},{24,16},{32,40},{40,32},{48,56},{56,48},{64,72... | collective-permute-start | bytes 2359304 | tf_op jit(solution)/shard_map/cond/branch_1_fun/ppermute | solution.py:222
  72.4 8.4 %collective-permute-start.6 = (bf16[1024,256]{1,0:T(8,128)(2,1)S(1)}, bf16[1024,256]{1,0:T(8,128)(2,1)S(1)}, u32[]{:S(2)}, u32[]{:S(2)}) collective-permute-start(bf16[1024,256]{1,0:T(8,128)(2,1)S(1)} %bitcast.19), channel_id=1, source_target_pairs={{0,8},{8,0},{16,24},{24,16},{32,40},{40,32},{48,56},{56,48},{64,72... | collective-permute-start | bytes 1572872 | tf_op jit(solution)/shard_map/ppermute | solution.py:246

commit v16 on v15

--- a/solution.py
+++ b/solution.py
@@ -28,6 +28,10 @@
     ]
 
 
+def x_next():
+    return [pair for pair in x_ring(1) if pair[0] < pair[1]]
+
+
 SWAP = [(i, i ^ 1) for i in range(2 * NX * NY)]
 Y_GROUPS = [[(x * NY + y) * 2 + c for y in range(NY)] for x in range(NX) for c in range(2)]
 
@@ -74,9 +78,12 @@
     return (key_rows >= row_start) & (key_rows <= query_rows)
 
 
-def own_kernel(meta_ref, mine_ref, side_ref, ids_ref, q_ref, qt_ref, m_ref, l_ref, acc_ref):
+def own_kernel(meta_ref, mine_ref, side_ref, ids_ref, q_ref, qt_ref, start_ref, limit_ref, m_ref, l_ref, acc_ref):
     own = meta_ref[0]
     row_start, first, last = starts_of(ids_ref, own)
+    start_ref[...] = row_start
+    limit_ref[0] = first
+    limit_ref[1] = last
     for g in range(GROUP):
         scaled = q_ref[:, g * D:(g + 1) * D].astype(jnp.float32) * SCALE2
         high = scaled.astype(jnp.bfloat16)
@@ -94,8 +101,8 @@
         fold(side_ref[:, :D], side_ref[:, D:], mask_of(own - 1, own, row_start), *state)
 
 
-def window(kv_ref, skip, slot, core, own, limits, qt_ref, m_ref, l_ref, acc_ref):
-    row_start, first, last = limits
+def window(kv_ref, skip, slot, core, own, start_ref, limit_ref, qt_ref, m_ref, l_ref, acc_ref):
+    first, last = limit_ref[0], limit_ref[1]
     chip = own // 2 - skip
     lowest = jnp.maximum((jnp.maximum(first // ROWS - core, -1) + 1) // 2, chip - NEAR)
     steps = jnp.maximum(chip - lowest + BLOCKS - 1, 0) // BLOCKS
@@ -117,7 +124,7 @@
         @pl.when(jnp.logical_not(whole))
         def _():
             mask = jnp.concatenate(
-                [mask_of(2 * (base + b) + core, own, row_start) for b in range(BLOCKS)], axis=0
+                [mask_of(2 * (base + b) + core, own, start_ref[...]) for b in range(BLOCKS)], axis=0
             )
             fold(keys, values, mask, qt_ref, m_ref, l_ref, acc_ref)
 
@@ -126,15 +133,15 @@
     lax.fori_loop(0, steps, step, 0)
 
 
-def near_kernel(meta_ref, kv_ref, ids_ref, qt_ref, m_in, l_in, acc_in, m_ref, l_ref, acc_ref):
-    m_ref[...] = m_in[...]
-    l_ref[...] = l_in[...]
-    acc_ref[...] = acc_in[...]
-    own = meta_ref[0]
-    window(kv_ref, 0, SLOT, own % 2, own, starts_of(ids_ref, own), qt_ref, m_ref, l_ref, acc_ref)
-
-
-def near_side_kernel(meta_ref, table_ref, kv_ref, side_ref, ids_ref, qt_ref, m_in, l_in, acc_in,
+def near_kernel(meta_ref, kv_ref, start_ref, limit_ref, qt_ref, m_in, l_in, acc_in, m_ref, l_ref, acc_ref):
+    m_ref[...] = m_in[...]
+    l_ref[...] = l_in[...]
+    acc_ref[...] = acc_in[...]
+    own = meta_ref[0]
+    window(kv_ref, 0, SLOT, own % 2, own, start_ref, limit_ref, qt_ref, m_ref, l_ref, acc_ref)
+
+
+def near_side_kernel(meta_ref, table_ref, kv_ref, side_ref, start_ref, limit_ref, qt_ref, m_in, l_in, acc_in,
                      m_ref, l_ref, acc_ref, prefix_ref):
     m_ref[...] = m_in[...]
     l_ref[...] = l_in[...]
@@ -148,23 +155,23 @@
         prefix_ref[i * PAGE:(i + 1) * PAGE, :] = jnp.where(page % 2 == core, kv_ref[rows, :], side_ref[rows, :])
 
     fold(prefix_ref[:, :D], prefix_ref[:, D:], None, qt_ref, m_ref, l_ref, acc_ref)
-    window(side_ref, 0, SLOT, 1 - core, own, starts_of(ids_ref, own), qt_ref, m_ref, l_ref, acc_ref)
-
-
-def far_kernel(meta_ref, kv_ref, ids_ref, qt_ref, m_in, l_in, acc_in, m_ref, l_ref, acc_ref):
-    m_ref[...] = m_in[...]
-    l_ref[...] = l_in[...]
-    acc_ref[...] = acc_in[...]
-    own = meta_ref[0]
-    window(kv_ref, NEAR, ROWS, own % 2, own, starts_of(ids_ref, own), qt_ref, m_ref, l_ref, acc_ref)
-
-
-def last_kernel(meta_ref, kv_ref, ids_ref, qt_ref, m_in, l_in, acc_in, out_ref, m_ref, l_ref, acc_ref):
-    m_ref[...] = m_in[...]
-    l_ref[...] = l_in[...]
-    acc_ref[...] = acc_in[...]
-    own = meta_ref[0]
-    window(kv_ref, NEAR, ROWS, 1 - own % 2, own, starts_of(ids_ref, own), qt_ref, m_ref, l_ref, acc_ref)
+    window(side_ref, 0, SLOT, 1 - core, own, start_ref, limit_ref, qt_ref, m_ref, l_ref, acc_ref)
+
+
+def far_kernel(meta_ref, kv_ref, start_ref, limit_ref, qt_ref, m_in, l_in, acc_in, m_ref, l_ref, acc_ref):
+    m_ref[...] = m_in[...]
+    l_ref[...] = l_in[...]
+    acc_ref[...] = acc_in[...]
+    own = meta_ref[0]
+    window(kv_ref, NEAR, ROWS, own % 2, own, start_ref, limit_ref, qt_ref, m_ref, l_ref, acc_ref)
+
+
+def last_kernel(meta_ref, kv_ref, start_ref, limit_ref, qt_ref, m_in, l_in, acc_in, out_ref, m_ref, l_ref, acc_ref):
+    m_ref[...] = m_in[...]
+    l_ref[...] = l_in[...]
+    acc_ref[...] = acc_in[...]
+    own = meta_ref[0]
+    window(kv_ref, NEAR, ROWS, 1 - own % 2, own, start_ref, limit_ref, qt_ref, m_ref, l_ref, acc_ref)
     result = (acc_ref[...] * (1.0 / l_ref[...])).astype(jnp.bfloat16)
     for g in range(GROUP):
         out_ref[:, g * D:(g + 1) * D] = result[:, g * ROWS:(g + 1) * ROWS].T
@@ -204,17 +211,21 @@
         jax.ShapeDtypeStruct((D, QR), jnp.float32),
     ]
     params = pltpu.CompilerParams(vmem_limit_bytes=40 * 1024 * 1024)
-    qt, *now = pl.pallas_call(
+    qt, starts, limits, *now = pl.pallas_call(
         own_kernel,
-        out_shape=[jax.ShapeDtypeStruct((PAIR, QR), jnp.bfloat16)] + state,
+        out_shape=[
+            jax.ShapeDtypeStruct((PAIR, QR), jnp.bfloat16),
+            jax.ShapeDtypeStruct((1, ROWS), jnp.int32),
+            jax.ShapeDtypeStruct((2,), jnp.int32),
+        ] + state,
         in_specs=[SM] + [VM] * 4,
-        out_specs=[VM] * 4,
+        out_specs=[VM, VM, SM] + [VM] * 3,
         compiler_params=params,
         cost_estimate=cost(256),
         name="own_chip",
     )(meta, own, side, ids, wide)
     near, qt, now = lax.optimization_barrier((near, qt, now))
-    far = lax.ppermute(near[:, :ROWS], "seq", x_ring(1))
+    far = lax.ppermute(near[:, :ROWS], "seq", x_next())
 
     def near_part(operands):
         near, qt, now = operands
@@ -223,22 +234,22 @@
         now = pl.pallas_call(
             near_kernel,
             out_shape=state,
-            in_specs=[SM] + [VM] * 6,
+            in_specs=[SM, VM, VM, SM] + [VM] * 4,
             out_specs=[VM] * 3,
             compiler_params=params,
             cost_estimate=cost(1024),
             name="near_window",
-        )(meta, near, ids, qt, *now)
+        )(meta, near, starts, limits, qt, *now)
         return list(pl.pallas_call(
             near_side_kernel,
             out_shape=state,
-            in_specs=[SM, SM] + [VM] * 7,
+            in_specs=[SM, SM, VM, VM, VM, SM] + [VM] * 4,
             out_specs=[VM] * 3,
             scratch_shapes=[pltpu.VMEM((PAGES * PAGE, PAIR), jnp.bfloat16)],
             compiler_params=params,
             cost_estimate=cost(1536),
             name="near_other_core_and_prefix",
-        )(meta, page_table.reshape(PAGES), near, near_side, ids, qt, *now))
+        )(meta, page_table.reshape(PAGES), near, near_side, starts, limits, qt, *now))
 
     now = lax.cond(me < 2 * NX * NY, near_part, lambda operands: list(operands[2]), (near, qt, now))
     far, now = lax.optimization_barrier((far, now))
@@ -247,16 +258,16 @@
     now = pl.pallas_call(
         far_kernel,
         out_shape=state,
-        in_specs=[SM] + [VM] * 6,
+        in_specs=[SM, VM, VM, SM] + [VM] * 4,
         out_specs=[VM] * 3,
         compiler_params=params,
         cost_estimate=cost(1024),
         name="far_window",
-    )(meta, far, ids, qt, *now)
+    )(meta, far, starts, limits, qt, *now)
     out = pl.pallas_call(
         last_kernel,
         out_shape=jax.ShapeDtypeStruct((ROWS, GROUP * D), jnp.bfloat16),
-        in_specs=[SM] + [VM] * 6,
+        in_specs=[SM, VM, VM, SM] + [VM] * 4,
         out_specs=VM,
         scratch_shapes=[
             pltpu.VMEM((1, QR), jnp.float32),
@@ -266,7 +277,7 @@
         compiler_params=params,
         cost_estimate=cost(1024),
         name="far_other_core",
-    )(meta, far_side, ids, qt, *now)
+    )(meta, far_side, starts, limits, qt, *now)
     out = lax.all_to_all(out.reshape(8, ROWS // 8, GROUP * D), "head", split_axis=0, concat_axis=0, tiled=True)
     return jnp.transpose(out, (1, 0, 2))
 

time: 97.3 us -> 95.6 us (0.983)
  the two profiles are of different devices: /device:TPU:1 before, /device:TPU:6 now
where the time goes in v16:
time: 95.6 us; the launch traced here: 94.9 us
  starting transfers between devices  35.8 us (37%)
  waiting for transfers between devices  28.6 us (30%)
  blocking collectives  16.1 us (17%)
  Pallas kernels  8.72 us (9%)
  local copies, waits for them, and re-layouts  2.89 us (3%)
  other arithmetic  2.55 us (3%)
    all_to_all x1, blocking collectives, per_device(): lax.all_to_all(out.reshape(8, ROWS // 8, GROUP * D), 'head', split_axis=0...  16.1 us
    all_to_all x1, waiting for transfers between devices, per_device(): lax.all_to_all(send, 'seq', split_axis=0, concat_axis=0, tiled=True, axis...  16 us
    ppermute x1, starting transfers between devices, per_device(): one_raw = lax.ppermute(raw, 'seq', x_ring(1))  7.75 us
    all_to_all x1, starting transfers between devices, per_device(): lax.all_to_all(send, 'seq', split_axis=0, concat_axis=0, tiled=True, axis...  7.23 us
    all_to_all x1, starting transfers between devices, per_device(): lax.all_to_all(wide, 'head', split_axis=0, concat_axis=0, tiled=True)  6.84 us
    ppermute x1, starting transfers between devices, per_device(): two_page = lax.ppermute(page, 'seq', x_ring(2))  4.23 us
    all_to_all x1, waiting for transfers between devices, per_device(): lax.all_to_all(wide, 'head', split_axis=0, concat_axis=0, tiled=True)  3.73 us
    pallas_call x1, Pallas kernels, near_part(): pl.pallas_call(near_side_kernel, out_shape=state, in_specs=[SM, SM, VM, V...  3.7 us
  transfers between devices with their start and end apart: 9, of which 7 were waited for; matrix products, arithmetic and copies ran while one was open for 1% of the time, Pallas kernels for 8%

profile of v16, /device:TPU:6, one launch (start us, length us, event | category | flops | bytes accessed | tf_op | source)
XLA Modules:
  0.0 94.9 jit_solution(5236973321869476746)
XLA Ops:
  0.0 0.9 copy.18
  0.9 0.7 pad_maximum_fusion.2
  1.6 7.7 %collective-permute-start.1 = (bf16[9,16,256]{2,1,0:T(8,128)(2,1)S(1)}, bf16[9,16,256]{2,1,0:T(8,128)(2,1)S(1)}, u32[]{:S(2)}, u32[]{:S(2)}) collective-permute-start(bf16[9,16,256]{2,1,0:T(8,128)(2,1)S(1)} %pad_maximum_fusion.2), channel_id=1, source_target_pairs={{0,128},{8,136},{16,144},{24,152},{32,160},{40,168},{48,176},{56,1... | collective-permute-start | bytes 221192 | tf_op jit(solution)/shard_map/ppermute | solution.py:193
  9.3 1.1 %copy.17 = bf16[16,8,1024]{2,0,1:T(8,128)(2,1)S(1)} copy(bf16[16,8,1024]{2,1,0:T(8,128)(2,1)} %param.7) | data formatting | bytes 524288 | tf_op args[0]
  10.4 0.9 collective-permute-done.1
  11.3 0.8 pad_maximum_fusion.1
  12.1 6.8 %all-to-all-start = ((bf16[8,16,1536]{2,1,0:T(8,128)(2,1)}), bf16[8,16,1536]{2,1,0:T(8,128)(2,1)S(1)}, u32[]{:S(2)}, u32[]{:S(2)}) async-start(bf16[8,16,1536]{2,1,0:T(8,128)(2,1)} %pad_maximum_fusion.1), calls=%async_computation | async-start | bytes 786432 | tf_op jit(solution)/shard_map/all_to_all | solution.py:195
  18.9 2.7 %collective-permute-start.3 = (bf16[1,16,256]{2,1,0:T(8,128)(2,1)S(1)}, bf16[1,16,256]{2,1,0:T(8,128)(2,1)S(1)}, u32[]{:S(2)}, u32[]{:S(2)}) collective-permute-start(bf16[1,16,256]{2,1,0:T(8,128)(2,1)S(1)} %bitcast.31), channel_id=1, source_target_pairs={{0,384},{8,392},{16,400},{24,408},{32,416},{40,424},{48,432},{56,4... | collective-permute-start | bytes 24584 | tf_op jit(solution)/shard_map/ppermute | solution.py:198
  21.7 4.2 %collective-permute-start.2 = (bf16[1,16,256]{2,1,0:T(8,128)(2,1)S(1)}, bf16[1,16,256]{2,1,0:T(8,128)(2,1)S(1)}, u32[]{:S(2)}, u32[]{:S(2)}) collective-permute-start(bf16[1,16,256]{2,1,0:T(8,128)(2,1)S(1)} %bitcast.32), channel_id=1, source_target_pairs={{0,256},{8,264},{16,272},{24,280},{32,288},{40,296},{48,304},{56,3... | collective-permute-start | bytes 24584 | tf_op jit(solution)/shard_map/ppermute | solution.py:197
  26.0 0.0 collective-permute-done.3
  26.0 2.7 %collective-permute-done.2 = bf16[1,16,256]{2,1,0:T(8,128)(2,1)S(1)} collective-permute-done((bf16[1,16,256]{2,1,0:T(8,128)(2,1)S(1)}, bf16[1,16,256]{2,1,0:T(8,128)(2,1)S(1)}, u32[]{:S(2)}, u32[]{:S(2)}) %collective-permute-start.2) | collective-permute-done | bytes 8224 | tf_op jit(solution)/shard_map/ppermute | solution.py:197
  28.7 3.7 %all-to-all-done = bf16[8,16,1536]{2,1,0:T(8,128)(2,1)S(1)} async-done(((bf16[8,16,1536]{2,1,0:T(8,128)(2,1)}), bf16[8,16,1536]{2,1,0:T(8,128)(2,1)S(1)}, u32[]{:S(2)}, u32[]{:S(2)}) %all-to-all-start) | async-done | bytes 393248 | tf_op jit(solution)/shard_map/all_to_all | solution.py:195
  32.5 0.1 broadcast_select_fusion
  32.6 0.9 pad_maximum_fusion
  33.5 7.2 %all-to-all-start.1 = ((bf16[8,192,256]{2,1,0:T(8,128)(2,1)}), bf16[8,192,256]{2,1,0:T(8,128)(2,1)S(1)}, u32[]{:S(2)}, u32[]{:S(2)}) async-start(bf16[8,192,256]{2,1,0:T(8,128)(2,1)} %pad_maximum_fusion), calls=%async_computation.1 | async-start | bytes 1572864 | tf_op jit(solution)/shard_map/all_to_all | solution.py:203
  40.8 1.9 %collective-permute-start.4 = (bf16[128,256]{1,0:T(8,128)(2,1)S(1)}, bf16[128,256]{1,0:T(8,128)(2,1)S(1)}, u32[]{:S(2)}, u32[]{:S(2)}) collective-permute-start(bf16[128,256]{1,0:T(8,128)(2,1)S(1)} %get-tuple-element.63.mine_ref), channel_id=1, source_target_pairs={{0,8},{8,0},{16,24},{24,16},{32,40},{40,32},{48,56},{56,48},{64,72... | collective-permute-start | bytes 196616 | tf_op jit(solution)/shard_map/ppermute | solution.py:205
  42.7 1.2 %collective-permute-done.4.side_ref = bf16[128,256]{1,0:T(8,128)(2,1)S(1)} collective-permute-done((bf16[128,256]{1,0:T(8,128)(2,1)S(1)}, bf16[128,256]{1,0:T(8,128)(2,1)S(1)}, u32[]{:S(2)}, u32[]{:S(2)}) %collective-permute-start.4) | collective-permute-done | bytes 65568 | tf_op jit(solution)/shard_map/ppermute | solution.py:205
  43.9 1.3 %own_chip.1 = (bf16[256,1024]{1,0:T(8,128)(2,1)S(1)}, s32[1,128]{1,0:T(1,128)S(1)}, s32[2]{0:T(128)S(1)}, f32[1,1024]{1,0:T(1,128)S(1)}, f32[1,1024]{1,0:T(1,128)S(1)}, /*index=5*/f32[128,1024]{1,0:T(8,128)S(1)}) custom-call(s32[1]{0:T(128)} %bitcast.2.meta_ref, bf16[128,256]{1,0:T(8,128)(2,1)S(1)} %get-tuple-element.63.mine_ref, ...), custom_call_target="tpu_custom_call" | custom-call | flops 134217728 | bytes 1048576 | tf_op jit(solution)/shard_map/own_chip/pallas_call | solution.py:214
  45.2 16.0 %all-to-all-done.1 = bf16[8,192,256]{2,1,0:T(8,128)(2,1)S(1)} async-done(((bf16[8,192,256]{2,1,0:T(8,128)(2,1)}), bf16[8,192,256]{2,1,0:T(8,128)(2,1)S(1)}, u32[]{:S(2)}, u32[]{:S(2)}) %all-to-all-start.1) | async-done | bytes 786464 | tf_op jit(solution)/shard_map/all_to_all | solution.py:203
  61.2 1.3 %collective-permute-start.5 = (bf16[8,128,256]{2,1,0:T(8,128)(2,1)S(1)}, bf16[8,128,256]{2,1,0:T(8,128)(2,1)S(1)}, u32[]{:S(2)}, u32[]{:S(2)}) collective-permute-start(bf16[8,128,256]{2,1,0:T(8,128)(2,1)S(1)} %slice.19), channel_id=1, source_target_pairs={{0,128},{8,136},{16,144},{24,152},{32,160},{40,168},{48,176},{56,1... | collective-permute-start | bytes 1572872 | tf_op jit(solution)/shard_map/ppermute | solution.py:228
  62.5 8.1 %conditional.1 = ((f32[1,1024]{1,0:T(1,128)S(1)}, f32[1,1024]{1,0:T(1,128)S(1)}, f32[128,1024]{1,0:T(8,128)S(1)})) conditional(s32[]{:T(128)} %convert_element_type.3, (f32[1,1024]{1,0:T(1,128)S(1)}, f32[1,1024]{1,0:T(1,128)S(1)}, f32[128,1024]{1,0:T(8,128)S(1)}) %tuple.16, (s32[1,32]{1,0:T(1,128)S(1)}, bf16[8,192,256]{2,1,0:T(8,128)(2,1)S(1)}, ...), branch_computations={%region_0.1_spmd, %region_1.2_spmd} | conditional | flops 1342177280 | bytes 5242928 | solution.py:254
  62.5 1.9 %collective-permute-start = (bf16[1536,256]{1,0:T(8,128)(2,1)S(1)}, bf16[1536,256]{1,0:T(8,128)(2,1)S(1)}, u32[]{:S(2)}, u32[]{:S(2)}) collective-permute-start(bf16[1536,256]{1,0:T(8,128)(2,1)S(1)} %bitcast.22), channel_id=1, source_target_pairs={{0,8},{8,0},{16,24},{24,16},{32,40},{40,32},{48,56},{56,48},{64,72... | collective-permute-start | bytes 2359304 | tf_op jit(solution)/shard_map/cond/branch_1_fun/ppermute | solution.py:233
  64.4 2.5 %near_window.1 = (f32[1,1024]{1,0:T(1,128)S(1)}, f32[1,1024]{1,0:T(1,128)S(1)}, f32[128,1024]{1,0:T(8,128)S(1)}) custom-call(s32[1]{0:T(128)} %get-tuple-element.29.meta_ref, bf16[1536,256]{1,0:T(8,128)(2,1)S(1)} %bitcast.23, s32[1,128]{1,0:T(1,128)S(1)} %get-tuple-element.32.start_ref, s32[2]{0:T(128)S(1)} %get-tuple-element.33.limit_ref, ...), custom_call_target="tpu_custom_call" | custom-call | flops 536870912 | bytes 1048576 | tf_op jit(solution)/shard_map/cond/branch_1_fun/near_window/pallas_call | solution.py:234
  66.9 0.0 collective-permute-done.side_ref
  66.9 3.7 %near_other_core_and_prefix.1 = (f32[1,1024]{1,0:T(1,128)S(1)}, f32[1,1024]{1,0:T(1,128)S(1)}, f32[128,1024]{1,0:T(8,128)S(1)}) custom-call(s32[1]{0:T(128)} %get-tuple-element.29.meta_ref, s32[32]{0:T(128)S(1)} %bitcast.34, bf16[1536,256]{1,0:T(8,128)(2,1)S(1)} %bitcast.24, bf16[1536,256]{1,0:T(8,128)(2,1)S(1)} %collective-permute-done.side_ref, ...), custom_call_target="tpu_custom_call" | custom-call | flops 805306368 | bytes 1048576 | tf_op jit(solution)/shard_map/cond/branch_1_fun/near_other_core_and_prefix/pallas_call | solution.py:243
  70.6 2.8 %collective-permute-done.5 = bf16[8,128,256]{2,1,0:T(8,128)(2,1)S(1)} collective-permute-done((bf16[8,128,256]{2,1,0:T(8,128)(2,1)S(1)}, bf16[8,128,256]{2,1,0:T(8,128)(2,1)S(1)}, u32[]{:S(2)}, u32[]{:S(2)}) %collective-permute-start.5) | collective-permute-done | bytes 524320 | tf_op jit(solution)/shard_map/ppermute | solution.py:228
  73.4 1.9 %collective-permute-start.6 = (bf16[1024,256]{1,0:T(8,128)(2,1)S(1)}, bf16[1024,256]{1,0:T(8,128)(2,1)S(1)}, u32[]{:S(2)}, u32[]{:S(2)}) collective-permute-start(bf16[1024,256]{1,0:T(8,128)(2,1)S(1)} %bitcast.20), channel_id=1, source_target_pairs={{0,8},{8,0},{16,24},{24,16},{32,40},{40,32},{48,56},{56,48},{64,72... | collective-permute-start | bytes 1572872 | tf_op jit(solution)/shard_map/ppermute | solution.py:257
  75.3 0.6 far_window.1
  75.9 1.3 %collective-permute-done.6.kv_ref = bf16[1024,256]{1,0:T(8,128)(2,1)S(1)} collective-permute-done((bf16[1024,256]{1,0:T(8,128)(2,1)S(1)}, bf16[1024,256]{1,0:T(8,128)(2,1)S(1)}, u32[]{:S(2)}, u32[]{:S(2)}) %collective-permute-start.6) | collective-permute-done | bytes 524320 | tf_op jit(solution)/shard_map/ppermute | solution.py:257
  77.2 0.7 far_other_core.1
  77.9 16.1 %all_to_all.15 = bf16[8,16,1024]{2,1,0:T(8,128)(2,1)S(1)} all-to-all(bf16[8,16,1024]{2,1,0:T(8,128)(2,1)S(1)} %bitcast.18), channel_id=1, replica_groups=mesh['seq'=64,'head'=8] {'head'}, dimensions={0} | all-to-all | bytes 524288 | tf_op jit(solution)/shard_map/all_to_all | solution.py:281
  94.0 0.9 copy.14
  (13 shorter events, 0.1 us)
Async XLA Ops:
  1.6 9.7 %collective-permute-start.1 = (bf16[9,16,256]{2,1,0:T(8,128)(2,1)S(1)}, bf16[9,16,256]{2,1,0:T(8,128)(2,1)S(1)}, u32[]{:S(2)}, u32[]{:S(2)}) collective-permute-start(bf16[9,16,256]{2,1,0:T(8,128)(2,1)S(1)} %pad_maximum_fusion.2), channel_id=1, source_target_pairs={{0,128},{8,136},{16,144},{24,152},{32,160},{40,168},{48,176},{56,1... | collective-permute-start | bytes 221192 | tf_op jit(solution)/shard_map/ppermute | solution.py:193
  11.3 7.6 %copy-start.1 = (bf16[1,16,1,256]{3,1,2,0:T(8,128)(2,1)S(1)}, bf16[1,16,1,256]{3,1,2,0:T(8,128)(2,1)}, u32[]{:S(2)}) copy-start(bf16[1,16,1,256]{3,1,2,0:T(8,128)(2,1)} %param.10) | copy-start | bytes 24580
  12.1 20.4 %all-to-all-start = ((bf16[8,16,1536]{2,1,0:T(8,128)(2,1)}), bf16[8,16,1536]{2,1,0:T(8,128)(2,1)S(1)}, u32[]{:S(2)}, u32[]{:S(2)}) async-start(bf16[8,16,1536]{2,1,0:T(8,128)(2,1)} %pad_maximum_fusion.1), calls=%async_computation | async-start | bytes 786432 | tf_op jit(solution)/shard_map/all_to_all | solution.py:195
  18.9 7.0 %collective-permute-start.3 = (bf16[1,16,256]{2,1,0:T(8,128)(2,1)S(1)}, bf16[1,16,256]{2,1,0:T(8,128)(2,1)S(1)}, u32[]{:S(2)}, u32[]{:S(2)}) collective-permute-start(bf16[1,16,256]{2,1,0:T(8,128)(2,1)S(1)} %bitcast.31), channel_id=1, source_target_pairs={{0,384},{8,392},{16,400},{24,408},{32,416},{40,424},{48,432},{56,4... | collective-permute-start | bytes 24584 | tf_op jit(solution)/shard_map/ppermute | solution.py:198
  21.7 7.0 %collective-permute-start.2 = (bf16[1,16,256]{2,1,0:T(8,128)(2,1)S(1)}, bf16[1,16,256]{2,1,0:T(8,128)(2,1)S(1)}, u32[]{:S(2)}, u32[]{:S(2)}) collective-permute-start(bf16[1,16,256]{2,1,0:T(8,128)(2,1)S(1)} %bitcast.32), channel_id=1, source_target_pairs={{0,256},{8,264},{16,272},{24,280},{32,288},{40,296},{48,304},{56,3... | collective-permute-start | bytes 24584 | tf_op jit(solution)/shard_map/ppermute | solution.py:197
  33.5 10.4 %copy-start = (s32[8192]{0:T(1024)S(1)}, s32[8192]{0:T(1024)}, u32[]{:S(2)}) copy-start(s32[8192]{0:T(1024)} %param.9) | copy-start | bytes 98308
  33.5 27.6 %all-to-all-start.1 = ((bf16[8,192,256]{2,1,0:T(8,128)(2,1)}), bf16[8,192,256]{2,1,0:T(8,128)(2,1)S(1)}, u32[]{:S(2)}, u32[]{:S(2)}) async-start(bf16[8,192,256]{2,1,0:T(8,128)(2,1)} %pad_maximum_fusion), calls=%async_computation.1 | async-start | bytes 1572864 | tf_op jit(solution)/shard_map/all_to_all | solution.py:203
  40.8 3.1 %collective-permute-start.4 = (bf16[128,256]{1,0:T(8,128)(2,1)S(1)}, bf16[128,256]{1,0:T(8,128)(2,1)S(1)}, u32[]{:S(2)}, u32[]{:S(2)}) collective-permute-start(bf16[128,256]{1,0:T(8,128)(2,1)S(1)} %get-tuple-element.63.mine_ref), channel_id=1, source_target_pairs={{0,8},{8,0},{16,24},{24,16},{32,40},{40,32},{48,56},{56,48},{64,72... | collective-permute-start | bytes 196616 | tf_op jit(solution)/shard_map/ppermute | solution.py:205
  43.9 18.6 %copy-start.2 = (s32[1,32]{1,0:T(1,128)S(1)}, s32[1,32]{1,0:T(1,128)}, u32[]{:S(2)}) copy-start(s32[1,32]{1,0:T(1,128)} %param.11) | copy-start | bytes 388
  61.2 12.2 %collective-permute-start.5 = (bf16[8,128,256]{2,1,0:T(8,128)(2,1)S(1)}, bf16[8,128,256]{2,1,0:T(8,128)(2,1)S(1)}, u32[]{:S(2)}, u32[]{:S(2)}) collective-permute-start(bf16[8,128,256]{2,1,0:T(8,128)(2,1)S(1)} %slice.19), channel_id=1, source_target_pairs={{0,128},{8,136},{16,144},{24,152},{32,160},{40,168},{48,176},{56,1... | collective-permute-start | bytes 1572872 | tf_op jit(solution)/shard_map/ppermute | solution.py:228
  62.5 4.4 %collective-permute-start = (bf16[1536,256]{1,0:T(8,128)(2,1)S(1)}, bf16[1536,256]{1,0:T(8,128)(2,1)S(1)}, u32[]{:S(2)}, u32[]{:S(2)}) collective-permute-start(bf16[1536,256]{1,0:T(8,128)(2,1)S(1)} %bitcast.22), channel_id=1, source_target_pairs={{0,8},{8,0},{16,24},{24,16},{32,40},{40,32},{48,56},{56,48},{64,72... | collective-permute-start | bytes 2359304 | tf_op jit(solution)/shard_map/cond/branch_1_fun/ppermute | solution.py:233
  73.4 3.8 %collective-permute-start.6 = (bf16[1024,256]{1,0:T(8,128)(2,1)S(1)}, bf16[1024,256]{1,0:T(8,128)(2,1)S(1)}, u32[]{:S(2)}, u32[]{:S(2)}) collective-permute-start(bf16[1024,256]{1,0:T(8,128)(2,1)S(1)} %bitcast.20), channel_id=1, source_target_pairs={{0,8},{8,0},{16,24},{24,16},{32,40},{40,32},{48,56},{56,48},{64,72... | collective-permute-start | bytes 1572872 | tf_op jit(solution)/shard_map/ppermute | solution.py:257

commit v17 on v8

--- a/solution.py
+++ b/solution.py
@@ -28,6 +28,10 @@
     ]
 
 
+def x_next():
+    return [pair for pair in x_ring(1) if pair[0] < pair[1]]
+
+
 SWAP = [(i, i ^ 1) for i in range(2 * NX * NY)]
 Y_GROUPS = [[(x * NY + y) * 2 + c for y in range(NY)] for x in range(NX) for c in range(2)]
 
@@ -94,7 +98,7 @@
         fold(side_ref[:, :D], side_ref[:, D:], mask_of(own - 1, own, row_start), *state)
 
 
-def window(kv_ref, skip, core, own, limits, qt_ref, m_ref, l_ref, acc_ref):
+def window(kv_ref, skip, slot, core, own, limits, qt_ref, m_ref, l_ref, acc_ref):
     row_start, first, last = limits
     chip = own // 2 - skip
     lowest = jnp.maximum((jnp.maximum(first // ROWS - core, -1) + 1) // 2, chip - NEAR)
@@ -104,7 +108,7 @@
         base = chip - BLOCKS * (i + 1)
         pairs = []
         for b in range(BLOCKS):
-            start = (base + b + 4 * NY) % NY * SLOT
+            start = (base + b + 4 * NY) % NY * slot
             pairs.append(kv_ref[pl.ds(pl.multiple_of(start, PAGE), ROWS), :])
         keys = jnp.concatenate([pair[:, :D] for pair in pairs], axis=0)
         values = jnp.concatenate([pair[:, D:] for pair in pairs], axis=0)
@@ -126,14 +130,20 @@
     lax.fori_loop(0, steps, step, 0)
 
 
-def near_kernel(meta_ref, kv_ref, side_ref, ids_ref, qt_ref, m_in, l_in, acc_in, m_ref, l_ref, acc_ref):
-    m_ref[...] = m_in[...]
-    l_ref[...] = l_in[...]
-    acc_ref[...] = acc_in[...]
-    own = meta_ref[0]
-    limits = starts_of(ids_ref, own)
-    window(kv_ref, 0, own % 2, own, limits, qt_ref, m_ref, l_ref, acc_ref)
-    window(side_ref, 0, 1 - own % 2, own, limits, qt_ref, m_ref, l_ref, acc_ref)
+def near_kernel(meta_ref, kv_ref, ids_ref, qt_ref, m_in, l_in, acc_in, m_ref, l_ref, acc_ref):
+    m_ref[...] = m_in[...]
+    l_ref[...] = l_in[...]
+    acc_ref[...] = acc_in[...]
+    own = meta_ref[0]
+    window(kv_ref, 0, SLOT, own % 2, own, starts_of(ids_ref, own), qt_ref, m_ref, l_ref, acc_ref)
+
+
+def near_side_kernel(meta_ref, kv_ref, ids_ref, qt_ref, m_in, l_in, acc_in, m_ref, l_ref, acc_ref):
+    m_ref[...] = m_in[...]
+    l_ref[...] = l_in[...]
+    acc_ref[...] = acc_in[...]
+    own = meta_ref[0]
+    window(kv_ref, 0, SLOT, 1 - own % 2, own, starts_of(ids_ref, own), qt_ref, m_ref, l_ref, acc_ref)
 
 
 def far_kernel(meta_ref, kv_ref, ids_ref, qt_ref, m_in, l_in, acc_in, m_ref, l_ref, acc_ref):
@@ -141,7 +151,7 @@
     l_ref[...] = l_in[...]
     acc_ref[...] = acc_in[...]
     own = meta_ref[0]
-    window(kv_ref, NEAR, own % 2, own, starts_of(ids_ref, own), qt_ref, m_ref, l_ref, acc_ref)
+    window(kv_ref, NEAR, SLOT, own % 2, own, starts_of(ids_ref, own), qt_ref, m_ref, l_ref, acc_ref)
 
 
 def last_kernel(meta_ref, table_ref, near_ref, near_side_ref, far_ref, far_side_ref, two_ref, three_ref, ids_ref,
@@ -155,22 +165,21 @@
         page = table_ref[i]
         yy = (page // 2) % NY
         back = (x + NX - page // (2 * NY)) % NX
-        side = jnp.where(page % 2 == core, 0, 1)
+        mine = page % 2 == core
         in_slot = pl.ds(pl.multiple_of(yy * SLOT + ROWS, PAGE), PAGE)
-        in_page = pl.ds(pl.multiple_of((side * NY + yy) * PAGE, PAGE), PAGE)
-        into = slice(i * PAGE, (i + 1) * PAGE)
-        places = [
-            (near_ref, in_slot), (near_side_ref, in_slot), (far_ref, in_slot), (far_side_ref, in_slot),
-            (two_ref, in_page), (three_ref, in_page),
-        ]
-        for n, (ref, rows) in enumerate(places):
-
-            @pl.when(jnp.where(back < 2, 2 * back + side, back + 2) == n)
-            def _():
-                prefix_ref[into, :] = ref[rows, :]
+        in_page = pl.ds(pl.multiple_of((jnp.where(mine, 0, NY) + yy) * PAGE, PAGE), PAGE)
+        prefix_ref[i * PAGE:(i + 1) * PAGE, :] = jnp.where(
+            back < 2,
+            jnp.where(
+                back == 0,
+                jnp.where(mine, near_ref[in_slot, :], near_side_ref[in_slot, :]),
+                jnp.where(mine, far_ref[in_slot, :], far_side_ref[in_slot, :]),
+            ),
+            jnp.where(back == 2, two_ref[in_page, :], three_ref[in_page, :]),
+        )
 
     fold(prefix_ref[:, :D], prefix_ref[:, D:], None, qt_ref, m_ref, l_ref, acc_ref)
-    window(far_side_ref, NEAR, 1 - core, own, starts_of(ids_ref, own), qt_ref, m_ref, l_ref, acc_ref)
+    window(far_side_ref, NEAR, SLOT, 1 - core, own, starts_of(ids_ref, own), qt_ref, m_ref, l_ref, acc_ref)
     result = (acc_ref[...] * (1.0 / l_ref[...])).astype(jnp.bfloat16)
     for g in range(GROUP):
         out_ref[:, g * D:(g + 1) * D] = result[:, g * ROWS:(g + 1) * ROWS].T
@@ -188,24 +197,16 @@
     me = lax.axis_index("seq")
     y = (me // 2) % NY
     page = pool.reshape(PAGE, PAIR)
-    raw = jnp.transpose(branch_key_value, (1, 0, 2))
-    one_raw = lax.ppermute(raw, "seq", x_ring(1))
-    wide = jnp.concatenate([jnp.transpose(queries, (1, 0, 2)), raw, one_raw], axis=2)
+    wide = jnp.transpose(jnp.concatenate([queries, branch_key_value], axis=2), (1, 0, 2))
     wide = lax.all_to_all(wide, "head", split_axis=0, concat_axis=0, tiled=True).reshape(ROWS, -1)
-    own, before = wide[:, GROUP * D:GROUP * D + PAIR], wide[:, GROUP * D + PAIR:]
+    own = wide[:, GROUP * D:]
+    before = lax.ppermute(own, "seq", x_next())
     target = jnp.arange(NY, dtype=jnp.int32)[:, None, None]
     block = jnp.where(target > y, own[None], before[None])
     send = jnp.concatenate([block, jnp.broadcast_to(page[None], (NY, PAGE, PAIR))], axis=1)
     near = lax.all_to_all(send, "seq", split_axis=0, concat_axis=0, tiled=True, axis_index_groups=Y_GROUPS)
-    far = lax.ppermute(near, "seq", x_ring(1))
     later, _ = lax.optimization_barrier((own, send))
     side = lax.ppermute(later, "seq", SWAP)
-    near_side = lax.ppermute(near, "seq", SWAP)
-    far_side = lax.ppermute(far, "seq", SWAP)
-    pages = jnp.concatenate([near[:, ROWS:], near_side[:, ROWS:]], axis=0).reshape(2 * NY * PAGE, PAIR)
-    two_pages = lax.ppermute(pages, "seq", x_ring(2))
-    three_pages = lax.ppermute(pages, "seq", x_ring(3))
-    near, near_side, far, far_side = (a.reshape(NY * SLOT, PAIR) for a in (near, near_side, far, far_side))
 
     ids = branch_ids.reshape(2 * NX * NY, ROWS)
     meta = me.astype(jnp.int32).reshape(1)
@@ -224,15 +225,34 @@
         cost_estimate=cost(256),
         name="own_chip",
     )(meta, own, side, ids, wide)
-    now = pl.pallas_call(
-        near_kernel,
-        out_shape=state,
-        in_specs=[SM] + [VM] * 7,
-        out_specs=[VM] * 3,
-        compiler_params=params,
-        cost_estimate=cost(2048),
-        name="near_window",
-    )(meta, near, near_side, ids, qt, *now)
+    near, qt, now = lax.optimization_barrier((near, qt, now))
+    near = near.reshape(NY * SLOT, PAIR)
+    far = lax.ppermute(near, "seq", x_ring(1))
+
+    def near_part(operands):
+        near, qt, now = operands
+        near_side = lax.ppermute(near, "seq", SWAP)
+        for kernel, kv in ((near_kernel, near), (near_side_kernel, near_side)):
+            now = pl.pallas_call(
+                kernel,
+                out_shape=state,
+                in_specs=[SM] + [VM] * 6,
+                out_specs=[VM] * 3,
+                compiler_params=params,
+                cost_estimate=cost(1024),
+                name=kernel.__name__,
+            )(meta, kv, ids, qt, *now)
+        return near_side, list(now)
+
+    near_side, now = lax.cond(
+        me < 2 * NX * NY, near_part, lambda operands: (operands[0], list(operands[2])), (near, qt, now)
+    )
+    pages = jnp.concatenate([a.reshape(NY, SLOT, PAIR)[:, ROWS:] for a in (near, near_side)], axis=0)
+    pages = pages.reshape(2 * NY * PAGE, PAIR)
+    two_pages = lax.ppermute(pages, "seq", x_ring(2))
+    three_pages = lax.ppermute(pages, "seq", x_ring(3))
+    far, now = lax.optimization_barrier((far, now))
+    far_side = lax.ppermute(far, "seq", SWAP)
     now = pl.pallas_call(
         far_kernel,
         out_shape=state,

time: 110 us -> 105 us (0.955)
  blocking collectives: 39.7 us -> 14.2 us
  waiting for transfers between devices: 21.7 us -> 39.9 us
  starting transfers between devices: 32 us -> 33.4 us
    all_to_all x1 -> x0, blocking collectives: 23 us -> none  [per_device(): lax.all_to_all(send, 'seq', split_axis=0, concat_axis=0, tiled=True, axis...]
    all_to_all x0 -> x1, waiting for transfers between devices: none -> 12.3 us  [per_device(): lax.all_to_all(send, 'seq', split_axis=0, concat_axis=0, tiled=True, axis...]
    all_to_all x0 -> x1, starting transfers between devices: none -> 7.23 us  [per_device(): lax.all_to_all(send, 'seq', split_axis=0, concat_axis=0, tiled=True, axis...]
    ppermute x2, starting transfers between devices: 9.68 us -> 3.2 us  [the longest x1 1.92 us: near_part(): near_side = lax.ppermute(near, 'seq', SWAP)]
    ppermute x2, waiting for transfers between devices: 0.78 us -> 4.85 us  [the longest x1 4.85 us: per_device(): before = lax.ppermute(own, 'seq', x_next())]
    all_to_all x1, starting transfers between devices: 6.82 us -> 10.4 us  [per_device(): lax.all_to_all(wide, 'head', split_axis=0, concat_axis=0, tiled=True)]
    ppermute x1, waiting for transfers between devices: 0.01 us -> 2.8 us  [per_device(): two_pages = lax.ppermute(pages, 'seq', x_ring(2))]
    all_to_all x1, blocking collectives: 16.7 us -> 14.2 us  [per_device(): lax.all_to_all(out.reshape(8, ROWS // 8, GROUP * D), 'head', split_axis=0...]
  transfers between devices with their start and end apart: 8 -> 9, of which waited for: 4 -> 7; matrix products, arithmetic and copies ran while one was open for 1% -> 1% of each run, Pallas kernels for 6% -> 7%
where the time goes in v17:
time: 105 us; the launch traced here: 104 us
  waiting for transfers between devices  39.9 us (38%)
  starting transfers between devices  33.4 us (32%)
  blocking collectives  14.2 us (14%)
  Pallas kernels  11.2 us (11%)
  local copies, waits for them, and re-layouts  3.69 us (4%)
  other arithmetic  1.75 us (2%)
    all_to_all x1, blocking collectives, per_device(): lax.all_to_all(out.reshape(8, ROWS // 8, GROUP * D), 'head', split_axis=0...  14.2 us
    all_to_all x1, waiting for transfers between devices, per_device(): lax.all_to_all(wide, 'head', split_axis=0, concat_axis=0, tiled=True)  13.3 us
    all_to_all x1, waiting for transfers between devices, per_device(): lax.all_to_all(send, 'seq', split_axis=0, concat_axis=0, tiled=True, axis...  12.3 us
    all_to_all x1, starting transfers between devices, per_device(): lax.all_to_all(wide, 'head', split_axis=0, concat_axis=0, tiled=True)  10.4 us
    all_to_all x1, starting transfers between devices, per_device(): lax.all_to_all(send, 'seq', split_axis=0, concat_axis=0, tiled=True, axis...  7.23 us
    pallas_call x2, Pallas kernels, near_part(): pl.pallas_call(kernel, out_shape=state, in_specs=[SM] + [VM] * 6, out_spe...  5.57 us
    ppermute x1, waiting for transfers between devices, per_device(): before = lax.ppermute(own, 'seq', x_next())  4.85 us
    ppermute x1, waiting for transfers between devices, per_device(): far = lax.ppermute(near, 'seq', x_ring(1))  4.54 us
  transfers between devices with their start and end apart: 9, of which 7 were waited for; matrix products, arithmetic and copies ran while one was open for 1% of the time, Pallas kernels for 7%

profile of v17, /device:TPU:6, one launch (start us, length us, event | category | flops | bytes accessed | tf_op | source)
XLA Modules:
  0.0 104.2 jit_solution(5885197618773028896)
XLA Ops:
  0.0 0.9 copy.9
  0.9 1.1 %copy.8 = bf16[16,8,1024]{2,0,1:T(8,128)(2,1)S(1)} copy(bf16[16,8,1024]{2,1,0:T(8,128)(2,1)} %param.7) | data formatting | bytes 524288 | tf_op args[0]
  2.0 0.8 maximum_bitcast_fusion
  2.7 10.4 %all-to-all-start = ((bf16[8,16,1280]{2,1,0:T(8,128)(2,1)}), bf16[8,16,1280]{2,1,0:T(8,128)(2,1)S(1)}, u32[]{:S(2)}, u32[]{:S(2)}) async-start(bf16[8,16,1280]{2,1,0:T(8,128)(2,1)} %maximum_bitcast_fusion), calls=%async_computation | async-start | bytes 655360 | tf_op jit(solution)/shard_map/all_to_all | solution.py:201
  13.2 13.3 %all-to-all-done = bf16[8,16,1280]{2,1,0:T(8,128)(2,1)S(1)} async-done(((bf16[8,16,1280]{2,1,0:T(8,128)(2,1)}), bf16[8,16,1280]{2,1,0:T(8,128)(2,1)S(1)}, u32[]{:S(2)}, u32[]{:S(2)}) %all-to-all-start) | async-done | bytes 327712 | tf_op jit(solution)/shard_map/all_to_all | solution.py:201
  26.5 1.3 %collective-permute-start.1 = (bf16[128,256]{1,0:T(8,128)(2,1)S(1)}, bf16[128,256]{1,0:T(8,128)(2,1)S(1)}, u32[]{:S(2)}, u32[]{:S(2)}) collective-permute-start(bf16[128,256]{1,0:T(8,128)(2,1)S(1)} %slice.21.mine_ref), channel_id=1, source_target_pairs={{0,128},{8,136},{16,144},{24,152},{32,160},{40,168},{48,176},{56,1... | collective-permute-start | bytes 196616 | tf_op jit(solution)/shard_map/ppermute | solution.py:203
  27.8 4.8 %collective-permute-done.1 = bf16[128,256]{1,0:T(8,128)(2,1)S(1)} collective-permute-done((bf16[128,256]{1,0:T(8,128)(2,1)S(1)}, bf16[128,256]{1,0:T(8,128)(2,1)S(1)}, u32[]{:S(2)}, u32[]{:S(2)}) %collective-permute-start.1) | collective-permute-done | bytes 65568 | tf_op jit(solution)/shard_map/ppermute | solution.py:203
  32.6 0.1 broadcast_select_fusion
  32.7 0.9 pad_maximum_fusion
  33.6 7.2 %all-to-all-start.1 = ((bf16[8,144,256]{2,1,0:T(8,128)(2,1)}), bf16[8,144,256]{2,1,0:T(8,128)(2,1)S(1)}, u32[]{:S(2)}, u32[]{:S(2)}) async-start(bf16[8,144,256]{2,1,0:T(8,128)(2,1)} %pad_maximum_fusion), calls=%async_computation.1 | async-start | bytes 1179648 | tf_op jit(solution)/shard_map/all_to_all | solution.py:207
  40.8 1.9 %collective-permute-start.2 = (bf16[128,256]{1,0:T(8,128)(2,1)S(1)}, bf16[128,256]{1,0:T(8,128)(2,1)S(1)}, u32[]{:S(2)}, u32[]{:S(2)}) collective-permute-start(bf16[128,256]{1,0:T(8,128)(2,1)S(1)} %slice.21.mine_ref), channel_id=1, source_target_pairs={{0,8},{8,0},{16,24},{24,16},{32,40},{40,32},{48,56},{56,48},{64,72... | collective-permute-start | bytes 196616 | tf_op jit(solution)/shard_map/ppermute | solution.py:209
  42.8 1.2 %collective-permute-done.2.side_ref = bf16[128,256]{1,0:T(8,128)(2,1)S(1)} collective-permute-done((bf16[128,256]{1,0:T(8,128)(2,1)S(1)}, bf16[128,256]{1,0:T(8,128)(2,1)S(1)}, u32[]{:S(2)}, u32[]{:S(2)}) %collective-permute-start.2) | collective-permute-done | bytes 65568 | tf_op jit(solution)/shard_map/ppermute | solution.py:209
  44.0 0.7 own_chip.1
  44.7 12.3 %all-to-all-done.1 = bf16[8,144,256]{2,1,0:T(8,128)(2,1)S(1)} async-done(((bf16[8,144,256]{2,1,0:T(8,128)(2,1)}), bf16[8,144,256]{2,1,0:T(8,128)(2,1)S(1)}, u32[]{:S(2)}, u32[]{:S(2)}) %all-to-all-start.1) | async-done | bytes 589856 | tf_op jit(solution)/shard_map/all_to_all | solution.py:207
  57.0 1.9 %collective-permute-start.3 = (bf16[1152,256]{1,0:T(8,128)(2,1)S(1)}, bf16[1152,256]{1,0:T(8,128)(2,1)S(1)}, u32[]{:S(2)}, u32[]{:S(2)}) collective-permute-start(bf16[1152,256]{1,0:T(8,128)(2,1)S(1)} %bitcast.16), channel_id=1, source_target_pairs={{0,128},{8,136},{16,144},{24,152},{32,160},{40,168},{48,176},{56,1... | collective-permute-start | bytes 1769480 | tf_op jit(solution)/shard_map/ppermute | solution.py:230
  58.9 7.5 %conditional.1 = (bf16[1152,256]{1,0:T(8,128)(2,1)}, f32[1,1024]{1,0:T(1,128)S(1)}, f32[1,1024]{1,0:T(1,128)S(1)}, f32[128,1024]{1,0:T(8,128)S(1)}) conditional(s32[]{:T(128)} %convert_element_type.3, (bf16[1152,256]{1,0:T(8,128)(2,1)S(1)}, f32[1,1024]{1,0:T(1,128)S(1)}, f32[1,1024]{1,0:T(1,128)S(1)}, f32[128,1024]{1,0:T(8,128)S(1)}) %tuple.37, ...), branch_computations={%region_0.1_spmd, %region_1.2_spmd} | conditional | flops 1073741824 | bytes 4456520 | solution.py:247
  58.9 1.9 %collective-permute-start = (bf16[1152,256]{1,0:T(8,128)(2,1)S(1)}, bf16[1152,256]{1,0:T(8,128)(2,1)}, u32[]{:S(2)}, u32[]{:S(2)}) collective-permute-start(bf16[1152,256]{1,0:T(8,128)(2,1)S(1)} %get-tuple-element.45.kv_ref), channel_id=1, source_target_pairs={{0,8},{8,0},{16,24},{24,16},{32,40},{40,32},{48,56},{56,48},{64,72... | collective-permute-start | bytes 1769480 | tf_op jit(solution)/shard_map/cond/branch_1_fun/ppermute | solution.py:234
  60.8 2.2 %near_kernel.1 = (f32[1,1024]{1,0:T(1,128)S(1)}, f32[1,1024]{1,0:T(1,128)S(1)}, f32[128,1024]{1,0:T(8,128)S(1)}) custom-call(s32[1]{0:T(128)} %get-tuple-element.46.meta_ref, bf16[1152,256]{1,0:T(8,128)(2,1)S(1)} %get-tuple-element.45.kv_ref, s32[64,128]{1,0:T(8,128)S(1)} %get-tuple-element.47.ids_ref, bf16[256,1024]{1,0:T(8,128)(2,1)S(1)} %get-tuple-element.48.qt_ref, ...), custom_call_target="tpu_custom_call" | custom-call | flops 536870912 | bytes 1048576 | tf_op jit(solution)/shard_map/cond/branch_1_fun/near_kernel/pallas_call | solution.py:236
  63.1 3.3 %near_side_kernel.1 = (f32[1,1024]{1,0:T(1,128)S(1)}, f32[1,1024]{1,0:T(1,128)S(1)}, f32[128,1024]{1,0:T(8,128)S(1)}) custom-call(s32[1]{0:T(128)} %get-tuple-element.46.meta_ref, bf16[1152,256]{1,0:T(8,128)(2,1)} %collective-permute-done.kv_ref, s32[64,128]{1,0:T(8,128)S(1)} %get-tuple-element.47.ids_ref, bf16[256,1024]{1,0:T(8,128)(2,1)S(1)} %get-tuple-element.48.qt_ref, ...), custom_call_target="tpu_custom_call" | custom-call | flops 536870912 | bytes 1048576 | tf_op jit(solution)/shard_map/cond/branch_1_fun/near_side_kernel/pallas_call | solution.py:236
  66.4 4.5 %collective-permute-done.3.kv_ref.far_ref = bf16[1152,256]{1,0:T(8,128)(2,1)S(1)} collective-permute-done((bf16[1152,256]{1,0:T(8,128)(2,1)S(1)}, bf16[1152,256]{1,0:T(8,128)(2,1)S(1)}, u32[]{:S(2)}, u32[]{:S(2)}) %collective-permute-start.3) | collective-permute-done | bytes 589856 | tf_op jit(solution)/shard_map/ppermute | solution.py:230
  70.9 1.9 %collective-permute-start.4 = (bf16[1152,256]{1,0:T(8,128)(2,1)S(1)}, bf16[1152,256]{1,0:T(8,128)(2,1)S(1)}, u32[]{:S(2)}, u32[]{:S(2)}) collective-permute-start(bf16[1152,256]{1,0:T(8,128)(2,1)S(1)} %collective-permute-done.3.kv_ref.far_ref), channel_id=1, source_target_pairs={{0,8},{8,0},{16,24},{24,16},{32,40},{40,32},{48,56},{56,48},{64,72... | collective-permute-start | bytes 1769480 | tf_op jit(solution)/shard_map/ppermute | solution.py:255
  72.9 0.9 slice.22
  73.7 0.0 copy-start
  73.8 2.7 %collective-permute-start.6 = (bf16[256,256]{1,0:T(8,128)(2,1)S(1)}, bf16[256,256]{1,0:T(8,128)(2,1)S(1)}, u32[]{:S(2)}, u32[]{:S(2)}) collective-permute-start(bf16[256,256]{1,0:T(8,128)(2,1)S(1)} %bitcast.21), channel_id=1, source_target_pairs={{0,384},{8,392},{16,400},{24,408},{32,416},{40,424},{48,432},{56,4... | collective-permute-start | bytes 393224 | tf_op jit(solution)/shard_map/ppermute | solution.py:253
  76.5 4.0 %collective-permute-start.5 = (bf16[256,256]{1,0:T(8,128)(2,1)S(1)}, bf16[256,256]{1,0:T(8,128)(2,1)S(1)}, u32[]{:S(2)}, u32[]{:S(2)}) collective-permute-start(bf16[256,256]{1,0:T(8,128)(2,1)S(1)} %bitcast.22), channel_id=1, source_target_pairs={{0,256},{8,264},{16,272},{24,280},{32,288},{40,296},{48,304},{56,3... | collective-permute-start | bytes 393224 | tf_op jit(solution)/shard_map/ppermute | solution.py:252
  80.6 1.3 %far_window.1 = (f32[1,1024]{1,0:T(1,128)S(1)}, f32[1,1024]{1,0:T(1,128)S(1)}, f32[128,1024]{1,0:T(8,128)S(1)}) custom-call(s32[1]{0:T(128)} %bitcast.meta_ref, bf16[1152,256]{1,0:T(8,128)(2,1)S(1)} %collective-permute-done.3.kv_ref.far_ref, s32[64,128]{1,0:T(8,128)S(1)} %bitcast.25, bf16[256,1024]{1,0:T(8,128)(2,1)S(1)} %get-tuple-element.88.qt_ref, ...), custom_call_target="tpu_custom_call" | custom-call | flops 536870912 | bytes 1048576 | tf_op jit(solution)/shard_map/far_window/pallas_call | solution.py:256
  81.9 0.9 collective-permute-done.6.three_ref
  82.8 2.8 %collective-permute-done.5.two_ref = bf16[256,256]{1,0:T(8,128)(2,1)S(1)} collective-permute-done((bf16[256,256]{1,0:T(8,128)(2,1)S(1)}, bf16[256,256]{1,0:T(8,128)(2,1)S(1)}, u32[]{:S(2)}, u32[]{:S(2)}) %collective-permute-start.5) | collective-permute-done | bytes 131104 | tf_op jit(solution)/shard_map/ppermute | solution.py:252
  85.6 0.0 collective-permute-done.4.far_side_ref
  85.6 3.6 %far_other_core_and_prefix.1 = bf16[128,1024]{1,0:T(8,128)(2,1)S(1)} custom-call(s32[1]{0:T(128)} %bitcast.meta_ref, s32[32]{0:T(128)S(1)} %bitcast.15, bf16[1152,256]{1,0:T(8,128)(2,1)S(1)} %bitcast.19, bf16[1152,256]{1,0:T(8,128)(2,1)} %get-tuple-element.105.near_side_ref, bf16[1152,256]{1,0:T(8,128)(2,1)S(1)} %collective-permute-done.3.kv_ref.far_ref, ...), custom_call_target="tpu_custom_call" | custom-call | flops 805306368 | bytes 1048576 | tf_op jit(solution)/shard_map/far_other_core_and_prefix/pallas_call | solution.py:265
  89.2 14.2 %all_to_all.15 = bf16[8,16,1024]{2,1,0:T(8,128)(2,1)S(1)} all-to-all(bf16[8,16,1024]{2,1,0:T(8,128)(2,1)S(1)} %bitcast.12), channel_id=1, replica_groups=mesh['seq'=64,'head'=8] {'head'}, dimensions={0} | all-to-all | bytes 524288 | tf_op jit(solution)/shard_map/all_to_all | solution.py:280
  103.4 0.9 copy.10
  (11 shorter events, 0.0 us)
Async XLA Ops:
  2.7 30.0 %copy-start.2 = (bf16[1,16,1,256]{3,1,2,0:T(8,128)(2,1)S(1)}, bf16[1,16,1,256]{3,1,2,0:T(8,128)(2,1)}, u32[]{:S(2)}) copy-start(bf16[1,16,1,256]{3,1,2,0:T(8,128)(2,1)} %param.10) | copy-start | bytes 24580
  2.7 23.7 %all-to-all-start = ((bf16[8,16,1280]{2,1,0:T(8,128)(2,1)}), bf16[8,16,1280]{2,1,0:T(8,128)(2,1)S(1)}, u32[]{:S(2)}, u32[]{:S(2)}) async-start(bf16[8,16,1280]{2,1,0:T(8,128)(2,1)} %maximum_bitcast_fusion), calls=%async_computation | async-start | bytes 655360 | tf_op jit(solution)/shard_map/all_to_all | solution.py:201
  26.5 6.1 %collective-permute-start.1 = (bf16[128,256]{1,0:T(8,128)(2,1)S(1)}, bf16[128,256]{1,0:T(8,128)(2,1)S(1)}, u32[]{:S(2)}, u32[]{:S(2)}) collective-permute-start(bf16[128,256]{1,0:T(8,128)(2,1)S(1)} %slice.21.mine_ref), channel_id=1, source_target_pairs={{0,128},{8,136},{16,144},{24,152},{32,160},{40,168},{48,176},{56,1... | collective-permute-start | bytes 196616 | tf_op jit(solution)/shard_map/ppermute | solution.py:203
  33.6 10.4 %copy-start.1 = (s32[8192]{0:T(1024)S(1)}, s32[8192]{0:T(1024)}, u32[]{:S(2)}) copy-start(s32[8192]{0:T(1024)} %param.9) | copy-start | bytes 98308
  33.6 23.3 %all-to-all-start.1 = ((bf16[8,144,256]{2,1,0:T(8,128)(2,1)}), bf16[8,144,256]{2,1,0:T(8,128)(2,1)S(1)}, u32[]{:S(2)}, u32[]{:S(2)}) async-start(bf16[8,144,256]{2,1,0:T(8,128)(2,1)} %pad_maximum_fusion), calls=%async_computation.1 | async-start | bytes 1179648 | tf_op jit(solution)/shard_map/all_to_all | solution.py:207
  40.8 3.1 %collective-permute-start.2 = (bf16[128,256]{1,0:T(8,128)(2,1)S(1)}, bf16[128,256]{1,0:T(8,128)(2,1)S(1)}, u32[]{:S(2)}, u32[]{:S(2)}) collective-permute-start(bf16[128,256]{1,0:T(8,128)(2,1)S(1)} %slice.21.mine_ref), channel_id=1, source_target_pairs={{0,8},{8,0},{16,24},{24,16},{32,40},{40,32},{48,56},{56,48},{64,72... | collective-permute-start | bytes 196616 | tf_op jit(solution)/shard_map/ppermute | solution.py:209
  57.0 14.0 %collective-permute-start.3 = (bf16[1152,256]{1,0:T(8,128)(2,1)S(1)}, bf16[1152,256]{1,0:T(8,128)(2,1)S(1)}, u32[]{:S(2)}, u32[]{:S(2)}) collective-permute-start(bf16[1152,256]{1,0:T(8,128)(2,1)S(1)} %bitcast.16), channel_id=1, source_target_pairs={{0,128},{8,136},{16,144},{24,152},{32,160},{40,168},{48,176},{56,1... | collective-permute-start | bytes 1769480 | tf_op jit(solution)/shard_map/ppermute | solution.py:230
  58.9 4.2 %collective-permute-start = (bf16[1152,256]{1,0:T(8,128)(2,1)S(1)}, bf16[1152,256]{1,0:T(8,128)(2,1)}, u32[]{:S(2)}, u32[]{:S(2)}) collective-permute-start(bf16[1152,256]{1,0:T(8,128)(2,1)S(1)} %get-tuple-element.45.kv_ref), channel_id=1, source_target_pairs={{0,8},{8,0},{16,24},{24,16},{32,40},{40,32},{48,56},{56,48},{64,72... | collective-permute-start | bytes 1769480 | tf_op jit(solution)/shard_map/cond/branch_1_fun/ppermute | solution.py:234
  70.9 14.6 %collective-permute-start.4 = (bf16[1152,256]{1,0:T(8,128)(2,1)S(1)}, bf16[1152,256]{1,0:T(8,128)(2,1)S(1)}, u32[]{:S(2)}, u32[]{:S(2)}) collective-permute-start(bf16[1152,256]{1,0:T(8,128)(2,1)S(1)} %collective-permute-done.3.kv_ref.far_ref), channel_id=1, source_target_pairs={{0,8},{8,0},{16,24},{24,16},{32,40},{40,32},{48,56},{56,48},{64,72... | collective-permute-start | bytes 1769480 | tf_op jit(solution)/shard_map/ppermute | solution.py:255
  73.7 11.8 %copy-start = (s32[1,32]{1,0:T(1,128)S(1)}, s32[1,32]{1,0:T(1,128)}, u32[]{:S(2)}) copy-start(s32[1,32]{1,0:T(1,128)} %param.11) | copy-start | bytes 388
  73.8 9.0 %collective-permute-start.6 = (bf16[256,256]{1,0:T(8,128)(2,1)S(1)}, bf16[256,256]{1,0:T(8,128)(2,1)S(1)}, u32[]{:S(2)}, u32[]{:S(2)}) collective-permute-start(bf16[256,256]{1,0:T(8,128)(2,1)S(1)} %bitcast.21), channel_id=1, source_target_pairs={{0,384},{8,392},{16,400},{24,408},{32,416},{40,424},{48,432},{56,4... | collective-permute-start | bytes 393224 | tf_op jit(solution)/shard_map/ppermute | solution.py:253
  76.5 9.1 %collective-permute-start.5 = (bf16[256,256]{1,0:T(8,128)(2,1)S(1)}, bf16[256,256]{1,0:T(8,128)(2,1)S(1)}, u32[]{:S(2)}, u32[]{:S(2)}) collective-permute-start(bf16[256,256]{1,0:T(8,128)(2,1)S(1)} %bitcast.22), channel_id=1, source_target_pairs={{0,256},{8,264},{16,272},{24,280},{32,288},{40,296},{48,304},{56,3... | collective-permute-start | bytes 393224 | tf_op jit(solution)/shard_map/ppermute | solution.py:252

commit v18 on v15

--- a/solution.py
+++ b/solution.py
@@ -28,6 +28,10 @@
     ]
 
 
+def x_next():
+    return [pair for pair in x_ring(1) if pair[0] < pair[1]]
+
+
 SWAP = [(i, i ^ 1) for i in range(2 * NX * NY)]
 Y_GROUPS = [[(x * NY + y) * 2 + c for y in range(NY)] for x in range(NX) for c in range(2)]
 
@@ -184,11 +188,12 @@
     page = pool.reshape(1, PAGE, PAIR)
     raw = jnp.concatenate([jnp.transpose(branch_key_value, (1, 0, 2)), page], axis=0)
     one_raw = lax.ppermute(raw, "seq", x_ring(1))
+    three_page = lax.ppermute(page, "seq", x_ring(3))
+    one_raw, three_page = lax.optimization_barrier((one_raw, three_page))
     wide = jnp.concatenate([jnp.transpose(queries, (1, 0, 2)), raw[:8], one_raw[:8]], axis=2)
     wide = lax.all_to_all(wide, "head", split_axis=0, concat_axis=0, tiled=True).reshape(ROWS, -1)
     own, before = wide[:, GROUP * D:GROUP * D + PAIR], wide[:, GROUP * D + PAIR:]
     two_page = lax.ppermute(page, "seq", x_ring(2))
-    three_page = lax.ppermute(page, "seq", x_ring(3))
     target = jnp.arange(NY, dtype=jnp.int32)[:, None, None]
     block = jnp.where(target > y, own[None], before[None])
     pages = jnp.concatenate([page, one_raw[8:], two_page, three_page], axis=0).reshape(1, NX * PAGE, PAIR)
@@ -214,7 +219,7 @@
         name="own_chip",
     )(meta, own, side, ids, wide)
     near, qt, now = lax.optimization_barrier((near, qt, now))
-    far = lax.ppermute(near[:, :ROWS], "seq", x_ring(1))
+    far = lax.ppermute(near[:, :ROWS], "seq", x_next())
 
     def near_part(operands):
         near, qt, now = operands

time: 97.3 us -> 98.5 us (1.012)
  the two profiles are of different devices: /device:TPU:1 before, /device:TPU:6 now
where the time goes in v18:
time: 98.5 us; the launch traced here: 97.9 us
  waiting for transfers between devices  35 us (36%)
  starting transfers between devices  32 us (32%)
  blocking collectives  15.9 us (16%)
  Pallas kernels  9.35 us (9%)
  local copies, waits for them, and re-layouts  2.89 us (3%)
  other arithmetic  2.55 us (3%)
    all_to_all x1, waiting for transfers between devices, per_device(): lax.all_to_all(send, 'seq', split_axis=0, concat_axis=0, tiled=True, axis...  16.4 us
    all_to_all x1, blocking collectives, per_device(): lax.all_to_all(out.reshape(8, ROWS // 8, GROUP * D), 'head', split_axis=0...  15.9 us
    ppermute x1, starting transfers between devices, per_device(): one_raw = lax.ppermute(raw, 'seq', x_ring(1))  7.75 us
    all_to_all x1, starting transfers between devices, per_device(): lax.all_to_all(send, 'seq', split_axis=0, concat_axis=0, tiled=True, axis...  7.23 us
    all_to_all x1, waiting for transfers between devices, per_device(): lax.all_to_all(wide, 'head', split_axis=0, concat_axis=0, tiled=True)  6.19 us
    all_to_all x1, starting transfers between devices, per_device(): lax.all_to_all(wide, 'head', split_axis=0, concat_axis=0, tiled=True)  4.94 us
    ppermute x1, waiting for transfers between devices, per_device(): three_page = lax.ppermute(page, 'seq', x_ring(3))  3.93 us
    ppermute x1, waiting for transfers between devices, per_device(): two_page = lax.ppermute(page, 'seq', x_ring(2))  3.87 us
  transfers between devices with their start and end apart: 9, of which 7 were waited for; matrix products, arithmetic and copies ran while one was open for 1% of the time, Pallas kernels for 8%

profile of v18, /device:TPU:6, one launch (start us, length us, event | category | flops | bytes accessed | tf_op | source)
XLA Modules:
  0.0 97.9 jit_solution(138142375947798432)
XLA Ops:
  0.0 0.9 copy.18
  0.9 0.7 pad_maximum_fusion.2
  1.6 7.7 %collective-permute-start.1 = (bf16[9,16,256]{2,1,0:T(8,128)(2,1)S(1)}, bf16[9,16,256]{2,1,0:T(8,128)(2,1)S(1)}, u32[]{:S(2)}, u32[]{:S(2)}) collective-permute-start(bf16[9,16,256]{2,1,0:T(8,128)(2,1)S(1)} %pad_maximum_fusion.2), channel_id=1, source_target_pairs={{0,128},{8,136},{16,144},{24,152},{32,160},{40,168},{48,176},{56,1... | collective-permute-start | bytes 221192 | tf_op jit(solution)/shard_map/ppermute | solution.py:190
  9.3 1.9 %collective-permute-start.2 = (bf16[1,16,256]{2,1,0:T(8,128)(2,1)}, bf16[1,16,256]{2,1,0:T(8,128)(2,1)S(1)}, u32[]{:S(2)}, u32[]{:S(2)}) collective-permute-start(bf16[1,16,256]{2,1,0:T(8,128)(2,1)} %bitcast.34), channel_id=1, source_target_pairs={{0,384},{8,392},{16,400},{24,408},{32,416},{40,424},{48,432},{56,4... | collective-permute-start | bytes 24584 | tf_op jit(solution)/shard_map/ppermute | solution.py:191
  11.3 1.1 %copy.17 = bf16[16,8,1024]{2,0,1:T(8,128)(2,1)S(1)} copy(bf16[16,8,1024]{2,1,0:T(8,128)(2,1)} %param.7) | data formatting | bytes 524288 | tf_op args[0]
  12.4 3.9 %collective-permute-done.2 = bf16[1,16,256]{2,1,0:T(8,128)(2,1)S(1)} collective-permute-done((bf16[1,16,256]{2,1,0:T(8,128)(2,1)}, bf16[1,16,256]{2,1,0:T(8,128)(2,1)S(1)}, u32[]{:S(2)}, u32[]{:S(2)}) %collective-permute-start.2) | collective-permute-done | bytes 8224 | tf_op jit(solution)/shard_map/ppermute | solution.py:191
  16.3 0.0 copy-start.1
  16.3 0.8 pad_maximum_fusion.1
  17.1 4.9 %all-to-all-start = ((bf16[8,16,1536]{2,1,0:T(8,128)(2,1)}), bf16[8,16,1536]{2,1,0:T(8,128)(2,1)S(1)}, u32[]{:S(2)}, u32[]{:S(2)}) async-start(bf16[8,16,1536]{2,1,0:T(8,128)(2,1)} %pad_maximum_fusion.1), calls=%async_computation | async-start | bytes 786432 | tf_op jit(solution)/shard_map/all_to_all | solution.py:194
  22.0 3.1 %collective-permute-start.3 = (bf16[1,16,256]{2,1,0:T(8,128)(2,1)S(1)}, bf16[1,16,256]{2,1,0:T(8,128)(2,1)S(1)}, u32[]{:S(2)}, u32[]{:S(2)}) collective-permute-start(bf16[1,16,256]{2,1,0:T(8,128)(2,1)S(1)} %bitcast.35), channel_id=1, source_target_pairs={{0,256},{8,264},{16,272},{24,280},{32,288},{40,296},{48,304},{56,3... | collective-permute-start | bytes 24584 | tf_op jit(solution)/shard_map/ppermute | solution.py:196
  25.2 3.9 %collective-permute-done.3 = bf16[1,16,256]{2,1,0:T(8,128)(2,1)S(1)} collective-permute-done((bf16[1,16,256]{2,1,0:T(8,128)(2,1)S(1)}, bf16[1,16,256]{2,1,0:T(8,128)(2,1)S(1)}, u32[]{:S(2)}, u32[]{:S(2)}) %collective-permute-start.3) | collective-permute-done | bytes 8224 | tf_op jit(solution)/shard_map/ppermute | solution.py:196
  29.1 6.2 %all-to-all-done = bf16[8,16,1536]{2,1,0:T(8,128)(2,1)S(1)} async-done(((bf16[8,16,1536]{2,1,0:T(8,128)(2,1)}), bf16[8,16,1536]{2,1,0:T(8,128)(2,1)S(1)}, u32[]{:S(2)}, u32[]{:S(2)}) %all-to-all-start) | async-done | bytes 393248 | tf_op jit(solution)/shard_map/all_to_all | solution.py:194
  35.3 0.1 broadcast_select_fusion
  35.5 0.9 pad_maximum_fusion
  36.4 7.2 %all-to-all-start.1 = ((bf16[8,192,256]{2,1,0:T(8,128)(2,1)}), bf16[8,192,256]{2,1,0:T(8,128)(2,1)S(1)}, u32[]{:S(2)}, u32[]{:S(2)}) async-start(bf16[8,192,256]{2,1,0:T(8,128)(2,1)} %pad_maximum_fusion), calls=%async_computation.1 | async-start | bytes 1572864 | tf_op jit(solution)/shard_map/all_to_all | solution.py:201
  43.6 1.9 %collective-permute-start.4 = (bf16[128,256]{1,0:T(8,128)(2,1)S(1)}, bf16[128,256]{1,0:T(8,128)(2,1)S(1)}, u32[]{:S(2)}, u32[]{:S(2)}) collective-permute-start(bf16[128,256]{1,0:T(8,128)(2,1)S(1)} %get-tuple-element.62.mine_ref), channel_id=1, source_target_pairs={{0,8},{8,0},{16,24},{24,16},{32,40},{40,32},{48,56},{56,48},{64,72... | collective-permute-start | bytes 196616 | tf_op jit(solution)/shard_map/ppermute | solution.py:203
  45.5 1.2 %collective-permute-done.4.side_ref = bf16[128,256]{1,0:T(8,128)(2,1)S(1)} collective-permute-done((bf16[128,256]{1,0:T(8,128)(2,1)S(1)}, bf16[128,256]{1,0:T(8,128)(2,1)S(1)}, u32[]{:S(2)}, u32[]{:S(2)}) %collective-permute-start.4) | collective-permute-done | bytes 65568 | tf_op jit(solution)/shard_map/ppermute | solution.py:203
  46.8 0.7 own_chip.1
  47.4 16.4 %all-to-all-done.1 = bf16[8,192,256]{2,1,0:T(8,128)(2,1)S(1)} async-done(((bf16[8,192,256]{2,1,0:T(8,128)(2,1)}), bf16[8,192,256]{2,1,0:T(8,128)(2,1)S(1)}, u32[]{:S(2)}, u32[]{:S(2)}) %all-to-all-start.1) | async-done | bytes 786464 | tf_op jit(solution)/shard_map/all_to_all | solution.py:201
  63.8 1.3 %collective-permute-start.5 = (bf16[8,128,256]{2,1,0:T(8,128)(2,1)S(1)}, bf16[8,128,256]{2,1,0:T(8,128)(2,1)S(1)}, u32[]{:S(2)}, u32[]{:S(2)}) collective-permute-start(bf16[8,128,256]{2,1,0:T(8,128)(2,1)S(1)} %slice.19), channel_id=1, source_target_pairs={{0,128},{8,136},{16,144},{24,152},{32,160},{40,168},{48,176},{56,1... | collective-permute-start | bytes 1572872 | tf_op jit(solution)/shard_map/ppermute | solution.py:222
  65.2 7.9 %conditional.1 = ((f32[1,1024]{1,0:T(1,128)S(1)}, f32[1,1024]{1,0:T(1,128)S(1)}, f32[128,1024]{1,0:T(8,128)S(1)})) conditional(s32[]{:T(128)} %convert_element_type.3, (f32[1,1024]{1,0:T(1,128)S(1)}, f32[1,1024]{1,0:T(1,128)S(1)}, f32[128,1024]{1,0:T(8,128)S(1)}) %tuple.18, (s32[1,32]{1,0:T(1,128)S(1)}, bf16[8,192,256]{2,1,0:T(8,128)(2,1)S(1)}, ...), branch_computations={%region_0.1_spmd, %region_1.2_spmd} | conditional | flops 1342177280 | bytes 5242928 | solution.py:248
  65.2 1.9 %collective-permute-start = (bf16[1536,256]{1,0:T(8,128)(2,1)S(1)}, bf16[1536,256]{1,0:T(8,128)(2,1)S(1)}, u32[]{:S(2)}, u32[]{:S(2)}) collective-permute-start(bf16[1536,256]{1,0:T(8,128)(2,1)S(1)} %bitcast.21), channel_id=1, source_target_pairs={{0,8},{8,0},{16,24},{24,16},{32,40},{40,32},{48,56},{56,48},{64,72... | collective-permute-start | bytes 2359304 | tf_op jit(solution)/shard_map/cond/branch_1_fun/ppermute | solution.py:227
  67.1 2.2 %near_window.1 = (f32[1,1024]{1,0:T(1,128)S(1)}, f32[1,1024]{1,0:T(1,128)S(1)}, f32[128,1024]{1,0:T(8,128)S(1)}) custom-call(s32[1]{0:T(128)} %get-tuple-element.27.meta_ref, bf16[1536,256]{1,0:T(8,128)(2,1)S(1)} %bitcast.22, s32[64,128]{1,0:T(8,128)S(1)} %get-tuple-element.30.ids_ref, bf16[256,1024]{1,0:T(8,128)(2,1)S(1)} %get-tuple-element.31.qt_ref, ...), custom_call_target="tpu_custom_call" | custom-call | flops 536870912 | bytes 1048576 | tf_op jit(solution)/shard_map/cond/branch_1_fun/near_window/pallas_call | solution.py:228
  69.3 0.0 collective-permute-done.side_ref
  69.4 3.7 %near_other_core_and_prefix.1 = (f32[1,1024]{1,0:T(1,128)S(1)}, f32[1,1024]{1,0:T(1,128)S(1)}, f32[128,1024]{1,0:T(8,128)S(1)}) custom-call(s32[1]{0:T(128)} %get-tuple-element.27.meta_ref, s32[32]{0:T(128)S(1)} %bitcast.37, bf16[1536,256]{1,0:T(8,128)(2,1)S(1)} %bitcast.23, bf16[1536,256]{1,0:T(8,128)(2,1)S(1)} %collective-permute-done.side_ref, ...), custom_call_target="tpu_custom_call" | custom-call | flops 805306368 | bytes 1048576 | tf_op jit(solution)/shard_map/cond/branch_1_fun/near_other_core_and_prefix/pallas_call | solution.py:237
  73.0 2.9 %collective-permute-done.5 = bf16[8,128,256]{2,1,0:T(8,128)(2,1)S(1)} collective-permute-done((bf16[8,128,256]{2,1,0:T(8,128)(2,1)S(1)}, bf16[8,128,256]{2,1,0:T(8,128)(2,1)S(1)}, u32[]{:S(2)}, u32[]{:S(2)}) %collective-permute-start.5) | collective-permute-done | bytes 524320 | tf_op jit(solution)/shard_map/ppermute | solution.py:222
  75.9 1.9 %collective-permute-start.6 = (bf16[1024,256]{1,0:T(8,128)(2,1)S(1)}, bf16[1024,256]{1,0:T(8,128)(2,1)S(1)}, u32[]{:S(2)}, u32[]{:S(2)}) collective-permute-start(bf16[1024,256]{1,0:T(8,128)(2,1)S(1)} %bitcast.19), channel_id=1, source_target_pairs={{0,8},{8,0},{16,24},{24,16},{32,40},{40,32},{48,56},{56,48},{64,72... | collective-permute-start | bytes 1572872 | tf_op jit(solution)/shard_map/ppermute | solution.py:251
  77.8 1.3 %far_window.1 = (f32[1,1024]{1,0:T(1,128)S(1)}, f32[1,1024]{1,0:T(1,128)S(1)}, f32[128,1024]{1,0:T(8,128)S(1)}) custom-call(s32[1]{0:T(128)} %bitcast.2.meta_ref, bf16[1024,256]{1,0:T(8,128)(2,1)S(1)} %bitcast.20, s32[64,128]{1,0:T(8,128)S(1)} %bitcast.31, bf16[256,1024]{1,0:T(8,128)(2,1)S(1)} %get-tuple-element.71.qt_ref, ...), custom_call_target="tpu_custom_call" | custom-call | flops 536870912 | bytes 1048576 | tf_op jit(solution)/shard_map/far_window/pallas_call | solution.py:252
  79.2 0.5 collective-permute-done.6.kv_ref
  79.7 1.4 %far_other_core.1 = bf16[128,1024]{1,0:T(8,128)(2,1)S(1)} custom-call(s32[1]{0:T(128)} %bitcast.2.meta_ref, bf16[1024,256]{1,0:T(8,128)(2,1)S(1)} %collective-permute-done.6.kv_ref, s32[64,128]{1,0:T(8,128)S(1)} %bitcast.32, bf16[256,1024]{1,0:T(8,128)(2,1)S(1)} %get-tuple-element.71.qt_ref, f32[1,1024]{1,0:T(1,128)S(1)} %get-tuple-element.79.m_in, ...), custom_call_target="tpu_custom_call" | custom-call | flops 536870912 | bytes 1048576 | tf_op jit(solution)/shard_map/far_other_core/pallas_call | solution.py:261
  81.1 15.9 %all_to_all.15 = bf16[8,16,1024]{2,1,0:T(8,128)(2,1)S(1)} all-to-all(bf16[8,16,1024]{2,1,0:T(8,128)(2,1)S(1)} %bitcast.18), channel_id=1, replica_groups=mesh['seq'=64,'head'=8] {'head'}, dimensions={0} | all-to-all | bytes 524288 | tf_op jit(solution)/shard_map/all_to_all | solution.py:275
  97.0 0.9 copy.14
  (13 shorter events, 0.1 us)
Async XLA Ops:
  1.6 14.7 %collective-permute-start.1 = (bf16[9,16,256]{2,1,0:T(8,128)(2,1)S(1)}, bf16[9,16,256]{2,1,0:T(8,128)(2,1)S(1)}, u32[]{:S(2)}, u32[]{:S(2)}) collective-permute-start(bf16[9,16,256]{2,1,0:T(8,128)(2,1)S(1)} %pad_maximum_fusion.2), channel_id=1, source_target_pairs={{0,128},{8,136},{16,144},{24,152},{32,160},{40,168},{48,176},{56,1... | collective-permute-start | bytes 221192 | tf_op jit(solution)/shard_map/ppermute | solution.py:190
  9.3 7.0 %collective-permute-start.2 = (bf16[1,16,256]{2,1,0:T(8,128)(2,1)}, bf16[1,16,256]{2,1,0:T(8,128)(2,1)S(1)}, u32[]{:S(2)}, u32[]{:S(2)}) collective-permute-start(bf16[1,16,256]{2,1,0:T(8,128)(2,1)} %bitcast.34), channel_id=1, source_target_pairs={{0,384},{8,392},{16,400},{24,408},{32,416},{40,424},{48,432},{56,4... | collective-permute-start | bytes 24584 | tf_op jit(solution)/shard_map/ppermute | solution.py:191
  16.3 5.7 %copy-start.1 = (bf16[1,16,1,256]{3,1,2,0:T(8,128)(2,1)S(1)}, bf16[1,16,1,256]{3,1,2,0:T(8,128)(2,1)}, u32[]{:S(2)}) copy-start(bf16[1,16,1,256]{3,1,2,0:T(8,128)(2,1)} %param.10) | copy-start | bytes 24580
  17.1 18.2 %all-to-all-start = ((bf16[8,16,1536]{2,1,0:T(8,128)(2,1)}), bf16[8,16,1536]{2,1,0:T(8,128)(2,1)S(1)}, u32[]{:S(2)}, u32[]{:S(2)}) async-start(bf16[8,16,1536]{2,1,0:T(8,128)(2,1)} %pad_maximum_fusion.1), calls=%async_computation | async-start | bytes 786432 | tf_op jit(solution)/shard_map/all_to_all | solution.py:194
  22.0 7.0 %collective-permute-start.3 = (bf16[1,16,256]{2,1,0:T(8,128)(2,1)S(1)}, bf16[1,16,256]{2,1,0:T(8,128)(2,1)S(1)}, u32[]{:S(2)}, u32[]{:S(2)}) collective-permute-start(bf16[1,16,256]{2,1,0:T(8,128)(2,1)S(1)} %bitcast.35), channel_id=1, source_target_pairs={{0,256},{8,264},{16,272},{24,280},{32,288},{40,296},{48,304},{56,3... | collective-permute-start | bytes 24584 | tf_op jit(solution)/shard_map/ppermute | solution.py:196
  36.4 10.4 %copy-start = (s32[8192]{0:T(1024)S(1)}, s32[8192]{0:T(1024)}, u32[]{:S(2)}) copy-start(s32[8192]{0:T(1024)} %param.9) | copy-start | bytes 98308
  36.4 27.4 %all-to-all-start.1 = ((bf16[8,192,256]{2,1,0:T(8,128)(2,1)}), bf16[8,192,256]{2,1,0:T(8,128)(2,1)S(1)}, u32[]{:S(2)}, u32[]{:S(2)}) async-start(bf16[8,192,256]{2,1,0:T(8,128)(2,1)} %pad_maximum_fusion), calls=%async_computation.1 | async-start | bytes 1572864 | tf_op jit(solution)/shard_map/all_to_all | solution.py:201
  43.6 3.1 %collective-permute-start.4 = (bf16[128,256]{1,0:T(8,128)(2,1)S(1)}, bf16[128,256]{1,0:T(8,128)(2,1)S(1)}, u32[]{:S(2)}, u32[]{:S(2)}) collective-permute-start(bf16[128,256]{1,0:T(8,128)(2,1)S(1)} %get-tuple-element.62.mine_ref), channel_id=1, source_target_pairs={{0,8},{8,0},{16,24},{24,16},{32,40},{40,32},{48,56},{56,48},{64,72... | collective-permute-start | bytes 196616 | tf_op jit(solution)/shard_map/ppermute | solution.py:203
  46.8 18.4 %copy-start.2 = (s32[1,32]{1,0:T(1,128)S(1)}, s32[1,32]{1,0:T(1,128)}, u32[]{:S(2)}) copy-start(s32[1,32]{1,0:T(1,128)} %param.11) | copy-start | bytes 388
  63.8 12.1 %collective-permute-start.5 = (bf16[8,128,256]{2,1,0:T(8,128)(2,1)S(1)}, bf16[8,128,256]{2,1,0:T(8,128)(2,1)S(1)}, u32[]{:S(2)}, u32[]{:S(2)}) collective-permute-start(bf16[8,128,256]{2,1,0:T(8,128)(2,1)S(1)} %slice.19), channel_id=1, source_target_pairs={{0,128},{8,136},{16,144},{24,152},{32,160},{40,168},{48,176},{56,1... | collective-permute-start | bytes 1572872 | tf_op jit(solution)/shard_map/ppermute | solution.py:222
  65.2 4.2 %collective-permute-start = (bf16[1536,256]{1,0:T(8,128)(2,1)S(1)}, bf16[1536,256]{1,0:T(8,128)(2,1)S(1)}, u32[]{:S(2)}, u32[]{:S(2)}) collective-permute-start(bf16[1536,256]{1,0:T(8,128)(2,1)S(1)} %bitcast.21), channel_id=1, source_target_pairs={{0,8},{8,0},{16,24},{24,16},{32,40},{40,32},{48,56},{56,48},{64,72... | collective-permute-start | bytes 2359304 | tf_op jit(solution)/shard_map/cond/branch_1_fun/ppermute | solution.py:227
  75.9 3.8 %collective-permute-start.6 = (bf16[1024,256]{1,0:T(8,128)(2,1)S(1)}, bf16[1024,256]{1,0:T(8,128)(2,1)S(1)}, u32[]{:S(2)}, u32[]{:S(2)}) collective-permute-start(bf16[1024,256]{1,0:T(8,128)(2,1)S(1)} %bitcast.19), channel_id=1, source_target_pairs={{0,8},{8,0},{16,24},{24,16},{32,40},{40,32},{48,56},{56,48},{64,72... | collective-permute-start | bytes 1572872 | tf_op jit(solution)/shard_map/ppermute | solution.py:251

commit v19 on v18

--- a/solution.py
+++ b/solution.py
@@ -189,7 +189,6 @@
     raw = jnp.concatenate([jnp.transpose(branch_key_value, (1, 0, 2)), page], axis=0)
     one_raw = lax.ppermute(raw, "seq", x_ring(1))
     three_page = lax.ppermute(page, "seq", x_ring(3))
-    one_raw, three_page = lax.optimization_barrier((one_raw, three_page))
     wide = jnp.concatenate([jnp.transpose(queries, (1, 0, 2)), raw[:8], one_raw[:8]], axis=2)
     wide = lax.all_to_all(wide, "head", split_axis=0, concat_axis=0, tiled=True).reshape(ROWS, -1)
     own, before = wide[:, GROUP * D:GROUP * D + PAIR], wide[:, GROUP * D + PAIR:]

time: 98.5 us -> 95.4 us (0.969)
  starting transfers between devices: 32 us -> 35.8 us
  Pallas kernels: 9.35 us -> 5.66 us
  waiting for transfers between devices: 35 us -> 31.4 us
    ppermute x1, waiting for transfers between devices: 3.93 us -> 0.01 us  [per_device(): three_page = lax.ppermute(page, 'seq', x_ring(3))]
    all_to_all x1, waiting for transfers between devices: 6.19 us -> 3.73 us  [per_device(): lax.all_to_all(wide, 'head', split_axis=0, concat_axis=0, tiled=True)]
    all_to_all x1, starting transfers between devices: 4.94 us -> 6.84 us  [per_device(): lax.all_to_all(wide, 'head', split_axis=0, concat_axis=0, tiled=True)]
    ppermute x1, waiting for transfers between devices: 3.87 us -> 2.75 us  [per_device(): two_page = lax.ppermute(page, 'seq', x_ring(2))]
    ppermute x1, starting transfers between devices: 3.12 us -> 4.23 us  [per_device(): two_page = lax.ppermute(page, 'seq', x_ring(2))]
    ppermute x1, waiting for transfers between devices: 2.88 us -> 3.89 us  [per_device(): far = lax.ppermute(near[:, :ROWS], 'seq', x_next())]
  transfers between devices with their start and end apart: 9 -> 9, of which waited for: 7 -> 8; matrix products, arithmetic and copies ran while one was open for 1% -> 1% of each run, Pallas kernels for 8% -> 5%
where the time goes in v19:
time: 95.4 us; the launch traced here: 94.6 us
  starting transfers between devices  35.8 us (38%)
  waiting for transfers between devices  31.4 us (33%)
  blocking collectives  16.1 us (17%)
  Pallas kernels  5.66 us (6%)
  local copies, waits for them, and re-layouts  2.89 us (3%)
  other arithmetic  2.55 us (3%)
    all_to_all x1, waiting for transfers between devices, per_device(): lax.all_to_all(send, 'seq', split_axis=0, concat_axis=0, tiled=True, axis...  16.6 us
    all_to_all x1, blocking collectives, per_device(): lax.all_to_all(out.reshape(8, ROWS // 8, GROUP * D), 'head', split_axis=0...  16.1 us
    ppermute x1, starting transfers between devices, per_device(): one_raw = lax.ppermute(raw, 'seq', x_ring(1))  7.75 us
    all_to_all x1, starting transfers between devices, per_device(): lax.all_to_all(send, 'seq', split_axis=0, concat_axis=0, tiled=True, axis...  7.23 us
    all_to_all x1, starting transfers between devices, per_device(): lax.all_to_all(wide, 'head', split_axis=0, concat_axis=0, tiled=True)  6.84 us
    ppermute x1, starting transfers between devices, per_device(): two_page = lax.ppermute(page, 'seq', x_ring(2))  4.23 us
    ppermute x1, waiting for transfers between devices, per_device(): far = lax.ppermute(near[:, :ROWS], 'seq', x_next())  3.89 us
    all_to_all x1, waiting for transfers between devices, per_device(): lax.all_to_all(wide, 'head', split_axis=0, concat_axis=0, tiled=True)  3.73 us
  transfers between devices with their start and end apart: 9, of which 8 were waited for; matrix products, arithmetic and copies ran while one was open for 1% of the time, Pallas kernels for 5%

profile of v19, /device:TPU:6, one launch (start us, length us, event | category | flops | bytes accessed | tf_op | source)
XLA Modules:
  0.0 94.6 jit_solution(13941660695549147176)
XLA Ops:
  0.0 0.9 copy.18
  0.9 0.7 pad_maximum_fusion.2
  1.6 7.7 %collective-permute-start.1 = (bf16[9,16,256]{2,1,0:T(8,128)(2,1)S(1)}, bf16[9,16,256]{2,1,0:T(8,128)(2,1)S(1)}, u32[]{:S(2)}, u32[]{:S(2)}) collective-permute-start(bf16[9,16,256]{2,1,0:T(8,128)(2,1)S(1)} %pad_maximum_fusion.2), channel_id=1, source_target_pairs={{0,128},{8,136},{16,144},{24,152},{32,160},{40,168},{48,176},{56,1... | collective-permute-start | bytes 221192 | tf_op jit(solution)/shard_map/ppermute | solution.py:190
  9.3 1.1 %copy.17 = bf16[16,8,1024]{2,0,1:T(8,128)(2,1)S(1)} copy(bf16[16,8,1024]{2,1,0:T(8,128)(2,1)} %param.7) | data formatting | bytes 524288 | tf_op args[0]
  10.4 0.9 collective-permute-done.1
  11.3 0.8 pad_maximum_fusion.1
  12.1 6.8 %all-to-all-start = ((bf16[8,16,1536]{2,1,0:T(8,128)(2,1)}), bf16[8,16,1536]{2,1,0:T(8,128)(2,1)S(1)}, u32[]{:S(2)}, u32[]{:S(2)}) async-start(bf16[8,16,1536]{2,1,0:T(8,128)(2,1)} %pad_maximum_fusion.1), calls=%async_computation | async-start | bytes 786432 | tf_op jit(solution)/shard_map/all_to_all | solution.py:193
  18.9 2.7 %collective-permute-start.3 = (bf16[1,16,256]{2,1,0:T(8,128)(2,1)S(1)}, bf16[1,16,256]{2,1,0:T(8,128)(2,1)S(1)}, u32[]{:S(2)}, u32[]{:S(2)}) collective-permute-start(bf16[1,16,256]{2,1,0:T(8,128)(2,1)S(1)} %bitcast.34), channel_id=1, source_target_pairs={{0,384},{8,392},{16,400},{24,408},{32,416},{40,424},{48,432},{56,4... | collective-permute-start | bytes 24584 | tf_op jit(solution)/shard_map/ppermute | solution.py:191
  21.7 4.2 %collective-permute-start.2 = (bf16[1,16,256]{2,1,0:T(8,128)(2,1)S(1)}, bf16[1,16,256]{2,1,0:T(8,128)(2,1)S(1)}, u32[]{:S(2)}, u32[]{:S(2)}) collective-permute-start(bf16[1,16,256]{2,1,0:T(8,128)(2,1)S(1)} %bitcast.35), channel_id=1, source_target_pairs={{0,256},{8,264},{16,272},{24,280},{32,288},{40,296},{48,304},{56,3... | collective-permute-start | bytes 24584 | tf_op jit(solution)/shard_map/ppermute | solution.py:195
  26.0 0.0 collective-permute-done.3
  26.0 2.7 %collective-permute-done.2 = bf16[1,16,256]{2,1,0:T(8,128)(2,1)S(1)} collective-permute-done((bf16[1,16,256]{2,1,0:T(8,128)(2,1)S(1)}, bf16[1,16,256]{2,1,0:T(8,128)(2,1)S(1)}, u32[]{:S(2)}, u32[]{:S(2)}) %collective-permute-start.2) | collective-permute-done | bytes 8224 | tf_op jit(solution)/shard_map/ppermute | solution.py:195
  28.7 3.7 %all-to-all-done = bf16[8,16,1536]{2,1,0:T(8,128)(2,1)S(1)} async-done(((bf16[8,16,1536]{2,1,0:T(8,128)(2,1)}), bf16[8,16,1536]{2,1,0:T(8,128)(2,1)S(1)}, u32[]{:S(2)}, u32[]{:S(2)}) %all-to-all-start) | async-done | bytes 393248 | tf_op jit(solution)/shard_map/all_to_all | solution.py:193
  32.5 0.1 broadcast_select_fusion
  32.6 0.9 pad_maximum_fusion
  33.5 7.2 %all-to-all-start.1 = ((bf16[8,192,256]{2,1,0:T(8,128)(2,1)}), bf16[8,192,256]{2,1,0:T(8,128)(2,1)S(1)}, u32[]{:S(2)}, u32[]{:S(2)}) async-start(bf16[8,192,256]{2,1,0:T(8,128)(2,1)} %pad_maximum_fusion), calls=%async_computation.1 | async-start | bytes 1572864 | tf_op jit(solution)/shard_map/all_to_all | solution.py:200
  40.8 1.9 %collective-permute-start.4 = (bf16[128,256]{1,0:T(8,128)(2,1)S(1)}, bf16[128,256]{1,0:T(8,128)(2,1)S(1)}, u32[]{:S(2)}, u32[]{:S(2)}) collective-permute-start(bf16[128,256]{1,0:T(8,128)(2,1)S(1)} %get-tuple-element.58.mine_ref), channel_id=1, source_target_pairs={{0,8},{8,0},{16,24},{24,16},{32,40},{40,32},{48,56},{56,48},{64,72... | collective-permute-start | bytes 196616 | tf_op jit(solution)/shard_map/ppermute | solution.py:202
  42.7 1.2 %collective-permute-done.4.side_ref = bf16[128,256]{1,0:T(8,128)(2,1)S(1)} collective-permute-done((bf16[128,256]{1,0:T(8,128)(2,1)S(1)}, bf16[128,256]{1,0:T(8,128)(2,1)S(1)}, u32[]{:S(2)}, u32[]{:S(2)}) %collective-permute-start.4) | collective-permute-done | bytes 65568 | tf_op jit(solution)/shard_map/ppermute | solution.py:202
  43.9 0.7 own_chip.1
  44.6 16.6 %all-to-all-done.1 = bf16[8,192,256]{2,1,0:T(8,128)(2,1)S(1)} async-done(((bf16[8,192,256]{2,1,0:T(8,128)(2,1)}), bf16[8,192,256]{2,1,0:T(8,128)(2,1)S(1)}, u32[]{:S(2)}, u32[]{:S(2)}) %all-to-all-start.1) | async-done | bytes 786464 | tf_op jit(solution)/shard_map/all_to_all | solution.py:200
  61.2 1.3 %collective-permute-start.5 = (bf16[8,128,256]{2,1,0:T(8,128)(2,1)S(1)}, bf16[8,128,256]{2,1,0:T(8,128)(2,1)S(1)}, u32[]{:S(2)}, u32[]{:S(2)}) collective-permute-start(bf16[8,128,256]{2,1,0:T(8,128)(2,1)S(1)} %slice.19), channel_id=1, source_target_pairs={{0,128},{8,136},{16,144},{24,152},{32,160},{40,168},{48,176},{56,1... | collective-permute-start | bytes 1572872 | tf_op jit(solution)/shard_map/ppermute | solution.py:221
  62.5 7.0 %conditional.1 = ((f32[1,1024]{1,0:T(1,128)S(1)}, f32[1,1024]{1,0:T(1,128)S(1)}, f32[128,1024]{1,0:T(8,128)S(1)})) conditional(s32[]{:T(128)} %convert_element_type.3, (f32[1,1024]{1,0:T(1,128)S(1)}, f32[1,1024]{1,0:T(1,128)S(1)}, f32[128,1024]{1,0:T(8,128)S(1)}) %tuple.16, (s32[1,32]{1,0:T(1,128)S(1)}, bf16[8,192,256]{2,1,0:T(8,128)(2,1)S(1)}, ...), branch_computations={%region_0.1_spmd, %region_1.2_spmd} | conditional | flops 1342177280 | bytes 5242928 | solution.py:247
  62.5 1.9 %collective-permute-start = (bf16[1536,256]{1,0:T(8,128)(2,1)S(1)}, bf16[1536,256]{1,0:T(8,128)(2,1)S(1)}, u32[]{:S(2)}, u32[]{:S(2)}) collective-permute-start(bf16[1536,256]{1,0:T(8,128)(2,1)S(1)} %bitcast.21), channel_id=1, source_target_pairs={{0,8},{8,0},{16,24},{24,16},{32,40},{40,32},{48,56},{56,48},{64,72... | collective-permute-start | bytes 2359304 | tf_op jit(solution)/shard_map/cond/branch_1_fun/ppermute | solution.py:226
  64.4 1.3 %near_window.1 = (f32[1,1024]{1,0:T(1,128)S(1)}, f32[1,1024]{1,0:T(1,128)S(1)}, f32[128,1024]{1,0:T(8,128)S(1)}) custom-call(s32[1]{0:T(128)} %get-tuple-element.27.meta_ref, bf16[1536,256]{1,0:T(8,128)(2,1)S(1)} %bitcast.22, s32[64,128]{1,0:T(8,128)S(1)} %get-tuple-element.30.ids_ref, bf16[256,1024]{1,0:T(8,128)(2,1)S(1)} %get-tuple-element.31.qt_ref, ...), custom_call_target="tpu_custom_call" | custom-call | flops 536870912 | bytes 1048576 | tf_op jit(solution)/shard_map/cond/branch_1_fun/near_window/pallas_call | solution.py:227
  65.8 0.9 collective-permute-done.side_ref
  66.7 2.8 %near_other_core_and_prefix.1 = (f32[1,1024]{1,0:T(1,128)S(1)}, f32[1,1024]{1,0:T(1,128)S(1)}, f32[128,1024]{1,0:T(8,128)S(1)}) custom-call(s32[1]{0:T(128)} %get-tuple-element.27.meta_ref, s32[32]{0:T(128)S(1)} %bitcast.37, bf16[1536,256]{1,0:T(8,128)(2,1)S(1)} %bitcast.23, bf16[1536,256]{1,0:T(8,128)(2,1)S(1)} %collective-permute-done.side_ref, ...), custom_call_target="tpu_custom_call" | custom-call | flops 805306368 | bytes 1048576 | tf_op jit(solution)/shard_map/cond/branch_1_fun/near_other_core_and_prefix/pallas_call | solution.py:236
  69.5 3.9 %collective-permute-done.5 = bf16[8,128,256]{2,1,0:T(8,128)(2,1)S(1)} collective-permute-done((bf16[8,128,256]{2,1,0:T(8,128)(2,1)S(1)}, bf16[8,128,256]{2,1,0:T(8,128)(2,1)S(1)}, u32[]{:S(2)}, u32[]{:S(2)}) %collective-permute-start.5) | collective-permute-done | bytes 524320 | tf_op jit(solution)/shard_map/ppermute | solution.py:221
  73.4 1.9 %collective-permute-start.6 = (bf16[1024,256]{1,0:T(8,128)(2,1)S(1)}, bf16[1024,256]{1,0:T(8,128)(2,1)S(1)}, u32[]{:S(2)}, u32[]{:S(2)}) collective-permute-start(bf16[1024,256]{1,0:T(8,128)(2,1)S(1)} %bitcast.19), channel_id=1, source_target_pairs={{0,8},{8,0},{16,24},{24,16},{32,40},{40,32},{48,56},{56,48},{64,72... | collective-permute-start | bytes 1572872 | tf_op jit(solution)/shard_map/ppermute | solution.py:250
  75.3 0.4 far_window.1
  75.7 1.5 %collective-permute-done.6.kv_ref = bf16[1024,256]{1,0:T(8,128)(2,1)S(1)} collective-permute-done((bf16[1024,256]{1,0:T(8,128)(2,1)S(1)}, bf16[1024,256]{1,0:T(8,128)(2,1)S(1)}, u32[]{:S(2)}, u32[]{:S(2)}) %collective-permute-start.6) | collective-permute-done | bytes 524320 | tf_op jit(solution)/shard_map/ppermute | solution.py:250
  77.2 0.5 far_other_core.1
  77.7 16.1 %all_to_all.15 = bf16[8,16,1024]{2,1,0:T(8,128)(2,1)S(1)} all-to-all(bf16[8,16,1024]{2,1,0:T(8,128)(2,1)S(1)} %bitcast.18), channel_id=1, replica_groups=mesh['seq'=64,'head'=8] {'head'}, dimensions={0} | all-to-all | bytes 524288 | tf_op jit(solution)/shard_map/all_to_all | solution.py:274
  93.8 0.9 copy.14
  (13 shorter events, 0.1 us)
Async XLA Ops:
  1.6 9.7 %collective-permute-start.1 = (bf16[9,16,256]{2,1,0:T(8,128)(2,1)S(1)}, bf16[9,16,256]{2,1,0:T(8,128)(2,1)S(1)}, u32[]{:S(2)}, u32[]{:S(2)}) collective-permute-start(bf16[9,16,256]{2,1,0:T(8,128)(2,1)S(1)} %pad_maximum_fusion.2), channel_id=1, source_target_pairs={{0,128},{8,136},{16,144},{24,152},{32,160},{40,168},{48,176},{56,1... | collective-permute-start | bytes 221192 | tf_op jit(solution)/shard_map/ppermute | solution.py:190
  11.3 7.6 %copy-start.1 = (bf16[1,16,1,256]{3,1,2,0:T(8,128)(2,1)S(1)}, bf16[1,16,1,256]{3,1,2,0:T(8,128)(2,1)}, u32[]{:S(2)}) copy-start(bf16[1,16,1,256]{3,1,2,0:T(8,128)(2,1)} %param.10) | copy-start | bytes 24580
  12.1 20.4 %all-to-all-start = ((bf16[8,16,1536]{2,1,0:T(8,128)(2,1)}), bf16[8,16,1536]{2,1,0:T(8,128)(2,1)S(1)}, u32[]{:S(2)}, u32[]{:S(2)}) async-start(bf16[8,16,1536]{2,1,0:T(8,128)(2,1)} %pad_maximum_fusion.1), calls=%async_computation | async-start | bytes 786432 | tf_op jit(solution)/shard_map/all_to_all | solution.py:193
  18.9 7.0 %collective-permute-start.3 = (bf16[1,16,256]{2,1,0:T(8,128)(2,1)S(1)}, bf16[1,16,256]{2,1,0:T(8,128)(2,1)S(1)}, u32[]{:S(2)}, u32[]{:S(2)}) collective-permute-start(bf16[1,16,256]{2,1,0:T(8,128)(2,1)S(1)} %bitcast.34), channel_id=1, source_target_pairs={{0,384},{8,392},{16,400},{24,408},{32,416},{40,424},{48,432},{56,4... | collective-permute-start | bytes 24584 | tf_op jit(solution)/shard_map/ppermute | solution.py:191
  21.7 7.0 %collective-permute-start.2 = (bf16[1,16,256]{2,1,0:T(8,128)(2,1)S(1)}, bf16[1,16,256]{2,1,0:T(8,128)(2,1)S(1)}, u32[]{:S(2)}, u32[]{:S(2)}) collective-permute-start(bf16[1,16,256]{2,1,0:T(8,128)(2,1)S(1)} %bitcast.35), channel_id=1, source_target_pairs={{0,256},{8,264},{16,272},{24,280},{32,288},{40,296},{48,304},{56,3... | collective-permute-start | bytes 24584 | tf_op jit(solution)/shard_map/ppermute | solution.py:195
  33.5 10.4 %copy-start = (s32[8192]{0:T(1024)S(1)}, s32[8192]{0:T(1024)}, u32[]{:S(2)}) copy-start(s32[8192]{0:T(1024)} %param.9) | copy-start | bytes 98308
  33.5 27.6 %all-to-all-start.1 = ((bf16[8,192,256]{2,1,0:T(8,128)(2,1)}), bf16[8,192,256]{2,1,0:T(8,128)(2,1)S(1)}, u32[]{:S(2)}, u32[]{:S(2)}) async-start(bf16[8,192,256]{2,1,0:T(8,128)(2,1)} %pad_maximum_fusion), calls=%async_computation.1 | async-start | bytes 1572864 | tf_op jit(solution)/shard_map/all_to_all | solution.py:200
  40.8 3.1 %collective-permute-start.4 = (bf16[128,256]{1,0:T(8,128)(2,1)S(1)}, bf16[128,256]{1,0:T(8,128)(2,1)S(1)}, u32[]{:S(2)}, u32[]{:S(2)}) collective-permute-start(bf16[128,256]{1,0:T(8,128)(2,1)S(1)} %get-tuple-element.58.mine_ref), channel_id=1, source_target_pairs={{0,8},{8,0},{16,24},{24,16},{32,40},{40,32},{48,56},{56,48},{64,72... | collective-permute-start | bytes 196616 | tf_op jit(solution)/shard_map/ppermute | solution.py:202
  43.9 18.6 %copy-start.2 = (s32[1,32]{1,0:T(1,128)S(1)}, s32[1,32]{1,0:T(1,128)}, u32[]{:S(2)}) copy-start(s32[1,32]{1,0:T(1,128)} %param.11) | copy-start | bytes 388
  61.2 12.2 %collective-permute-start.5 = (bf16[8,128,256]{2,1,0:T(8,128)(2,1)S(1)}, bf16[8,128,256]{2,1,0:T(8,128)(2,1)S(1)}, u32[]{:S(2)}, u32[]{:S(2)}) collective-permute-start(bf16[8,128,256]{2,1,0:T(8,128)(2,1)S(1)} %slice.19), channel_id=1, source_target_pairs={{0,128},{8,136},{16,144},{24,152},{32,160},{40,168},{48,176},{56,1... | collective-permute-start | bytes 1572872 | tf_op jit(solution)/shard_map/ppermute | solution.py:221
  62.5 4.2 %collective-permute-start = (bf16[1536,256]{1,0:T(8,128)(2,1)S(1)}, bf16[1536,256]{1,0:T(8,128)(2,1)S(1)}, u32[]{:S(2)}, u32[]{:S(2)}) collective-permute-start(bf16[1536,256]{1,0:T(8,128)(2,1)S(1)} %bitcast.21), channel_id=1, source_target_pairs={{0,8},{8,0},{16,24},{24,16},{32,40},{40,32},{48,56},{56,48},{64,72... | collective-permute-start | bytes 2359304 | tf_op jit(solution)/shard_map/cond/branch_1_fun/ppermute | solution.py:226
  73.4 3.8 %collective-permute-start.6 = (bf16[1024,256]{1,0:T(8,128)(2,1)S(1)}, bf16[1024,256]{1,0:T(8,128)(2,1)S(1)}, u32[]{:S(2)}, u32[]{:S(2)}) collective-permute-start(bf16[1024,256]{1,0:T(8,128)(2,1)S(1)} %bitcast.19), channel_id=1, source_target_pairs={{0,8},{8,0},{16,24},{24,16},{32,40},{40,32},{48,56},{56,48},{64,72... | collective-permute-start | bytes 1572872 | tf_op jit(solution)/shard_map/ppermute | solution.py:250

commit v20 on v19

--- a/solution.py
+++ b/solution.py
@@ -185,17 +185,17 @@
 def per_device(queries, branch_key_value, branch_ids, pool, page_table):
     me = lax.axis_index("seq")
     y = (me // 2) % NY
-    page = pool.reshape(1, PAGE, PAIR)
-    raw = jnp.concatenate([jnp.transpose(branch_key_value, (1, 0, 2)), page], axis=0)
-    one_raw = lax.ppermute(raw, "seq", x_ring(1))
-    three_page = lax.ppermute(page, "seq", x_ring(3))
-    wide = jnp.concatenate([jnp.transpose(queries, (1, 0, 2)), raw[:8], one_raw[:8]], axis=2)
+    page = pool.reshape(PAGE, PAIR)
+    wide = jnp.transpose(jnp.concatenate([queries, branch_key_value], axis=2), (1, 0, 2))
     wide = lax.all_to_all(wide, "head", split_axis=0, concat_axis=0, tiled=True).reshape(ROWS, -1)
-    own, before = wide[:, GROUP * D:GROUP * D + PAIR], wide[:, GROUP * D + PAIR:]
     two_page = lax.ppermute(page, "seq", x_ring(2))
+    wide, two_page, later = lax.optimization_barrier((wide, two_page, page))
+    own = wide[:, GROUP * D:]
+    one_back = lax.ppermute(jnp.concatenate([own, page], axis=0), "seq", x_ring(1))
+    three_page = lax.ppermute(later, "seq", x_ring(3))
     target = jnp.arange(NY, dtype=jnp.int32)[:, None, None]
-    block = jnp.where(target > y, own[None], before[None])
-    pages = jnp.concatenate([page, one_raw[8:], two_page, three_page], axis=0).reshape(1, NX * PAGE, PAIR)
+    block = jnp.where(target > y, own[None], one_back[None, :ROWS])
+    pages = jnp.concatenate([page, one_back[ROWS:], two_page, three_page], axis=0)[None]
     send = jnp.concatenate([block, jnp.broadcast_to(pages, (NY, NX * PAGE, PAIR))], axis=1)
     near = lax.all_to_all(send, "seq", split_axis=0, concat_axis=0, tiled=True, axis_index_groups=Y_GROUPS)
     later, _ = lax.optimization_barrier((own, send))

time: 95.4 us -> 97.7 us (1.024)
  waiting for transfers between devices: 31.4 us -> 36.8 us
  starting transfers between devices: 35.8 us -> 33.7 us
    ppermute x2, starting transfers between devices: 10.5 us -> 5.84 us  [the longest x1 3.46 us: per_device(): three_page = lax.ppermute(later, 'seq', x_ring(3))]
    all_to_all x1, starting transfers between devices: 6.84 us -> 10.3 us  [per_device(): lax.all_to_all(wide, 'head', split_axis=0, concat_axis=0, tiled=True)]
    all_to_all x1, waiting for transfers between devices: 3.73 us -> 6.23 us  [per_device(): lax.all_to_all(wide, 'head', split_axis=0, concat_axis=0, tiled=True)]
    ppermute x2, waiting for transfers between devices: 0.86 us -> 3.16 us  [the longest x1 2.78 us: per_device(): three_page = lax.ppermute(later, 'seq', x_ring(3))]
    concatenate x3 -> x2, other arithmetic: 1.5 us -> 0.01 us  [the longest x1 0.01 us: per_device(): jnp.concatenate([own, page], axis=0)]
  transfers between devices with their start and end apart: 9 -> 9, of which waited for: 8 -> 9; matrix products, arithmetic and copies ran while one was open for 1% -> 0% of each run, Pallas kernels for 5% -> 5%
where the time goes in v20:
time: 97.7 us; the launch traced here: 96.5 us
  waiting for transfers between devices  36.8 us (38%)
  starting transfers between devices  33.7 us (34%)
  blocking collectives  15.5 us (16%)
  Pallas kernels  5.61 us (6%)
  local copies, waits for them, and re-layouts  2.89 us (3%)
  other arithmetic  1.82 us (2%)
    all_to_all x1, waiting for transfers between devices, per_device(): lax.all_to_all(send, 'seq', split_axis=0, concat_axis=0, tiled=True, axis...  16.3 us
    all_to_all x1, blocking collectives, per_device(): lax.all_to_all(out.reshape(8, ROWS // 8, GROUP * D), 'head', split_axis=0...  15.5 us
    all_to_all x1, starting transfers between devices, per_device(): lax.all_to_all(wide, 'head', split_axis=0, concat_axis=0, tiled=True)  10.3 us
    all_to_all x1, starting transfers between devices, per_device(): lax.all_to_all(send, 'seq', split_axis=0, concat_axis=0, tiled=True, axis...  7.23 us
    all_to_all x1, waiting for transfers between devices, per_device(): lax.all_to_all(wide, 'head', split_axis=0, concat_axis=0, tiled=True)  6.23 us
    ppermute x1, waiting for transfers between devices, per_device(): far = lax.ppermute(near[:, :ROWS], 'seq', x_next())  3.82 us
    ppermute x1, waiting for transfers between devices, per_device(): two_page = lax.ppermute(page, 'seq', x_ring(2))  3.7 us
    ppermute x1, starting transfers between devices, per_device(): three_page = lax.ppermute(later, 'seq', x_ring(3))  3.46 us
  transfers between devices with their start and end apart: 9, of which 9 were waited for; matrix products, arithmetic and copies ran while one was open for 0% of the time, Pallas kernels for 5%

profile of v20, /device:TPU:6, one launch (start us, length us, event | category | flops | bytes accessed | tf_op | source)
XLA Modules:
  0.0 96.5 jit_solution(1194203985320014659)
XLA Ops:
  0.0 0.9 copy.10
  0.9 1.1 %copy.9 = bf16[16,8,1024]{2,0,1:T(8,128)(2,1)S(1)} copy(bf16[16,8,1024]{2,1,0:T(8,128)(2,1)} %param.7) | data formatting | bytes 524288 | tf_op args[0]
  2.0 0.0 copy-start
  2.0 0.7 maximum_bitcast_fusion
  2.7 10.3 %all-to-all-start = ((bf16[8,16,1280]{2,1,0:T(8,128)(2,1)}), bf16[8,16,1280]{2,1,0:T(8,128)(2,1)S(1)}, u32[]{:S(2)}, u32[]{:S(2)}) async-start(bf16[8,16,1280]{2,1,0:T(8,128)(2,1)} %maximum_bitcast_fusion), calls=%async_computation | async-start | bytes 655360 | tf_op jit(solution)/shard_map/all_to_all | solution.py:190
  13.0 3.3 %collective-permute-start.1 = (bf16[16,256]{1,0:T(8,128)(2,1)S(1)}, bf16[16,256]{1,0:T(8,128)(2,1)S(1)}, u32[]{:S(2)}, u32[]{:S(2)}) collective-permute-start(bf16[16,256]{1,0:T(8,128)(2,1)S(1)} %bitcast.20), channel_id=1, source_target_pairs={{0,256},{8,264},{16,272},{24,280},{32,288},{40,296},{48,304},{56,3... | collective-permute-start | bytes 24584 | tf_op jit(solution)/shard_map/ppermute | solution.py:191
  16.4 3.7 %collective-permute-done.1 = bf16[16,256]{1,0:T(8,128)(2,1)S(1)} collective-permute-done((bf16[16,256]{1,0:T(8,128)(2,1)S(1)}, bf16[16,256]{1,0:T(8,128)(2,1)S(1)}, u32[]{:S(2)}, u32[]{:S(2)}) %collective-permute-start.1) | collective-permute-done | bytes 8224 | tf_op jit(solution)/shard_map/ppermute | solution.py:191
  20.1 6.2 %all-to-all-done = bf16[8,16,1280]{2,1,0:T(8,128)(2,1)S(1)} async-done(((bf16[8,16,1280]{2,1,0:T(8,128)(2,1)}), bf16[8,16,1280]{2,1,0:T(8,128)(2,1)S(1)}, u32[]{:S(2)}, u32[]{:S(2)}) %all-to-all-start) | async-done | bytes 327712 | tf_op jit(solution)/shard_map/all_to_all | solution.py:190
  26.3 2.4 %collective-permute-start.2 = (bf16[144,256]{1,0:T(8,128)(2,1)S(1)}, bf16[144,256]{1,0:T(8,128)(2,1)S(1)}, u32[]{:S(2)}, u32[]{:S(2)}) collective-permute-start(bf16[144,256]{1,0:T(8,128)(2,1)S(1)} %pad_maximum_fusion.1), channel_id=1, source_target_pairs={{0,128},{8,136},{16,144},{24,152},{32,160},{40,168},{48,176},{56,1... | collective-permute-start | bytes 221192 | tf_op jit(solution)/shard_map/ppermute | solution.py:194
  28.7 3.5 %collective-permute-start.3 = (bf16[16,256]{1,0:T(8,128)(2,1)S(1)}, bf16[16,256]{1,0:T(8,128)(2,1)S(1)}, u32[]{:S(2)}, u32[]{:S(2)}) collective-permute-start(bf16[16,256]{1,0:T(8,128)(2,1)S(1)} %bitcast.22), channel_id=1, source_target_pairs={{0,384},{8,392},{16,400},{24,408},{32,416},{40,424},{48,432},{56,4... | collective-permute-start | bytes 24584 | tf_op jit(solution)/shard_map/ppermute | solution.py:195
  32.2 0.4 collective-permute-done.2
  32.6 0.1 broadcast_select_fusion
  32.7 2.8 %collective-permute-done.3 = bf16[16,256]{1,0:T(8,128)(2,1)S(1)} collective-permute-done((bf16[16,256]{1,0:T(8,128)(2,1)S(1)}, bf16[16,256]{1,0:T(8,128)(2,1)S(1)}, u32[]{:S(2)}, u32[]{:S(2)}) %collective-permute-start.3) | collective-permute-done | bytes 8224 | tf_op jit(solution)/shard_map/ppermute | solution.py:195
  35.5 0.9 pad_maximum_fusion
  36.5 7.2 %all-to-all-start.1 = ((bf16[8,192,256]{2,1,0:T(8,128)(2,1)}), bf16[8,192,256]{2,1,0:T(8,128)(2,1)S(1)}, u32[]{:S(2)}, u32[]{:S(2)}) async-start(bf16[8,192,256]{2,1,0:T(8,128)(2,1)} %pad_maximum_fusion), calls=%async_computation.1 | async-start | bytes 1572864 | tf_op jit(solution)/shard_map/all_to_all | solution.py:200
  43.7 1.9 %collective-permute-start.4 = (bf16[128,256]{1,0:T(8,128)(2,1)S(1)}, bf16[128,256]{1,0:T(8,128)(2,1)S(1)}, u32[]{:S(2)}, u32[]{:S(2)}) collective-permute-start(bf16[128,256]{1,0:T(8,128)(2,1)S(1)} %slice.12.mine_ref), channel_id=1, source_target_pairs={{0,8},{8,0},{16,24},{24,16},{32,40},{40,32},{48,56},{56,48},{64,72... | collective-permute-start | bytes 196616 | tf_op jit(solution)/shard_map/ppermute | solution.py:202
  45.6 1.2 %collective-permute-done.4.side_ref = bf16[128,256]{1,0:T(8,128)(2,1)S(1)} collective-permute-done((bf16[128,256]{1,0:T(8,128)(2,1)S(1)}, bf16[128,256]{1,0:T(8,128)(2,1)S(1)}, u32[]{:S(2)}, u32[]{:S(2)}) %collective-permute-start.4) | collective-permute-done | bytes 65568 | tf_op jit(solution)/shard_map/ppermute | solution.py:202
  46.9 0.7 own_chip.1
  47.5 16.3 %all-to-all-done.1 = bf16[8,192,256]{2,1,0:T(8,128)(2,1)S(1)} async-done(((bf16[8,192,256]{2,1,0:T(8,128)(2,1)}), bf16[8,192,256]{2,1,0:T(8,128)(2,1)S(1)}, u32[]{:S(2)}, u32[]{:S(2)}) %all-to-all-start.1) | async-done | bytes 786464 | tf_op jit(solution)/shard_map/all_to_all | solution.py:200
  63.8 1.3 %collective-permute-start.5 = (bf16[8,128,256]{2,1,0:T(8,128)(2,1)S(1)}, bf16[8,128,256]{2,1,0:T(8,128)(2,1)S(1)}, u32[]{:S(2)}, u32[]{:S(2)}) collective-permute-start(bf16[8,128,256]{2,1,0:T(8,128)(2,1)S(1)} %slice.15), channel_id=1, source_target_pairs={{0,128},{8,136},{16,144},{24,152},{32,160},{40,168},{48,176},{56,1... | collective-permute-start | bytes 1572872 | tf_op jit(solution)/shard_map/ppermute | solution.py:221
  65.1 6.9 %conditional.1 = ((f32[1,1024]{1,0:T(1,128)S(1)}, f32[1,1024]{1,0:T(1,128)S(1)}, f32[128,1024]{1,0:T(8,128)S(1)})) conditional(s32[]{:T(128)} %convert_element_type.3, (f32[1,1024]{1,0:T(1,128)S(1)}, f32[1,1024]{1,0:T(1,128)S(1)}, f32[128,1024]{1,0:T(8,128)S(1)}) %tuple.18, (s32[1,32]{1,0:T(1,128)S(1)}, bf16[8,192,256]{2,1,0:T(8,128)(2,1)S(1)}, ...), branch_computations={%region_0.1_spmd, %region_1.2_spmd} | conditional | flops 1342177280 | bytes 5242928 | solution.py:247
  65.1 1.9 %collective-permute-start = (bf16[1536,256]{1,0:T(8,128)(2,1)S(1)}, bf16[1536,256]{1,0:T(8,128)(2,1)S(1)}, u32[]{:S(2)}, u32[]{:S(2)}) collective-permute-start(bf16[1536,256]{1,0:T(8,128)(2,1)S(1)} %bitcast.16), channel_id=1, source_target_pairs={{0,8},{8,0},{16,24},{24,16},{32,40},{40,32},{48,56},{56,48},{64,72... | collective-permute-start | bytes 2359304 | tf_op jit(solution)/shard_map/cond/branch_1_fun/ppermute | solution.py:226
  67.1 1.4 %near_window.1 = (f32[1,1024]{1,0:T(1,128)S(1)}, f32[1,1024]{1,0:T(1,128)S(1)}, f32[128,1024]{1,0:T(8,128)S(1)}) custom-call(s32[1]{0:T(128)} %get-tuple-element.27.meta_ref, bf16[1536,256]{1,0:T(8,128)(2,1)S(1)} %bitcast.17, s32[64,128]{1,0:T(8,128)S(1)} %get-tuple-element.30.ids_ref, bf16[256,1024]{1,0:T(8,128)(2,1)S(1)} %get-tuple-element.31.qt_ref, ...), custom_call_target="tpu_custom_call" | custom-call | flops 536870912 | bytes 1048576 | tf_op jit(solution)/shard_map/cond/branch_1_fun/near_window/pallas_call | solution.py:227
  68.4 0.9 collective-permute-done.side_ref
  69.3 2.8 %near_other_core_and_prefix.1 = (f32[1,1024]{1,0:T(1,128)S(1)}, f32[1,1024]{1,0:T(1,128)S(1)}, f32[128,1024]{1,0:T(8,128)S(1)}) custom-call(s32[1]{0:T(128)} %get-tuple-element.27.meta_ref, s32[32]{0:T(128)S(1)} %bitcast.28, bf16[1536,256]{1,0:T(8,128)(2,1)S(1)} %bitcast.18, bf16[1536,256]{1,0:T(8,128)(2,1)S(1)} %collective-permute-done.side_ref, ...), custom_call_target="tpu_custom_call" | custom-call | flops 805306368 | bytes 1048576 | tf_op jit(solution)/shard_map/cond/branch_1_fun/near_other_core_and_prefix/pallas_call | solution.py:236
  72.1 3.8 %collective-permute-done.5 = bf16[8,128,256]{2,1,0:T(8,128)(2,1)S(1)} collective-permute-done((bf16[8,128,256]{2,1,0:T(8,128)(2,1)S(1)}, bf16[8,128,256]{2,1,0:T(8,128)(2,1)S(1)}, u32[]{:S(2)}, u32[]{:S(2)}) %collective-permute-start.5) | collective-permute-done | bytes 524320 | tf_op jit(solution)/shard_map/ppermute | solution.py:221
  75.9 1.9 %collective-permute-start.6 = (bf16[1024,256]{1,0:T(8,128)(2,1)S(1)}, bf16[1024,256]{1,0:T(8,128)(2,1)S(1)}, u32[]{:S(2)}, u32[]{:S(2)}) collective-permute-start(bf16[1024,256]{1,0:T(8,128)(2,1)S(1)} %bitcast.14), channel_id=1, source_target_pairs={{0,8},{8,0},{16,24},{24,16},{32,40},{40,32},{48,56},{56,48},{64,72... | collective-permute-start | bytes 1572872 | tf_op jit(solution)/shard_map/ppermute | solution.py:250
  77.8 0.4 far_window.1
  78.2 1.5 %collective-permute-done.6.kv_ref = bf16[1024,256]{1,0:T(8,128)(2,1)S(1)} collective-permute-done((bf16[1024,256]{1,0:T(8,128)(2,1)S(1)}, bf16[1024,256]{1,0:T(8,128)(2,1)S(1)}, u32[]{:S(2)}, u32[]{:S(2)}) %collective-permute-start.6) | collective-permute-done | bytes 524320 | tf_op jit(solution)/shard_map/ppermute | solution.py:250
  79.7 0.5 far_other_core.1
  80.2 15.5 %all_to_all.15 = bf16[8,16,1024]{2,1,0:T(8,128)(2,1)S(1)} all-to-all(bf16[8,16,1024]{2,1,0:T(8,128)(2,1)S(1)} %bitcast.13), channel_id=1, replica_groups=mesh['seq'=64,'head'=8] {'head'}, dimensions={0} | all-to-all | bytes 524288 | tf_op jit(solution)/shard_map/all_to_all | solution.py:274
  95.7 0.9 copy.11
  (13 shorter events, 0.1 us)
Async XLA Ops:
  2.0 11.1 %copy-start = (bf16[1,16,1,256]{3,1,2,0:T(8,128)(2,1)S(1)}, bf16[1,16,1,256]{3,1,2,0:T(8,128)(2,1)}, u32[]{:S(2)}) copy-start(bf16[1,16,1,256]{3,1,2,0:T(8,128)(2,1)} %param.10) | copy-start | bytes 24580
  2.7 23.6 %all-to-all-start = ((bf16[8,16,1280]{2,1,0:T(8,128)(2,1)}), bf16[8,16,1280]{2,1,0:T(8,128)(2,1)S(1)}, u32[]{:S(2)}, u32[]{:S(2)}) async-start(bf16[8,16,1280]{2,1,0:T(8,128)(2,1)} %maximum_bitcast_fusion), calls=%async_computation | async-start | bytes 655360 | tf_op jit(solution)/shard_map/all_to_all | solution.py:190
  13.0 7.0 %collective-permute-start.1 = (bf16[16,256]{1,0:T(8,128)(2,1)S(1)}, bf16[16,256]{1,0:T(8,128)(2,1)S(1)}, u32[]{:S(2)}, u32[]{:S(2)}) collective-permute-start(bf16[16,256]{1,0:T(8,128)(2,1)S(1)} %bitcast.20), channel_id=1, source_target_pairs={{0,256},{8,264},{16,272},{24,280},{32,288},{40,296},{48,304},{56,3... | collective-permute-start | bytes 24584 | tf_op jit(solution)/shard_map/ppermute | solution.py:191
  26.3 6.2 %collective-permute-start.2 = (bf16[144,256]{1,0:T(8,128)(2,1)S(1)}, bf16[144,256]{1,0:T(8,128)(2,1)S(1)}, u32[]{:S(2)}, u32[]{:S(2)}) collective-permute-start(bf16[144,256]{1,0:T(8,128)(2,1)S(1)} %pad_maximum_fusion.1), channel_id=1, source_target_pairs={{0,128},{8,136},{16,144},{24,152},{32,160},{40,168},{48,176},{56,1... | collective-permute-start | bytes 221192 | tf_op jit(solution)/shard_map/ppermute | solution.py:194
  28.7 6.8 %collective-permute-start.3 = (bf16[16,256]{1,0:T(8,128)(2,1)S(1)}, bf16[16,256]{1,0:T(8,128)(2,1)S(1)}, u32[]{:S(2)}, u32[]{:S(2)}) collective-permute-start(bf16[16,256]{1,0:T(8,128)(2,1)S(1)} %bitcast.22), channel_id=1, source_target_pairs={{0,384},{8,392},{16,400},{24,408},{32,416},{40,424},{48,432},{56,4... | collective-permute-start | bytes 24584 | tf_op jit(solution)/shard_map/ppermute | solution.py:195
  36.5 10.4 %copy-start.1 = (s32[8192]{0:T(1024)S(1)}, s32[8192]{0:T(1024)}, u32[]{:S(2)}) copy-start(s32[8192]{0:T(1024)} %param.9) | copy-start | bytes 98308
  36.5 27.3 %all-to-all-start.1 = ((bf16[8,192,256]{2,1,0:T(8,128)(2,1)}), bf16[8,192,256]{2,1,0:T(8,128)(2,1)S(1)}, u32[]{:S(2)}, u32[]{:S(2)}) async-start(bf16[8,192,256]{2,1,0:T(8,128)(2,1)} %pad_maximum_fusion), calls=%async_computation.1 | async-start | bytes 1572864 | tf_op jit(solution)/shard_map/all_to_all | solution.py:200
  43.7 21.4 %copy-start.2 = (s32[1,32]{1,0:T(1,128)S(1)}, s32[1,32]{1,0:T(1,128)}, u32[]{:S(2)}) copy-start(s32[1,32]{1,0:T(1,128)} %param.11) | copy-start | bytes 388
  43.7 3.1 %collective-permute-start.4 = (bf16[128,256]{1,0:T(8,128)(2,1)S(1)}, bf16[128,256]{1,0:T(8,128)(2,1)S(1)}, u32[]{:S(2)}, u32[]{:S(2)}) collective-permute-start(bf16[128,256]{1,0:T(8,128)(2,1)S(1)} %slice.12.mine_ref), channel_id=1, source_target_pairs={{0,8},{8,0},{16,24},{24,16},{32,40},{40,32},{48,56},{56,48},{64,72... | collective-permute-start | bytes 196616 | tf_op jit(solution)/shard_map/ppermute | solution.py:202
  63.8 12.1 %collective-permute-start.5 = (bf16[8,128,256]{2,1,0:T(8,128)(2,1)S(1)}, bf16[8,128,256]{2,1,0:T(8,128)(2,1)S(1)}, u32[]{:S(2)}, u32[]{:S(2)}) collective-permute-start(bf16[8,128,256]{2,1,0:T(8,128)(2,1)S(1)} %slice.15), channel_id=1, source_target_pairs={{0,128},{8,136},{16,144},{24,152},{32,160},{40,168},{48,176},{56,1... | collective-permute-start | bytes 1572872 | tf_op jit(solution)/shard_map/ppermute | solution.py:221
  65.1 4.2 %collective-permute-start = (bf16[1536,256]{1,0:T(8,128)(2,1)S(1)}, bf16[1536,256]{1,0:T(8,128)(2,1)S(1)}, u32[]{:S(2)}, u32[]{:S(2)}) collective-permute-start(bf16[1536,256]{1,0:T(8,128)(2,1)S(1)} %bitcast.16), channel_id=1, source_target_pairs={{0,8},{8,0},{16,24},{24,16},{32,40},{40,32},{48,56},{56,48},{64,72... | collective-permute-start | bytes 2359304 | tf_op jit(solution)/shard_map/cond/branch_1_fun/ppermute | solution.py:226
  75.9 3.8 %collective-permute-start.6 = (bf16[1024,256]{1,0:T(8,128)(2,1)S(1)}, bf16[1024,256]{1,0:T(8,128)(2,1)S(1)}, u32[]{:S(2)}, u32[]{:S(2)}) collective-permute-start(bf16[1024,256]{1,0:T(8,128)(2,1)S(1)} %bitcast.14), channel_id=1, source_target_pairs={{0,8},{8,0},{16,24},{24,16},{32,40},{40,32},{48,56},{56,48},{64,72... | collective-permute-start | bytes 1572872 | tf_op jit(solution)/shard_map/ppermute | solution.py:250

commit v21 on v20

--- a/solution.py
+++ b/solution.py
@@ -78,6 +78,11 @@
     return (key_rows >= row_start) & (key_rows <= query_rows)
 
 
+def by_head_kernel(q_ref, kv_ref, out_ref):
+    out_ref[:, :, :GROUP * D] = jnp.transpose(q_ref[...], (1, 0, 2))
+    out_ref[:, :, GROUP * D:] = jnp.transpose(kv_ref[...], (1, 0, 2))
+
+
 def own_kernel(meta_ref, mine_ref, side_ref, ids_ref, q_ref, qt_ref, m_ref, l_ref, acc_ref):
     own = meta_ref[0]
     row_start, first, last = starts_of(ids_ref, own)
@@ -186,16 +191,21 @@
     me = lax.axis_index("seq")
     y = (me // 2) % NY
     page = pool.reshape(PAGE, PAIR)
-    wide = jnp.transpose(jnp.concatenate([queries, branch_key_value], axis=2), (1, 0, 2))
+    wide = pl.pallas_call(
+        by_head_kernel,
+        out_shape=jax.ShapeDtypeStruct((8, ROWS // 8, GROUP * D + PAIR), jnp.bfloat16),
+        in_specs=[VM] * 2,
+        out_specs=VM,
+        name="by_head",
+    )(queries, branch_key_value)
     wide = lax.all_to_all(wide, "head", split_axis=0, concat_axis=0, tiled=True).reshape(ROWS, -1)
     two_page = lax.ppermute(page, "seq", x_ring(2))
-    wide, two_page, later = lax.optimization_barrier((wide, two_page, page))
+    wide, two_page = lax.optimization_barrier((wide, two_page))
     own = wide[:, GROUP * D:]
-    one_back = lax.ppermute(jnp.concatenate([own, page], axis=0), "seq", x_ring(1))
-    three_page = lax.ppermute(later, "seq", x_ring(3))
+    one_back = lax.ppermute(jnp.concatenate([own, page, two_page], axis=0), "seq", x_ring(1))
     target = jnp.arange(NY, dtype=jnp.int32)[:, None, None]
     block = jnp.where(target > y, own[None], one_back[None, :ROWS])
-    pages = jnp.concatenate([page, one_back[ROWS:], two_page, three_page], axis=0)[None]
+    pages = jnp.concatenate([page, one_back[ROWS:ROWS + PAGE], two_page, one_back[ROWS + PAGE:]], axis=0)[None]
     send = jnp.concatenate([block, jnp.broadcast_to(pages, (NY, NX * PAGE, PAIR))], axis=1)
     near = lax.all_to_all(send, "seq", split_axis=0, concat_axis=0, tiled=True, axis_index_groups=Y_GROUPS)
     later, _ = lax.optimization_barrier((own, send))

time: 97.7 us -> 95 us (0.972)
  starting transfers between devices: 33.7 us -> 30.3 us
  waiting for transfers between devices: 36.8 us -> 38.9 us
  local copies, waits for them, and re-layouts: 2.89 us -> 0.93 us
    ppermute x2 -> x1, starting transfers between devices: 5.84 us -> 2.39 us  [per_device(): lax.ppermute(jnp.concatenate([own, page, two_page], axis=0), 'seq', x_rin...]
    unnamed x8 -> x6, local copies, waits for them, and re-layouts: 1.97 us -> 0.01 us
    pallas_call x0 -> x1, Pallas kernels: none -> 1.77 us  [per_device(): pl.pallas_call(by_head_kernel, out_shape=jax.ShapeDtypeStruct((8, ROWS //...]
    pallas_call x1, Pallas kernels: 1.36 us -> 0.36 us  [near_part(): pl.pallas_call(near_kernel, out_shape=state, in_specs=[SM] + [VM] * 6, ou...]
    ppermute x1, waiting for transfers between devices: 0.88 us -> 1.88 us  [near_part(): near_side = lax.ppermute(near, 'seq', SWAP)]
    ppermute x2 -> x1, waiting for transfers between devices: 3.16 us -> 3.93 us  [per_device(): lax.ppermute(jnp.concatenate([own, page, two_page], axis=0), 'seq', x_rin...]
  transfers between devices with their start and end apart: 9 -> 8, of which waited for: 9 -> 8; matrix products, arithmetic and copies ran while one was open for 0% -> 0% of each run, Pallas kernels for 5% -> 4%
where the time goes in v21:
time: 95 us; the launch traced here: 93.4 us
  waiting for transfers between devices  38.9 us (41%)
  starting transfers between devices  30.3 us (32%)
  blocking collectives  15.7 us (17%)
  Pallas kernels  6.44 us (7%)
  other arithmetic  1.07 us (1%)
    all_to_all x1, waiting for transfers between devices, per_device(): lax.all_to_all(send, 'seq', split_axis=0, concat_axis=0, tiled=True, axis...  16.5 us
    all_to_all x1, blocking collectives, per_device(): lax.all_to_all(out.reshape(8, ROWS // 8, GROUP * D), 'head', split_axis=0...  15.7 us
    all_to_all x1, starting transfers between devices, per_device(): lax.all_to_all(wide, 'head', split_axis=0, concat_axis=0, tiled=True)  10.3 us
    all_to_all x1, starting transfers between devices, per_device(): lax.all_to_all(send, 'seq', split_axis=0, concat_axis=0, tiled=True, axis...  7.23 us
    all_to_all x1, waiting for transfers between devices, per_device(): lax.all_to_all(wide, 'head', split_axis=0, concat_axis=0, tiled=True)  6.23 us
    ppermute x1, waiting for transfers between devices, per_device(): lax.ppermute(jnp.concatenate([own, page, two_page], axis=0), 'seq', x_rin...  3.93 us
    ppermute x1, waiting for transfers between devices, per_device(): far = lax.ppermute(near[:, :ROWS], 'seq', x_next())  3.88 us
    ppermute x1, waiting for transfers between devices, per_device(): two_page = lax.ppermute(page, 'seq', x_ring(2))  3.7 us
  transfers between devices with their start and end apart: 8, of which 8 were waited for; matrix products, arithmetic and copies ran while one was open for 0% of the time, Pallas kernels for 4%

profile of v21, /device:TPU:6, one launch (start us, length us, event | category | flops | bytes accessed | tf_op | source)
XLA Modules:
  0.0 93.4 jit_solution(11170151769542298168)
XLA Ops:
  0.0 0.0 copy-start
  0.0 1.8 %by_head.1 = bf16[8,16,1280]{2,1,0:T(8,128)(2,1)} custom-call(bf16[16,8,1024]{2,1,0:T(8,128)(2,1)} %q_ref.1, bf16[16,8,256]{2,1,0:T(8,128)(2,1)} %kv_ref.1), custom_call_target="tpu_custom_call" | custom-call | tf_op jit(solution)/shard_map/by_head/pallas_call | solution.py:194
  1.8 10.3 %all-to-all-start = ((bf16[8,16,1280]{2,1,0:T(8,128)(2,1)}), bf16[8,16,1280]{2,1,0:T(8,128)(2,1)S(1)}, u32[]{:S(2)}, u32[]{:S(2)}) async-start(bf16[8,16,1280]{2,1,0:T(8,128)(2,1)} %by_head.1), calls=%async_computation | async-start | bytes 655360 | tf_op jit(solution)/shard_map/all_to_all | solution.py:201
  12.1 0.0 copy-done
  12.1 3.3 %collective-permute-start.1 = (bf16[16,256]{1,0:T(8,128)(2,1)S(1)}, bf16[16,256]{1,0:T(8,128)(2,1)S(1)}, u32[]{:S(2)}, u32[]{:S(2)}) collective-permute-start(bf16[16,256]{1,0:T(8,128)(2,1)S(1)} %bitcast.18), channel_id=1, source_target_pairs={{0,256},{8,264},{16,272},{24,280},{32,288},{40,296},{48,304},{56,3... | collective-permute-start | bytes 24584 | tf_op jit(solution)/shard_map/ppermute | solution.py:202
  15.4 3.7 %collective-permute-done.1 = bf16[16,256]{1,0:T(8,128)(2,1)S(1)} collective-permute-done((bf16[16,256]{1,0:T(8,128)(2,1)S(1)}, bf16[16,256]{1,0:T(8,128)(2,1)S(1)}, u32[]{:S(2)}, u32[]{:S(2)}) %collective-permute-start.1) | collective-permute-done | bytes 8224 | tf_op jit(solution)/shard_map/ppermute | solution.py:202
  19.1 6.2 %all-to-all-done = bf16[8,16,1280]{2,1,0:T(8,128)(2,1)S(1)} async-done(((bf16[8,16,1280]{2,1,0:T(8,128)(2,1)}), bf16[8,16,1280]{2,1,0:T(8,128)(2,1)S(1)}, u32[]{:S(2)}, u32[]{:S(2)}) %all-to-all-start) | async-done | bytes 327712 | tf_op jit(solution)/shard_map/all_to_all | solution.py:201
  25.4 2.4 %collective-permute-start.2 = (bf16[160,256]{1,0:T(8,128)(2,1)S(1)}, bf16[160,256]{1,0:T(8,128)(2,1)S(1)}, u32[]{:S(2)}, u32[]{:S(2)}) collective-permute-start(bf16[160,256]{1,0:T(8,128)(2,1)S(1)} %pad_maximum_fusion.1), channel_id=1, source_target_pairs={{0,128},{8,136},{16,144},{24,152},{32,160},{40,168},{48,176},{56,1... | collective-permute-start | bytes 245768 | tf_op jit(solution)/shard_map/ppermute | solution.py:205
  27.8 3.9 %collective-permute-done.2 = bf16[160,256]{1,0:T(8,128)(2,1)S(1)} collective-permute-done((bf16[160,256]{1,0:T(8,128)(2,1)S(1)}, bf16[160,256]{1,0:T(8,128)(2,1)S(1)}, u32[]{:S(2)}, u32[]{:S(2)}) %collective-permute-start.2) | collective-permute-done | bytes 81952 | tf_op jit(solution)/shard_map/ppermute | solution.py:205
  31.7 0.1 broadcast_select_fusion
  31.9 0.9 %pad_maximum_fusion = bf16[8,192,256]{2,1,0:T(8,128)(2,1)} fusion(bf16[8,64,256]{2,1,0:T(8,128)(2,1)S(1)} %broadcast_in_dim.36, bf16[8,128,256]{2,1,0:T(8,128)(2,1)S(1)} %broadcast_select_fusion), kind=kLoop, calls=%fused_computation | loop fusion | flops 1572864 | bytes 1572864 | tf_op jit(solution)/shard_map/concatenate | solution.py:209
  32.8 0.0 copy-start.1
  32.8 7.2 %all-to-all-start.1 = ((bf16[8,192,256]{2,1,0:T(8,128)(2,1)}), bf16[8,192,256]{2,1,0:T(8,128)(2,1)S(1)}, u32[]{:S(2)}, u32[]{:S(2)}) async-start(bf16[8,192,256]{2,1,0:T(8,128)(2,1)} %pad_maximum_fusion), calls=%async_computation.1 | async-start | bytes 1572864 | tf_op jit(solution)/shard_map/all_to_all | solution.py:210
  40.1 1.9 %collective-permute-start.3 = (bf16[128,256]{1,0:T(8,128)(2,1)S(1)}, bf16[128,256]{1,0:T(8,128)(2,1)S(1)}, u32[]{:S(2)}, u32[]{:S(2)}) collective-permute-start(bf16[128,256]{1,0:T(8,128)(2,1)S(1)} %slice.15.mine_ref), channel_id=1, source_target_pairs={{0,8},{8,0},{16,24},{24,16},{32,40},{40,32},{48,56},{56,48},{64,72... | collective-permute-start | bytes 196616 | tf_op jit(solution)/shard_map/ppermute | solution.py:212
  42.0 1.2 %collective-permute-done.3.side_ref = bf16[128,256]{1,0:T(8,128)(2,1)S(1)} collective-permute-done((bf16[128,256]{1,0:T(8,128)(2,1)S(1)}, bf16[128,256]{1,0:T(8,128)(2,1)S(1)}, u32[]{:S(2)}, u32[]{:S(2)}) %collective-permute-start.3) | collective-permute-done | bytes 65568 | tf_op jit(solution)/shard_map/ppermute | solution.py:212
  43.2 0.0 copy-done.1
  43.2 0.7 own_chip.1
  43.9 16.5 %all-to-all-done.1 = bf16[8,192,256]{2,1,0:T(8,128)(2,1)S(1)} async-done(((bf16[8,192,256]{2,1,0:T(8,128)(2,1)}), bf16[8,192,256]{2,1,0:T(8,128)(2,1)S(1)}, u32[]{:S(2)}, u32[]{:S(2)}) %all-to-all-start.1) | async-done | bytes 786464 | tf_op jit(solution)/shard_map/all_to_all | solution.py:210
  60.5 1.3 %collective-permute-start.4 = (bf16[8,128,256]{2,1,0:T(8,128)(2,1)S(1)}, bf16[8,128,256]{2,1,0:T(8,128)(2,1)S(1)}, u32[]{:S(2)}, u32[]{:S(2)}) collective-permute-start(bf16[8,128,256]{2,1,0:T(8,128)(2,1)S(1)} %slice.19), channel_id=1, source_target_pairs={{0,128},{8,136},{16,144},{24,152},{32,160},{40,168},{48,176},{56,1... | collective-permute-start | bytes 1572872 | tf_op jit(solution)/shard_map/ppermute | solution.py:231
  61.8 0.0 copy-done.2
  61.8 7.0 %conditional.1 = ((f32[1,1024]{1,0:T(1,128)S(1)}, f32[1,1024]{1,0:T(1,128)S(1)}, f32[128,1024]{1,0:T(8,128)S(1)})) conditional(s32[]{:T(128)} %convert_element_type.3, (f32[1,1024]{1,0:T(1,128)S(1)}, f32[1,1024]{1,0:T(1,128)S(1)}, f32[128,1024]{1,0:T(8,128)S(1)}) %tuple.18, (s32[1,32]{1,0:T(1,128)S(1)}, bf16[8,192,256]{2,1,0:T(8,128)(2,1)S(1)}, ...), branch_computations={%region_0.1_spmd, %region_1.2_spmd} | conditional | flops 1342177280 | bytes 5242928 | solution.py:257
  61.8 1.9 %collective-permute-start = (bf16[1536,256]{1,0:T(8,128)(2,1)S(1)}, bf16[1536,256]{1,0:T(8,128)(2,1)S(1)}, u32[]{:S(2)}, u32[]{:S(2)}) collective-permute-start(bf16[1536,256]{1,0:T(8,128)(2,1)S(1)} %bitcast.14), channel_id=1, source_target_pairs={{0,8},{8,0},{16,24},{24,16},{32,40},{40,32},{48,56},{56,48},{64,72... | collective-permute-start | bytes 2359304 | tf_op jit(solution)/shard_map/cond/branch_1_fun/ppermute | solution.py:236
  63.7 0.4 near_window.1
  64.1 1.9 %collective-permute-done.side_ref = bf16[1536,256]{1,0:T(8,128)(2,1)S(1)} collective-permute-done((bf16[1536,256]{1,0:T(8,128)(2,1)S(1)}, bf16[1536,256]{1,0:T(8,128)(2,1)S(1)}, u32[]{:S(2)}, u32[]{:S(2)}) %collective-permute-start) | collective-permute-done | bytes 786464 | tf_op jit(solution)/shard_map/cond/branch_1_fun/ppermute | solution.py:236
  66.0 2.8 %near_other_core_and_prefix.1 = (f32[1,1024]{1,0:T(1,128)S(1)}, f32[1,1024]{1,0:T(1,128)S(1)}, f32[128,1024]{1,0:T(8,128)S(1)}) custom-call(s32[1]{0:T(128)} %get-tuple-element.27.meta_ref, s32[32]{0:T(128)S(1)} %bitcast.25, bf16[1536,256]{1,0:T(8,128)(2,1)S(1)} %bitcast.16, bf16[1536,256]{1,0:T(8,128)(2,1)S(1)} %collective-permute-done.side_ref, ...), custom_call_target="tpu_custom_call" | custom-call | flops 805306368 | bytes 1048576 | tf_op jit(solution)/shard_map/cond/branch_1_fun/near_other_core_and_prefix/pallas_call | solution.py:246
  68.8 3.9 %collective-permute-done.4 = bf16[8,128,256]{2,1,0:T(8,128)(2,1)S(1)} collective-permute-done((bf16[8,128,256]{2,1,0:T(8,128)(2,1)S(1)}, bf16[8,128,256]{2,1,0:T(8,128)(2,1)S(1)}, u32[]{:S(2)}, u32[]{:S(2)}) %collective-permute-start.4) | collective-permute-done | bytes 524320 | tf_op jit(solution)/shard_map/ppermute | solution.py:231
  72.6 1.9 %collective-permute-start.5 = (bf16[1024,256]{1,0:T(8,128)(2,1)S(1)}, bf16[1024,256]{1,0:T(8,128)(2,1)S(1)}, u32[]{:S(2)}, u32[]{:S(2)}) collective-permute-start(bf16[1024,256]{1,0:T(8,128)(2,1)S(1)} %bitcast.12), channel_id=1, source_target_pairs={{0,8},{8,0},{16,24},{24,16},{32,40},{40,32},{48,56},{56,48},{64,72... | collective-permute-start | bytes 1572872 | tf_op jit(solution)/shard_map/ppermute | solution.py:260
  74.6 0.4 far_window.1
  74.9 1.5 %collective-permute-done.5.kv_ref = bf16[1024,256]{1,0:T(8,128)(2,1)S(1)} collective-permute-done((bf16[1024,256]{1,0:T(8,128)(2,1)S(1)}, bf16[1024,256]{1,0:T(8,128)(2,1)S(1)}, u32[]{:S(2)}, u32[]{:S(2)}) %collective-permute-start.5) | collective-permute-done | bytes 524320 | tf_op jit(solution)/shard_map/ppermute | solution.py:260
  76.4 0.5 far_other_core.1
  76.9 15.7 %all_to_all.15 = bf16[8,16,1024]{2,1,0:T(8,128)(2,1)S(1)} all-to-all(bf16[8,16,1024]{2,1,0:T(8,128)(2,1)S(1)} %bitcast.11), channel_id=1, replica_groups=mesh['seq'=64,'head'=8] {'head'}, dimensions={0} | all-to-all | bytes 524288 | tf_op jit(solution)/shard_map/all_to_all | solution.py:284
  92.6 0.9 copy.8
  (9 shorter events, 0.1 us)
Async XLA Ops:
  0.0 12.1 %copy-start = (bf16[1,16,1,256]{3,1,2,0:T(8,128)(2,1)S(1)}, bf16[1,16,1,256]{3,1,2,0:T(8,128)(2,1)}, u32[]{:S(2)}) copy-start(bf16[1,16,1,256]{3,1,2,0:T(8,128)(2,1)} %param.10) | copy-start | bytes 24580
  1.8 23.6 %all-to-all-start = ((bf16[8,16,1280]{2,1,0:T(8,128)(2,1)}), bf16[8,16,1280]{2,1,0:T(8,128)(2,1)S(1)}, u32[]{:S(2)}, u32[]{:S(2)}) async-start(bf16[8,16,1280]{2,1,0:T(8,128)(2,1)} %by_head.1), calls=%async_computation | async-start | bytes 655360 | tf_op jit(solution)/shard_map/all_to_all | solution.py:201
  12.1 7.0 %collective-permute-start.1 = (bf16[16,256]{1,0:T(8,128)(2,1)S(1)}, bf16[16,256]{1,0:T(8,128)(2,1)S(1)}, u32[]{:S(2)}, u32[]{:S(2)}) collective-permute-start(bf16[16,256]{1,0:T(8,128)(2,1)S(1)} %bitcast.18), channel_id=1, source_target_pairs={{0,256},{8,264},{16,272},{24,280},{32,288},{40,296},{48,304},{56,3... | collective-permute-start | bytes 24584 | tf_op jit(solution)/shard_map/ppermute | solution.py:202
  25.4 6.3 %collective-permute-start.2 = (bf16[160,256]{1,0:T(8,128)(2,1)S(1)}, bf16[160,256]{1,0:T(8,128)(2,1)S(1)}, u32[]{:S(2)}, u32[]{:S(2)}) collective-permute-start(bf16[160,256]{1,0:T(8,128)(2,1)S(1)} %pad_maximum_fusion.1), channel_id=1, source_target_pairs={{0,128},{8,136},{16,144},{24,152},{32,160},{40,168},{48,176},{56,1... | collective-permute-start | bytes 245768 | tf_op jit(solution)/shard_map/ppermute | solution.py:205
  32.8 10.4 %copy-start.1 = (s32[8192]{0:T(1024)S(1)}, s32[8192]{0:T(1024)}, u32[]{:S(2)}) copy-start(s32[8192]{0:T(1024)} %param.9) | copy-start | bytes 98308
  32.8 27.6 %all-to-all-start.1 = ((bf16[8,192,256]{2,1,0:T(8,128)(2,1)}), bf16[8,192,256]{2,1,0:T(8,128)(2,1)S(1)}, u32[]{:S(2)}, u32[]{:S(2)}) async-start(bf16[8,192,256]{2,1,0:T(8,128)(2,1)} %pad_maximum_fusion), calls=%async_computation.1 | async-start | bytes 1572864 | tf_op jit(solution)/shard_map/all_to_all | solution.py:210
  40.1 21.7 %copy-start.2 = (s32[1,32]{1,0:T(1,128)S(1)}, s32[1,32]{1,0:T(1,128)}, u32[]{:S(2)}) copy-start(s32[1,32]{1,0:T(1,128)} %param.11) | copy-start | bytes 388
  40.1 3.1 %collective-permute-start.3 = (bf16[128,256]{1,0:T(8,128)(2,1)S(1)}, bf16[128,256]{1,0:T(8,128)(2,1)S(1)}, u32[]{:S(2)}, u32[]{:S(2)}) collective-permute-start(bf16[128,256]{1,0:T(8,128)(2,1)S(1)} %slice.15.mine_ref), channel_id=1, source_target_pairs={{0,8},{8,0},{16,24},{24,16},{32,40},{40,32},{48,56},{56,48},{64,72... | collective-permute-start | bytes 196616 | tf_op jit(solution)/shard_map/ppermute | solution.py:212
  60.5 12.2 %collective-permute-start.4 = (bf16[8,128,256]{2,1,0:T(8,128)(2,1)S(1)}, bf16[8,128,256]{2,1,0:T(8,128)(2,1)S(1)}, u32[]{:S(2)}, u32[]{:S(2)}) collective-permute-start(bf16[8,128,256]{2,1,0:T(8,128)(2,1)S(1)} %slice.19), channel_id=1, source_target_pairs={{0,128},{8,136},{16,144},{24,152},{32,160},{40,168},{48,176},{56,1... | collective-permute-start | bytes 1572872 | tf_op jit(solution)/shard_map/ppermute | solution.py:231
  61.8 4.2 %collective-permute-start = (bf16[1536,256]{1,0:T(8,128)(2,1)S(1)}, bf16[1536,256]{1,0:T(8,128)(2,1)S(1)}, u32[]{:S(2)}, u32[]{:S(2)}) collective-permute-start(bf16[1536,256]{1,0:T(8,128)(2,1)S(1)} %bitcast.14), channel_id=1, source_target_pairs={{0,8},{8,0},{16,24},{24,16},{32,40},{40,32},{48,56},{56,48},{64,72... | collective-permute-start | bytes 2359304 | tf_op jit(solution)/shard_map/cond/branch_1_fun/ppermute | solution.py:236
  72.6 3.8 %collective-permute-start.5 = (bf16[1024,256]{1,0:T(8,128)(2,1)S(1)}, bf16[1024,256]{1,0:T(8,128)(2,1)S(1)}, u32[]{:S(2)}, u32[]{:S(2)}) collective-permute-start(bf16[1024,256]{1,0:T(8,128)(2,1)S(1)} %bitcast.12), channel_id=1, source_target_pairs={{0,8},{8,0},{16,24},{24,16},{32,40},{40,32},{48,56},{56,48},{64,72... | collective-permute-start | bytes 1572872 | tf_op jit(solution)/shard_map/ppermute | solution.py:260

commit v22 on v21

--- a/solution.py
+++ b/solution.py
@@ -17,7 +17,6 @@
 TILE = 512
 SCALE2 = D ** (-0.5) * 1.4426950408889634
 LOW = -1e30
-SLOT = ROWS + NX * PAGE
 NEAR = 8
 
 
@@ -30,6 +29,13 @@
 
 def x_next():
     return [pair for pair in x_ring(1) if pair[0] < pair[1]]
+
+
+def y_ring(by):
+    return [
+        ((x * NY + y) * 2 + c, (x * NY + (y + by) % NY) * 2 + c)
+        for x in range(NX) for y in range(NY) for c in range(2)
+    ]
 
 
 SWAP = [(i, i ^ 1) for i in range(2 * NX * NY)]
@@ -83,7 +89,7 @@
     out_ref[:, :, GROUP * D:] = jnp.transpose(kv_ref[...], (1, 0, 2))
 
 
-def own_kernel(meta_ref, mine_ref, side_ref, ids_ref, q_ref, qt_ref, m_ref, l_ref, acc_ref):
+def own_kernel(meta_ref, table_ref, mine_ref, side_ref, ids_ref, q_ref, qt_ref, m_ref, l_ref, acc_ref, prefix_ref):
     own = meta_ref[0]
     row_start, first, last = starts_of(ids_ref, own)
     for g in range(GROUP):
@@ -96,14 +102,24 @@
     l_ref[...] = jnp.zeros_like(l_ref)
     acc_ref[...] = jnp.zeros_like(acc_ref)
     state = (qt_ref, m_ref, l_ref, acc_ref)
-    fold(mine_ref[:, :D], mine_ref[:, D:], mask_of(own, own, row_start), *state)
+    fold(mine_ref[:ROWS, :D], mine_ref[:ROWS, D:], mask_of(own, own, row_start), *state)
 
     @pl.when((own % 2 == 1) & (own * ROWS > first))
     def _():
-        fold(side_ref[:, :D], side_ref[:, D:], mask_of(own - 1, own, row_start), *state)
-
-
-def window(kv_ref, skip, slot, core, own, limits, qt_ref, m_ref, l_ref, acc_ref):
+        fold(side_ref[:ROWS, :D], side_ref[:ROWS, D:], mask_of(own - 1, own, row_start), *state)
+
+    core, y, x = own % 2, (own // 2) % NY, own // (2 * NY)
+    for i in range(PAGES):
+        page = table_ref[i]
+        off = (y + NY - (page // 2) % NY) % NY
+        unit = NY * ((x + NX - page // (2 * NY)) % NX) + off // 4 + 2 * (off // 2 % 2) + 4 * (off % 2)
+        rows = pl.ds(pl.multiple_of(ROWS + unit * PAGE, PAGE), PAGE)
+        prefix_ref[i * PAGE:(i + 1) * PAGE, :] = jnp.where(page % 2 == core, mine_ref[rows, :], side_ref[rows, :])
+
+    fold(prefix_ref[:, :D], prefix_ref[:, D:], None, *state)
+
+
+def window(kv_ref, skip, core, own, limits, qt_ref, m_ref, l_ref, acc_ref):
     row_start, first, last = limits
     chip = own // 2 - skip
     lowest = jnp.maximum((jnp.maximum(first // ROWS - core, -1) + 1) // 2, chip - NEAR)
@@ -113,7 +129,7 @@
         base = chip - BLOCKS * (i + 1)
         pairs = []
         for b in range(BLOCKS):
-            start = (base + b + 4 * NY) % NY * slot
+            start = (base + b + 4 * NY) % NY * ROWS
             pairs.append(kv_ref[pl.ds(pl.multiple_of(start, PAGE), ROWS), :])
         keys = jnp.concatenate([pair[:, :D] for pair in pairs], axis=0)
         values = jnp.concatenate([pair[:, D:] for pair in pairs], axis=0)
@@ -140,24 +156,15 @@
     l_ref[...] = l_in[...]
     acc_ref[...] = acc_in[...]
     own = meta_ref[0]
-    window(kv_ref, 0, SLOT, own % 2, own, starts_of(ids_ref, own), qt_ref, m_ref, l_ref, acc_ref)
-
-
-def near_side_kernel(meta_ref, table_ref, kv_ref, side_ref, ids_ref, qt_ref, m_in, l_in, acc_in,
-                     m_ref, l_ref, acc_ref, prefix_ref):
+    window(kv_ref, 0, own % 2, own, starts_of(ids_ref, own), qt_ref, m_ref, l_ref, acc_ref)
+
+
+def near_side_kernel(meta_ref, kv_ref, ids_ref, qt_ref, m_in, l_in, acc_in, m_ref, l_ref, acc_ref):
     m_ref[...] = m_in[...]
     l_ref[...] = l_in[...]
     acc_ref[...] = acc_in[...]
     own = meta_ref[0]
-    core, x = own % 2, own // (2 * NY)
-    for i in range(PAGES):
-        page = table_ref[i]
-        start = (page // 2) % NY * SLOT + ROWS + (x + NX - page // (2 * NY)) % NX * PAGE
-        rows = pl.ds(pl.multiple_of(start, PAGE), PAGE)
-        prefix_ref[i * PAGE:(i + 1) * PAGE, :] = jnp.where(page % 2 == core, kv_ref[rows, :], side_ref[rows, :])
-
-    fold(prefix_ref[:, :D], prefix_ref[:, D:], None, qt_ref, m_ref, l_ref, acc_ref)
-    window(side_ref, 0, SLOT, 1 - core, own, starts_of(ids_ref, own), qt_ref, m_ref, l_ref, acc_ref)
+    window(kv_ref, 0, 1 - own % 2, own, starts_of(ids_ref, own), qt_ref, m_ref, l_ref, acc_ref)
 
 
 def far_kernel(meta_ref, kv_ref, ids_ref, qt_ref, m_in, l_in, acc_in, m_ref, l_ref, acc_ref):
@@ -165,7 +172,7 @@
     l_ref[...] = l_in[...]
     acc_ref[...] = acc_in[...]
     own = meta_ref[0]
-    window(kv_ref, NEAR, ROWS, own % 2, own, starts_of(ids_ref, own), qt_ref, m_ref, l_ref, acc_ref)
+    window(kv_ref, NEAR, own % 2, own, starts_of(ids_ref, own), qt_ref, m_ref, l_ref, acc_ref)
 
 
 def last_kernel(meta_ref, kv_ref, ids_ref, qt_ref, m_in, l_in, acc_in, out_ref, m_ref, l_ref, acc_ref):
@@ -173,7 +180,7 @@
     l_ref[...] = l_in[...]
     acc_ref[...] = acc_in[...]
     own = meta_ref[0]
-    window(kv_ref, NEAR, ROWS, 1 - own % 2, own, starts_of(ids_ref, own), qt_ref, m_ref, l_ref, acc_ref)
+    window(kv_ref, NEAR, 1 - own % 2, own, starts_of(ids_ref, own), qt_ref, m_ref, l_ref, acc_ref)
     result = (acc_ref[...] * (1.0 / l_ref[...])).astype(jnp.bfloat16)
     for g in range(GROUP):
         out_ref[:, g * D:(g + 1) * D] = result[:, g * ROWS:(g + 1) * ROWS].T
@@ -190,7 +197,8 @@
 def per_device(queries, branch_key_value, branch_ids, pool, page_table):
     me = lax.axis_index("seq")
     y = (me // 2) % NY
-    page = pool.reshape(PAGE, PAIR)
+    pages = pool.reshape(PAGE, PAIR)
+    pages = jnp.concatenate([pages, lax.ppermute(pages, "seq", y_ring(4))], axis=0)
     wide = pl.pallas_call(
         by_head_kernel,
         out_shape=jax.ShapeDtypeStruct((8, ROWS // 8, GROUP * D + PAIR), jnp.bfloat16),
@@ -199,17 +207,19 @@
         name="by_head",
     )(queries, branch_key_value)
     wide = lax.all_to_all(wide, "head", split_axis=0, concat_axis=0, tiled=True).reshape(ROWS, -1)
-    two_page = lax.ppermute(page, "seq", x_ring(2))
-    wide, two_page = lax.optimization_barrier((wide, two_page))
+    pages = jnp.concatenate([pages, lax.ppermute(pages, "seq", y_ring(2))], axis=0)
+    wide, pages = lax.optimization_barrier((wide, pages))
     own = wide[:, GROUP * D:]
-    one_back = lax.ppermute(jnp.concatenate([own, page, two_page], axis=0), "seq", x_ring(1))
+    before = lax.ppermute(own, "seq", x_next())
+    last_pages = lax.ppermute(pages, "seq", y_ring(1))
+    own, before, pages, last_pages = lax.optimization_barrier((own, before, pages, last_pages))
     target = jnp.arange(NY, dtype=jnp.int32)[:, None, None]
-    block = jnp.where(target > y, own[None], one_back[None, :ROWS])
-    pages = jnp.concatenate([page, one_back[ROWS:ROWS + PAGE], two_page, one_back[ROWS + PAGE:]], axis=0)[None]
-    send = jnp.concatenate([block, jnp.broadcast_to(pages, (NY, NX * PAGE, PAIR))], axis=1)
+    send = jnp.where(target > y, own[None], before[None])
     near = lax.all_to_all(send, "seq", split_axis=0, concat_axis=0, tiled=True, axis_index_groups=Y_GROUPS)
-    later, _ = lax.optimization_barrier((own, send))
-    side = lax.ppermute(later, "seq", SWAP)
+    pages, own, _ = lax.optimization_barrier((jnp.concatenate([pages, last_pages], axis=0), own, send))
+    mine = jnp.concatenate([own, pages] + [lax.ppermute(pages, "seq", x_ring(k)) for k in (1, 2, 3)], axis=0)
+    side = lax.ppermute(mine, "seq", SWAP)
+
     ids = branch_ids.reshape(2 * NX * NY, ROWS)
     meta = me.astype(jnp.int32).reshape(1)
     state = [
@@ -221,18 +231,19 @@
     qt, *now = pl.pallas_call(
         own_kernel,
         out_shape=[jax.ShapeDtypeStruct((PAIR, QR), jnp.bfloat16)] + state,
-        in_specs=[SM] + [VM] * 4,
+        in_specs=[SM, SM] + [VM] * 4,
         out_specs=[VM] * 4,
+        scratch_shapes=[pltpu.VMEM((PAGES * PAGE, PAIR), jnp.bfloat16)],
         compiler_params=params,
-        cost_estimate=cost(256),
-        name="own_chip",
-    )(meta, own, side, ids, wide)
+        cost_estimate=cost(768),
+        name="own_chip_and_prefix",
+    )(meta, page_table.reshape(PAGES), mine, side, ids, wide)
     near, qt, now = lax.optimization_barrier((near, qt, now))
-    far = lax.ppermute(near[:, :ROWS], "seq", x_next())
+    far = lax.ppermute(near, "seq", x_next())
 
     def near_part(operands):
         near, qt, now = operands
-        near = near.reshape(NY * SLOT, PAIR)
+        near = near.reshape(NY * ROWS, PAIR)
         near_side = lax.ppermute(near, "seq", SWAP)
         now = pl.pallas_call(
             near_kernel,
@@ -246,13 +257,12 @@
         return list(pl.pallas_call(
             near_side_kernel,
             out_shape=state,
-            in_specs=[SM, SM] + [VM] * 7,
+            in_specs=[SM] + [VM] * 6,
             out_specs=[VM] * 3,
-            scratch_shapes=[pltpu.VMEM((PAGES * PAGE, PAIR), jnp.bfloat16)],
             compiler_params=params,
-            cost_estimate=cost(1536),
-            name="near_other_core_and_prefix",
-        )(meta, page_table.reshape(PAGES), near, near_side, ids, qt, *now))
+            cost_estimate=cost(1024),
+            name="near_other_core",
+        )(meta, near_side, ids, qt, *now))
 
     now = lax.cond(me < 2 * NX * NY, near_part, lambda operands: list(operands[2]), (near, qt, now))
     far, now = lax.optimization_barrier((far, now))

time: 95 us -> 110 us (1.16)
  the two profiles are of different devices: /device:TPU:6 before, /device:TPU:47 now
where the time goes in v22:
time: 110 us; the launch traced here: 109 us
  starting transfers between devices  48 us (44%)
  waiting for transfers between devices  24.3 us (22%)
  blocking collectives  19.1 us (17%)
  Pallas kernels  15.3 us (14%)
  local copies, waits for them, and re-layouts  1.55 us (1%)
    all_to_all x1, blocking collectives, per_device(): lax.all_to_all(out.reshape(8, ROWS // 8, GROUP * D), 'head', split_axis=0...  19.1 us
    all_to_all x1, starting transfers between devices, per_device(): lax.all_to_all(wide, 'head', split_axis=0, concat_axis=0, tiled=True)  10.2 us
    ppermute x3, starting transfers between devices, per_device(): lax.ppermute(pages, 'seq', x_ring(k))  8.92 us
    ppermute x1, starting transfers between devices, per_device(): side = lax.ppermute(mine, 'seq', SWAP)  8.18 us
    ppermute x1, waiting for transfers between devices, per_device(): far = lax.ppermute(near, 'seq', x_next())  7.49 us
    all_to_all x1, starting transfers between devices, per_device(): lax.all_to_all(send, 'seq', split_axis=0, concat_axis=0, tiled=True, axis...  6.92 us
    ppermute x1, waiting for transfers between devices, per_device(): lax.ppermute(pages, 'seq', y_ring(4))  5.66 us
    ppermute x1, waiting for transfers between devices, per_device(): lax.ppermute(pages, 'seq', y_ring(2))  4.14 us
  transfers between devices with their start and end apart: 13, of which 7 were waited for; matrix products, arithmetic and copies ran while one was open for 0% of the time, Pallas kernels for 10%

profile of v22, /device:TPU:47, one launch (start us, length us, event | category | flops | bytes accessed | tf_op | source)
XLA Modules:
  0.0 109.4 jit_solution(993131296337164807)
XLA Ops:
  0.0 1.7 %by_head.1 = bf16[8,16,1280]{2,1,0:T(8,128)(2,1)} custom-call(bf16[16,8,1024]{2,1,0:T(8,128)(2,1)} %q_ref.1, bf16[16,8,256]{2,1,0:T(8,128)(2,1)} %kv_ref.1), custom_call_target="tpu_custom_call" | custom-call | tf_op jit(solution)/shard_map/by_head/pallas_call | solution.py:202
  1.8 10.2 %all-to-all-start = ((bf16[8,16,1280]{2,1,0:T(8,128)(2,1)}), bf16[8,16,1280]{2,1,0:T(8,128)(2,1)S(1)}, u32[]{:S(2)}, u32[]{:S(2)}) async-start(bf16[8,16,1280]{2,1,0:T(8,128)(2,1)} %by_head.1), calls=%async_computation | async-start | bytes 655360 | tf_op jit(solution)/shard_map/all_to_all | solution.py:209
  11.9 2.6 %collective-permute-start.1 = (bf16[16,256]{1,0:T(8,128)(2,1)S(1)}, bf16[16,256]{1,0:T(8,128)(2,1)S(1)}, u32[]{:S(2)}, u32[]{:S(2)}) collective-permute-start(bf16[16,256]{1,0:T(8,128)(2,1)S(1)} %bitcast.16), channel_id=1, source_target_pairs={{0,64},{8,72},{16,80},{24,88},{32,96},{40,104},{48,112},{56,120},{... | collective-permute-start | bytes 24584 | tf_op jit(solution)/shard_map/ppermute | solution.py:201
  14.6 5.7 %collective-permute-done.1 = bf16[16,256]{1,0:T(8,128)(2,1)S(1)} collective-permute-done((bf16[16,256]{1,0:T(8,128)(2,1)S(1)}, bf16[16,256]{1,0:T(8,128)(2,1)S(1)}, u32[]{:S(2)}, u32[]{:S(2)}) %collective-permute-start.1) | collective-permute-done | bytes 8224 | tf_op jit(solution)/shard_map/ppermute | solution.py:201
  20.2 2.4 %collective-permute-start.2 = (bf16[32,256]{1,0:T(8,128)(2,1)S(1)}, bf16[32,256]{1,0:T(8,128)(2,1)S(1)}, u32[]{:S(2)}, u32[]{:S(2)}) collective-permute-start(bf16[32,256]{1,0:T(8,128)(2,1)S(1)} %pad_maximum_fusion.2), channel_id=1, source_target_pairs={{0,32},{8,40},{16,48},{24,56},{32,64},{40,72},{48,80},{56,88},{64,... | collective-permute-start | bytes 49160 | tf_op jit(solution)/shard_map/ppermute | solution.py:210
  22.7 4.1 %collective-permute-done.2 = bf16[32,256]{1,0:T(8,128)(2,1)S(1)} collective-permute-done((bf16[32,256]{1,0:T(8,128)(2,1)S(1)}, bf16[32,256]{1,0:T(8,128)(2,1)S(1)}, u32[]{:S(2)}, u32[]{:S(2)}) %collective-permute-start.2) | collective-permute-done | bytes 16416 | tf_op jit(solution)/shard_map/ppermute | solution.py:210
  26.8 1.9 %collective-permute-start.4 = (bf16[64,256]{1,0:T(8,128)(2,1)S(1)}, bf16[64,256]{1,0:T(8,128)(2,1)S(1)}, u32[]{:S(2)}, u32[]{:S(2)}) collective-permute-start(bf16[64,256]{1,0:T(8,128)(2,1)S(1)} %pad_maximum_fusion.1), channel_id=1, source_target_pairs={{0,16},{8,24},{16,32},{24,40},{32,48},{40,56},{48,64},{56,72},{64,... | collective-permute-start | bytes 98312 | tf_op jit(solution)/shard_map/ppermute | solution.py:214
  28.8 1.3 %collective-permute-start.3 = (bf16[128,256]{1,0:T(8,128)(2,1)S(1)}, bf16[128,256]{1,0:T(8,128)(2,1)S(1)}, u32[]{:S(2)}, u32[]{:S(2)}) collective-permute-start(bf16[128,256]{1,0:T(8,128)(2,1)S(1)} %slice.3), channel_id=1, source_target_pairs={{0,128},{8,136},{16,144},{24,152},{32,160},{40,168},{48,176},{56,1... | collective-permute-start | bytes 196616 | tf_op jit(solution)/shard_map/ppermute | solution.py:213
  30.1 1.4 %collective-permute-done.4 = bf16[64,256]{1,0:T(8,128)(2,1)S(1)} collective-permute-done((bf16[64,256]{1,0:T(8,128)(2,1)S(1)}, bf16[64,256]{1,0:T(8,128)(2,1)S(1)}, u32[]{:S(2)}, u32[]{:S(2)}) %collective-permute-start.4) | collective-permute-done | bytes 32800 | tf_op jit(solution)/shard_map/ppermute | solution.py:214
  31.5 2.3 %collective-permute-done.3 = bf16[128,256]{1,0:T(8,128)(2,1)S(1)} collective-permute-done((bf16[128,256]{1,0:T(8,128)(2,1)S(1)}, bf16[128,256]{1,0:T(8,128)(2,1)S(1)}, u32[]{:S(2)}, u32[]{:S(2)}) %collective-permute-start.3) | collective-permute-done | bytes 65568 | tf_op jit(solution)/shard_map/ppermute | solution.py:213
  33.8 0.9 broadcast_select_fusion
  34.7 6.9 %all-to-all-start.1 = ((bf16[8,128,256]{2,1,0:T(8,128)(2,1)}), bf16[8,128,256]{2,1,0:T(8,128)(2,1)}, u32[]{:S(2)}, u32[]{:S(2)}) async-start(bf16[8,128,256]{2,1,0:T(8,128)(2,1)} %broadcast_select_fusion), calls=%async_computation.1 | async-start | bytes 1048576 | tf_op jit(solution)/shard_map/all_to_all | solution.py:218
  41.6 2.5 %collective-permute-start.7 = (bf16[128,256]{1,0:T(8,128)(2,1)S(1)}, bf16[128,256]{1,0:T(8,128)(2,1)S(1)}, u32[]{:S(2)}, u32[]{:S(2)}) collective-permute-start(bf16[128,256]{1,0:T(8,128)(2,1)S(1)} %pad_maximum_fusion), channel_id=1, source_target_pairs={{0,384},{8,392},{16,400},{24,408},{32,416},{40,424},{48,432},{56,4... | collective-permute-start | bytes 196616 | tf_op jit(solution)/shard_map/ppermute | solution.py:220
  44.1 2.5 %collective-permute-start.6 = (bf16[128,256]{1,0:T(8,128)(2,1)S(1)}, bf16[128,256]{1,0:T(8,128)(2,1)S(1)}, u32[]{:S(2)}, u32[]{:S(2)}) collective-permute-start(bf16[128,256]{1,0:T(8,128)(2,1)S(1)} %pad_maximum_fusion), channel_id=1, source_target_pairs={{0,256},{8,264},{16,272},{24,280},{32,288},{40,296},{48,304},{56,3... | collective-permute-start | bytes 196616 | tf_op jit(solution)/shard_map/ppermute | solution.py:220
  46.6 4.0 %collective-permute-start.5 = (bf16[128,256]{1,0:T(8,128)(2,1)S(1)}, bf16[128,256]{1,0:T(8,128)(2,1)S(1)}, u32[]{:S(2)}, u32[]{:S(2)}) collective-permute-start(bf16[128,256]{1,0:T(8,128)(2,1)S(1)} %pad_maximum_fusion), channel_id=1, source_target_pairs={{0,128},{8,136},{16,144},{24,152},{32,160},{40,168},{48,176},{56,1... | collective-permute-start | bytes 196616 | tf_op jit(solution)/shard_map/ppermute | solution.py:220
  50.6 2.1 %collective-permute-done.5 = bf16[128,256]{1,0:T(8,128)(2,1)S(1)} collective-permute-done((bf16[128,256]{1,0:T(8,128)(2,1)S(1)}, bf16[128,256]{1,0:T(8,128)(2,1)S(1)}, u32[]{:S(2)}, u32[]{:S(2)}) %collective-permute-start.5) | collective-permute-done | bytes 65568 | tf_op jit(solution)/shard_map/ppermute | solution.py:220
  52.7 0.0 copy-start.2
  52.7 8.2 %collective-permute-start.8 = (bf16[640,256]{1,0:T(8,128)(2,1)S(1)}, bf16[640,256]{1,0:T(8,128)(2,1)S(1)}, u32[]{:S(2)}, u32[]{:S(2)}) collective-permute-start(bf16[640,256]{1,0:T(8,128)(2,1)S(1)} %constant_dynamic-update-slice_fusion.mine_ref), channel_id=1, source_target_pairs={{0,8},{8,0},{16,24},{24,16},{32,40},{40,32},{48,56},{56,48},{64,72... | collective-permute-start | bytes 983048 | tf_op jit(solution)/shard_map/ppermute | solution.py:221
  60.9 1.2 %collective-permute-done.8.side_ref = bf16[640,256]{1,0:T(8,128)(2,1)S(1)} collective-permute-done((bf16[640,256]{1,0:T(8,128)(2,1)S(1)}, bf16[640,256]{1,0:T(8,128)(2,1)S(1)}, u32[]{:S(2)}, u32[]{:S(2)}) %collective-permute-start.8) | collective-permute-done | bytes 327712 | tf_op jit(solution)/shard_map/ppermute | solution.py:221
  62.1 0.7 copy-done
  62.8 3.4 %own_chip_and_prefix.1 = (bf16[256,1024]{1,0:T(8,128)(2,1)S(1)}, f32[1,1024]{1,0:T(1,128)S(1)}, f32[1,1024]{1,0:T(1,128)S(1)}, f32[128,1024]{1,0:T(8,128)S(1)}) custom-call(s32[1]{0:T(128)} %bitcast.1.meta_ref, s32[32]{0:T(128)S(1)} %bitcast.14, bf16[640,256]{1,0:T(8,128)(2,1)S(1)} %constant_dynamic-update-slice_fusion.mine_ref, ...), custom_call_target="tpu_custom_call" | custom-call | flops 402653184 | bytes 1048576 | tf_op jit(solution)/shard_map/own_chip_and_prefix/pallas_call | solution.py:231
  66.2 1.3 %collective-permute-start.9 = (bf16[8,128,256]{2,1,0:T(8,128)(2,1)}, bf16[8,128,256]{2,1,0:T(8,128)(2,1)S(1)}, u32[]{:S(2)}, u32[]{:S(2)}) collective-permute-start(bf16[8,128,256]{2,1,0:T(8,128)(2,1)} %all-to-all-done.1), channel_id=1, source_target_pairs={{0,128},{8,136},{16,144},{24,152},{32,160},{40,168},{48,176},{56,1... | collective-permute-start | bytes 1572872 | tf_op jit(solution)/shard_map/ppermute | solution.py:242
  67.5 7.5 %conditional.1 = ((f32[1,1024]{1,0:T(1,128)S(1)}, f32[1,1024]{1,0:T(1,128)S(1)}, f32[128,1024]{1,0:T(8,128)S(1)})) conditional(s32[]{:T(128)} %convert_element_type.3, (f32[1,1024]{1,0:T(1,128)S(1)}, f32[1,1024]{1,0:T(1,128)S(1)}, f32[128,1024]{1,0:T(8,128)S(1)}) %tuple.20, (bf16[8,128,256]{2,1,0:T(8,128)(2,1)}, s32[1]{0:T(128)}, ...), branch_computations={%region_0.1_spmd, %region_1.2_spmd} | conditional | flops 1073741824 | bytes 4194352 | solution.py:267
  67.5 1.9 %collective-permute-start = (bf16[1024,256]{1,0:T(8,128)(2,1)}, bf16[1024,256]{1,0:T(8,128)(2,1)S(1)}, u32[]{:S(2)}, u32[]{:S(2)}) collective-permute-start(bf16[1024,256]{1,0:T(8,128)(2,1)} %bitcast.kv_ref), channel_id=1, source_target_pairs={{0,8},{8,0},{16,24},{24,16},{32,40},{40,32},{48,56},{56,48},{64,72... | collective-permute-start | bytes 1572872 | tf_op jit(solution)/shard_map/cond/branch_1_fun/ppermute | solution.py:247
  69.4 3.3 %near_window.1 = (f32[1,1024]{1,0:T(1,128)S(1)}, f32[1,1024]{1,0:T(1,128)S(1)}, f32[128,1024]{1,0:T(8,128)S(1)}) custom-call(s32[1]{0:T(128)} %get-tuple-element.25.meta_ref, bf16[1024,256]{1,0:T(8,128)(2,1)} %bitcast.kv_ref, s32[64,128]{1,0:T(8,128)S(1)} %get-tuple-element.27.ids_ref, bf16[256,1024]{1,0:T(8,128)(2,1)S(1)} %get-tuple-element.28.qt_ref, ...), custom_call_target="tpu_custom_call" | custom-call | flops 536870912 | bytes 1048576 | tf_op jit(solution)/shard_map/cond/branch_1_fun/near_window/pallas_call | solution.py:248
  72.7 2.2 %near_other_core.1 = (f32[1,1024]{1,0:T(1,128)S(1)}, f32[1,1024]{1,0:T(1,128)S(1)}, f32[128,1024]{1,0:T(8,128)S(1)}) custom-call(s32[1]{0:T(128)} %get-tuple-element.25.meta_ref, bf16[1024,256]{1,0:T(8,128)(2,1)S(1)} %collective-permute-done.kv_ref, s32[64,128]{1,0:T(8,128)S(1)} %get-tuple-element.27.ids_ref, ...), custom_call_target="tpu_custom_call" | custom-call | flops 536870912 | bytes 1048576 | tf_op jit(solution)/shard_map/cond/branch_1_fun/near_other_core/pallas_call | solution.py:257
  74.9 7.5 %collective-permute-done.9 = bf16[8,128,256]{2,1,0:T(8,128)(2,1)S(1)} collective-permute-done((bf16[8,128,256]{2,1,0:T(8,128)(2,1)}, bf16[8,128,256]{2,1,0:T(8,128)(2,1)S(1)}, u32[]{:S(2)}, u32[]{:S(2)}) %collective-permute-start.9) | collective-permute-done | bytes 524320 | tf_op jit(solution)/shard_map/ppermute | solution.py:242
  82.4 2.4 %collective-permute-start.10 = (bf16[1024,256]{1,0:T(8,128)(2,1)S(1)}, bf16[1024,256]{1,0:T(8,128)(2,1)S(1)}, u32[]{:S(2)}, u32[]{:S(2)}) collective-permute-start(bf16[1024,256]{1,0:T(8,128)(2,1)S(1)} %bitcast.12), channel_id=1, source_target_pairs={{0,8},{8,0},{16,24},{24,16},{32,40},{40,32},{48,56},{56,48},{64,72... | collective-permute-start | bytes 1572872 | tf_op jit(solution)/shard_map/ppermute | solution.py:270
  84.8 2.3 %far_window.1 = (f32[1,1024]{1,0:T(1,128)S(1)}, f32[1,1024]{1,0:T(1,128)S(1)}, f32[128,1024]{1,0:T(8,128)S(1)}) custom-call(s32[1]{0:T(128)} %bitcast.1.meta_ref, bf16[1024,256]{1,0:T(8,128)(2,1)S(1)} %bitcast.13, s32[64,128]{1,0:T(8,128)S(1)} %bitcast.21, bf16[256,1024]{1,0:T(8,128)(2,1)S(1)} %get-tuple-element.78.qt_ref, ...), custom_call_target="tpu_custom_call" | custom-call | flops 536870912 | bytes 1048576 | tf_op jit(solution)/shard_map/far_window/pallas_call | solution.py:271
  87.1 2.4 %far_other_core.1 = bf16[128,1024]{1,0:T(8,128)(2,1)S(1)} custom-call(s32[1]{0:T(128)} %bitcast.1.meta_ref, bf16[1024,256]{1,0:T(8,128)(2,1)S(1)} %collective-permute-done.10.kv_ref, s32[64,128]{1,0:T(8,128)S(1)} %bitcast.22, bf16[256,1024]{1,0:T(8,128)(2,1)S(1)} %get-tuple-element.78.qt_ref, f32[1,1024]{1,0:T(1,128)S(1)} %get-tuple-element.86.m_in, ...), custom_call_target="tpu_custom_call" | custom-call | flops 536870912 | bytes 1048576 | tf_op jit(solution)/shard_map/far_other_core/pallas_call | solution.py:280
  89.5 19.1 %all_to_all.15 = bf16[8,16,1024]{2,1,0:T(8,128)(2,1)S(1)} all-to-all(bf16[8,16,1024]{2,1,0:T(8,128)(2,1)S(1)} %bitcast.11), channel_id=1, replica_groups=mesh['seq'=64,'head'=8] {'head'}, dimensions={0} | all-to-all | bytes 524288 | tf_op jit(solution)/shard_map/all_to_all | solution.py:294
  108.6 0.9 copy.7
  (20 shorter events, 0.1 us)
Async XLA Ops:
  1.8 10.2 %copy-start.1 = (bf16[1,16,1,256]{3,1,2,0:T(8,128)(2,1)S(1)}, bf16[1,16,1,256]{3,1,2,0:T(8,128)(2,1)}, u32[]{:S(2)}) copy-start(bf16[1,16,1,256]{3,1,2,0:T(8,128)(2,1)} %param.10) | copy-start | bytes 24580
  1.8 25.1 %all-to-all-start = ((bf16[8,16,1280]{2,1,0:T(8,128)(2,1)}), bf16[8,16,1280]{2,1,0:T(8,128)(2,1)S(1)}, u32[]{:S(2)}, u32[]{:S(2)}) async-start(bf16[8,16,1280]{2,1,0:T(8,128)(2,1)} %by_head.1), calls=%async_computation | async-start | bytes 655360 | tf_op jit(solution)/shard_map/all_to_all | solution.py:209
  11.9 8.3 %collective-permute-start.1 = (bf16[16,256]{1,0:T(8,128)(2,1)S(1)}, bf16[16,256]{1,0:T(8,128)(2,1)S(1)}, u32[]{:S(2)}, u32[]{:S(2)}) collective-permute-start(bf16[16,256]{1,0:T(8,128)(2,1)S(1)} %bitcast.16), channel_id=1, source_target_pairs={{0,64},{8,72},{16,80},{24,88},{32,96},{40,104},{48,112},{56,120},{... | collective-permute-start | bytes 24584 | tf_op jit(solution)/shard_map/ppermute | solution.py:201
  20.2 6.6 %collective-permute-start.2 = (bf16[32,256]{1,0:T(8,128)(2,1)S(1)}, bf16[32,256]{1,0:T(8,128)(2,1)S(1)}, u32[]{:S(2)}, u32[]{:S(2)}) collective-permute-start(bf16[32,256]{1,0:T(8,128)(2,1)S(1)} %pad_maximum_fusion.2), channel_id=1, source_target_pairs={{0,32},{8,40},{16,48},{24,56},{32,64},{40,72},{48,80},{56,88},{64,... | collective-permute-start | bytes 49160 | tf_op jit(solution)/shard_map/ppermute | solution.py:210
  26.8 4.6 %collective-permute-start.4 = (bf16[64,256]{1,0:T(8,128)(2,1)S(1)}, bf16[64,256]{1,0:T(8,128)(2,1)S(1)}, u32[]{:S(2)}, u32[]{:S(2)}) collective-permute-start(bf16[64,256]{1,0:T(8,128)(2,1)S(1)} %pad_maximum_fusion.1), channel_id=1, source_target_pairs={{0,16},{8,24},{16,32},{24,40},{32,48},{40,56},{48,64},{56,72},{64,... | collective-permute-start | bytes 98312 | tf_op jit(solution)/shard_map/ppermute | solution.py:214
  28.8 5.0 %collective-permute-start.3 = (bf16[128,256]{1,0:T(8,128)(2,1)S(1)}, bf16[128,256]{1,0:T(8,128)(2,1)S(1)}, u32[]{:S(2)}, u32[]{:S(2)}) collective-permute-start(bf16[128,256]{1,0:T(8,128)(2,1)S(1)} %slice.3), channel_id=1, source_target_pairs={{0,128},{8,136},{16,144},{24,152},{32,160},{40,168},{48,176},{56,1... | collective-permute-start | bytes 196616 | tf_op jit(solution)/shard_map/ppermute | solution.py:213
  34.7 31.5 %all-to-all-start.1 = ((bf16[8,128,256]{2,1,0:T(8,128)(2,1)}), bf16[8,128,256]{2,1,0:T(8,128)(2,1)}, u32[]{:S(2)}, u32[]{:S(2)}) async-start(bf16[8,128,256]{2,1,0:T(8,128)(2,1)} %broadcast_select_fusion), calls=%async_computation.1 | async-start | bytes 1048576 | tf_op jit(solution)/shard_map/all_to_all | solution.py:218
  41.6 11.1 %collective-permute-start.7 = (bf16[128,256]{1,0:T(8,128)(2,1)S(1)}, bf16[128,256]{1,0:T(8,128)(2,1)S(1)}, u32[]{:S(2)}, u32[]{:S(2)}) collective-permute-start(bf16[128,256]{1,0:T(8,128)(2,1)S(1)} %pad_maximum_fusion), channel_id=1, source_target_pairs={{0,384},{8,392},{16,400},{24,408},{32,416},{40,424},{48,432},{56,4... | collective-permute-start | bytes 196616 | tf_op jit(solution)/shard_map/ppermute | solution.py:220
  44.1 8.6 %collective-permute-start.6 = (bf16[128,256]{1,0:T(8,128)(2,1)S(1)}, bf16[128,256]{1,0:T(8,128)(2,1)S(1)}, u32[]{:S(2)}, u32[]{:S(2)}) collective-permute-start(bf16[128,256]{1,0:T(8,128)(2,1)S(1)} %pad_maximum_fusion), channel_id=1, source_target_pairs={{0,256},{8,264},{16,272},{24,280},{32,288},{40,296},{48,304},{56,3... | collective-permute-start | bytes 196616 | tf_op jit(solution)/shard_map/ppermute | solution.py:220
  46.6 6.1 %collective-permute-start.5 = (bf16[128,256]{1,0:T(8,128)(2,1)S(1)}, bf16[128,256]{1,0:T(8,128)(2,1)S(1)}, u32[]{:S(2)}, u32[]{:S(2)}) collective-permute-start(bf16[128,256]{1,0:T(8,128)(2,1)S(1)} %pad_maximum_fusion), channel_id=1, source_target_pairs={{0,128},{8,136},{16,144},{24,152},{32,160},{40,168},{48,176},{56,1... | collective-permute-start | bytes 196616 | tf_op jit(solution)/shard_map/ppermute | solution.py:220
  52.7 9.5 %copy-start.2 = (s32[8192]{0:T(1024)S(1)}, s32[8192]{0:T(1024)}, u32[]{:S(2)}) copy-start(s32[8192]{0:T(1024)} %param.9) | copy-start | bytes 98308
  52.7 9.4 %collective-permute-start.8 = (bf16[640,256]{1,0:T(8,128)(2,1)S(1)}, bf16[640,256]{1,0:T(8,128)(2,1)S(1)}, u32[]{:S(2)}, u32[]{:S(2)}) collective-permute-start(bf16[640,256]{1,0:T(8,128)(2,1)S(1)} %constant_dynamic-update-slice_fusion.mine_ref), channel_id=1, source_target_pairs={{0,8},{8,0},{16,24},{24,16},{32,40},{40,32},{48,56},{56,48},{64,72... | collective-permute-start | bytes 983048 | tf_op jit(solution)/shard_map/ppermute | solution.py:221
  62.1 0.7 copy-start
  66.2 16.3 %collective-permute-start.9 = (bf16[8,128,256]{2,1,0:T(8,128)(2,1)}, bf16[8,128,256]{2,1,0:T(8,128)(2,1)S(1)}, u32[]{:S(2)}, u32[]{:S(2)}) collective-permute-start(bf16[8,128,256]{2,1,0:T(8,128)(2,1)} %all-to-all-done.1), channel_id=1, source_target_pairs={{0,128},{8,136},{16,144},{24,152},{32,160},{40,168},{48,176},{56,1... | collective-permute-start | bytes 1572872 | tf_op jit(solution)/shard_map/ppermute | solution.py:242
  67.5 5.2 %collective-permute-start = (bf16[1024,256]{1,0:T(8,128)(2,1)}, bf16[1024,256]{1,0:T(8,128)(2,1)S(1)}, u32[]{:S(2)}, u32[]{:S(2)}) collective-permute-start(bf16[1024,256]{1,0:T(8,128)(2,1)} %bitcast.kv_ref), channel_id=1, source_target_pairs={{0,8},{8,0},{16,24},{24,16},{32,40},{40,32},{48,56},{56,48},{64,72... | collective-permute-start | bytes 1572872 | tf_op jit(solution)/shard_map/cond/branch_1_fun/ppermute | solution.py:247
  82.4 4.7 %collective-permute-start.10 = (bf16[1024,256]{1,0:T(8,128)(2,1)S(1)}, bf16[1024,256]{1,0:T(8,128)(2,1)S(1)}, u32[]{:S(2)}, u32[]{:S(2)}) collective-permute-start(bf16[1024,256]{1,0:T(8,128)(2,1)S(1)} %bitcast.12), channel_id=1, source_target_pairs={{0,8},{8,0},{16,24},{24,16},{32,40},{40,32},{48,56},{56,48},{64,72... | collective-permute-start | bytes 1572872 | tf_op jit(solution)/shard_map/ppermute | solution.py:270

commit v23 on v17

--- a/solution.py
+++ b/solution.py
@@ -17,7 +17,7 @@
 TILE = 512
 SCALE2 = D ** (-0.5) * 1.4426950408889634
 LOW = -1e30
-SLOT = ROWS + PAGE
+SLOT = ROWS + 2 * PAGE
 NEAR = 8
 
 
@@ -78,6 +78,11 @@
     return (key_rows >= row_start) & (key_rows <= query_rows)
 
 
+def by_head_kernel(q_ref, kv_ref, out_ref):
+    out_ref[:, :, :GROUP * D] = jnp.transpose(q_ref[...], (1, 0, 2))
+    out_ref[:, :, GROUP * D:] = jnp.transpose(kv_ref[...], (1, 0, 2))
+
+
 def own_kernel(meta_ref, mine_ref, side_ref, ids_ref, q_ref, qt_ref, m_ref, l_ref, acc_ref):
     own = meta_ref[0]
     row_start, first, last = starts_of(ids_ref, own)
@@ -98,7 +103,7 @@
         fold(side_ref[:, :D], side_ref[:, D:], mask_of(own - 1, own, row_start), *state)
 
 
-def window(kv_ref, skip, slot, core, own, limits, qt_ref, m_ref, l_ref, acc_ref):
+def window(kv_ref, skip, core, own, limits, qt_ref, m_ref, l_ref, acc_ref):
     row_start, first, last = limits
     chip = own // 2 - skip
     lowest = jnp.maximum((jnp.maximum(first // ROWS - core, -1) + 1) // 2, chip - NEAR)
@@ -108,7 +113,7 @@
         base = chip - BLOCKS * (i + 1)
         pairs = []
         for b in range(BLOCKS):
-            start = (base + b + 4 * NY) % NY * slot
+            start = (base + b + 4 * NY) % NY * SLOT
             pairs.append(kv_ref[pl.ds(pl.multiple_of(start, PAGE), ROWS), :])
         keys = jnp.concatenate([pair[:, :D] for pair in pairs], axis=0)
         values = jnp.concatenate([pair[:, D:] for pair in pairs], axis=0)
@@ -135,7 +140,7 @@
     l_ref[...] = l_in[...]
     acc_ref[...] = acc_in[...]
     own = meta_ref[0]
-    window(kv_ref, 0, SLOT, own % 2, own, starts_of(ids_ref, own), qt_ref, m_ref, l_ref, acc_ref)
+    window(kv_ref, 0, own % 2, own, starts_of(ids_ref, own), qt_ref, m_ref, l_ref, acc_ref)
 
 
 def near_side_kernel(meta_ref, kv_ref, ids_ref, qt_ref, m_in, l_in, acc_in, m_ref, l_ref, acc_ref):
@@ -143,7 +148,7 @@
     l_ref[...] = l_in[...]
     acc_ref[...] = acc_in[...]
     own = meta_ref[0]
-    window(kv_ref, 0, SLOT, 1 - own % 2, own, starts_of(ids_ref, own), qt_ref, m_ref, l_ref, acc_ref)
+    window(kv_ref, 0, 1 - own % 2, own, starts_of(ids_ref, own), qt_ref, m_ref, l_ref, acc_ref)
 
 
 def far_kernel(meta_ref, kv_ref, ids_ref, qt_ref, m_in, l_in, acc_in, m_ref, l_ref, acc_ref):
@@ -151,11 +156,11 @@
     l_ref[...] = l_in[...]
     acc_ref[...] = acc_in[...]
     own = meta_ref[0]
-    window(kv_ref, NEAR, SLOT, own % 2, own, starts_of(ids_ref, own), qt_ref, m_ref, l_ref, acc_ref)
-
-
-def last_kernel(meta_ref, table_ref, near_ref, near_side_ref, far_ref, far_side_ref, two_ref, three_ref, ids_ref,
-                qt_ref, m_in, l_in, acc_in, out_ref, m_ref, l_ref, acc_ref, prefix_ref):
+    window(kv_ref, NEAR, own % 2, own, starts_of(ids_ref, own), qt_ref, m_ref, l_ref, acc_ref)
+
+
+def last_kernel(meta_ref, table_ref, near_ref, near_side_ref, far_ref, kv_ref, ids_ref, qt_ref, m_in, l_in, acc_in,
+                out_ref, m_ref, l_ref, acc_ref, prefix_ref):
     m_ref[...] = m_in[...]
     l_ref[...] = l_in[...]
     acc_ref[...] = acc_in[...]
@@ -163,23 +168,17 @@
     core, x = own % 2, own // (2 * NY)
     for i in range(PAGES):
         page = table_ref[i]
-        yy = (page // 2) % NY
         back = (x + NX - page // (2 * NY)) % NX
-        mine = page % 2 == core
-        in_slot = pl.ds(pl.multiple_of(yy * SLOT + ROWS, PAGE), PAGE)
-        in_page = pl.ds(pl.multiple_of((jnp.where(mine, 0, NY) + yy) * PAGE, PAGE), PAGE)
+        start = (page // 2) % NY * SLOT + ROWS + back // 2 * PAGE
+        rows = pl.ds(pl.multiple_of(start, PAGE), PAGE)
         prefix_ref[i * PAGE:(i + 1) * PAGE, :] = jnp.where(
-            back < 2,
-            jnp.where(
-                back == 0,
-                jnp.where(mine, near_ref[in_slot, :], near_side_ref[in_slot, :]),
-                jnp.where(mine, far_ref[in_slot, :], far_side_ref[in_slot, :]),
-            ),
-            jnp.where(back == 2, two_ref[in_page, :], three_ref[in_page, :]),
+            page % 2 == core,
+            jnp.where(back % 2 == 0, near_ref[rows, :], far_ref[rows, :]),
+            jnp.where(back % 2 == 0, near_side_ref[rows, :], kv_ref[rows, :]),
         )
 
     fold(prefix_ref[:, :D], prefix_ref[:, D:], None, qt_ref, m_ref, l_ref, acc_ref)
-    window(far_side_ref, NEAR, SLOT, 1 - core, own, starts_of(ids_ref, own), qt_ref, m_ref, l_ref, acc_ref)
+    window(kv_ref, NEAR, 1 - core, own, starts_of(ids_ref, own), qt_ref, m_ref, l_ref, acc_ref)
     result = (acc_ref[...] * (1.0 / l_ref[...])).astype(jnp.bfloat16)
     for g in range(GROUP):
         out_ref[:, g * D:(g + 1) * D] = result[:, g * ROWS:(g + 1) * ROWS].T
@@ -197,17 +196,25 @@
     me = lax.axis_index("seq")
     y = (me // 2) % NY
     page = pool.reshape(PAGE, PAIR)
-    wide = jnp.transpose(jnp.concatenate([queries, branch_key_value], axis=2), (1, 0, 2))
+    wide = pl.pallas_call(
+        by_head_kernel,
+        out_shape=jax.ShapeDtypeStruct((8, ROWS // 8, GROUP * D + PAIR), jnp.bfloat16),
+        in_specs=[VM] * 2,
+        out_specs=VM,
+        name="by_head",
+    )(queries, branch_key_value)
     wide = lax.all_to_all(wide, "head", split_axis=0, concat_axis=0, tiled=True).reshape(ROWS, -1)
+    two_page = lax.ppermute(page, "seq", x_ring(2))
+    wide, two_page = lax.optimization_barrier((wide, two_page))
     own = wide[:, GROUP * D:]
     before = lax.ppermute(own, "seq", x_next())
     target = jnp.arange(NY, dtype=jnp.int32)[:, None, None]
     block = jnp.where(target > y, own[None], before[None])
-    send = jnp.concatenate([block, jnp.broadcast_to(page[None], (NY, PAGE, PAIR))], axis=1)
+    pages = jnp.concatenate([page, two_page], axis=0)[None]
+    send = jnp.concatenate([block, jnp.broadcast_to(pages, (NY, 2 * PAGE, PAIR))], axis=1)
     near = lax.all_to_all(send, "seq", split_axis=0, concat_axis=0, tiled=True, axis_index_groups=Y_GROUPS)
     later, _ = lax.optimization_barrier((own, send))
     side = lax.ppermute(later, "seq", SWAP)
-
     ids = branch_ids.reshape(2 * NX * NY, ROWS)
     meta = me.astype(jnp.int32).reshape(1)
     state = [
@@ -247,10 +254,6 @@
     near_side, now = lax.cond(
         me < 2 * NX * NY, near_part, lambda operands: (operands[0], list(operands[2])), (near, qt, now)
     )
-    pages = jnp.concatenate([a.reshape(NY, SLOT, PAIR)[:, ROWS:] for a in (near, near_side)], axis=0)
-    pages = pages.reshape(2 * NY * PAGE, PAIR)
-    two_pages = lax.ppermute(pages, "seq", x_ring(2))
-    three_pages = lax.ppermute(pages, "seq", x_ring(3))
     far, now = lax.optimization_barrier((far, now))
     far_side = lax.ppermute(far, "seq", SWAP)
     now = pl.pallas_call(
@@ -265,7 +268,7 @@
     out = pl.pallas_call(
         last_kernel,
         out_shape=jax.ShapeDtypeStruct((ROWS, GROUP * D), jnp.bfloat16),
-        in_specs=[SM, SM] + [VM] * 11,
+        in_specs=[SM, SM] + [VM] * 9,
         out_specs=VM,
         scratch_shapes=[
             pltpu.VMEM((1, QR), jnp.float32),
@@ -276,7 +279,7 @@
         compiler_params=params,
         cost_estimate=cost(1536),
         name="far_other_core_and_prefix",
-    )(meta, page_table.reshape(PAGES), near, near_side, far, far_side, two_pages, three_pages, ids, qt, *now)
+    )(meta, page_table.reshape(PAGES), near, near_side, far, far_side, ids, qt, *now)
     out = lax.all_to_all(out.reshape(8, ROWS // 8, GROUP * D), "head", split_axis=0, concat_axis=0, tiled=True)
     return jnp.transpose(out, (1, 0, 2))
 

time: 105 us -> 97.6 us (0.930)
  the two profiles are of different devices: /device:TPU:6 before, /device:TPU:1 now
where the time goes in v23:
time: 97.6 us; the launch traced here: 97 us
  starting transfers between devices  46.3 us (47%)
  waiting for transfers between devices  26.7 us (27%)
  blocking collectives  14.1 us (14%)
  Pallas kernels  7.81 us (8%)
  other arithmetic  1.01 us (1%)
    all_to_all x1, blocking collectives, per_device(): lax.all_to_all(out.reshape(8, ROWS // 8, GROUP * D), 'head', split_axis=0...  14.1 us
    all_to_all x1, starting transfers between devices, per_device(): lax.all_to_all(wide, 'head', split_axis=0, concat_axis=0, tiled=True)  10.9 us
    all_to_all x1, waiting for transfers between devices, per_device(): lax.all_to_all(send, 'seq', split_axis=0, concat_axis=0, tiled=True, axis...  10.4 us
    all_to_all x1, starting transfers between devices, per_device(): lax.all_to_all(send, 'seq', split_axis=0, concat_axis=0, tiled=True, axis...  6.95 us
    ppermute x1, starting transfers between devices, per_device(): far_side = lax.ppermute(far, 'seq', SWAP)  6.02 us
    all_to_all x1, waiting for transfers between devices, per_device(): lax.all_to_all(wide, 'head', split_axis=0, concat_axis=0, tiled=True)  6.01 us
    ppermute x1, starting transfers between devices, near_part(): near_side = lax.ppermute(near, 'seq', SWAP)  5.53 us
    ppermute x1, starting transfers between devices, per_device(): side = lax.ppermute(later, 'seq', SWAP)  5.35 us
  transfers between devices with their start and end apart: 8, of which 8 were waited for; matrix products, arithmetic and copies ran while one was open for 0% of the time, Pallas kernels for 3%

profile of v23, /device:TPU:1, one launch (start us, length us, event | category | flops | bytes accessed | tf_op | source)
XLA Modules:
  0.0 97.0 jit_solution(9135216460801582439)
XLA Ops:
  0.0 0.0 copy-start.2
  0.0 1.8 %by_head.1 = bf16[8,16,1280]{2,1,0:T(8,128)(2,1)} custom-call(bf16[16,8,1024]{2,1,0:T(8,128)(2,1)} %q_ref.1, bf16[16,8,256]{2,1,0:T(8,128)(2,1)} %kv_ref.1), custom_call_target="tpu_custom_call" | custom-call | tf_op jit(solution)/shard_map/by_head/pallas_call | solution.py:199
  1.8 10.9 %all-to-all-start = ((bf16[8,16,1280]{2,1,0:T(8,128)(2,1)}), bf16[8,16,1280]{2,1,0:T(8,128)(2,1)S(1)}, u32[]{:S(2)}, u32[]{:S(2)}) async-start(bf16[8,16,1280]{2,1,0:T(8,128)(2,1)} %by_head.1), calls=%async_computation | async-start | bytes 655360 | tf_op jit(solution)/shard_map/all_to_all | solution.py:206
  12.6 0.0 copy-done.2
  12.6 4.7 %collective-permute-start.1 = (bf16[16,256]{1,0:T(8,128)(2,1)S(1)}, bf16[16,256]{1,0:T(8,128)(2,1)S(1)}, u32[]{:S(2)}, u32[]{:S(2)}) collective-permute-start(bf16[16,256]{1,0:T(8,128)(2,1)S(1)} %bitcast.21), channel_id=1, source_target_pairs={{0,256},{8,264},{16,272},{24,280},{32,288},{40,296},{48,304},{56,3... | collective-permute-start | bytes 24584 | tf_op jit(solution)/shard_map/ppermute | solution.py:207
  17.3 1.2 %collective-permute-done.1 = bf16[16,256]{1,0:T(8,128)(2,1)S(1)} collective-permute-done((bf16[16,256]{1,0:T(8,128)(2,1)S(1)}, bf16[16,256]{1,0:T(8,128)(2,1)S(1)}, u32[]{:S(2)}, u32[]{:S(2)}) %collective-permute-start.1) | collective-permute-done | bytes 8224 | tf_op jit(solution)/shard_map/ppermute | solution.py:207
  18.5 6.0 %all-to-all-done = bf16[8,16,1280]{2,1,0:T(8,128)(2,1)S(1)} async-done(((bf16[8,16,1280]{2,1,0:T(8,128)(2,1)}), bf16[8,16,1280]{2,1,0:T(8,128)(2,1)S(1)}, u32[]{:S(2)}, u32[]{:S(2)}) %all-to-all-start) | async-done | bytes 327712 | tf_op jit(solution)/shard_map/all_to_all | solution.py:206
  24.6 3.1 %collective-permute-start.2 = (bf16[128,256]{1,0:T(8,128)(2,1)S(1)}, bf16[128,256]{1,0:T(8,128)(2,1)S(1)}, u32[]{:S(2)}, u32[]{:S(2)}) collective-permute-start(bf16[128,256]{1,0:T(8,128)(2,1)S(1)} %slice.3.mine_ref), channel_id=1, source_target_pairs={{0,128},{8,136},{16,144},{24,152},{32,160},{40,168},{48,176},{56,1... | collective-permute-start | bytes 196616 | tf_op jit(solution)/shard_map/ppermute | solution.py:210
  27.7 1.3 %collective-permute-done.2 = bf16[128,256]{1,0:T(8,128)(2,1)S(1)} collective-permute-done((bf16[128,256]{1,0:T(8,128)(2,1)S(1)}, bf16[128,256]{1,0:T(8,128)(2,1)S(1)}, u32[]{:S(2)}, u32[]{:S(2)}) %collective-permute-start.2) | collective-permute-done | bytes 65568 | tf_op jit(solution)/shard_map/ppermute | solution.py:210
  29.0 0.1 broadcast_select_fusion
  29.1 0.9 pad_maximum_fusion
  30.0 0.0 copy-start.1
  30.0 7.0 %all-to-all-start.1 = ((bf16[8,160,256]{2,1,0:T(8,128)(2,1)}), bf16[8,160,256]{2,1,0:T(8,128)(2,1)S(1)}, u32[]{:S(2)}, u32[]{:S(2)}) async-start(bf16[8,160,256]{2,1,0:T(8,128)(2,1)} %pad_maximum_fusion), calls=%async_computation.1 | async-start | bytes 1310720 | tf_op jit(solution)/shard_map/all_to_all | solution.py:215
  37.0 5.3 %collective-permute-start.3 = (bf16[128,256]{1,0:T(8,128)(2,1)S(1)}, bf16[128,256]{1,0:T(8,128)(2,1)S(1)}, u32[]{:S(2)}, u32[]{:S(2)}) collective-permute-start(bf16[128,256]{1,0:T(8,128)(2,1)S(1)} %slice.3.mine_ref), channel_id=1, source_target_pairs={{0,8},{8,0},{16,24},{24,16},{32,40},{40,32},{48,56},{56,48},{64,72... | collective-permute-start | bytes 196616 | tf_op jit(solution)/shard_map/ppermute | solution.py:217
  42.3 0.9 collective-permute-done.3.side_ref
  43.2 0.0 copy-done.1
  43.2 1.1 %own_chip.1 = (bf16[256,1024]{1,0:T(8,128)(2,1)S(1)}, f32[1,1024]{1,0:T(1,128)S(1)}, f32[1,1024]{1,0:T(1,128)S(1)}, f32[128,1024]{1,0:T(8,128)S(1)}) custom-call(s32[1]{0:T(128)} %bitcast.meta_ref, bf16[128,256]{1,0:T(8,128)(2,1)S(1)} %slice.3.mine_ref, bf16[128,256]{1,0:T(8,128)(2,1)S(1)} %collective-permute-done.3.side_ref, s32[64,128]{1,0:T(8,128)S(1)} %bitcast.17, ...), custom_call_target="tpu_custom_call" | custom-call | flops 134217728 | bytes 1048576 | tf_op jit(solution)/shard_map/own_chip/pallas_call | solution.py:226
  44.4 10.4 %all-to-all-done.1 = bf16[8,160,256]{2,1,0:T(8,128)(2,1)S(1)} async-done(((bf16[8,160,256]{2,1,0:T(8,128)(2,1)}), bf16[8,160,256]{2,1,0:T(8,128)(2,1)S(1)}, u32[]{:S(2)}, u32[]{:S(2)}) %all-to-all-start.1) | async-done | bytes 655392 | tf_op jit(solution)/shard_map/all_to_all | solution.py:215
  54.8 3.8 %collective-permute-start.4 = (bf16[1280,256]{1,0:T(8,128)(2,1)S(1)}, bf16[1280,256]{1,0:T(8,128)(2,1)S(1)}, u32[]{:S(2)}, u32[]{:S(2)}) collective-permute-start(bf16[1280,256]{1,0:T(8,128)(2,1)S(1)} %bitcast.12), channel_id=1, source_target_pairs={{0,128},{8,136},{16,144},{24,152},{32,160},{40,168},{48,176},{56,1... | collective-permute-start | bytes 1966088 | tf_op jit(solution)/shard_map/ppermute | solution.py:237
  58.6 8.9 %conditional.1 = (bf16[1280,256]{1,0:T(8,128)(2,1)}, f32[1,1024]{1,0:T(1,128)S(1)}, f32[1,1024]{1,0:T(1,128)S(1)}, f32[128,1024]{1,0:T(8,128)S(1)}) conditional(s32[]{:T(128)} %convert_element_type.3, (bf16[1280,256]{1,0:T(8,128)(2,1)S(1)}, f32[1,1024]{1,0:T(1,128)S(1)}, f32[1,1024]{1,0:T(1,128)S(1)}, f32[128,1024]{1,0:T(8,128)S(1)}) %tuple.24, ...), branch_computations={%region_0.1_spmd, %region_1.2_spmd} | conditional | flops 1073741824 | bytes 4718664 | solution.py:254
  58.6 5.5 %collective-permute-start = (bf16[1280,256]{1,0:T(8,128)(2,1)S(1)}, bf16[1280,256]{1,0:T(8,128)(2,1)}, u32[]{:S(2)}, u32[]{:S(2)}) collective-permute-start(bf16[1280,256]{1,0:T(8,128)(2,1)S(1)} %get-tuple-element.27.kv_ref), channel_id=1, source_target_pairs={{0,8},{8,0},{16,24},{24,16},{32,40},{40,32},{48,56},{56,48},{64,72... | collective-permute-start | bytes 1966088 | tf_op jit(solution)/shard_map/cond/branch_1_fun/ppermute | solution.py:241
  64.2 0.4 near_kernel.1
  64.5 1.5 %collective-permute-done.kv_ref = bf16[1280,256]{1,0:T(8,128)(2,1)} collective-permute-done((bf16[1280,256]{1,0:T(8,128)(2,1)S(1)}, bf16[1280,256]{1,0:T(8,128)(2,1)}, u32[]{:S(2)}, u32[]{:S(2)}) %collective-permute-start) | collective-permute-done | bytes 655392 | tf_op jit(solution)/shard_map/cond/branch_1_fun/ppermute | solution.py:241
  66.0 1.5 %near_side_kernel.1 = (f32[1,1024]{1,0:T(1,128)S(1)}, f32[1,1024]{1,0:T(1,128)S(1)}, f32[128,1024]{1,0:T(8,128)S(1)}) custom-call(s32[1]{0:T(128)} %get-tuple-element.28.meta_ref, bf16[1280,256]{1,0:T(8,128)(2,1)} %collective-permute-done.kv_ref, s32[64,128]{1,0:T(8,128)S(1)} %get-tuple-element.29.ids_ref, bf16[256,1024]{1,0:T(8,128)(2,1)S(1)} %get-tuple-element.30.qt_ref, ...), custom_call_target="tpu_custom_call" | custom-call | flops 536870912 | bytes 1048576 | tf_op jit(solution)/shard_map/cond/branch_1_fun/near_side_kernel/pallas_call | solution.py:243
  67.5 4.1 %collective-permute-done.4.kv_ref.far_ref = bf16[1280,256]{1,0:T(8,128)(2,1)S(1)} collective-permute-done((bf16[1280,256]{1,0:T(8,128)(2,1)S(1)}, bf16[1280,256]{1,0:T(8,128)(2,1)S(1)}, u32[]{:S(2)}, u32[]{:S(2)}) %collective-permute-start.4) | collective-permute-done | bytes 655392 | tf_op jit(solution)/shard_map/ppermute | solution.py:237
  71.6 6.0 %collective-permute-start.5 = (bf16[1280,256]{1,0:T(8,128)(2,1)S(1)}, bf16[1280,256]{1,0:T(8,128)(2,1)S(1)}, u32[]{:S(2)}, u32[]{:S(2)}) collective-permute-start(bf16[1280,256]{1,0:T(8,128)(2,1)S(1)} %collective-permute-done.4.kv_ref.far_ref), channel_id=1, source_target_pairs={{0,8},{8,0},{16,24},{24,16},{32,40},{40,32},{48,56},{56,48},{64,72... | collective-permute-start | bytes 1966088 | tf_op jit(solution)/shard_map/ppermute | solution.py:258
  77.6 0.4 far_window.1
  78.0 1.3 %collective-permute-done.5.kv_ref = bf16[1280,256]{1,0:T(8,128)(2,1)S(1)} collective-permute-done((bf16[1280,256]{1,0:T(8,128)(2,1)S(1)}, bf16[1280,256]{1,0:T(8,128)(2,1)S(1)}, u32[]{:S(2)}, u32[]{:S(2)}) %collective-permute-start.5) | collective-permute-done | bytes 655392 | tf_op jit(solution)/shard_map/ppermute | solution.py:258
  79.3 0.0 copy-done
  79.3 2.7 %far_other_core_and_prefix.1 = bf16[128,1024]{1,0:T(8,128)(2,1)S(1)} custom-call(s32[1]{0:T(128)} %bitcast.meta_ref, s32[32]{0:T(128)S(1)} %bitcast.11, bf16[1280,256]{1,0:T(8,128)(2,1)S(1)} %bitcast.15, bf16[1280,256]{1,0:T(8,128)(2,1)} %get-tuple-element.75.near_side_ref, bf16[1280,256]{1,0:T(8,128)(2,1)S(1)} %collective-permute-done.4.kv_ref.far_ref, ...), custom_call_target="tpu_custom_call" | custom-call | flops 805306368 | bytes 1048576 | tf_op jit(solution)/shard_map/far_other_core_and_prefix/pallas_call | solution.py:268
  82.0 14.1 %all_to_all.15 = bf16[8,16,1024]{2,1,0:T(8,128)(2,1)S(1)} all-to-all(bf16[8,16,1024]{2,1,0:T(8,128)(2,1)S(1)} %bitcast.8), channel_id=1, replica_groups=mesh['seq'=64,'head'=8] {'head'}, dimensions={0} | all-to-all | bytes 524288 | tf_op jit(solution)/shard_map/all_to_all | solution.py:283
  96.1 0.9 copy.7
  (5 shorter events, 0.0 us)
Async XLA Ops:
  0.0 12.6 %copy-start.2 = (bf16[1,16,1,256]{3,1,2,0:T(8,128)(2,1)S(1)}, bf16[1,16,1,256]{3,1,2,0:T(8,128)(2,1)}, u32[]{:S(2)}) copy-start(bf16[1,16,1,256]{3,1,2,0:T(8,128)(2,1)} %param.10) | copy-start | bytes 24580
  1.8 22.8 %all-to-all-start = ((bf16[8,16,1280]{2,1,0:T(8,128)(2,1)}), bf16[8,16,1280]{2,1,0:T(8,128)(2,1)S(1)}, u32[]{:S(2)}, u32[]{:S(2)}) async-start(bf16[8,16,1280]{2,1,0:T(8,128)(2,1)} %by_head.1), calls=%async_computation | async-start | bytes 655360 | tf_op jit(solution)/shard_map/all_to_all | solution.py:206
  12.6 5.9 %collective-permute-start.1 = (bf16[16,256]{1,0:T(8,128)(2,1)S(1)}, bf16[16,256]{1,0:T(8,128)(2,1)S(1)}, u32[]{:S(2)}, u32[]{:S(2)}) collective-permute-start(bf16[16,256]{1,0:T(8,128)(2,1)S(1)} %bitcast.21), channel_id=1, source_target_pairs={{0,256},{8,264},{16,272},{24,280},{32,288},{40,296},{48,304},{56,3... | collective-permute-start | bytes 24584 | tf_op jit(solution)/shard_map/ppermute | solution.py:207
  24.6 4.4 %collective-permute-start.2 = (bf16[128,256]{1,0:T(8,128)(2,1)S(1)}, bf16[128,256]{1,0:T(8,128)(2,1)S(1)}, u32[]{:S(2)}, u32[]{:S(2)}) collective-permute-start(bf16[128,256]{1,0:T(8,128)(2,1)S(1)} %slice.3.mine_ref), channel_id=1, source_target_pairs={{0,128},{8,136},{16,144},{24,152},{32,160},{40,168},{48,176},{56,1... | collective-permute-start | bytes 196616 | tf_op jit(solution)/shard_map/ppermute | solution.py:210
  30.0 13.2 %copy-start.1 = (s32[8192]{0:T(1024)S(1)}, s32[8192]{0:T(1024)}, u32[]{:S(2)}) copy-start(s32[8192]{0:T(1024)} %param.9) | copy-start | bytes 98308
  30.0 24.8 %all-to-all-start.1 = ((bf16[8,160,256]{2,1,0:T(8,128)(2,1)}), bf16[8,160,256]{2,1,0:T(8,128)(2,1)S(1)}, u32[]{:S(2)}, u32[]{:S(2)}) async-start(bf16[8,160,256]{2,1,0:T(8,128)(2,1)} %pad_maximum_fusion), calls=%async_computation.1 | async-start | bytes 1310720 | tf_op jit(solution)/shard_map/all_to_all | solution.py:215
  37.0 6.2 %collective-permute-start.3 = (bf16[128,256]{1,0:T(8,128)(2,1)S(1)}, bf16[128,256]{1,0:T(8,128)(2,1)S(1)}, u32[]{:S(2)}, u32[]{:S(2)}) collective-permute-start(bf16[128,256]{1,0:T(8,128)(2,1)S(1)} %slice.3.mine_ref), channel_id=1, source_target_pairs={{0,8},{8,0},{16,24},{24,16},{32,40},{40,32},{48,56},{56,48},{64,72... | collective-permute-start | bytes 196616 | tf_op jit(solution)/shard_map/ppermute | solution.py:217
  54.8 16.8 %collective-permute-start.4 = (bf16[1280,256]{1,0:T(8,128)(2,1)S(1)}, bf16[1280,256]{1,0:T(8,128)(2,1)S(1)}, u32[]{:S(2)}, u32[]{:S(2)}) collective-permute-start(bf16[1280,256]{1,0:T(8,128)(2,1)S(1)} %bitcast.12), channel_id=1, source_target_pairs={{0,128},{8,136},{16,144},{24,152},{32,160},{40,168},{48,176},{56,1... | collective-permute-start | bytes 1966088 | tf_op jit(solution)/shard_map/ppermute | solution.py:237
  58.6 7.4 %collective-permute-start = (bf16[1280,256]{1,0:T(8,128)(2,1)S(1)}, bf16[1280,256]{1,0:T(8,128)(2,1)}, u32[]{:S(2)}, u32[]{:S(2)}) collective-permute-start(bf16[1280,256]{1,0:T(8,128)(2,1)S(1)} %get-tuple-element.27.kv_ref), channel_id=1, source_target_pairs={{0,8},{8,0},{16,24},{24,16},{32,40},{40,32},{48,56},{56,48},{64,72... | collective-permute-start | bytes 1966088 | tf_op jit(solution)/shard_map/cond/branch_1_fun/ppermute | solution.py:241
  71.6 7.7 %copy-start = (s32[1,32]{1,0:T(1,128)S(1)}, s32[1,32]{1,0:T(1,128)}, u32[]{:S(2)}) copy-start(s32[1,32]{1,0:T(1,128)} %param.11) | copy-start | bytes 388
  71.6 7.7 %collective-permute-start.5 = (bf16[1280,256]{1,0:T(8,128)(2,1)S(1)}, bf16[1280,256]{1,0:T(8,128)(2,1)S(1)}, u32[]{:S(2)}, u32[]{:S(2)}) collective-permute-start(bf16[1280,256]{1,0:T(8,128)(2,1)S(1)} %collective-permute-done.4.kv_ref.far_ref), channel_id=1, source_target_pairs={{0,8},{8,0},{16,24},{24,16},{32,40},{40,32},{48,56},{56,48},{64,72... | collective-permute-start | bytes 1966088 | tf_op jit(solution)/shard_map/ppermute | solution.py:258

commit v24 on v21

--- a/solution.py
+++ b/solution.py
@@ -103,16 +103,16 @@
         fold(side_ref[:, :D], side_ref[:, D:], mask_of(own - 1, own, row_start), *state)
 
 
-def window(kv_ref, skip, slot, core, own, limits, qt_ref, m_ref, l_ref, acc_ref):
+def window(kv_ref, skip, slot, blocks, core, own, limits, qt_ref, m_ref, l_ref, acc_ref):
     row_start, first, last = limits
     chip = own // 2 - skip
     lowest = jnp.maximum((jnp.maximum(first // ROWS - core, -1) + 1) // 2, chip - NEAR)
-    steps = jnp.maximum(chip - lowest + BLOCKS - 1, 0) // BLOCKS
+    steps = jnp.maximum(chip - lowest + blocks - 1, 0) // blocks
 
     def step(i, carry):
-        base = chip - BLOCKS * (i + 1)
+        base = chip - blocks * (i + 1)
         pairs = []
-        for b in range(BLOCKS):
+        for b in range(blocks):
             start = (base + b + 4 * NY) % NY * slot
             pairs.append(kv_ref[pl.ds(pl.multiple_of(start, PAGE), ROWS), :])
         keys = jnp.concatenate([pair[:, :D] for pair in pairs], axis=0)
@@ -126,7 +126,7 @@
         @pl.when(jnp.logical_not(whole))
         def _():
             mask = jnp.concatenate(
-                [mask_of(2 * (base + b) + core, own, row_start) for b in range(BLOCKS)], axis=0
+                [mask_of(2 * (base + b) + core, own, row_start) for b in range(blocks)], axis=0
             )
             fold(keys, values, mask, qt_ref, m_ref, l_ref, acc_ref)
 
@@ -140,7 +140,7 @@
     l_ref[...] = l_in[...]
     acc_ref[...] = acc_in[...]
     own = meta_ref[0]
-    window(kv_ref, 0, SLOT, own % 2, own, starts_of(ids_ref, own), qt_ref, m_ref, l_ref, acc_ref)
+    window(kv_ref, 0, SLOT, NEAR, own % 2, own, starts_of(ids_ref, own), qt_ref, m_ref, l_ref, acc_ref)
 
 
 def near_side_kernel(meta_ref, table_ref, kv_ref, side_ref, ids_ref, qt_ref, m_in, l_in, acc_in,
@@ -157,7 +157,7 @@
         prefix_ref[i * PAGE:(i + 1) * PAGE, :] = jnp.where(page % 2 == core, kv_ref[rows, :], side_ref[rows, :])
 
     fold(prefix_ref[:, :D], prefix_ref[:, D:], None, qt_ref, m_ref, l_ref, acc_ref)
-    window(side_ref, 0, SLOT, 1 - core, own, starts_of(ids_ref, own), qt_ref, m_ref, l_ref, acc_ref)
+    window(side_ref, 0, SLOT, NEAR, 1 - core, own, starts_of(ids_ref, own), qt_ref, m_ref, l_ref, acc_ref)
 
 
 def far_kernel(meta_ref, kv_ref, ids_ref, qt_ref, m_in, l_in, acc_in, m_ref, l_ref, acc_ref):
@@ -165,7 +165,7 @@
     l_ref[...] = l_in[...]
     acc_ref[...] = acc_in[...]
     own = meta_ref[0]
-    window(kv_ref, NEAR, ROWS, own % 2, own, starts_of(ids_ref, own), qt_ref, m_ref, l_ref, acc_ref)
+    window(kv_ref, NEAR, ROWS, BLOCKS, own % 2, own, starts_of(ids_ref, own), qt_ref, m_ref, l_ref, acc_ref)
 
 
 def last_kernel(meta_ref, kv_ref, ids_ref, qt_ref, m_in, l_in, acc_in, out_ref, m_ref, l_ref, acc_ref):
@@ -173,7 +173,7 @@
     l_ref[...] = l_in[...]
     acc_ref[...] = acc_in[...]
     own = meta_ref[0]
-    window(kv_ref, NEAR, ROWS, 1 - own % 2, own, starts_of(ids_ref, own), qt_ref, m_ref, l_ref, acc_ref)
+    window(kv_ref, NEAR, ROWS, BLOCKS, 1 - own % 2, own, starts_of(ids_ref, own), qt_ref, m_ref, l_ref, acc_ref)
     result = (acc_ref[...] * (1.0 / l_ref[...])).astype(jnp.bfloat16)
     for g in range(GROUP):
         out_ref[:, g * D:(g + 1) * D] = result[:, g * ROWS:(g + 1) * ROWS].T
@@ -257,7 +257,7 @@
     now = lax.cond(me < 2 * NX * NY, near_part, lambda operands: list(operands[2]), (near, qt, now))
     far, now = lax.optimization_barrier((far, now))
     far = far.reshape(NY * ROWS, PAIR)
-    far_side = lax.ppermute(far, "seq", SWAP)
+    far_side = lax.ppermute(far, "seq", SWAP[2 * NY:])
     now = pl.pallas_call(
         far_kernel,
         out_shape=state,

time: 95 us -> 94.5 us (level)
  transfers between devices with their start and end apart: 8 -> 8, of which waited for: 8 -> 8; matrix products, arithmetic and copies ran while one was open for 0% -> 0% of each run, Pallas kernels for 4% -> 5%
where the time goes in v24:
time: 94.5 us; the launch traced here: 93.4 us
  waiting for transfers between devices  38.2 us (40%)
  starting transfers between devices  30.3 us (32%)
  blocking collectives  15.7 us (17%)
  Pallas kernels  7.13 us (8%)
  other arithmetic  1.07 us (1%)
    all_to_all x1, waiting for transfers between devices, per_device(): lax.all_to_all(send, 'seq', split_axis=0, concat_axis=0, tiled=True, axis...  16.5 us
    all_to_all x1, blocking collectives, per_device(): lax.all_to_all(out.reshape(8, ROWS // 8, GROUP * D), 'head', split_axis=0...  15.7 us
    all_to_all x1, starting transfers between devices, per_device(): lax.all_to_all(wide, 'head', split_axis=0, concat_axis=0, tiled=True)  10.3 us
    all_to_all x1, starting transfers between devices, per_device(): lax.all_to_all(send, 'seq', split_axis=0, concat_axis=0, tiled=True, axis...  7.23 us
    all_to_all x1, waiting for transfers between devices, per_device(): lax.all_to_all(wide, 'head', split_axis=0, concat_axis=0, tiled=True)  6.23 us
    ppermute x1, waiting for transfers between devices, per_device(): lax.ppermute(jnp.concatenate([own, page, two_page], axis=0), 'seq', x_rin...  3.93 us
    ppermute x1, waiting for transfers between devices, per_device(): two_page = lax.ppermute(page, 'seq', x_ring(2))  3.7 us
    pallas_call x1, Pallas kernels, near_part(): pl.pallas_call(near_side_kernel, out_shape=state, in_specs=[SM, SM] + [VM...  3.5 us
  transfers between devices with their start and end apart: 8, of which 8 were waited for; matrix products, arithmetic and copies ran while one was open for 0% of the time, Pallas kernels for 5%

profile of v24, /device:TPU:6, one launch (start us, length us, event | category | flops | bytes accessed | tf_op | source)
XLA Modules:
  0.0 93.4 jit_solution(1718268044084120652)
XLA Ops:
  0.0 0.0 copy-start
  0.0 1.8 %by_head.1 = bf16[8,16,1280]{2,1,0:T(8,128)(2,1)} custom-call(bf16[16,8,1024]{2,1,0:T(8,128)(2,1)} %q_ref.1, bf16[16,8,256]{2,1,0:T(8,128)(2,1)} %kv_ref.1), custom_call_target="tpu_custom_call" | custom-call | tf_op jit(solution)/shard_map/by_head/pallas_call | solution.py:194
  1.8 10.3 %all-to-all-start = ((bf16[8,16,1280]{2,1,0:T(8,128)(2,1)}), bf16[8,16,1280]{2,1,0:T(8,128)(2,1)S(1)}, u32[]{:S(2)}, u32[]{:S(2)}) async-start(bf16[8,16,1280]{2,1,0:T(8,128)(2,1)} %by_head.1), calls=%async_computation | async-start | bytes 655360 | tf_op jit(solution)/shard_map/all_to_all | solution.py:201
  12.1 0.0 copy-done
  12.1 3.3 %collective-permute-start.1 = (bf16[16,256]{1,0:T(8,128)(2,1)S(1)}, bf16[16,256]{1,0:T(8,128)(2,1)S(1)}, u32[]{:S(2)}, u32[]{:S(2)}) collective-permute-start(bf16[16,256]{1,0:T(8,128)(2,1)S(1)} %bitcast.18), channel_id=1, source_target_pairs={{0,256},{8,264},{16,272},{24,280},{32,288},{40,296},{48,304},{56,3... | collective-permute-start | bytes 24584 | tf_op jit(solution)/shard_map/ppermute | solution.py:202
  15.4 3.7 %collective-permute-done.1 = bf16[16,256]{1,0:T(8,128)(2,1)S(1)} collective-permute-done((bf16[16,256]{1,0:T(8,128)(2,1)S(1)}, bf16[16,256]{1,0:T(8,128)(2,1)S(1)}, u32[]{:S(2)}, u32[]{:S(2)}) %collective-permute-start.1) | collective-permute-done | bytes 8224 | tf_op jit(solution)/shard_map/ppermute | solution.py:202
  19.1 6.2 %all-to-all-done = bf16[8,16,1280]{2,1,0:T(8,128)(2,1)S(1)} async-done(((bf16[8,16,1280]{2,1,0:T(8,128)(2,1)}), bf16[8,16,1280]{2,1,0:T(8,128)(2,1)S(1)}, u32[]{:S(2)}, u32[]{:S(2)}) %all-to-all-start) | async-done | bytes 327712 | tf_op jit(solution)/shard_map/all_to_all | solution.py:201
  25.4 2.4 %collective-permute-start.2 = (bf16[160,256]{1,0:T(8,128)(2,1)S(1)}, bf16[160,256]{1,0:T(8,128)(2,1)S(1)}, u32[]{:S(2)}, u32[]{:S(2)}) collective-permute-start(bf16[160,256]{1,0:T(8,128)(2,1)S(1)} %pad_maximum_fusion.1), channel_id=1, source_target_pairs={{0,128},{8,136},{16,144},{24,152},{32,160},{40,168},{48,176},{56,1... | collective-permute-start | bytes 245768 | tf_op jit(solution)/shard_map/ppermute | solution.py:205
  27.8 3.9 %collective-permute-done.2 = bf16[160,256]{1,0:T(8,128)(2,1)S(1)} collective-permute-done((bf16[160,256]{1,0:T(8,128)(2,1)S(1)}, bf16[160,256]{1,0:T(8,128)(2,1)S(1)}, u32[]{:S(2)}, u32[]{:S(2)}) %collective-permute-start.2) | collective-permute-done | bytes 81952 | tf_op jit(solution)/shard_map/ppermute | solution.py:205
  31.7 0.1 broadcast_select_fusion
  31.9 0.9 %pad_maximum_fusion = bf16[8,192,256]{2,1,0:T(8,128)(2,1)} fusion(bf16[8,64,256]{2,1,0:T(8,128)(2,1)S(1)} %broadcast_in_dim.36, bf16[8,128,256]{2,1,0:T(8,128)(2,1)S(1)} %broadcast_select_fusion), kind=kLoop, calls=%fused_computation | loop fusion | flops 1572864 | bytes 1572864 | tf_op jit(solution)/shard_map/concatenate | solution.py:209
  32.8 0.0 copy-start.1
  32.8 7.2 %all-to-all-start.1 = ((bf16[8,192,256]{2,1,0:T(8,128)(2,1)}), bf16[8,192,256]{2,1,0:T(8,128)(2,1)S(1)}, u32[]{:S(2)}, u32[]{:S(2)}) async-start(bf16[8,192,256]{2,1,0:T(8,128)(2,1)} %pad_maximum_fusion), calls=%async_computation.1 | async-start | bytes 1572864 | tf_op jit(solution)/shard_map/all_to_all | solution.py:210
  40.1 1.9 %collective-permute-start.3 = (bf16[128,256]{1,0:T(8,128)(2,1)S(1)}, bf16[128,256]{1,0:T(8,128)(2,1)S(1)}, u32[]{:S(2)}, u32[]{:S(2)}) collective-permute-start(bf16[128,256]{1,0:T(8,128)(2,1)S(1)} %slice.15.mine_ref), channel_id=1, source_target_pairs={{0,8},{8,0},{16,24},{24,16},{32,40},{40,32},{48,56},{56,48},{64,72... | collective-permute-start | bytes 196616 | tf_op jit(solution)/shard_map/ppermute | solution.py:212
  42.0 1.2 %collective-permute-done.3.side_ref = bf16[128,256]{1,0:T(8,128)(2,1)S(1)} collective-permute-done((bf16[128,256]{1,0:T(8,128)(2,1)S(1)}, bf16[128,256]{1,0:T(8,128)(2,1)S(1)}, u32[]{:S(2)}, u32[]{:S(2)}) %collective-permute-start.3) | collective-permute-done | bytes 65568 | tf_op jit(solution)/shard_map/ppermute | solution.py:212
  43.2 0.0 copy-done.1
  43.2 0.7 own_chip.1
  43.9 16.5 %all-to-all-done.1 = bf16[8,192,256]{2,1,0:T(8,128)(2,1)S(1)} async-done(((bf16[8,192,256]{2,1,0:T(8,128)(2,1)}), bf16[8,192,256]{2,1,0:T(8,128)(2,1)S(1)}, u32[]{:S(2)}, u32[]{:S(2)}) %all-to-all-start.1) | async-done | bytes 786464 | tf_op jit(solution)/shard_map/all_to_all | solution.py:210
  60.5 1.3 %collective-permute-start.4 = (bf16[8,128,256]{2,1,0:T(8,128)(2,1)S(1)}, bf16[8,128,256]{2,1,0:T(8,128)(2,1)S(1)}, u32[]{:S(2)}, u32[]{:S(2)}) collective-permute-start(bf16[8,128,256]{2,1,0:T(8,128)(2,1)S(1)} %slice.19), channel_id=1, source_target_pairs={{0,128},{8,136},{16,144},{24,152},{32,160},{40,168},{48,176},{56,1... | collective-permute-start | bytes 1572872 | tf_op jit(solution)/shard_map/ppermute | solution.py:231
  61.8 0.0 copy-done.2
  61.8 7.7 %conditional.1 = ((f32[1,1024]{1,0:T(1,128)S(1)}, f32[1,1024]{1,0:T(1,128)S(1)}, f32[128,1024]{1,0:T(8,128)S(1)})) conditional(s32[]{:T(128)} %convert_element_type.3, (f32[1,1024]{1,0:T(1,128)S(1)}, f32[1,1024]{1,0:T(1,128)S(1)}, f32[128,1024]{1,0:T(8,128)S(1)}) %tuple.18, (s32[1,32]{1,0:T(1,128)S(1)}, bf16[8,192,256]{2,1,0:T(8,128)(2,1)S(1)}, ...), branch_computations={%region_0.1_spmd, %region_1.2_spmd} | conditional | flops 1342177280 | bytes 5242928 | solution.py:257
  61.8 1.9 %collective-permute-start = (bf16[1536,256]{1,0:T(8,128)(2,1)S(1)}, bf16[1536,256]{1,0:T(8,128)(2,1)S(1)}, u32[]{:S(2)}, u32[]{:S(2)}) collective-permute-start(bf16[1536,256]{1,0:T(8,128)(2,1)S(1)} %bitcast.14), channel_id=1, source_target_pairs={{0,8},{8,0},{16,24},{24,16},{32,40},{40,32},{48,56},{56,48},{64,72... | collective-permute-start | bytes 2359304 | tf_op jit(solution)/shard_map/cond/branch_1_fun/ppermute | solution.py:236
  63.7 0.4 near_window.1
  64.1 1.9 %collective-permute-done.side_ref = bf16[1536,256]{1,0:T(8,128)(2,1)S(1)} collective-permute-done((bf16[1536,256]{1,0:T(8,128)(2,1)S(1)}, bf16[1536,256]{1,0:T(8,128)(2,1)S(1)}, u32[]{:S(2)}, u32[]{:S(2)}) %collective-permute-start) | collective-permute-done | bytes 786464 | tf_op jit(solution)/shard_map/cond/branch_1_fun/ppermute | solution.py:236
  66.0 3.5 %near_other_core_and_prefix.1 = (f32[1,1024]{1,0:T(1,128)S(1)}, f32[1,1024]{1,0:T(1,128)S(1)}, f32[128,1024]{1,0:T(8,128)S(1)}) custom-call(s32[1]{0:T(128)} %get-tuple-element.27.meta_ref, s32[32]{0:T(128)S(1)} %bitcast.25, bf16[1536,256]{1,0:T(8,128)(2,1)S(1)} %bitcast.16, bf16[1536,256]{1,0:T(8,128)(2,1)S(1)} %collective-permute-done.side_ref, ...), custom_call_target="tpu_custom_call" | custom-call | flops 805306368 | bytes 1048576 | tf_op jit(solution)/shard_map/cond/branch_1_fun/near_other_core_and_prefix/pallas_call | solution.py:246
  69.5 3.2 %collective-permute-done.4 = bf16[8,128,256]{2,1,0:T(8,128)(2,1)S(1)} collective-permute-done((bf16[8,128,256]{2,1,0:T(8,128)(2,1)S(1)}, bf16[8,128,256]{2,1,0:T(8,128)(2,1)S(1)}, u32[]{:S(2)}, u32[]{:S(2)}) %collective-permute-start.4) | collective-permute-done | bytes 524320 | tf_op jit(solution)/shard_map/ppermute | solution.py:231
  72.6 1.9 %collective-permute-start.5 = (bf16[1024,256]{1,0:T(8,128)(2,1)S(1)}, bf16[1024,256]{1,0:T(8,128)(2,1)S(1)}, u32[]{:S(2)}, u32[]{:S(2)}) collective-permute-start(bf16[1024,256]{1,0:T(8,128)(2,1)S(1)} %bitcast.12), channel_id=1, source_target_pairs={{128,136},{136,128},{144,152},{152,144},{160,168},{168,160},{176,1... | collective-permute-start | bytes 1572872 | tf_op jit(solution)/shard_map/ppermute | solution.py:260
  74.6 0.4 far_window.1
  74.9 1.5 %collective-permute-done.5.kv_ref = bf16[1024,256]{1,0:T(8,128)(2,1)S(1)} collective-permute-done((bf16[1024,256]{1,0:T(8,128)(2,1)S(1)}, bf16[1024,256]{1,0:T(8,128)(2,1)S(1)}, u32[]{:S(2)}, u32[]{:S(2)}) %collective-permute-start.5) | collective-permute-done | bytes 524320 | tf_op jit(solution)/shard_map/ppermute | solution.py:260
  76.4 0.5 far_other_core.1
  76.9 15.7 %all_to_all.15 = bf16[8,16,1024]{2,1,0:T(8,128)(2,1)S(1)} all-to-all(bf16[8,16,1024]{2,1,0:T(8,128)(2,1)S(1)} %bitcast.11), channel_id=1, replica_groups=mesh['seq'=64,'head'=8] {'head'}, dimensions={0} | all-to-all | bytes 524288 | tf_op jit(solution)/shard_map/all_to_all | solution.py:284
  92.6 0.9 copy.8
  (9 shorter events, 0.1 us)
Async XLA Ops:
  0.0 12.1 %copy-start = (bf16[1,16,1,256]{3,1,2,0:T(8,128)(2,1)S(1)}, bf16[1,16,1,256]{3,1,2,0:T(8,128)(2,1)}, u32[]{:S(2)}) copy-start(bf16[1,16,1,256]{3,1,2,0:T(8,128)(2,1)} %param.10) | copy-start | bytes 24580
  1.8 23.6 %all-to-all-start = ((bf16[8,16,1280]{2,1,0:T(8,128)(2,1)}), bf16[8,16,1280]{2,1,0:T(8,128)(2,1)S(1)}, u32[]{:S(2)}, u32[]{:S(2)}) async-start(bf16[8,16,1280]{2,1,0:T(8,128)(2,1)} %by_head.1), calls=%async_computation | async-start | bytes 655360 | tf_op jit(solution)/shard_map/all_to_all | solution.py:201
  12.1 7.0 %collective-permute-start.1 = (bf16[16,256]{1,0:T(8,128)(2,1)S(1)}, bf16[16,256]{1,0:T(8,128)(2,1)S(1)}, u32[]{:S(2)}, u32[]{:S(2)}) collective-permute-start(bf16[16,256]{1,0:T(8,128)(2,1)S(1)} %bitcast.18), channel_id=1, source_target_pairs={{0,256},{8,264},{16,272},{24,280},{32,288},{40,296},{48,304},{56,3... | collective-permute-start | bytes 24584 | tf_op jit(solution)/shard_map/ppermute | solution.py:202
  25.4 6.3 %collective-permute-start.2 = (bf16[160,256]{1,0:T(8,128)(2,1)S(1)}, bf16[160,256]{1,0:T(8,128)(2,1)S(1)}, u32[]{:S(2)}, u32[]{:S(2)}) collective-permute-start(bf16[160,256]{1,0:T(8,128)(2,1)S(1)} %pad_maximum_fusion.1), channel_id=1, source_target_pairs={{0,128},{8,136},{16,144},{24,152},{32,160},{40,168},{48,176},{56,1... | collective-permute-start | bytes 245768 | tf_op jit(solution)/shard_map/ppermute | solution.py:205
  32.8 10.4 %copy-start.1 = (s32[8192]{0:T(1024)S(1)}, s32[8192]{0:T(1024)}, u32[]{:S(2)}) copy-start(s32[8192]{0:T(1024)} %param.9) | copy-start | bytes 98308
  32.8 27.6 %all-to-all-start.1 = ((bf16[8,192,256]{2,1,0:T(8,128)(2,1)}), bf16[8,192,256]{2,1,0:T(8,128)(2,1)S(1)}, u32[]{:S(2)}, u32[]{:S(2)}) async-start(bf16[8,192,256]{2,1,0:T(8,128)(2,1)} %pad_maximum_fusion), calls=%async_computation.1 | async-start | bytes 1572864 | tf_op jit(solution)/shard_map/all_to_all | solution.py:210
  40.1 21.7 %copy-start.2 = (s32[1,32]{1,0:T(1,128)S(1)}, s32[1,32]{1,0:T(1,128)}, u32[]{:S(2)}) copy-start(s32[1,32]{1,0:T(1,128)} %param.11) | copy-start | bytes 388
  40.1 3.1 %collective-permute-start.3 = (bf16[128,256]{1,0:T(8,128)(2,1)S(1)}, bf16[128,256]{1,0:T(8,128)(2,1)S(1)}, u32[]{:S(2)}, u32[]{:S(2)}) collective-permute-start(bf16[128,256]{1,0:T(8,128)(2,1)S(1)} %slice.15.mine_ref), channel_id=1, source_target_pairs={{0,8},{8,0},{16,24},{24,16},{32,40},{40,32},{48,56},{56,48},{64,72... | collective-permute-start | bytes 196616 | tf_op jit(solution)/shard_map/ppermute | solution.py:212
  60.5 12.2 %collective-permute-start.4 = (bf16[8,128,256]{2,1,0:T(8,128)(2,1)S(1)}, bf16[8,128,256]{2,1,0:T(8,128)(2,1)S(1)}, u32[]{:S(2)}, u32[]{:S(2)}) collective-permute-start(bf16[8,128,256]{2,1,0:T(8,128)(2,1)S(1)} %slice.19), channel_id=1, source_target_pairs={{0,128},{8,136},{16,144},{24,152},{32,160},{40,168},{48,176},{56,1... | collective-permute-start | bytes 1572872 | tf_op jit(solution)/shard_map/ppermute | solution.py:231
  61.8 4.2 %collective-permute-start = (bf16[1536,256]{1,0:T(8,128)(2,1)S(1)}, bf16[1536,256]{1,0:T(8,128)(2,1)S(1)}, u32[]{:S(2)}, u32[]{:S(2)}) collective-permute-start(bf16[1536,256]{1,0:T(8,128)(2,1)S(1)} %bitcast.14), channel_id=1, source_target_pairs={{0,8},{8,0},{16,24},{24,16},{32,40},{40,32},{48,56},{56,48},{64,72... | collective-permute-start | bytes 2359304 | tf_op jit(solution)/shard_map/cond/branch_1_fun/ppermute | solution.py:236
  72.6 3.8 %collective-permute-start.5 = (bf16[1024,256]{1,0:T(8,128)(2,1)S(1)}, bf16[1024,256]{1,0:T(8,128)(2,1)S(1)}, u32[]{:S(2)}, u32[]{:S(2)}) collective-permute-start(bf16[1024,256]{1,0:T(8,128)(2,1)S(1)} %bitcast.12), channel_id=1, source_target_pairs={{128,136},{136,128},{144,152},{152,144},{160,168},{168,160},{176,1... | collective-permute-start | bytes 1572872 | tf_op jit(solution)/shard_map/ppermute | solution.py:260

commit v25 on v24

--- a/solution.py
+++ b/solution.py
@@ -113,7 +113,7 @@
         base = chip - blocks * (i + 1)
         pairs = []
         for b in range(blocks):
-            start = (base + b + 4 * NY) % NY * slot
+            start = ((base + b) & (NY - 1)) * slot
             pairs.append(kv_ref[pl.ds(pl.multiple_of(start, PAGE), ROWS), :])
         keys = jnp.concatenate([pair[:, :D] for pair in pairs], axis=0)
         values = jnp.concatenate([pair[:, D:] for pair in pairs], axis=0)
@@ -152,12 +152,27 @@
     core, x = own % 2, own // (2 * NY)
     for i in range(PAGES):
         page = table_ref[i]
-        start = (page // 2) % NY * SLOT + ROWS + (x + NX - page // (2 * NY)) % NX * PAGE
+        start = ((page >> 1) & (NY - 1)) * SLOT + ROWS + ((x - (page >> 4)) & (NX - 1)) * PAGE
         rows = pl.ds(pl.multiple_of(start, PAGE), PAGE)
         prefix_ref[i * PAGE:(i + 1) * PAGE, :] = jnp.where(page % 2 == core, kv_ref[rows, :], side_ref[rows, :])
 
-    fold(prefix_ref[:, :D], prefix_ref[:, D:], None, qt_ref, m_ref, l_ref, acc_ref)
-    window(side_ref, 0, SLOT, NEAR, 1 - core, own, starts_of(ids_ref, own), qt_ref, m_ref, l_ref, acc_ref)
+    limits = starts_of(ids_ref, own)
+    base = own // 2 - NEAR
+    whole = (2 * base + 1 - core) * ROWS >= limits[2]
+
+    @pl.when(whole)
+    def _():
+        pairs = [prefix_ref[...]]
+        for b in range(NEAR):
+            start = ((base + b) & (NY - 1)) * SLOT
+            pairs.append(side_ref[pl.ds(pl.multiple_of(start, PAGE), ROWS), :])
+        pairs = jnp.concatenate(pairs, axis=0)
+        fold(pairs[:, :D], pairs[:, D:], None, qt_ref, m_ref, l_ref, acc_ref)
+
+    @pl.when(jnp.logical_not(whole))
+    def _():
+        fold(prefix_ref[:, :D], prefix_ref[:, D:], None, qt_ref, m_ref, l_ref, acc_ref)
+        window(side_ref, 0, SLOT, NEAR, 1 - core, own, limits, qt_ref, m_ref, l_ref, acc_ref)
 
 
 def far_kernel(meta_ref, kv_ref, ids_ref, qt_ref, m_in, l_in, acc_in, m_ref, l_ref, acc_ref):

time: 94.5 us -> 97 us (1.026)
  Pallas kernels: 7.13 us -> 12.4 us
  waiting for transfers between devices: 38.2 us -> 35.4 us
    pallas_call x1, Pallas kernels: 0.36 us -> 2.45 us  [per_device(): pl.pallas_call(far_kernel, out_shape=state, in_specs=[SM] + [VM] * 6, out...]
    pallas_call x1, Pallas kernels: 0.48 us -> 2.41 us  [per_device(): pl.pallas_call(last_kernel, out_shape=jax.ShapeDtypeStruct((ROWS, GROUP *...]
    ppermute x1, waiting for transfers between devices: 1.88 us -> 0.25 us  [near_part(): near_side = lax.ppermute(near, 'seq', SWAP)]
    pallas_call x1, Pallas kernels: 0.36 us -> 1.99 us  [near_part(): pl.pallas_call(near_kernel, out_shape=state, in_specs=[SM] + [VM] * 6, ou...]
    ppermute x1, waiting for transfers between devices: 1.51 us -> 0.01 us  [per_device(): far_side = lax.ppermute(far, 'seq', SWAP[2 * NY:])]
  transfers between devices with their start and end apart: 8 -> 8, of which waited for: 8 -> 7; matrix products, arithmetic and copies ran while one was open for 0% -> 0% of each run, Pallas kernels for 5% -> 9%
where the time goes in v25:
time: 97 us; the launch traced here: 96.3 us
  waiting for transfers between devices  35.4 us (36%)
  starting transfers between devices  30.3 us (31%)
  blocking collectives  16 us (16%)
  Pallas kernels  12.4 us (13%)
  other arithmetic  1.07 us (1%)
    all_to_all x1, waiting for transfers between devices, per_device(): lax.all_to_all(send, 'seq', split_axis=0, concat_axis=0, tiled=True, axis...  16.5 us
    all_to_all x1, blocking collectives, per_device(): lax.all_to_all(out.reshape(8, ROWS // 8, GROUP * D), 'head', split_axis=0...  16 us
    all_to_all x1, starting transfers between devices, per_device(): lax.all_to_all(wide, 'head', split_axis=0, concat_axis=0, tiled=True)  10.3 us
    all_to_all x1, starting transfers between devices, per_device(): lax.all_to_all(send, 'seq', split_axis=0, concat_axis=0, tiled=True, axis...  7.23 us
    all_to_all x1, waiting for transfers between devices, per_device(): lax.all_to_all(wide, 'head', split_axis=0, concat_axis=0, tiled=True)  6.23 us
    ppermute x1, waiting for transfers between devices, per_device(): lax.ppermute(jnp.concatenate([own, page, two_page], axis=0), 'seq', x_rin...  3.93 us
    ppermute x1, waiting for transfers between devices, per_device(): two_page = lax.ppermute(page, 'seq', x_ring(2))  3.7 us
    ppermute x1, waiting for transfers between devices, per_device(): far = lax.ppermute(near[:, :ROWS], 'seq', x_next())  3.54 us
  transfers between devices with their start and end apart: 8, of which 7 were waited for; matrix products, arithmetic and copies ran while one was open for 0% of the time, Pallas kernels for 9%

profile of v25, /device:TPU:6, one launch (start us, length us, event | category | flops | bytes accessed | tf_op | source)
XLA Modules:
  0.0 96.3 jit_solution(10401781909115624352)
XLA Ops:
  0.0 0.0 copy-start
  0.0 1.8 %by_head.1 = bf16[8,16,1280]{2,1,0:T(8,128)(2,1)} custom-call(bf16[16,8,1024]{2,1,0:T(8,128)(2,1)} %q_ref.1, bf16[16,8,256]{2,1,0:T(8,128)(2,1)} %kv_ref.1), custom_call_target="tpu_custom_call" | custom-call | tf_op jit(solution)/shard_map/by_head/pallas_call | solution.py:209
  1.8 10.3 %all-to-all-start = ((bf16[8,16,1280]{2,1,0:T(8,128)(2,1)}), bf16[8,16,1280]{2,1,0:T(8,128)(2,1)S(1)}, u32[]{:S(2)}, u32[]{:S(2)}) async-start(bf16[8,16,1280]{2,1,0:T(8,128)(2,1)} %by_head.1), calls=%async_computation | async-start | bytes 655360 | tf_op jit(solution)/shard_map/all_to_all | solution.py:216
  12.1 0.0 copy-done
  12.1 3.3 %collective-permute-start.1 = (bf16[16,256]{1,0:T(8,128)(2,1)S(1)}, bf16[16,256]{1,0:T(8,128)(2,1)S(1)}, u32[]{:S(2)}, u32[]{:S(2)}) collective-permute-start(bf16[16,256]{1,0:T(8,128)(2,1)S(1)} %bitcast.18), channel_id=1, source_target_pairs={{0,256},{8,264},{16,272},{24,280},{32,288},{40,296},{48,304},{56,3... | collective-permute-start | bytes 24584 | tf_op jit(solution)/shard_map/ppermute | solution.py:217
  15.4 3.7 %collective-permute-done.1 = bf16[16,256]{1,0:T(8,128)(2,1)S(1)} collective-permute-done((bf16[16,256]{1,0:T(8,128)(2,1)S(1)}, bf16[16,256]{1,0:T(8,128)(2,1)S(1)}, u32[]{:S(2)}, u32[]{:S(2)}) %collective-permute-start.1) | collective-permute-done | bytes 8224 | tf_op jit(solution)/shard_map/ppermute | solution.py:217
  19.1 6.2 %all-to-all-done = bf16[8,16,1280]{2,1,0:T(8,128)(2,1)S(1)} async-done(((bf16[8,16,1280]{2,1,0:T(8,128)(2,1)}), bf16[8,16,1280]{2,1,0:T(8,128)(2,1)S(1)}, u32[]{:S(2)}, u32[]{:S(2)}) %all-to-all-start) | async-done | bytes 327712 | tf_op jit(solution)/shard_map/all_to_all | solution.py:216
  25.4 2.4 %collective-permute-start.2 = (bf16[160,256]{1,0:T(8,128)(2,1)S(1)}, bf16[160,256]{1,0:T(8,128)(2,1)S(1)}, u32[]{:S(2)}, u32[]{:S(2)}) collective-permute-start(bf16[160,256]{1,0:T(8,128)(2,1)S(1)} %pad_maximum_fusion.1), channel_id=1, source_target_pairs={{0,128},{8,136},{16,144},{24,152},{32,160},{40,168},{48,176},{56,1... | collective-permute-start | bytes 245768 | tf_op jit(solution)/shard_map/ppermute | solution.py:220
  27.8 3.9 %collective-permute-done.2 = bf16[160,256]{1,0:T(8,128)(2,1)S(1)} collective-permute-done((bf16[160,256]{1,0:T(8,128)(2,1)S(1)}, bf16[160,256]{1,0:T(8,128)(2,1)S(1)}, u32[]{:S(2)}, u32[]{:S(2)}) %collective-permute-start.2) | collective-permute-done | bytes 81952 | tf_op jit(solution)/shard_map/ppermute | solution.py:220
  31.7 0.1 broadcast_select_fusion
  31.9 0.9 pad_maximum_fusion
  32.8 0.0 copy-start.1
  32.8 7.2 %all-to-all-start.1 = ((bf16[8,192,256]{2,1,0:T(8,128)(2,1)}), bf16[8,192,256]{2,1,0:T(8,128)(2,1)S(1)}, u32[]{:S(2)}, u32[]{:S(2)}) async-start(bf16[8,192,256]{2,1,0:T(8,128)(2,1)} %pad_maximum_fusion), calls=%async_computation.1 | async-start | bytes 1572864 | tf_op jit(solution)/shard_map/all_to_all | solution.py:225
  40.1 1.9 %collective-permute-start.3 = (bf16[128,256]{1,0:T(8,128)(2,1)S(1)}, bf16[128,256]{1,0:T(8,128)(2,1)S(1)}, u32[]{:S(2)}, u32[]{:S(2)}) collective-permute-start(bf16[128,256]{1,0:T(8,128)(2,1)S(1)} %slice.15.mine_ref), channel_id=1, source_target_pairs={{0,8},{8,0},{16,24},{24,16},{32,40},{40,32},{48,56},{56,48},{64,72... | collective-permute-start | bytes 196616 | tf_op jit(solution)/shard_map/ppermute | solution.py:227
  42.0 1.2 %collective-permute-done.3.side_ref = bf16[128,256]{1,0:T(8,128)(2,1)S(1)} collective-permute-done((bf16[128,256]{1,0:T(8,128)(2,1)S(1)}, bf16[128,256]{1,0:T(8,128)(2,1)S(1)}, u32[]{:S(2)}, u32[]{:S(2)}) %collective-permute-start.3) | collective-permute-done | bytes 65568 | tf_op jit(solution)/shard_map/ppermute | solution.py:227
  43.2 0.0 copy-done.1
  43.2 0.7 own_chip.1
  43.9 16.5 %all-to-all-done.1 = bf16[8,192,256]{2,1,0:T(8,128)(2,1)S(1)} async-done(((bf16[8,192,256]{2,1,0:T(8,128)(2,1)}), bf16[8,192,256]{2,1,0:T(8,128)(2,1)S(1)}, u32[]{:S(2)}, u32[]{:S(2)}) %all-to-all-start.1) | async-done | bytes 786464 | tf_op jit(solution)/shard_map/all_to_all | solution.py:225
  60.5 1.3 %collective-permute-start.4 = (bf16[8,128,256]{2,1,0:T(8,128)(2,1)S(1)}, bf16[8,128,256]{2,1,0:T(8,128)(2,1)S(1)}, u32[]{:S(2)}, u32[]{:S(2)}) collective-permute-start(bf16[8,128,256]{2,1,0:T(8,128)(2,1)S(1)} %slice.19), channel_id=1, source_target_pairs={{0,128},{8,136},{16,144},{24,152},{32,160},{40,168},{48,176},{56,1... | collective-permute-start | bytes 1572872 | tf_op jit(solution)/shard_map/ppermute | solution.py:246
  61.8 0.0 copy-done.2
  61.8 7.3 %conditional.1 = ((f32[1,1024]{1,0:T(1,128)S(1)}, f32[1,1024]{1,0:T(1,128)S(1)}, f32[128,1024]{1,0:T(8,128)S(1)})) conditional(s32[]{:T(128)} %convert_element_type.3, (f32[1,1024]{1,0:T(1,128)S(1)}, f32[1,1024]{1,0:T(1,128)S(1)}, f32[128,1024]{1,0:T(8,128)S(1)}) %tuple.18, (s32[1,32]{1,0:T(1,128)S(1)}, bf16[8,192,256]{2,1,0:T(8,128)(2,1)S(1)}, ...), branch_computations={%region_0.1_spmd, %region_1.2_spmd} | conditional | flops 1342177280 | bytes 5242928 | solution.py:272
  61.8 1.9 %collective-permute-start = (bf16[1536,256]{1,0:T(8,128)(2,1)S(1)}, bf16[1536,256]{1,0:T(8,128)(2,1)S(1)}, u32[]{:S(2)}, u32[]{:S(2)}) collective-permute-start(bf16[1536,256]{1,0:T(8,128)(2,1)S(1)} %bitcast.14), channel_id=1, source_target_pairs={{0,8},{8,0},{16,24},{24,16},{32,40},{40,32},{48,56},{56,48},{64,72... | collective-permute-start | bytes 2359304 | tf_op jit(solution)/shard_map/cond/branch_1_fun/ppermute | solution.py:251
  63.7 2.0 %near_window.1 = (f32[1,1024]{1,0:T(1,128)S(1)}, f32[1,1024]{1,0:T(1,128)S(1)}, f32[128,1024]{1,0:T(8,128)S(1)}) custom-call(s32[1]{0:T(128)} %get-tuple-element.27.meta_ref, bf16[1536,256]{1,0:T(8,128)(2,1)S(1)} %bitcast.15, s32[64,128]{1,0:T(8,128)S(1)} %get-tuple-element.30.ids_ref, bf16[256,1024]{1,0:T(8,128)(2,1)S(1)} %get-tuple-element.31.qt_ref, ...), custom_call_target="tpu_custom_call" | custom-call | flops 536870912 | bytes 1048576 | tf_op jit(solution)/shard_map/cond/branch_1_fun/near_window/pallas_call | solution.py:252
  65.7 0.3 collective-permute-done.side_ref
  66.0 3.1 %near_other_core_and_prefix.1 = (f32[1,1024]{1,0:T(1,128)S(1)}, f32[1,1024]{1,0:T(1,128)S(1)}, f32[128,1024]{1,0:T(8,128)S(1)}) custom-call(s32[1]{0:T(128)} %get-tuple-element.27.meta_ref, s32[32]{0:T(128)S(1)} %bitcast.25, bf16[1536,256]{1,0:T(8,128)(2,1)S(1)} %bitcast.16, bf16[1536,256]{1,0:T(8,128)(2,1)S(1)} %collective-permute-done.side_ref, ...), custom_call_target="tpu_custom_call" | custom-call | flops 805306368 | bytes 1048576 | tf_op jit(solution)/shard_map/cond/branch_1_fun/near_other_core_and_prefix/pallas_call | solution.py:261
  69.1 3.5 %collective-permute-done.4 = bf16[8,128,256]{2,1,0:T(8,128)(2,1)S(1)} collective-permute-done((bf16[8,128,256]{2,1,0:T(8,128)(2,1)S(1)}, bf16[8,128,256]{2,1,0:T(8,128)(2,1)S(1)}, u32[]{:S(2)}, u32[]{:S(2)}) %collective-permute-start.4) | collective-permute-done | bytes 524320 | tf_op jit(solution)/shard_map/ppermute | solution.py:246
  72.6 1.9 %collective-permute-start.5 = (bf16[1024,256]{1,0:T(8,128)(2,1)S(1)}, bf16[1024,256]{1,0:T(8,128)(2,1)S(1)}, u32[]{:S(2)}, u32[]{:S(2)}) collective-permute-start(bf16[1024,256]{1,0:T(8,128)(2,1)S(1)} %bitcast.12), channel_id=1, source_target_pairs={{128,136},{136,128},{144,152},{152,144},{160,168},{168,160},{176,1... | collective-permute-start | bytes 1572872 | tf_op jit(solution)/shard_map/ppermute | solution.py:275
  74.6 2.5 %far_window.1 = (f32[1,1024]{1,0:T(1,128)S(1)}, f32[1,1024]{1,0:T(1,128)S(1)}, f32[128,1024]{1,0:T(8,128)S(1)}) custom-call(s32[1]{0:T(128)} %bitcast.2.meta_ref, bf16[1024,256]{1,0:T(8,128)(2,1)S(1)} %bitcast.13, s32[64,128]{1,0:T(8,128)S(1)} %bitcast.23, bf16[256,1024]{1,0:T(8,128)(2,1)S(1)} %get-tuple-element.71.qt_ref, ...), custom_call_target="tpu_custom_call" | custom-call | flops 536870912 | bytes 1048576 | tf_op jit(solution)/shard_map/far_window/pallas_call | solution.py:276
  77.0 0.0 collective-permute-done.5.kv_ref
  77.0 2.4 %far_other_core.1 = bf16[128,1024]{1,0:T(8,128)(2,1)S(1)} custom-call(s32[1]{0:T(128)} %bitcast.2.meta_ref, bf16[1024,256]{1,0:T(8,128)(2,1)S(1)} %collective-permute-done.5.kv_ref, s32[64,128]{1,0:T(8,128)S(1)} %bitcast.24, bf16[256,1024]{1,0:T(8,128)(2,1)S(1)} %get-tuple-element.71.qt_ref, f32[1,1024]{1,0:T(1,128)S(1)} %get-tuple-element.79.m_in, ...), custom_call_target="tpu_custom_call" | custom-call | flops 536870912 | bytes 1048576 | tf_op jit(solution)/shard_map/far_other_core/pallas_call | solution.py:285
  79.4 16.0 %all_to_all.15 = bf16[8,16,1024]{2,1,0:T(8,128)(2,1)S(1)} all-to-all(bf16[8,16,1024]{2,1,0:T(8,128)(2,1)S(1)} %bitcast.11), channel_id=1, replica_groups=mesh['seq'=64,'head'=8] {'head'}, dimensions={0} | all-to-all | bytes 524288 | tf_op jit(solution)/shard_map/all_to_all | solution.py:299
  95.5 0.9 copy.8
  (9 shorter events, 0.1 us)
Async XLA Ops:
  0.0 12.1 %copy-start = (bf16[1,16,1,256]{3,1,2,0:T(8,128)(2,1)S(1)}, bf16[1,16,1,256]{3,1,2,0:T(8,128)(2,1)}, u32[]{:S(2)}) copy-start(bf16[1,16,1,256]{3,1,2,0:T(8,128)(2,1)} %param.10) | copy-start | bytes 24580
  1.8 23.6 %all-to-all-start = ((bf16[8,16,1280]{2,1,0:T(8,128)(2,1)}), bf16[8,16,1280]{2,1,0:T(8,128)(2,1)S(1)}, u32[]{:S(2)}, u32[]{:S(2)}) async-start(bf16[8,16,1280]{2,1,0:T(8,128)(2,1)} %by_head.1), calls=%async_computation | async-start | bytes 655360 | tf_op jit(solution)/shard_map/all_to_all | solution.py:216
  12.1 7.0 %collective-permute-start.1 = (bf16[16,256]{1,0:T(8,128)(2,1)S(1)}, bf16[16,256]{1,0:T(8,128)(2,1)S(1)}, u32[]{:S(2)}, u32[]{:S(2)}) collective-permute-start(bf16[16,256]{1,0:T(8,128)(2,1)S(1)} %bitcast.18), channel_id=1, source_target_pairs={{0,256},{8,264},{16,272},{24,280},{32,288},{40,296},{48,304},{56,3... | collective-permute-start | bytes 24584 | tf_op jit(solution)/shard_map/ppermute | solution.py:217
  25.4 6.3 %collective-permute-start.2 = (bf16[160,256]{1,0:T(8,128)(2,1)S(1)}, bf16[160,256]{1,0:T(8,128)(2,1)S(1)}, u32[]{:S(2)}, u32[]{:S(2)}) collective-permute-start(bf16[160,256]{1,0:T(8,128)(2,1)S(1)} %pad_maximum_fusion.1), channel_id=1, source_target_pairs={{0,128},{8,136},{16,144},{24,152},{32,160},{40,168},{48,176},{56,1... | collective-permute-start | bytes 245768 | tf_op jit(solution)/shard_map/ppermute | solution.py:220
  32.8 10.4 %copy-start.1 = (s32[8192]{0:T(1024)S(1)}, s32[8192]{0:T(1024)}, u32[]{:S(2)}) copy-start(s32[8192]{0:T(1024)} %param.9) | copy-start | bytes 98308
  32.8 27.6 %all-to-all-start.1 = ((bf16[8,192,256]{2,1,0:T(8,128)(2,1)}), bf16[8,192,256]{2,1,0:T(8,128)(2,1)S(1)}, u32[]{:S(2)}, u32[]{:S(2)}) async-start(bf16[8,192,256]{2,1,0:T(8,128)(2,1)} %pad_maximum_fusion), calls=%async_computation.1 | async-start | bytes 1572864 | tf_op jit(solution)/shard_map/all_to_all | solution.py:225
  40.1 21.7 %copy-start.2 = (s32[1,32]{1,0:T(1,128)S(1)}, s32[1,32]{1,0:T(1,128)}, u32[]{:S(2)}) copy-start(s32[1,32]{1,0:T(1,128)} %param.11) | copy-start | bytes 388
  40.1 3.1 %collective-permute-start.3 = (bf16[128,256]{1,0:T(8,128)(2,1)S(1)}, bf16[128,256]{1,0:T(8,128)(2,1)S(1)}, u32[]{:S(2)}, u32[]{:S(2)}) collective-permute-start(bf16[128,256]{1,0:T(8,128)(2,1)S(1)} %slice.15.mine_ref), channel_id=1, source_target_pairs={{0,8},{8,0},{16,24},{24,16},{32,40},{40,32},{48,56},{56,48},{64,72... | collective-permute-start | bytes 196616 | tf_op jit(solution)/shard_map/ppermute | solution.py:227
  60.5 12.2 %collective-permute-start.4 = (bf16[8,128,256]{2,1,0:T(8,128)(2,1)S(1)}, bf16[8,128,256]{2,1,0:T(8,128)(2,1)S(1)}, u32[]{:S(2)}, u32[]{:S(2)}) collective-permute-start(bf16[8,128,256]{2,1,0:T(8,128)(2,1)S(1)} %slice.19), channel_id=1, source_target_pairs={{0,128},{8,136},{16,144},{24,152},{32,160},{40,168},{48,176},{56,1... | collective-permute-start | bytes 1572872 | tf_op jit(solution)/shard_map/ppermute | solution.py:246
  61.8 4.2 %collective-permute-start = (bf16[1536,256]{1,0:T(8,128)(2,1)S(1)}, bf16[1536,256]{1,0:T(8,128)(2,1)S(1)}, u32[]{:S(2)}, u32[]{:S(2)}) collective-permute-start(bf16[1536,256]{1,0:T(8,128)(2,1)S(1)} %bitcast.14), channel_id=1, source_target_pairs={{0,8},{8,0},{16,24},{24,16},{32,40},{40,32},{48,56},{56,48},{64,72... | collective-permute-start | bytes 2359304 | tf_op jit(solution)/shard_map/cond/branch_1_fun/ppermute | solution.py:251
  72.6 4.4 %collective-permute-start.5 = (bf16[1024,256]{1,0:T(8,128)(2,1)S(1)}, bf16[1024,256]{1,0:T(8,128)(2,1)S(1)}, u32[]{:S(2)}, u32[]{:S(2)}) collective-permute-start(bf16[1024,256]{1,0:T(8,128)(2,1)S(1)} %bitcast.12), channel_id=1, source_target_pairs={{128,136},{136,128},{144,152},{152,144},{160,168},{168,160},{176,1... | collective-permute-start | bytes 1572872 | tf_op jit(solution)/shard_map/ppermute | solution.py:275

commit v26 on v24

--- a/solution.py
+++ b/solution.py
@@ -209,7 +209,7 @@
     send = jnp.concatenate([block, jnp.broadcast_to(pages, (NY, NX * PAGE, PAIR))], axis=1)
     near = lax.all_to_all(send, "seq", split_axis=0, concat_axis=0, tiled=True, axis_index_groups=Y_GROUPS)
     later, _ = lax.optimization_barrier((own, send))
-    side = lax.ppermute(later, "seq", SWAP)
+    side = lax.ppermute(later, "seq", SWAP[::2])
     ids = branch_ids.reshape(2 * NX * NY, ROWS)
     meta = me.astype(jnp.int32).reshape(1)
     state = [

time: 94.5 us -> 95.3 us (level)
  Pallas kernels: 7.13 us -> 8.93 us
  waiting for transfers between devices: 38.2 us -> 37 us
    pallas_call x1, Pallas kernels: 0.36 us -> 2.16 us  [near_part(): pl.pallas_call(near_kernel, out_shape=state, in_specs=[SM] + [VM] * 6, ou...]
    ppermute x1, waiting for transfers between devices: 1.88 us -> 0.08 us  [near_part(): near_side = lax.ppermute(near, 'seq', SWAP)]
    all_to_all x1, waiting for transfers between devices: 16.5 us -> 17.5 us  [per_device(): lax.all_to_all(send, 'seq', split_axis=0, concat_axis=0, tiled=True, axis...]
  transfers between devices with their start and end apart: 8 -> 8, of which waited for: 8 -> 8; matrix products, arithmetic and copies ran while one was open for 0% -> 0% of each run, Pallas kernels for 5% -> 7%
where the time goes in v26:
time: 95.3 us; the launch traced here: 93.4 us
  waiting for transfers between devices  37 us (39%)
  starting transfers between devices  29.7 us (31%)
  blocking collectives  15.7 us (16%)
  Pallas kernels  8.93 us (9%)
  other arithmetic  1.07 us (1%)
    all_to_all x1, waiting for transfers between devices, per_device(): lax.all_to_all(send, 'seq', split_axis=0, concat_axis=0, tiled=True, axis...  17.5 us
    all_to_all x1, blocking collectives, per_device(): lax.all_to_all(out.reshape(8, ROWS // 8, GROUP * D), 'head', split_axis=0...  15.7 us
    all_to_all x1, starting transfers between devices, per_device(): lax.all_to_all(wide, 'head', split_axis=0, concat_axis=0, tiled=True)  10.3 us
    all_to_all x1, starting transfers between devices, per_device(): lax.all_to_all(send, 'seq', split_axis=0, concat_axis=0, tiled=True, axis...  7.23 us
    all_to_all x1, waiting for transfers between devices, per_device(): lax.all_to_all(wide, 'head', split_axis=0, concat_axis=0, tiled=True)  6.23 us
    ppermute x1, waiting for transfers between devices, per_device(): lax.ppermute(jnp.concatenate([own, page, two_page], axis=0), 'seq', x_rin...  3.93 us
    ppermute x1, waiting for transfers between devices, per_device(): two_page = lax.ppermute(page, 'seq', x_ring(2))  3.7 us
    pallas_call x1, Pallas kernels, near_part(): pl.pallas_call(near_side_kernel, out_shape=state, in_specs=[SM, SM] + [VM...  3.5 us
  transfers between devices with their start and end apart: 8, of which 8 were waited for; matrix products, arithmetic and copies ran while one was open for 0% of the time, Pallas kernels for 7%

profile of v26, /device:TPU:6, one launch (start us, length us, event | category | flops | bytes accessed | tf_op | source)
XLA Modules:
  0.0 93.4 jit_solution(4333854564521787284)
XLA Ops:
  0.0 0.0 copy-start
  0.0 1.8 %by_head.1 = bf16[8,16,1280]{2,1,0:T(8,128)(2,1)} custom-call(bf16[16,8,1024]{2,1,0:T(8,128)(2,1)} %q_ref.1, bf16[16,8,256]{2,1,0:T(8,128)(2,1)} %kv_ref.1), custom_call_target="tpu_custom_call" | custom-call | tf_op jit(solution)/shard_map/by_head/pallas_call | solution.py:194
  1.8 10.3 %all-to-all-start = ((bf16[8,16,1280]{2,1,0:T(8,128)(2,1)}), bf16[8,16,1280]{2,1,0:T(8,128)(2,1)S(1)}, u32[]{:S(2)}, u32[]{:S(2)}) async-start(bf16[8,16,1280]{2,1,0:T(8,128)(2,1)} %by_head.1), calls=%async_computation | async-start | bytes 655360 | tf_op jit(solution)/shard_map/all_to_all | solution.py:201
  12.1 0.0 copy-done
  12.1 3.3 %collective-permute-start.1 = (bf16[16,256]{1,0:T(8,128)(2,1)S(1)}, bf16[16,256]{1,0:T(8,128)(2,1)S(1)}, u32[]{:S(2)}, u32[]{:S(2)}) collective-permute-start(bf16[16,256]{1,0:T(8,128)(2,1)S(1)} %bitcast.18), channel_id=1, source_target_pairs={{0,256},{8,264},{16,272},{24,280},{32,288},{40,296},{48,304},{56,3... | collective-permute-start | bytes 24584 | tf_op jit(solution)/shard_map/ppermute | solution.py:202
  15.4 3.7 %collective-permute-done.1 = bf16[16,256]{1,0:T(8,128)(2,1)S(1)} collective-permute-done((bf16[16,256]{1,0:T(8,128)(2,1)S(1)}, bf16[16,256]{1,0:T(8,128)(2,1)S(1)}, u32[]{:S(2)}, u32[]{:S(2)}) %collective-permute-start.1) | collective-permute-done | bytes 8224 | tf_op jit(solution)/shard_map/ppermute | solution.py:202
  19.1 6.2 %all-to-all-done = bf16[8,16,1280]{2,1,0:T(8,128)(2,1)S(1)} async-done(((bf16[8,16,1280]{2,1,0:T(8,128)(2,1)}), bf16[8,16,1280]{2,1,0:T(8,128)(2,1)S(1)}, u32[]{:S(2)}, u32[]{:S(2)}) %all-to-all-start) | async-done | bytes 327712 | tf_op jit(solution)/shard_map/all_to_all | solution.py:201
  25.4 2.4 %collective-permute-start.2 = (bf16[160,256]{1,0:T(8,128)(2,1)S(1)}, bf16[160,256]{1,0:T(8,128)(2,1)S(1)}, u32[]{:S(2)}, u32[]{:S(2)}) collective-permute-start(bf16[160,256]{1,0:T(8,128)(2,1)S(1)} %pad_maximum_fusion.1), channel_id=1, source_target_pairs={{0,128},{8,136},{16,144},{24,152},{32,160},{40,168},{48,176},{56,1... | collective-permute-start | bytes 245768 | tf_op jit(solution)/shard_map/ppermute | solution.py:205
  27.8 3.9 %collective-permute-done.2 = bf16[160,256]{1,0:T(8,128)(2,1)S(1)} collective-permute-done((bf16[160,256]{1,0:T(8,128)(2,1)S(1)}, bf16[160,256]{1,0:T(8,128)(2,1)S(1)}, u32[]{:S(2)}, u32[]{:S(2)}) %collective-permute-start.2) | collective-permute-done | bytes 81952 | tf_op jit(solution)/shard_map/ppermute | solution.py:205
  31.7 0.1 broadcast_select_fusion
  31.9 0.9 %pad_maximum_fusion = bf16[8,192,256]{2,1,0:T(8,128)(2,1)} fusion(bf16[8,64,256]{2,1,0:T(8,128)(2,1)S(1)} %broadcast_in_dim.36, bf16[8,128,256]{2,1,0:T(8,128)(2,1)S(1)} %broadcast_select_fusion), kind=kLoop, calls=%fused_computation | loop fusion | flops 1572864 | bytes 1572864 | tf_op jit(solution)/shard_map/concatenate | solution.py:209
  32.8 7.2 %all-to-all-start.1 = ((bf16[8,192,256]{2,1,0:T(8,128)(2,1)}), bf16[8,192,256]{2,1,0:T(8,128)(2,1)S(1)}, u32[]{:S(2)}, u32[]{:S(2)}) async-start(bf16[8,192,256]{2,1,0:T(8,128)(2,1)} %pad_maximum_fusion), calls=%async_computation.1 | async-start | bytes 1572864 | tf_op jit(solution)/shard_map/all_to_all | solution.py:210
  40.1 0.0 copy-start.2
  40.1 1.3 %collective-permute-start.3 = (bf16[128,256]{1,0:T(8,128)(2,1)S(1)}, bf16[128,256]{1,0:T(8,128)(2,1)S(1)}, u32[]{:S(2)}, u32[]{:S(2)}) collective-permute-start(bf16[128,256]{1,0:T(8,128)(2,1)S(1)} %slice.15.mine_ref), channel_id=1, source_target_pairs={{0,8},{16,24},{32,40},{48,56},{64,72},{80,88},{96,104},{112,120},{... | collective-permute-start | bytes 196616 | tf_op jit(solution)/shard_map/ppermute | solution.py:212
  41.4 0.9 collective-permute-done.3.side_ref
  42.2 0.0 copy-done.1
  42.2 0.7 own_chip.1
  42.9 17.5 %all-to-all-done.1 = bf16[8,192,256]{2,1,0:T(8,128)(2,1)S(1)} async-done(((bf16[8,192,256]{2,1,0:T(8,128)(2,1)}), bf16[8,192,256]{2,1,0:T(8,128)(2,1)S(1)}, u32[]{:S(2)}, u32[]{:S(2)}) %all-to-all-start.1) | async-done | bytes 786464 | tf_op jit(solution)/shard_map/all_to_all | solution.py:210
  60.5 1.3 %collective-permute-start.4 = (bf16[8,128,256]{2,1,0:T(8,128)(2,1)S(1)}, bf16[8,128,256]{2,1,0:T(8,128)(2,1)S(1)}, u32[]{:S(2)}, u32[]{:S(2)}) collective-permute-start(bf16[8,128,256]{2,1,0:T(8,128)(2,1)S(1)} %slice.19), channel_id=1, source_target_pairs={{0,128},{8,136},{16,144},{24,152},{32,160},{40,168},{48,176},{56,1... | collective-permute-start | bytes 1572872 | tf_op jit(solution)/shard_map/ppermute | solution.py:231
  61.8 0.0 copy-done.2
  61.8 7.7 %conditional.1 = ((f32[1,1024]{1,0:T(1,128)S(1)}, f32[1,1024]{1,0:T(1,128)S(1)}, f32[128,1024]{1,0:T(8,128)S(1)})) conditional(s32[]{:T(128)} %convert_element_type.3, (f32[1,1024]{1,0:T(1,128)S(1)}, f32[1,1024]{1,0:T(1,128)S(1)}, f32[128,1024]{1,0:T(8,128)S(1)}) %tuple.18, (s32[1,32]{1,0:T(1,128)S(1)}, bf16[8,192,256]{2,1,0:T(8,128)(2,1)S(1)}, ...), branch_computations={%region_0.1_spmd, %region_1.2_spmd} | conditional | flops 1342177280 | bytes 5242928 | solution.py:257
  61.8 1.9 %collective-permute-start = (bf16[1536,256]{1,0:T(8,128)(2,1)S(1)}, bf16[1536,256]{1,0:T(8,128)(2,1)S(1)}, u32[]{:S(2)}, u32[]{:S(2)}) collective-permute-start(bf16[1536,256]{1,0:T(8,128)(2,1)S(1)} %bitcast.14), channel_id=1, source_target_pairs={{0,8},{8,0},{16,24},{24,16},{32,40},{40,32},{48,56},{56,48},{64,72... | collective-permute-start | bytes 2359304 | tf_op jit(solution)/shard_map/cond/branch_1_fun/ppermute | solution.py:236
  63.7 2.2 %near_window.1 = (f32[1,1024]{1,0:T(1,128)S(1)}, f32[1,1024]{1,0:T(1,128)S(1)}, f32[128,1024]{1,0:T(8,128)S(1)}) custom-call(s32[1]{0:T(128)} %get-tuple-element.27.meta_ref, bf16[1536,256]{1,0:T(8,128)(2,1)S(1)} %bitcast.15, s32[64,128]{1,0:T(8,128)S(1)} %get-tuple-element.30.ids_ref, bf16[256,1024]{1,0:T(8,128)(2,1)S(1)} %get-tuple-element.31.qt_ref, ...), custom_call_target="tpu_custom_call" | custom-call | flops 536870912 | bytes 1048576 | tf_op jit(solution)/shard_map/cond/branch_1_fun/near_window/pallas_call | solution.py:237
  65.9 0.1 collective-permute-done.side_ref
  66.0 3.5 %near_other_core_and_prefix.1 = (f32[1,1024]{1,0:T(1,128)S(1)}, f32[1,1024]{1,0:T(1,128)S(1)}, f32[128,1024]{1,0:T(8,128)S(1)}) custom-call(s32[1]{0:T(128)} %get-tuple-element.27.meta_ref, s32[32]{0:T(128)S(1)} %bitcast.25, bf16[1536,256]{1,0:T(8,128)(2,1)S(1)} %bitcast.16, bf16[1536,256]{1,0:T(8,128)(2,1)S(1)} %collective-permute-done.side_ref, ...), custom_call_target="tpu_custom_call" | custom-call | flops 805306368 | bytes 1048576 | tf_op jit(solution)/shard_map/cond/branch_1_fun/near_other_core_and_prefix/pallas_call | solution.py:246
  69.5 3.2 %collective-permute-done.4 = bf16[8,128,256]{2,1,0:T(8,128)(2,1)S(1)} collective-permute-done((bf16[8,128,256]{2,1,0:T(8,128)(2,1)S(1)}, bf16[8,128,256]{2,1,0:T(8,128)(2,1)S(1)}, u32[]{:S(2)}, u32[]{:S(2)}) %collective-permute-start.4) | collective-permute-done | bytes 524320 | tf_op jit(solution)/shard_map/ppermute | solution.py:231
  72.6 1.9 %collective-permute-start.5 = (bf16[1024,256]{1,0:T(8,128)(2,1)S(1)}, bf16[1024,256]{1,0:T(8,128)(2,1)S(1)}, u32[]{:S(2)}, u32[]{:S(2)}) collective-permute-start(bf16[1024,256]{1,0:T(8,128)(2,1)S(1)} %bitcast.12), channel_id=1, source_target_pairs={{128,136},{136,128},{144,152},{152,144},{160,168},{168,160},{176,1... | collective-permute-start | bytes 1572872 | tf_op jit(solution)/shard_map/ppermute | solution.py:260
  74.6 0.4 far_window.1
  74.9 1.5 %collective-permute-done.5.kv_ref = bf16[1024,256]{1,0:T(8,128)(2,1)S(1)} collective-permute-done((bf16[1024,256]{1,0:T(8,128)(2,1)S(1)}, bf16[1024,256]{1,0:T(8,128)(2,1)S(1)}, u32[]{:S(2)}, u32[]{:S(2)}) %collective-permute-start.5) | collective-permute-done | bytes 524320 | tf_op jit(solution)/shard_map/ppermute | solution.py:260
  76.4 0.5 far_other_core.1
  76.9 15.7 %all_to_all.15 = bf16[8,16,1024]{2,1,0:T(8,128)(2,1)S(1)} all-to-all(bf16[8,16,1024]{2,1,0:T(8,128)(2,1)S(1)} %bitcast.11), channel_id=1, replica_groups=mesh['seq'=64,'head'=8] {'head'}, dimensions={0} | all-to-all | bytes 524288 | tf_op jit(solution)/shard_map/all_to_all | solution.py:284
  92.6 0.9 copy.8
  (9 shorter events, 0.1 us)
Async XLA Ops:
  0.0 12.1 %copy-start = (bf16[1,16,1,256]{3,1,2,0:T(8,128)(2,1)S(1)}, bf16[1,16,1,256]{3,1,2,0:T(8,128)(2,1)}, u32[]{:S(2)}) copy-start(bf16[1,16,1,256]{3,1,2,0:T(8,128)(2,1)} %param.10) | copy-start | bytes 24580
  1.8 23.6 %all-to-all-start = ((bf16[8,16,1280]{2,1,0:T(8,128)(2,1)}), bf16[8,16,1280]{2,1,0:T(8,128)(2,1)S(1)}, u32[]{:S(2)}, u32[]{:S(2)}) async-start(bf16[8,16,1280]{2,1,0:T(8,128)(2,1)} %by_head.1), calls=%async_computation | async-start | bytes 655360 | tf_op jit(solution)/shard_map/all_to_all | solution.py:201
  12.1 7.0 %collective-permute-start.1 = (bf16[16,256]{1,0:T(8,128)(2,1)S(1)}, bf16[16,256]{1,0:T(8,128)(2,1)S(1)}, u32[]{:S(2)}, u32[]{:S(2)}) collective-permute-start(bf16[16,256]{1,0:T(8,128)(2,1)S(1)} %bitcast.18), channel_id=1, source_target_pairs={{0,256},{8,264},{16,272},{24,280},{32,288},{40,296},{48,304},{56,3... | collective-permute-start | bytes 24584 | tf_op jit(solution)/shard_map/ppermute | solution.py:202
  25.4 6.3 %collective-permute-start.2 = (bf16[160,256]{1,0:T(8,128)(2,1)S(1)}, bf16[160,256]{1,0:T(8,128)(2,1)S(1)}, u32[]{:S(2)}, u32[]{:S(2)}) collective-permute-start(bf16[160,256]{1,0:T(8,128)(2,1)S(1)} %pad_maximum_fusion.1), channel_id=1, source_target_pairs={{0,128},{8,136},{16,144},{24,152},{32,160},{40,168},{48,176},{56,1... | collective-permute-start | bytes 245768 | tf_op jit(solution)/shard_map/ppermute | solution.py:205
  32.8 9.4 %copy-start.1 = (s32[8192]{0:T(1024)S(1)}, s32[8192]{0:T(1024)}, u32[]{:S(2)}) copy-start(s32[8192]{0:T(1024)} %param.9) | copy-start | bytes 98308
  32.8 27.6 %all-to-all-start.1 = ((bf16[8,192,256]{2,1,0:T(8,128)(2,1)}), bf16[8,192,256]{2,1,0:T(8,128)(2,1)S(1)}, u32[]{:S(2)}, u32[]{:S(2)}) async-start(bf16[8,192,256]{2,1,0:T(8,128)(2,1)} %pad_maximum_fusion), calls=%async_computation.1 | async-start | bytes 1572864 | tf_op jit(solution)/shard_map/all_to_all | solution.py:210
  40.1 21.7 %copy-start.2 = (s32[1,32]{1,0:T(1,128)S(1)}, s32[1,32]{1,0:T(1,128)}, u32[]{:S(2)}) copy-start(s32[1,32]{1,0:T(1,128)} %param.11) | copy-start | bytes 388
  40.1 2.2 %collective-permute-start.3 = (bf16[128,256]{1,0:T(8,128)(2,1)S(1)}, bf16[128,256]{1,0:T(8,128)(2,1)S(1)}, u32[]{:S(2)}, u32[]{:S(2)}) collective-permute-start(bf16[128,256]{1,0:T(8,128)(2,1)S(1)} %slice.15.mine_ref), channel_id=1, source_target_pairs={{0,8},{16,24},{32,40},{48,56},{64,72},{80,88},{96,104},{112,120},{... | collective-permute-start | bytes 196616 | tf_op jit(solution)/shard_map/ppermute | solution.py:212
  60.5 12.2 %collective-permute-start.4 = (bf16[8,128,256]{2,1,0:T(8,128)(2,1)S(1)}, bf16[8,128,256]{2,1,0:T(8,128)(2,1)S(1)}, u32[]{:S(2)}, u32[]{:S(2)}) collective-permute-start(bf16[8,128,256]{2,1,0:T(8,128)(2,1)S(1)} %slice.19), channel_id=1, source_target_pairs={{0,128},{8,136},{16,144},{24,152},{32,160},{40,168},{48,176},{56,1... | collective-permute-start | bytes 1572872 | tf_op jit(solution)/shard_map/ppermute | solution.py:231
  61.8 4.2 %collective-permute-start = (bf16[1536,256]{1,0:T(8,128)(2,1)S(1)}, bf16[1536,256]{1,0:T(8,128)(2,1)S(1)}, u32[]{:S(2)}, u32[]{:S(2)}) collective-permute-start(bf16[1536,256]{1,0:T(8,128)(2,1)S(1)} %bitcast.14), channel_id=1, source_target_pairs={{0,8},{8,0},{16,24},{24,16},{32,40},{40,32},{48,56},{56,48},{64,72... | collective-permute-start | bytes 2359304 | tf_op jit(solution)/shard_map/cond/branch_1_fun/ppermute | solution.py:236
  72.6 3.8 %collective-permute-start.5 = (bf16[1024,256]{1,0:T(8,128)(2,1)S(1)}, bf16[1024,256]{1,0:T(8,128)(2,1)S(1)}, u32[]{:S(2)}, u32[]{:S(2)}) collective-permute-start(bf16[1024,256]{1,0:T(8,128)(2,1)S(1)} %bitcast.12), channel_id=1, source_target_pairs={{128,136},{136,128},{144,152},{152,144},{160,168},{168,160},{176,1... | collective-permute-start | bytes 1572872 | tf_op jit(solution)/shard_map/ppermute | solution.py:260
